TPU v7x, 256 devices: a whole 4x4x8 slice. The times are simulated.
256 devices in a mesh: section: 32 (over x_hi, z, core), tensor: 2 (over x_lo), dp: 4 (over y).
Axes of the slice: x: 4 (x_hi: 2, x_lo: 2; x = x_hi * 2 + x_lo), y: 4, z: 8, core: 2. Of those that a mesh axis runs over, the one named last changes fastest.
Arguments:
- queries: bfloat16 [32, 12, 128, 4096], P('section', 'dp', None, 'tensor'), may hold values from -6 to 6
- context_gradient: bfloat16 [32, 12, 128, 4096], P('section', 'dp', None, 'tensor'), may hold values from -0.59765625 to 0.59765625
- vision_feature_states: bfloat16 [12, 64, 8192], P('dp', 'section', 'tensor'), may hold values from -6 to 6
- key_value_weight: bfloat16 [32, 2, 8192, 512], P('section', None, None, 'tensor'), may hold values from -0.0625 to 0.0625
- adapter_down_maps: bfloat16 [32, 2, 16, 8192], P('section'), may hold values from -0.0625 to 0.0625
- adapter_up_maps: bfloat16 [32, 2, 16, 512], P('section'), may hold values from -0.375 to 0.375
- norm_gain_pair: bfloat16 [32, 2, 128], P('section'), may hold values from 0.5 to 1.5
- image_tile_count: int32 [12], P('dp'), may hold values from 1 to 4
- text_start_position: int32 [12], P('dp'), may hold values from 0 to 63
Outputs:
- vision_grad: float32 [12, 64, 8192], P('dp', 'section', 'tensor')
- down_grad: float32 [32, 2, 16, 8192], P('section')
- up_grad: float32 [32, 2, 16, 512], P('section')
All inputs are finite; a program needn't handle non-finite values.
Results may differ from a plain program's by a relative error of at most 0.03.
Values may be sent and summed in bfloat16 or wider, within the bound.
No kernel may reach another device: no remote copies, remote signals or barrier semaphores. Data moves between devices by JAX's collectives and lax.ppermute only.
A program may use at most 128 MiB of HBM per device.

v0:
```python
import jax
import jax.numpy as jnp
from jax import lax
from jax.sharding import PartitionSpec as P

TILES = 4


ADAPTER_SCALE = 2.0
EPS = 1e-05


def mult_narrow(pattern, first_op, second_op):
    return jnp.einsum(pattern, first_op, second_op, preferred_element_type=jnp.float32)


def section_terms(
    vision_rows,
    layer_weights,
    down_projection,
    up_map_shard,
    norm_gains,
    queries,
    context_gradient,
    count,
    start,
    matrix_product,
):
    head_dim = norm_gains.shape[1]
    kv_width = layer_weights.shape[2]
    kv_heads = kv_width // head_dim
    q_heads = queries.shape[1] // head_dim
    group_size = q_heads // kv_heads
    text_len = queries.shape[0]
    vision_len = vision_rows.shape[0]
    tile_len = vision_len // TILES
    reduced_gradient = matrix_product("vd,crd->cvr", vision_rows, down_projection).astype(
        jnp.bfloat16
    )
    projected_states = matrix_product(
        "xo,noj->nxj", vision_rows, layer_weights
    ) + ADAPTER_SCALE * matrix_product("uqy,uyi->uqi", reduced_gradient, up_map_shard)
    key_raw = projected_states[0].reshape(vision_len, kv_heads, head_dim)
    key_scale = lax.rsqrt(jnp.mean(key_raw * key_raw, axis=-1, keepdims=True) + EPS)
    key_gain = norm_gains[1].astype(jnp.float32)
    unit_keys = key_raw * key_scale
    key_heads = (unit_keys * key_gain).astype(jnp.bfloat16)
    value_heads = projected_states[1].astype(jnp.bfloat16).reshape(vision_len, kv_heads, head_dim)
    query_raw = queries.astype(jnp.float32).reshape(text_len, kv_heads, group_size, head_dim)
    query_scale = lax.rsqrt(jnp.mean(query_raw * query_raw, axis=-1, keepdims=True) + EPS)
    normed = (query_raw * query_scale * norm_gains[0].astype(jnp.float32)).astype(jnp.bfloat16)
    scores = matrix_product("tkgh,vkh->kgtv", normed, key_heads) * head_dim ** (-0.5)
    key_allowed = jnp.arange(vision_len) < count * tile_len
    row_allowed = (jnp.arange(text_len) >= start).astype(jnp.float32)
    weighted = jnp.where(key_allowed, jnp.exp(scores), 0.0)
    denominator = jnp.sum(weighted, axis=-1, keepdims=True)
    attention = weighted / denominator * row_allowed[:, None]
    attention_low = attention.astype(jnp.bfloat16)
    grad_context = context_gradient.reshape(text_len, kv_heads, group_size, head_dim)
    grad_probs = matrix_product("tkgh,vkh->kgtv", grad_context, value_heads)
    grad_scores = (
        attention
        * (grad_probs - jnp.sum(attention * grad_probs, axis=-1, keepdims=True))
        * head_dim ** (-0.5)
    )
    grad_scores_low = grad_scores.astype(jnp.bfloat16)
    grad_keys = matrix_product("kgtv,tkgh->vkh", grad_scores_low, normed)
    grad_values = matrix_product("kgtv,tkgh->vkh", attention_low, grad_context)
    gain_grad = grad_keys * key_gain
    grad_key_raw = key_scale * (
        gain_grad - unit_keys * jnp.mean(gain_grad * unit_keys, axis=-1, keepdims=True)
    )
    unnormed_gradient = jnp.stack(
        [grad_key_raw.reshape(vision_len, kv_width), grad_values.reshape(vision_len, kv_width)]
    ).astype(jnp.bfloat16)
    up_map_gradient = ADAPTER_SCALE * matrix_product(
        "lha,lhq->laq", reduced_gradient, unnormed_gradient
    )
    middle_product = matrix_product("cvw,crw->cvr", unnormed_gradient, up_map_shard).astype(
        jnp.bfloat16
    )
    down_map_gradient = ADAPTER_SCALE * matrix_product("npz,py->nzy", middle_product, vision_rows)
    vision_gradient = matrix_product(
        "osx,okx->sk", unnormed_gradient, layer_weights
    ) + ADAPTER_SCALE * matrix_product("ugq,uqe->ge", middle_product, down_projection)
    return (vision_gradient, down_map_gradient, up_map_gradient)


def place_columns(up_map_gradient, complete_width, first_column):
    widened = jnp.zeros(
        (up_map_gradient.shape[0], up_map_gradient.shape[1], complete_width), jnp.float32
    )
    return lax.dynamic_update_slice_in_dim(widened, up_map_gradient, first_column, 2)


def per_device(
    queries,
    context_gradient,
    vision_feature_states,
    key_value_weight,
    adapter_down_maps,
    adapter_up_maps,
    norm_gain_pair,
    image_tile_count,
    text_start_position,
):
    layer_weights = key_value_weight[0]
    down_projection = adapter_down_maps[0]
    norm_gains = norm_gain_pair[0]
    shard_width = layer_weights.shape[2]
    complete_width = adapter_up_maps.shape[3]
    first_column = lax.axis_index("tensor") * shard_width
    up_map_shard = lax.dynamic_slice_in_dim(adapter_up_maps[0], first_column, shard_width, 2)
    micro_count = vision_feature_states.shape[0]
    down_total = jnp.zeros(down_projection.shape, jnp.float32)
    up_partial = jnp.zeros(up_map_shard.shape, jnp.float32)
    own_grads = []
    for micro_index in range(micro_count):
        shard_rows = vision_feature_states[micro_index]
        row_block = lax.all_gather(shard_rows, "section", axis=0, tiled=True)
        vision_rows = lax.all_gather(row_block, "tensor", axis=1, tiled=True)
        vision_gradient, down_map_gradient, up_map_gradient = section_terms(
            vision_rows,
            layer_weights,
            down_projection,
            up_map_shard,
            norm_gains,
            queries[0, micro_index],
            context_gradient[0, micro_index],
            image_tile_count[micro_index],
            text_start_position[micro_index],
            mult_narrow,
        )
        summed = lax.psum_scatter(
            vision_gradient.astype(jnp.bfloat16), "section", scatter_dimension=0, tiled=True
        )
        own_grad = lax.psum_scatter(summed, "tensor", scatter_dimension=1, tiled=True).astype(
            jnp.float32
        )
        own_grads.append(own_grad)
        down_total = down_total + down_map_gradient
        up_partial = up_partial + up_map_gradient
    down_total, up_total = (
        lax.psum(down_total.astype(jnp.bfloat16), ("tensor", "dp")).astype(jnp.float32),
        lax.psum(
            place_columns(up_partial, complete_width, first_column).astype(jnp.bfloat16),
            ("tensor", "dp"),
        ).astype(jnp.float32),
    )
    return (jnp.stack(own_grads), down_total[None], up_total[None])


def solution(mesh):
    in_specs = (
        P("section", "dp", None, "tensor"),
        P("section", "dp", None, "tensor"),
        P("dp", "section", "tensor"),
        P("section", None, None, "tensor"),
        P("section", None, None, None),
        P("section", None, None, None),
        P("section", None, None),
        P("dp"),
        P("dp"),
    )
    out_specs = (
        P("dp", "section", "tensor"),
        P("section", None, None, None),
        P("section", None, None, None),
    )
    return jax.shard_map(
        per_device, mesh=mesh, in_specs=in_specs, out_specs=out_specs, check_vma=False
    )
```

profile of v0, /device:TPU:24, one launch (start us, length us, event | category | flops | bytes accessed | tf_op | source)
XLA Modules:
  0.0 734.1 jit_solution(11453548163630325635)
XLA Ops:
  8.1 47.5 %all-gather = bf16[1,64,4096]{2,0,1:T(2,128)(2,1)S(1)} all-gather(bf16[1,2,4096]{2,0,1:T(2,128)(2,1)S(1)} %copy.192), channel_id=2, replica_groups=mesh['section'=32,'tensor'=2,'dp'=4] {'section'}, dimensions={1}, use_global_device_ids=true | all-gather | bytes 540672 | tf_op jit(solution)/shard_map/all_gather | solution.py:120
  57.1 39.9 %all-gather.2 = bf16[1,64,4096]{2,0,1:T(2,128)(2,1)S(1)} all-gather(bf16[1,2,4096]{2,0,1:T(2,128)(2,1)S(1)} %copy.194), channel_id=4, replica_groups=mesh['section'=32,'tensor'=2,'dp'=4] {'section'}, dimensions={1}, use_global_device_ids=true | all-gather | bytes 540672 | tf_op jit(solution)/shard_map/all_gather | solution.py:120
  98.5 41.3 %all-gather.4 = bf16[1,64,4096]{2,0,1:T(2,128)(2,1)S(1)} all-gather(bf16[1,2,4096]{2,0,1:T(2,128)(2,1)S(1)} %copy.196), channel_id=6, replica_groups=mesh['section'=32,'tensor'=2,'dp'=4] {'section'}, dimensions={1}, use_global_device_ids=true | all-gather | bytes 540672 | tf_op jit(solution)/shard_map/all_gather | solution.py:120
  141.2 1.6 convert_bitcast_fusion.2
  153.3 2.5 fusion.135
  155.7 2.0 copy.193
  160.2 2.0 copy.195
  165.6 2.8 multiply_convert_fusion.2
  168.5 1.7 convolution_convert_fusion.2
  170.2 4.9 fusion.51
  175.4 1.7 convolution_convert_fusion.1
  177.2 4.9 fusion.48
  183.6 1.7 convolution_convert_fusion
  185.4 5.0 fusion.45
  195.2 2.3 fusion.68
  201.3 1.6 multiply_reduce_fusion.10
  210.0 2.3 fusion.67
  216.1 1.6 multiply_reduce_fusion.8
  223.9 2.3 fusion.66
  238.5 7.3 fusion.9
  246.3 3.8 fusion.10
  250.5 3.6 fusion.11
  258.9 264.7 %all-reduce.9.cloned.1.call-done = (bf16[64,8192]{1,0:T(8,128)(2,1)}, bf16[64,8192]{1,0:T(8,128)(2,1)}, bf16[64,8192]{1,0:T(8,128)(2,1)}) async-done(((bf16[64,8192]{1,0:T(8,128)(2,1)}, bf16[64,8192]{1,0:T(8,128)(2,1)}, bf16[64,8192]{1,0:T(8,128)(2,1)}), (bf16[64,8192]{1,0:T(8,128)(2,1)}, bf16[64,8192]{1,0:T(8,128)(2,1)}, bf16[64,8192]{1,0:T(8,128)(2,1)})) %all-reduce.9.cloned.1.call-update) | async-done | bytes 3145744
  524.6 1.9 copy.188
  526.7 1.9 copy.190
  529.6 1.9 copy.186
  531.6 30.3 %psum.15 = bf16[1,2,16,512]{3,2,1,0:T(8,128)(2,1)S(1)} all-reduce(bf16[1,2,16,512]{3,2,1,0:T(8,128)(2,1)S(1)} %bitcast.296), channel_id=1, replica_groups=mesh['section'=32,'tensor'=2,'dp'=4] {'tensor','dp'}, use_global_device_ids=true, to_apply=%region_22.23 | all-reduce | flops 16384 | bytes 65536 | tf_op jit(solution)/shard_map/psum | solution.py:145
  562.5 40.5 %all-reduce.7.cloned.1.call-done = bf16[1,2,16,8192]{3,2,1,0:T(8,128)(2,1)} async-done(((bf16[1,2,16,8192]{3,2,1,0:T(8,128)(2,1)}), bf16[1,2,16,8192]{3,2,1,0:T(8,128)(2,1)}) %all-reduce.7.cloned.1.call-update) | async-done | bytes 524304 | tf_op jit(solution)/shard_map/psum | solution.py:144
  603.0 2.1 broadcast_in_dim.60
  605.1 38.8 %reduce-scatter.12.cloned.1.call-done = bf16[4096,2]{1,0:T(8,128)(2,1)} async-done(((bf16[8192,2]{1,0:T(8,128)(2,1)}), bf16[4096,2]{1,0:T(8,128)(2,1)}) %reduce-scatter.12.cloned.1.call-update) | async-done | bytes 16400
  645.6 39.0 %reduce-scatter.14.cloned.1.call-done = bf16[4096,2]{1,0:T(8,128)(2,1)} async-done(((bf16[8192,2]{1,0:T(8,128)(2,1)}), bf16[4096,2]{1,0:T(8,128)(2,1)}) %reduce-scatter.14.cloned.1.call-update) | async-done | bytes 16400
  686.1 38.8 %reduce-scatter.10.cloned.1.call-done = bf16[4096,2]{1,0:T(8,128)(2,1)} async-done(((bf16[8192,2]{1,0:T(8,128)(2,1)}), bf16[4096,2]{1,0:T(8,128)(2,1)}) %reduce-scatter.10.cloned.1.call-update) | async-done | bytes 16400
  (199 shorter events, 72.5 us)
Async XLA Ops:
  7.2 161.3 %copy-start = (bf16[1,2,16,8192]{3,2,1,0:T(8,128)(2,1)S(1)}, bf16[1,2,16,8192]{3,2,1,0:T(8,128)(2,1)}, u32[]{:S(2)}) copy-start(bf16[1,2,16,8192]{3,2,1,0:T(8,128)(2,1)} %param.13) | copy-start | bytes 1572868
  7.2 161.3 %all-gather.10.cloned.1.call-start = ((), (), s32[]{:S(2)}) async-start(), calls=%async_computation.4 | async-start | bytes 1572864 | tf_op jit(solution)/shard_map/all_gather | solution.py:121
  57.0 118.4 %all-gather.12.cloned.1.call-start = ((), (), s32[]{:S(2)}) async-start(), calls=%async_computation.5 | async-start | bytes 1572864 | tf_op jit(solution)/shard_map/all_gather | solution.py:121
  98.4 42.8 %copy-start.6 = (bf16[1,3,128,2048]{3,2,1,0:T(8,128)(2,1)S(1)}, bf16[1,3,128,2048]{3,2,1,0:T(8,128)(2,1)}, u32[]{:S(2)}) copy-start(bf16[1,3,128,2048]{3,2,1,0:T(8,128)(2,1)} %param.9) | copy-start | bytes 4718596
  98.4 85.2 %all-gather.14.cloned.1.call-start = ((), (), s32[]{:S(2)}) async-start(), calls=%async_computation.6 | async-start | bytes 1572864 | tf_op jit(solution)/shard_map/all_gather | solution.py:121
  141.1 382.4 %all-reduce.9.cloned.1.call-start = ((), (), s32[]{:S(2)}) async-start(), calls=%async_computation.10 | async-start | bytes 6291456
  145.6 3.4 copy-start.22
  145.6 4.0 copy-start.20
  145.6 5.8 copy-start.21
  168.4 1.7 copy-start.2
  170.2 5.0 copy-start.14
  170.2 5.0 copy-start.13
  175.4 6.7 copy-start.11
  175.4 1.7 copy-start.1
  183.6 1.7 copy-start.3
  185.3 6.5 slice-start.2
  185.3 6.8 copy-start.16
  185.4 6.8 copy-start.23
  185.4 9.0 %copy-start.27 = (f32[128]{0:T(128)S(1)}, f32[128]{0:T(128)}, u32[]{:S(2)}) copy-start(f32[128]{0:T(128)} %compare_convert_fusion.2) | copy-start | bytes 1540
  192.1 5.4 copy-start.19
  198.7 7.1 slice-start.3
  201.3 7.8 %copy-start.26 = (f32[128]{0:T(128)S(1)}, f32[128]{0:T(128)}, u32[]{:S(2)}) copy-start(f32[128]{0:T(128)} %compare_convert_fusion.1) | copy-start | bytes 1540
  212.3 3.8 copy-start.17
  216.0 7.0 copy-start.25
  220.4 5.8 copy-start.18
  234.5 4.0 copy-start.7
  238.0 8.2 %slice-start = ((s8[8388608]{0:T(1024)(128)(4,1)}), s8[4194304]{0:T(1024)(128)(4,1)S(1)}, s32[]{:S(2)}) async-start(s8[8388608]{0:T(1024)(128)(4,1)} %bitcast.273), calls=%async_computation.11 | async-start | bytes 8388608
  238.5 7.7 %slice-start.1 = ((s8[8388608]{0:T(1024)(128)(4,1)}), s8[4194304]{0:T(1024)(128)(4,1)S(1)}, s32[]{:S(2)}) async-start(s8[8388608]{0:T(1024)(128)(4,1)} %bitcast.273), calls=%async_computation.12 | async-start | bytes 8388608
  254.2 348.9 %all-reduce.7.cloned.1.call-start = ((), (), s32[]{:S(2)}) async-start(), calls=%async_computation.3 | async-start | bytes 1048576 | tf_op jit(solution)/shard_map/psum | solution.py:144
  258.8 385.2 %reduce-scatter.12.cloned.1.call-start = ((), (), s32[]{:S(2)}) async-start(), calls=%async_computation.8 | async-start | bytes 3145728
  526.5 158.0 %reduce-scatter.14.cloned.1.call-start = ((), (), s32[]{:S(2)}) async-start(), calls=%async_computation.9 | async-start | bytes 3145728
  528.6 196.4 %reduce-scatter.10.cloned.1.call-start = ((), (), s32[]{:S(2)}) async-start(), calls=%async_computation.7 | async-start | bytes 3145728
  (8 other events, 7.0 us)
Sparse Core Ops, SparseCore 0:
  57.2 22.3 all-gather.9
  98.5 23.4 all-gather.11
  141.3 20.5 all-gather.13
  254.3 269.2 all-reduce.8
  526.2 76.7 all-reduce.6
  605.4 38.5 reduce-scatter.11
  646.6 37.8 reduce-scatter.13
  687.0 37.8 reduce-scatter.9
where the time goes:
time: 737 us; the launch traced here: 734 us
  waiting for transfers between devices  422 us (57%)
  blocking collectives  159 us (22%)
  matrix products  60.4 us (8%)
  local copies, waits for them, and re-layouts  51.1 us (7%)
  other arithmetic  23.8 us (3%)
  between operations  17.4 us (2%)
    unnamed x12, waiting for transfers between devices  382 us
    all_gather x3, blocking collectives, per_device(): row_block = lax.all_gather(shard_rows, 'section', axis=0, tiled=True)  129 us
    dot_general x36, matrix products, mult_narrow(): jnp.einsum(pattern, first_op, second_op, preferred_element_type=jnp.float32)  60.4 us
    psum x1, waiting for transfers between devices, per_device(): lax.psum(down_total.astype(jnp.bfloat16), ('tensor', 'dp'))  40.5 us
    psum x1, blocking collectives, per_device(): lax.psum(place_columns(up_partial, complete_width, first_column).astype(j...  30.3 us
    unnamed x81, local copies, waits for them, and re-layouts  27.5 us
  transfers between devices with their start and end apart: 8, of which 5 were waited for; matrix products, arithmetic and copies ran while one was open for 8% of the time, Pallas kernels for 0%

commit v1 on v0

v1 whole, which is shorter than its diff:
```python
import jax
import jax.numpy as jnp
from jax import lax
from jax.sharding import PartitionSpec as P

TILES = 4
ADAPTER_SCALE = 2.0
EPS = 1e-05
PLANE = ("section", "tensor")
NZ = 8


def plane_pairs(route):
    def index(x, z, core):
        return (((x // 2) * NZ + z) * 2 + core) * 2 + x % 2

    return [
        (index(x, z, core), index(*route(x, z, core)))
        for x in range(4)
        for z in range(NZ)
        for core in range(2)
    ]


SIBLING = plane_pairs(lambda x, z, core: (x, z, 1 - core))
RISE = {
    k: plane_pairs(lambda x, z, core, k=k: (x, (z + (k if core == 0 else -k)) % NZ, core))
    for k in (1, 2, 3, 4)
}
FALL = {
    k: plane_pairs(lambda x, z, core, k=k: (x, (z - (k if core == 0 else -k)) % NZ, core))
    for k in (1, 2, 3, 4)
}
NEAR = plane_pairs(lambda x, z, core: (x ^ 1 if core == 0 else 3 - x, z, core))
FAR = plane_pairs(lambda x, z, core: (3 - x if core == 0 else x ^ 1, z, core))
TENSOR_SWAP = [(0, 1), (1, 0)]
DP_NEAR = [(i, i ^ 1) for i in range(4)]
DP_FAR = [(i, 3 - i) for i in range(4)]


def move(block, pairs):
    return lax.ppermute(block, PLANE, pairs)


def mm(pattern, first, second, precision=None):
    return jnp.einsum(
        pattern, first, second, preferred_element_type=jnp.float32, precision=precision
    )


def gather_rows(own):
    chip = jnp.concatenate([own, move(own, SIBLING)])
    parts = [move(chip, RISE[k]) for k in (1, 2, 3)] + [move(own, RISE[4]), own]
    base = jnp.concatenate(parts)
    first = move(base, NEAR)
    second = move(base, FAR)
    third = move(first, FAR)
    here = [base, third, first, second]
    there = [move(block, SIBLING) for block in here]
    return here, there


def row_tokens(x_hi, z, core, x_lo):
    def base_rows(chain, x_high):
        step = jnp.where(chain == 0, 1, -1)
        places = []
        for k in (1, 2, 3):
            for other in (0, 1):
                places.append(((z - step * k) % NZ, jnp.where(other == 0, chain, 1 - chain)))
        places += [((z - step * 4) % NZ, chain), (z, chain)]
        rows = []
        for level, which in places:
            token = ((x_high * NZ + level) * 2 + which) * 2
            for batch in range(3):
                rows += [batch * 64 + token, batch * 64 + token + 1]
        return jnp.stack(rows)

    own_half, other_half = [], []
    for chain in (core, 1 - core):
        own_half += [base_rows(chain, x_hi), base_rows(chain, 1 - x_hi)]
        near = jnp.where(chain == 0, x_hi, 1 - x_hi)
        other_half += [base_rows(chain, near), base_rows(chain, 1 - near)]
    return jnp.concatenate(own_half), jnp.concatenate(other_half)


def scatter_rows(here, there):
    f32, low = jnp.float32, jnp.bfloat16
    base, third, first, second = (
        mine.astype(f32) + move(theirs, SIBLING).astype(f32) for mine, theirs in zip(here, there)
    )
    first = first + move(third.astype(low), FAR).astype(f32)
    base = base + move(second.astype(low), FAR).astype(f32)
    base = base + move(first.astype(low), NEAR).astype(f32)
    sent = base[:42].astype(low)
    own = base[42:] + move(sent[36:42], FALL[4]).astype(f32)
    chip = sum(
        move(sent[12 * i : 12 * i + 12], FALL[k]).astype(f32) for i, k in enumerate((1, 2, 3))
    )
    return own + chip[:6] + move(chip[6:].astype(low), SIBLING).astype(f32)


def per_device(
    queries,
    context_gradient,
    vision_feature_states,
    key_value_weight,
    adapter_down_maps,
    adapter_up_maps,
    norm_gain_pair,
    image_tile_count,
    text_start_position,
):
    low, f32 = jnp.bfloat16, jnp.float32
    weights = key_value_weight[0]
    down_maps = adapter_down_maps[0]
    gains = norm_gain_pair[0].astype(f32)
    section, side = lax.axis_index("section"), lax.axis_index("tensor")
    width = weights.shape[2]
    up_maps = lax.dynamic_slice_in_dim(adapter_up_maps[0], side * width, width, 2)
    batches, _, half = vision_feature_states.shape
    head = gains.shape[1]
    kv_heads = width // head
    text = queries.shape[2]
    group = queries.shape[3] // width
    tokens = 64

    here, there = gather_rows(vision_feature_states.reshape(-1, half))
    own_rows = jnp.concatenate(here[:2] + there[:2])
    other_rows = jnp.concatenate(here[2:] + there[2:])
    own_token, other_token = row_tokens(section // 16, (section // 2) % NZ, section % 2, side)
    line = jnp.arange(batches * tokens)[:, None]
    own_map = (line == own_token[None]).astype(low)
    other_map = (line == other_token[None]).astype(low)

    own_w = lax.dynamic_slice_in_dim(weights, side * half, half, 1)
    other_w = lax.dynamic_slice_in_dim(weights, (1 - side) * half, half, 1)
    own_a = lax.dynamic_slice_in_dim(down_maps, side * half, half, 2)
    other_a = lax.dynamic_slice_in_dim(down_maps, (1 - side) * half, half, 2)

    def ordered(own, other):
        own = mm("vr,cro->cvo", own_map.astype(f32), own, lax.Precision.HIGHEST)
        return own + mm("vr,cro->cvo", other_map.astype(f32), other, lax.Precision.HIGHEST)

    reduced = ordered(
        mm("rf,caf->cra", own_rows, own_a), mm("rf,caf->cra", other_rows, other_a)
    ).astype(low)
    projected = ordered(
        mm("rf,cfo->cro", own_rows, own_w), mm("rf,cfo->cro", other_rows, other_w)
    ) + ADAPTER_SCALE * mm("cva,cao->cvo", reduced, up_maps)

    key_raw = projected[0].reshape(batches, tokens, kv_heads, head)
    key_scale = lax.rsqrt(jnp.mean(key_raw * key_raw, axis=-1, keepdims=True) + EPS)
    unit = key_raw * key_scale
    keys = (unit * gains[1]).astype(low)
    values = projected[1].astype(low).reshape(batches, tokens, kv_heads, head)
    query_raw = queries[0].astype(f32).reshape(batches, text, kv_heads, group, head)
    query_scale = lax.rsqrt(jnp.mean(query_raw * query_raw, axis=-1, keepdims=True) + EPS)
    normed = (query_raw * query_scale * gains[0]).astype(low)
    context = context_gradient[0].reshape(batches, text, kv_heads, group, head)
    scores = mm("bvkh,btkgh->bkvgt", keys, normed) * head ** (-0.5)
    allowed = jnp.arange(tokens)[None] < image_tile_count[:, None] * (tokens // TILES)
    live = (jnp.arange(text)[None] >= text_start_position[:, None]).astype(f32)
    weighted = jnp.where(allowed[:, None, :, None, None], jnp.exp(scores), 0.0)
    attention = weighted / jnp.sum(weighted, axis=2, keepdims=True) * live[:, None, None, None]
    grad_probs = mm("bvkh,btkgh->bkvgt", values, context)
    grad_scores = (
        attention
        * (grad_probs - jnp.sum(attention * grad_probs, axis=2, keepdims=True))
        * head ** (-0.5)
    ).astype(low)
    grad_keys = mm("bkvgt,btkgh->bvkh", grad_scores, normed)
    grad_values = mm("bkvgt,btkgh->bvkh", attention.astype(low), context)
    gain_grad = grad_keys * gains[1]
    grad_key_raw = key_scale * (
        gain_grad - unit * jnp.mean(gain_grad * unit, axis=-1, keepdims=True)
    )
    rows = batches * tokens
    grad_raw = jnp.stack(
        [grad_key_raw.reshape(rows, width), grad_values.reshape(rows, width)]
    ).astype(low)

    up_part = ADAPTER_SCALE * mm("cva,cvo->cao", reduced, grad_raw)
    middle = mm("cvo,cao->cva", grad_raw, up_maps).astype(low)

    def arrival(mapping, values):
        return mm("vr,cvo->cro", mapping, values).astype(low)

    pieces = []
    downs = []
    for mapping, w, a, x in (
        (own_map, own_w, own_a, own_rows),
        (other_map, other_w, other_a, other_rows),
    ):
        part, mid = arrival(mapping, grad_raw), arrival(mapping, middle)
        pieces.append(
            (
                mm("cro,cfo->rf", part, w) + ADAPTER_SCALE * mm("cra,caf->rf", mid, a)
            ).astype(low)
        )
        downs.append(ADAPTER_SCALE * mm("cra,rf->caf", mid, x))
    v_own, v_other = pieces
    cut = v_own.shape[0] // 4
    own_grad = scatter_rows(
        [v_own[:cut], v_own[cut : 2 * cut], v_other[:cut], v_other[cut : 2 * cut]],
        [v_own[2 * cut : 3 * cut], v_own[3 * cut :], v_other[2 * cut : 3 * cut], v_other[3 * cut :]],
    )

    ranks = 2 * down_maps.shape[1]
    down = downs[0] + lax.ppermute(downs[1].astype(low), "tensor", TENSOR_SWAP).astype(f32)
    sums = jnp.concatenate([down.reshape(ranks, half), up_part.reshape(ranks, width)], 1)
    for pairs in (DP_NEAR, DP_FAR):
        sums = sums.astype(low)
        sums = sums.astype(f32) + lax.ppermute(sums, "dp", pairs).astype(f32)
    sums = sums.astype(low)
    facing = lax.ppermute(sums, "tensor", TENSOR_SWAP)
    left = jnp.where(side == 0, sums, facing).astype(f32)
    right = jnp.where(side == 0, facing, sums).astype(f32)
    down_total = jnp.concatenate([left[:, :half], right[:, :half]], 1)
    up_total = jnp.concatenate([left[:, half:], right[:, half:]], 1)
    return (
        own_grad.reshape(vision_feature_states.shape),
        down_total.reshape(1, 2, ranks // 2, 2 * half),
        up_total.reshape(1, 2, ranks // 2, 2 * width),
    )


def solution(mesh):
    in_specs = (
        P("section", "dp", None, "tensor"),
        P("section", "dp", None, "tensor"),
        P("dp", "section", "tensor"),
        P("section", None, None, "tensor"),
        P("section", None, None, None),
        P("section", None, None, None),
        P("section", None, None),
        P("dp"),
        P("dp"),
    )
    out_specs = (
        P("dp", "section", "tensor"),
        P("section", None, None, None),
        P("section", None, None, None),
    )
    return jax.shard_map(
        per_device, mesh=mesh, in_specs=in_specs, out_specs=out_specs, check_vma=False
    )
```

time: 737 us -> 153 us (0.21)
  waiting for transfers between devices: 422 us -> 63.5 us
  blocking collectives: 159 us -> 0 us
  local copies, waits for them, and re-layouts: 51.1 us -> 17.2 us
  matrix products: 60.4 us -> 34.1 us
  starting transfers between devices: 0.33 us -> 26.5 us
  between operations: 17.4 us -> 1.25 us
  other arithmetic: 23.8 us -> 8.4 us
    unnamed x12 -> x0, waiting for transfers between devices: 382 us -> none
    all_gather x3 -> x0, blocking collectives: 129 us -> none  [per_device(): row_block = lax.all_gather(shard_rows, 'section', axis=0, tiled=True)]
    ppermute x0 -> x28, waiting for transfers between devices: none -> 63.5 us  [the longest x24 35.7 us: move(): return lax.ppermute(block, PLANE, pairs)]
    psum x1 -> x0, waiting for transfers between devices: 40.5 us -> none  [per_device(): lax.psum(down_total.astype(jnp.bfloat16), ('tensor', 'dp'))]
    psum x1 -> x0, blocking collectives: 30.3 us -> none  [per_device(): lax.psum(place_columns(up_partial, complete_width, first_column).astype(j...]
    ppermute x0 -> x28, starting transfers between devices: none -> 26.5 us  [the longest x24 24.5 us: move(): return lax.ppermute(block, PLANE, pairs)]
    dot_general x36 -> x23, matrix products: 60.4 us -> 34.1 us  [mm(): jnp.einsum(pattern, first, second, preferred_element_type=jnp.float32, pr...]
    unnamed x81 -> x39, local copies, waits for them, and re-layouts: 27.5 us -> 7.21 us
  transfers between devices with their start and end apart: 8 -> 28, of which waited for: 5 -> 14; matrix products, arithmetic and copies ran while one was open for 8% -> 13% of each run, Pallas kernels for 0% -> 0%
where the time goes in v1:
time: 153 us; the launch traced here: 151 us
  waiting for transfers between devices  63.5 us (42%)
  matrix products  34.1 us (22%)
  starting transfers between devices  26.5 us (17%)
  local copies, waits for them, and re-layouts  17.2 us (11%)
  other arithmetic  8.4 us (5%)
    ppermute x24, waiting for transfers between devices, move(): return lax.ppermute(block, PLANE, pairs)  35.7 us
    dot_general x23, matrix products, mm(): jnp.einsum(pattern, first, second, preferred_element_type=jnp.float32, pr...  34.1 us
    ppermute x24, starting transfers between devices, move(): return lax.ppermute(block, PLANE, pairs)  24.5 us
    ppermute x2, waiting for transfers between devices, per_device(): sums = sums.astype(f32) + lax.ppermute(sums, 'dp', pairs).astype(f32)  14.9 us
    unnamed x39, local copies, waits for them, and re-layouts  7.21 us
    ppermute x1, waiting for transfers between devices, per_device(): facing = lax.ppermute(sums, 'tensor', TENSOR_SWAP)  7.12 us
    ppermute x1, waiting for transfers between devices, per_device(): lax.ppermute(downs[1].astype(low), 'tensor', TENSOR_SWAP).astype(f32)  5.72 us
    concatenate x1, local copies, waits for them, and re-layouts, per_device(): own_rows = jnp.concatenate(here[:2] + there[:2])  4.4 us
  transfers between devices with their start and end apart: 28, of which 14 were waited for; matrix products, arithmetic and copies ran while one was open for 13% of the time, Pallas kernels for 0%

profile of v1, /device:TPU:24, one launch (start us, length us, event | category | flops | bytes accessed | tf_op | source)
XLA Modules:
  0.0 151.0 jit_solution(12844676214916724958)
XLA Ops:
  1.6 7.3 %collective-permute-start.4 = (bf16[6,4096]{1,0:T(8,128)(2,1)S(1)}, bf16[6,4096]{1,0:T(8,128)(2,1)S(1)}, u32[]{:S(2)}, u32[]{:S(2)}) collective-permute-start(bf16[6,4096]{1,0:T(8,128)(2,1)S(1)} %reshape.108), channel_id=1, source_target_pairs={{0,64},{8,72},{16,80},{24,88},{32,96},{40,104},{48,112},{56,120},{... | collective-permute-start | bytes 147464 | tf_op jit(solution)/shard_map/ppermute | solution.py:42
  8.9 1.8 %copy.73 = f32[48,8,16,128]{3,2,1,0:T(8,128)S(1)} copy(bf16[48,8,16,128]{3,1,2,0:T(8,128)(2,1)} %bitcast.584) | data formatting | bytes 4718592
  10.7 1.6 %copy-done.1 = f32[48,8,16,128]{3,2,1,0:T(8,128)} copy-done((f32[48,8,16,128]{3,2,1,0:T(8,128)}, f32[48,8,16,128]{3,2,1,0:T(8,128)S(1)}, u32[]{:S(2)}) %copy-start.1) | copy-done | bytes 3145752
  16.7 3.4 %collective-permute-done.1 = bf16[12,4096]{1,0:T(8,128)(2,1)S(1)} collective-permute-done((bf16[12,4096]{1,0:T(8,128)(2,1)S(1)}, bf16[12,4096]{1,0:T(8,128)(2,1)S(1)}, u32[]{:S(2)}, u32[]{:S(2)}) %collective-permute-start.1) | collective-permute-done | bytes 98336 | tf_op jit(solution)/shard_map/ppermute | solution.py:42
  20.1 5.5 %collective-permute-done.2 = bf16[12,4096]{1,0:T(8,128)(2,1)S(1)} collective-permute-done((bf16[12,4096]{1,0:T(8,128)(2,1)S(1)}, bf16[12,4096]{1,0:T(8,128)(2,1)S(1)}, u32[]{:S(2)}, u32[]{:S(2)}) %collective-permute-start.2) | collective-permute-done | bytes 98336 | tf_op jit(solution)/shard_map/ppermute | solution.py:42
  25.6 1.7 %collective-permute-done.3 = bf16[12,4096]{1,0:T(8,128)(2,1)S(1)} collective-permute-done((bf16[12,4096]{1,0:T(8,128)(2,1)S(1)}, bf16[12,4096]{1,0:T(8,128)(2,1)S(1)}, u32[]{:S(2)}, u32[]{:S(2)}) %collective-permute-start.3) | collective-permute-done | bytes 98336 | tf_op jit(solution)/shard_map/ppermute | solution.py:42
  29.4 2.1 %collective-permute-start.9 = (bf16[48,4096]{1,0:T(8,128)(2,1)S(1)}, bf16[48,4096]{1,0:T(8,128)(2,1)}, u32[]{:S(2)}, u32[]{:S(2)}) collective-permute-start(bf16[48,4096]{1,0:T(8,128)(2,1)S(1)} %concatenate.30), channel_id=1, source_target_pairs={{0,132},{8,12},{16,148},{24,28},{32,164},{40,44},{48,180},{56,60},... | collective-permute-start | bytes 1179656 | tf_op jit(solution)/shard_map/ppermute | solution.py:42
  31.5 3.4 %multiply_convert_fusion = bf16[3,128,2,8,128]{4,3,2,1,0:T(8,128)(2,1)} fusion(f32[3,128,2,8,128]{4,3,2,1,0:T(8,128)} %bitcast.578, f32[128]{0:T(128)S(1)} %get-tuple-element.17, f32[3,128,2,8]{3,2,1,0:T(2,128)S(1)} %copy.51), kind=kLoop, calls=%fused_computation.26 | loop fusion | flops 2359296 | bytes 4743680 | tf_op jit(solution)/shard_map/convert_element_type | solution.py:158
  34.9 1.6 %copy.74 = bf16[48,8,16,128]{3,2,1,0:T(8,128)(2,1)} copy(bf16[48,8,16,128]{3,1,2,0:T(8,128)(2,1)S(1)} %bitcast.583) | data formatting | bytes 3145728
  37.1 3.0 %collective-permute-done.5 = bf16[48,4096]{1,0:T(8,128)(2,1)} collective-permute-done((bf16[48,4096]{1,0:T(8,128)(2,1)S(1)}, bf16[48,4096]{1,0:T(8,128)(2,1)}, u32[]{:S(2)}, u32[]{:S(2)}) %collective-permute-start.5) | collective-permute-done | bytes 393248 | tf_op jit(solution)/shard_map/ppermute | solution.py:42
  40.9 8.4 %collective-permute-done.6 = bf16[48,4096]{1,0:T(8,128)(2,1)S(1)} collective-permute-done((bf16[48,4096]{1,0:T(8,128)(2,1)}, bf16[48,4096]{1,0:T(8,128)(2,1)S(1)}, u32[]{:S(2)}, u32[]{:S(2)}) %collective-permute-start.6) | collective-permute-done | bytes 393248 | tf_op jit(solution)/shard_map/ppermute | solution.py:42
  49.3 2.0 %convolution_bitcast_fusion.4 = f32[2,192,16]{1,2,0:T(8,128)S(1)} fusion(bf16[1,2,16,8192]{3,2,1,0:T(8,128)(2,1)S(1)} %copy-done, s32[]{:T(128)S(6)} %select_n.259, bf16[48,4096]{1,0:T(8,128)(2,1)S(1)} %collective-permute-done.11, bf16[48,4096]{1,0:T(8,128)(2,1)S(1)} %collective-permute-done.10, bf16[48,4096]{1,0:T(8,128)(2,1)} %collective-permute-done.9, ...), kind=kOutput, calls=%fused_computation.69 | convolution fusion | flops 56623104 | bytes 1859588 | tf_op jit(solution)/shard_map/rf,caf->cra/dot_general | solution.py:46
  51.4 4.2 %fusion.45 = f32[2,192,256]{2,1,0:T(8,128)} fusion(bf16[1,2,8192,256]{3,2,1,0:T(8,128)(2,1)} %param.12, s32[]{:T(128)S(6)} %select_n.259, bf16[48,4096]{1,0:T(8,128)(2,1)S(1)} %collective-permute-done.11, bf16[48,4096]{1,0:T(8,128)(2,1)S(1)} %collective-permute-done.10, bf16[48,4096]{1,0:T(8,128)(2,1)} %collective-permute-done.9, ...), kind=kOutput, calls=%fused_computation.55 | convolution fusion | flops 811597824 | bytes 6160388 | tf_op jit(solution)/shard_map/rf,cfo->cro/dot_general | solution.py:46
  56.3 4.4 %concatenate.31 = bf16[192,4096]{1,0:T(8,128)(2,1)S(1)} concatenate(bf16[12,4096]{1,0:T(8,128)(2,1)S(1)} %collective-permute-done.1, bf16[12,4096]{1,0:T(8,128)(2,1)S(1)} %collective-permute-done.2, bf16[12,4096]{1,0:T(8,128)(2,1)S(1)} %collective-permute-done.3, bf16[6,4096]{1,0:T(8,128)(2,1)S(1)} %collective-permute-done.4, bf16[6,4096]{1,0:T(8,128)(2,1)S(1)} %reshape.108, ...), dimensions={0} | concatenate | bytes 3145728 | tf_op jit(solution)/shard_map/concatenate | solution.py:128
  61.3 3.2 %fusion.40 = f32[2,192,256]{2,1,0:T(8,128)S(1)} fusion(bf16[1,2,8192,256]{3,2,1,0:T(8,128)(2,1)} %param.12, s32[]{:T(128)S(6)} %select_n.244, bf16[192,4096]{1,0:T(8,128)(2,1)S(1)} %concatenate.31), kind=kOutput, calls=%fused_computation.54 | convolution fusion | flops 805306368 | bytes 6160388 | tf_op jit(solution)/shard_map/rf,cfo->cro/dot_general | solution.py:46
  66.7 2.3 %bitcast_reduce_fusion = (f32[3,2,8,128]{3,2,1,0:T(8,128)S(1)}, f32[3,2,128,8,64]{2,4,3,1,0:T(8,128)S(1)}) fusion(f32[3,64,2,128]{3,2,1,0:T(2,128)S(1)} %reshape_squeeze.6, f32[128]{0:T(128)S(1)} %get-tuple-element.16, f32[3,64,2]{1,2,0:T(2,128)S(1)} %add_rsqrt_fusion.1, bf16[3,128,2,8,128]{4,3,2,1,0:T(8,128)(2,1)} %multiply_convert_fusion, ...), kind=kOutput, calls=%fused_computation.35 | convolution fusion | flops 101984256 | bytes 3369152 | tf_op jit(solution)/shard_map/bvkh,btkgh->bkvgt/dot_general | solution.py:46
  70.3 2.2 %fusion.36 = f32[3,2,64,128,8]{3,2,4,1,0:T(8,128)S(1)} fusion(bf16[3,128,2,8,128]{4,3,2,1,0:T(8,128)(2,1)} %bitcast.579, bf16[3,64,2,128,1]{3,2,1,0,4:T(2,128)(2,1)S(1)} %bitcast.586), kind=kOutput, calls=%fused_computation.48 | convolution fusion | flops 100663296 | bytes 3244032 | tf_op jit(solution)/shard_map/bvkh,btkgh->bkvgt/dot_general | solution.py:46
  73.0 1.7 %copy.57 = bf16[3,2,64,8,128]{2,3,4,1,0:T(8,128)(2,1)} copy(bf16[3,2,64,8,128]{4,2,3,1,0:T(8,128)(2,1)S(1)} %fusion.22) | data formatting | bytes 1572864 | tf_op jit(solution)/shard_map/convert_element_type | solution.py:170
  74.8 2.6 %multiply_reduce_fusion.1 = (f32[3,64,2]{1,2,0:T(2,128)S(1)}, f32[3,64,2,128]{3,1,2,0:T(8,128)S(1)}) fusion(f32[3,64,2,128]{3,2,1,0:T(2,128)S(1)} %reshape_squeeze.6, f32[3,64,2]{1,2,0:T(2,128)S(1)} %add_rsqrt_fusion.1, f32[128]{0:T(128)S(1)} %get-tuple-element.16, bf16[3,2,64,8,128]{2,3,4,1,0:T(8,128)(2,1)} %copy.57, ...), kind=kOutput, calls=%fused_computation.101 | convolution fusion | flops 100859520 | bytes 2756096 | tf_op jit(solution)/shard_map/bkvgt,btkgh->bvkh/dot_general | solution.py:46
  78.3 5.6 %convolution_bitcast_fusion.3 = f32[192,4096]{1,0:T(8,128)} fusion(bf16[1,2,8192,256]{3,2,1,0:T(8,128)(2,1)} %param.12, s32[]{:T(128)S(6)} %select_n.244, bf16[2,192,256]{2,1,0:T(8,128)(2,1)S(1)} %constant_dynamic-update-slice_fusion, s32[192]{0:T(256)S(1)} %concatenate.32), kind=kOutput, calls=%fused_computation.8 | convolution fusion | flops 843190272 | bytes 7537412 | tf_op jit(solution)/shard_map/cro,cfo->rf/dot_general | solution.py:46
  83.8 5.5 %convolution_bitcast_fusion.1 = f32[192,4096]{1,0:T(8,128)} fusion(bf16[1,2,8192,256]{3,2,1,0:T(8,128)(2,1)} %param.12, s32[]{:T(128)S(6)} %select_n.259, bf16[2,192,256]{2,1,0:T(8,128)(2,1)S(1)} %constant_dynamic-update-slice_fusion, s32[192]{0:T(256)S(1)} %concatenate.34), kind=kOutput, calls=%fused_computation.4 | convolution fusion | flops 843190272 | bytes 7537412 | tf_op jit(solution)/shard_map/cro,cfo->rf/dot_general | solution.py:46
  89.4 1.7 %fusion.9 = bf16[2,16,4096]{2,1,0:T(8,128)(2,1)S(1)} fusion(bf16[2,192,16]{1,2,0:T(8,128)(2,1)S(1)} %fusion.74, bf16[48,4096]{1,0:T(8,128)(2,1)S(1)} %copy-done.13, bf16[48,4096]{1,0:T(8,128)(2,1)S(1)} %copy-done.11, bf16[48,4096]{1,0:T(8,128)(2,1)} %collective-permute-done.9, bf16[48,4096]{1,0:T(8,128)(2,1)} %collective-permute-done.5), kind=kOutput, calls=%fused_computation.15 | convolution fusion | flops 56885248 | bytes 1847296 | tf_op jit(solution)/shard_map/cra,rf->caf/dot_general | solution.py:46
  94.2 5.7 %collective-permute-done.24 = bf16[2,16,4096]{2,1,0:T(8,128)(2,1)S(1)} collective-permute-done((bf16[2,16,4096]{2,1,0:T(8,128)(2,1)S(1)}, bf16[2,16,4096]{2,1,0:T(8,128)(2,1)S(1)}, u32[]{:S(2)}, u32[]{:S(2)}) %collective-permute-start.24) | collective-permute-done | bytes 262176 | tf_op jit(solution)/shard_map/ppermute | solution.py:209
  101.9 6.8 %collective-permute-done.25 = bf16[32,4352]{1,0:T(8,128)(2,1)S(1)} collective-permute-done((bf16[32,4352]{1,0:T(8,128)(2,1)S(1)}, bf16[32,4352]{1,0:T(8,128)(2,1)S(1)}, u32[]{:S(2)}, u32[]{:S(2)}) %collective-permute-start.25) | collective-permute-done | bytes 278560 | tf_op jit(solution)/shard_map/ppermute | solution.py:213
  109.3 8.2 %collective-permute-done.26 = bf16[32,4352]{1,0:T(8,128)(2,1)S(1)} collective-permute-done((bf16[32,4352]{1,0:T(8,128)(2,1)S(1)}, bf16[32,4352]{1,0:T(8,128)(2,1)S(1)}, u32[]{:S(2)}, u32[]{:S(2)}) %collective-permute-start.26) | collective-permute-done | bytes 278560 | tf_op jit(solution)/shard_map/ppermute | solution.py:213
  120.1 7.1 %collective-permute-done.27 = bf16[32,4352]{1,0:T(8,128)(2,1)S(1)} collective-permute-done((bf16[32,4352]{1,0:T(8,128)(2,1)S(1)}, bf16[32,4352]{1,0:T(8,128)(2,1)S(1)}, u32[]{:S(2)}, u32[]{:S(2)}) %collective-permute-start.27) | collective-permute-done | bytes 278560 | tf_op jit(solution)/shard_map/ppermute | solution.py:215
  127.4 2.2 %collective-permute-done.14 = bf16[48,4096]{1,0:T(8,128)(2,1)S(1)} collective-permute-done((bf16[48,4096]{1,0:T(8,128)(2,1)S(1)}, bf16[48,4096]{1,0:T(8,128)(2,1)S(1)}, u32[]{:S(2)}, u32[]{:S(2)}) %collective-permute-start.14) | collective-permute-done | bytes 393248 | tf_op jit(solution)/shard_map/ppermute | solution.py:42
  129.6 2.9 %collective-permute-done.18 = bf16[48,4096]{1,0:T(8,128)(2,1)S(1)} collective-permute-done((bf16[48,4096]{1,0:T(8,128)(2,1)S(1)}, bf16[48,4096]{1,0:T(8,128)(2,1)S(1)}, u32[]{:S(2)}, u32[]{:S(2)}) %collective-permute-start.18) | collective-permute-done | bytes 393248 | tf_op jit(solution)/shard_map/ppermute | solution.py:42
  132.8 3.2 %collective-permute-start.21 = (bf16[12,4096]{1,0:T(8,128)(2,1)S(1)}, bf16[12,4096]{1,0:T(8,128)(2,1)S(1)}, u32[]{:S(2)}, u32[]{:S(2)}) collective-permute-start(bf16[12,4096]{1,0:T(8,128)(2,1)S(1)} %get-tuple-element.15), channel_id=1, source_target_pairs={{0,96},{8,40},{16,112},{24,56},{32,0},{40,72},{48,16},{56,88},{64,... | collective-permute-start | bytes 294920 | tf_op jit(solution)/shard_map/ppermute | solution.py:42
  137.1 3.7 %collective-permute-start.19 = (bf16[6,4096]{1,0:T(8,128)(2,1)S(1)}, bf16[6,4096]{1,0:T(8,128)(2,1)S(1)}, u32[]{:S(2)}, u32[]{:S(2)}) collective-permute-start(bf16[6,4096]{1,0:T(8,128)(2,1)S(1)} %slice.114), channel_id=1, source_target_pairs={{0,64},{8,72},{16,80},{24,88},{32,96},{40,104},{48,112},{56,120},{... | collective-permute-start | bytes 147464 | tf_op jit(solution)/shard_map/ppermute | solution.py:42
  140.8 1.8 %collective-permute-done.21 = bf16[12,4096]{1,0:T(8,128)(2,1)S(1)} collective-permute-done((bf16[12,4096]{1,0:T(8,128)(2,1)S(1)}, bf16[12,4096]{1,0:T(8,128)(2,1)S(1)}, u32[]{:S(2)}, u32[]{:S(2)}) %collective-permute-start.21) | collective-permute-done | bytes 98336 | tf_op jit(solution)/shard_map/ppermute | solution.py:42
  142.6 6.2 %collective-permute-done.22 = bf16[12,4096]{1,0:T(8,128)(2,1)S(1)} collective-permute-done((bf16[12,4096]{1,0:T(8,128)(2,1)S(1)}, bf16[12,4096]{1,0:T(8,128)(2,1)S(1)}, u32[]{:S(2)}, u32[]{:S(2)}) %collective-permute-start.22) | collective-permute-done | bytes 98336 | tf_op jit(solution)/shard_map/ppermute | solution.py:42
  (139 shorter events, 26.8 us)
Async XLA Ops:
  0.6 48.7 %copy-start = (bf16[1,2,16,8192]{3,2,1,0:T(8,128)(2,1)S(1)}, bf16[1,2,16,8192]{3,2,1,0:T(8,128)(2,1)}, u32[]{:S(2)}) copy-start(bf16[1,2,16,8192]{3,2,1,0:T(8,128)(2,1)} %param.13) | copy-start | bytes 1572868
  1.5 12.3 %collective-permute-start = (bf16[6,4096]{1,0:T(8,128)(2,1)S(1)}, bf16[6,4096]{1,0:T(8,128)(2,1)S(1)}, u32[]{:S(2)}, u32[]{:S(2)}) collective-permute-start(bf16[6,4096]{1,0:T(8,128)(2,1)S(1)} %reshape.108), channel_id=1, source_target_pairs={{0,8},{8,0},{16,24},{24,16},{32,40},{40,32},{48,56},{56,48},{64,72... | collective-permute-start | bytes 147464 | tf_op jit(solution)/shard_map/ppermute | solution.py:42
  1.6 15.1 %collective-permute-start.4 = (bf16[6,4096]{1,0:T(8,128)(2,1)S(1)}, bf16[6,4096]{1,0:T(8,128)(2,1)S(1)}, u32[]{:S(2)}, u32[]{:S(2)}) collective-permute-start(bf16[6,4096]{1,0:T(8,128)(2,1)S(1)} %reshape.108), channel_id=1, source_target_pairs={{0,64},{8,72},{16,80},{24,88},{32,96},{40,104},{48,112},{56,120},{... | collective-permute-start | bytes 147464 | tf_op jit(solution)/shard_map/ppermute | solution.py:42
  13.9 6.3 %collective-permute-start.1 = (bf16[12,4096]{1,0:T(8,128)(2,1)S(1)}, bf16[12,4096]{1,0:T(8,128)(2,1)S(1)}, u32[]{:S(2)}, u32[]{:S(2)}) collective-permute-start(bf16[12,4096]{1,0:T(8,128)(2,1)S(1)} %pad_maximum_fusion.2), channel_id=1, source_target_pairs={{0,16},{8,120},{16,32},{24,8},{32,48},{40,24},{48,64},{56,40},{64,... | collective-permute-start | bytes 294920 | tf_op jit(solution)/shard_map/ppermute | solution.py:42
  15.0 10.6 %collective-permute-start.2 = (bf16[12,4096]{1,0:T(8,128)(2,1)S(1)}, bf16[12,4096]{1,0:T(8,128)(2,1)S(1)}, u32[]{:S(2)}, u32[]{:S(2)}) collective-permute-start(bf16[12,4096]{1,0:T(8,128)(2,1)S(1)} %pad_maximum_fusion.2), channel_id=1, source_target_pairs={{0,32},{8,104},{16,48},{24,120},{32,64},{40,8},{48,80},{56,24},{64... | collective-permute-start | bytes 294920 | tf_op jit(solution)/shard_map/ppermute | solution.py:42
  16.4 10.9 %collective-permute-start.3 = (bf16[12,4096]{1,0:T(8,128)(2,1)S(1)}, bf16[12,4096]{1,0:T(8,128)(2,1)S(1)}, u32[]{:S(2)}, u32[]{:S(2)}) collective-permute-start(bf16[12,4096]{1,0:T(8,128)(2,1)S(1)} %pad_maximum_fusion.2), channel_id=1, source_target_pairs={{0,48},{8,88},{16,64},{24,104},{32,80},{40,120},{48,96},{56,8},{64... | collective-permute-start | bytes 294920 | tf_op jit(solution)/shard_map/ppermute | solution.py:42
  27.9 12.2 %collective-permute-start.5 = (bf16[48,4096]{1,0:T(8,128)(2,1)S(1)}, bf16[48,4096]{1,0:T(8,128)(2,1)}, u32[]{:S(2)}, u32[]{:S(2)}) collective-permute-start(bf16[48,4096]{1,0:T(8,128)(2,1)S(1)} %concatenate.30), channel_id=1, source_target_pairs={{0,4},{8,140},{16,20},{24,156},{32,36},{40,172},{48,52},{56,188},{... | collective-permute-start | bytes 1179656 | tf_op jit(solution)/shard_map/ppermute | solution.py:42
  29.4 10.7 %collective-permute-start.9 = (bf16[48,4096]{1,0:T(8,128)(2,1)S(1)}, bf16[48,4096]{1,0:T(8,128)(2,1)}, u32[]{:S(2)}, u32[]{:S(2)}) collective-permute-start(bf16[48,4096]{1,0:T(8,128)(2,1)S(1)} %concatenate.30), channel_id=1, source_target_pairs={{0,132},{8,12},{16,148},{24,28},{32,164},{40,44},{48,180},{56,60},... | collective-permute-start | bytes 1179656 | tf_op jit(solution)/shard_map/ppermute | solution.py:42
  34.9 5.8 %copy-start.9 = (s32[3]{0:T(128)S(1)}, s32[3]{0:T(128)}, u32[]{:S(2)}) copy-start(s32[3]{0:T(128)} %param.17) | copy-start | bytes 40
  40.1 9.2 %collective-permute-start.6 = (bf16[48,4096]{1,0:T(8,128)(2,1)}, bf16[48,4096]{1,0:T(8,128)(2,1)S(1)}, u32[]{:S(2)}, u32[]{:S(2)}) collective-permute-start(bf16[48,4096]{1,0:T(8,128)(2,1)} %collective-permute-done.5), channel_id=1, source_target_pairs={{0,132},{8,12},{16,148},{24,28},{32,164},{40,44},{48,180},{56,60},... | collective-permute-start | bytes 1179656 | tf_op jit(solution)/shard_map/ppermute | solution.py:42
  40.1 9.2 %collective-permute-start.10 = (bf16[48,4096]{1,0:T(8,128)(2,1)}, bf16[48,4096]{1,0:T(8,128)(2,1)S(1)}, u32[]{:S(2)}, u32[]{:S(2)}) collective-permute-start(bf16[48,4096]{1,0:T(8,128)(2,1)} %collective-permute-done.5), channel_id=1, source_target_pairs={{0,8},{8,0},{16,24},{24,16},{32,40},{40,32},{48,56},{56,48},{64,72... | collective-permute-start | bytes 1179656 | tf_op jit(solution)/shard_map/ppermute | solution.py:42
  40.1 9.2 %collective-permute-start.11 = (bf16[48,4096]{1,0:T(8,128)(2,1)}, bf16[48,4096]{1,0:T(8,128)(2,1)S(1)}, u32[]{:S(2)}, u32[]{:S(2)}) collective-permute-start(bf16[48,4096]{1,0:T(8,128)(2,1)} %collective-permute-done.9), channel_id=1, source_target_pairs={{0,8},{8,0},{16,24},{24,16},{32,40},{40,32},{48,56},{56,48},{64,72... | collective-permute-start | bytes 1179656 | tf_op jit(solution)/shard_map/ppermute | solution.py:42
  40.8 14.8 %collective-permute-start.7 = (bf16[48,4096]{1,0:T(8,128)(2,1)S(1)}, bf16[48,4096]{1,0:T(8,128)(2,1)S(1)}, u32[]{:S(2)}, u32[]{:S(2)}) collective-permute-start(bf16[48,4096]{1,0:T(8,128)(2,1)S(1)} %concatenate.30), channel_id=1, source_target_pairs={{0,8},{8,0},{16,24},{24,16},{32,40},{40,32},{48,56},{56,48},{64,72... | collective-permute-start | bytes 1179656 | tf_op jit(solution)/shard_map/ppermute | solution.py:42
  49.3 7.0 %collective-permute-start.8 = (bf16[48,4096]{1,0:T(8,128)(2,1)S(1)}, bf16[48,4096]{1,0:T(8,128)(2,1)}, u32[]{:S(2)}, u32[]{:S(2)}) collective-permute-start(bf16[48,4096]{1,0:T(8,128)(2,1)S(1)} %collective-permute-done.6), channel_id=1, source_target_pairs={{0,8},{8,0},{16,24},{24,16},{32,40},{40,32},{48,56},{56,48},{64,72... | collective-permute-start | bytes 1179656 | tf_op jit(solution)/shard_map/ppermute | solution.py:42
  83.8 5.6 %copy-start.11 = (bf16[48,4096]{1,0:T(8,128)(2,1)S(1)}, bf16[48,4096]{1,0:T(8,128)(2,1)}, u32[]{:S(2)}) copy-start(bf16[48,4096]{1,0:T(8,128)(2,1)} %copy-done.10) | copy-start | bytes 1179652
  83.8 5.6 %copy-start.13 = (bf16[48,4096]{1,0:T(8,128)(2,1)S(1)}, bf16[48,4096]{1,0:T(8,128)(2,1)}, u32[]{:S(2)}) copy-start(bf16[48,4096]{1,0:T(8,128)(2,1)} %copy-done.12) | copy-start | bytes 1179652
  91.1 8.8 %collective-permute-start.24 = (bf16[2,16,4096]{2,1,0:T(8,128)(2,1)S(1)}, bf16[2,16,4096]{2,1,0:T(8,128)(2,1)S(1)}, u32[]{:S(2)}, u32[]{:S(2)}) collective-permute-start(bf16[2,16,4096]{2,1,0:T(8,128)(2,1)S(1)} %fusion.9), channel_id=1, source_target_pairs={{0,4},{4,0},{1,5},{5,1},{2,6},{6,2},{3,7},{7,3},{8,12},{12,8},{9,1... | collective-permute-start | bytes 786440 | tf_op jit(solution)/shard_map/ppermute | solution.py:209
  92.2 16.9 %collective-permute-start.16 = (bf16[48,4096]{1,0:T(8,128)(2,1)S(1)}, bf16[48,4096]{1,0:T(8,128)(2,1)S(1)}, u32[]{:S(2)}, u32[]{:S(2)}) collective-permute-start(bf16[48,4096]{1,0:T(8,128)(2,1)S(1)} %get-tuple-element.6), channel_id=1, source_target_pairs={{0,8},{8,0},{16,24},{24,16},{32,40},{40,32},{48,56},{56,48},{64,72... | collective-permute-start | bytes 1179656 | tf_op jit(solution)/shard_map/ppermute | solution.py:42
  100.3 8.4 %collective-permute-start.25 = (bf16[32,4352]{1,0:T(8,128)(2,1)S(1)}, bf16[32,4352]{1,0:T(8,128)(2,1)S(1)}, u32[]{:S(2)}, u32[]{:S(2)}) collective-permute-start(bf16[32,4352]{1,0:T(8,128)(2,1)S(1)} %pad_maximum_fusion.1), channel_id=1, source_target_pairs={{0,1},{1,0},{2,3},{3,2},{4,5},{5,4},{6,7},{7,6},{8,9},{9,8},{10,11... | collective-permute-start | bytes 835592 | tf_op jit(solution)/shard_map/ppermute | solution.py:213
  101.2 17.1 %collective-permute-start.13 = (bf16[48,4096]{1,0:T(8,128)(2,1)S(1)}, bf16[48,4096]{1,0:T(8,128)(2,1)S(1)}, u32[]{:S(2)}, u32[]{:S(2)}) collective-permute-start(bf16[48,4096]{1,0:T(8,128)(2,1)S(1)} %get-tuple-element.9), channel_id=1, source_target_pairs={{0,8},{8,0},{16,24},{24,16},{32,40},{40,32},{48,56},{56,48},{64,72... | collective-permute-start | bytes 1179656 | tf_op jit(solution)/shard_map/ppermute | solution.py:42
  101.3 17.0 %collective-permute-start.15 = (bf16[48,4096]{1,0:T(8,128)(2,1)S(1)}, bf16[48,4096]{1,0:T(8,128)(2,1)S(1)}, u32[]{:S(2)}, u32[]{:S(2)}) collective-permute-start(bf16[48,4096]{1,0:T(8,128)(2,1)S(1)} %get-tuple-element.10), channel_id=1, source_target_pairs={{0,8},{8,0},{16,24},{24,16},{32,40},{40,32},{48,56},{56,48},{64,72... | collective-permute-start | bytes 1179656 | tf_op jit(solution)/shard_map/ppermute | solution.py:42
  101.8 25.6 %collective-permute-start.12 = (bf16[48,4096]{1,0:T(8,128)(2,1)S(1)}, bf16[48,4096]{1,0:T(8,128)(2,1)S(1)}, u32[]{:S(2)}, u32[]{:S(2)}) collective-permute-start(bf16[48,4096]{1,0:T(8,128)(2,1)S(1)} %get-tuple-element.5), channel_id=1, source_target_pairs={{0,8},{8,0},{16,24},{24,16},{32,40},{40,32},{48,56},{56,48},{64,72... | collective-permute-start | bytes 1179656 | tf_op jit(solution)/shard_map/ppermute | solution.py:42
  108.8 8.7 %collective-permute-start.26 = (bf16[32,4352]{1,0:T(8,128)(2,1)S(1)}, bf16[32,4352]{1,0:T(8,128)(2,1)S(1)}, u32[]{:S(2)}, u32[]{:S(2)}) collective-permute-start(bf16[32,4352]{1,0:T(8,128)(2,1)S(1)} %add_convert_fusion.4), channel_id=1, source_target_pairs={{0,3},{1,2},{2,1},{3,0},{4,7},{5,6},{6,5},{7,4},{8,11},{9,10},{10,... | collective-permute-start | bytes 835592 | tf_op jit(solution)/shard_map/ppermute | solution.py:213
  109.2 9.1 %collective-permute-start.17 = (bf16[48,4096]{1,0:T(8,128)(2,1)S(1)}, bf16[48,4096]{1,0:T(8,128)(2,1)S(1)}, u32[]{:S(2)}, u32[]{:S(2)}) collective-permute-start(bf16[48,4096]{1,0:T(8,128)(2,1)S(1)} %add_convert_fusion.1), channel_id=1, source_target_pairs={{0,132},{8,12},{16,148},{24,28},{32,164},{40,44},{48,180},{56,60},... | collective-permute-start | bytes 1179656 | tf_op jit(solution)/shard_map/ppermute | solution.py:42
  117.5 9.7 %collective-permute-start.27 = (bf16[32,4352]{1,0:T(8,128)(2,1)S(1)}, bf16[32,4352]{1,0:T(8,128)(2,1)S(1)}, u32[]{:S(2)}, u32[]{:S(2)}) collective-permute-start(bf16[32,4352]{1,0:T(8,128)(2,1)S(1)} %add_convert_fusion.3), channel_id=1, source_target_pairs={{0,4},{4,0},{1,5},{5,1},{2,6},{6,2},{3,7},{7,3},{8,12},{12,8},{9,1... | collective-permute-start | bytes 835592 | tf_op jit(solution)/shard_map/ppermute | solution.py:215
  118.6 11.0 %collective-permute-start.14 = (bf16[48,4096]{1,0:T(8,128)(2,1)S(1)}, bf16[48,4096]{1,0:T(8,128)(2,1)S(1)}, u32[]{:S(2)}, u32[]{:S(2)}) collective-permute-start(bf16[48,4096]{1,0:T(8,128)(2,1)S(1)} %get-tuple-element.7), channel_id=1, source_target_pairs={{0,132},{8,12},{16,148},{24,28},{32,164},{40,44},{48,180},{56,60},... | collective-permute-start | bytes 1179656 | tf_op jit(solution)/shard_map/ppermute | solution.py:42
  118.7 13.8 %collective-permute-start.18 = (bf16[48,4096]{1,0:T(8,128)(2,1)S(1)}, bf16[48,4096]{1,0:T(8,128)(2,1)S(1)}, u32[]{:S(2)}, u32[]{:S(2)}) collective-permute-start(bf16[48,4096]{1,0:T(8,128)(2,1)S(1)} %get-tuple-element.8), channel_id=1, source_target_pairs={{0,4},{8,140},{16,20},{24,156},{32,36},{40,172},{48,52},{56,188},{... | collective-permute-start | bytes 1179656 | tf_op jit(solution)/shard_map/ppermute | solution.py:42
  132.8 8.0 %collective-permute-start.20 = (bf16[12,4096]{1,0:T(8,128)(2,1)S(1)}, bf16[12,4096]{1,0:T(8,128)(2,1)S(1)}, u32[]{:S(2)}, u32[]{:S(2)}) collective-permute-start(bf16[12,4096]{1,0:T(8,128)(2,1)S(1)} %get-tuple-element.13), channel_id=1, source_target_pairs={{0,112},{8,24},{16,0},{24,40},{32,16},{40,56},{48,32},{56,72},{64,... | collective-permute-start | bytes 294920 | tf_op jit(solution)/shard_map/ppermute | solution.py:42
  132.8 9.8 %collective-permute-start.21 = (bf16[12,4096]{1,0:T(8,128)(2,1)S(1)}, bf16[12,4096]{1,0:T(8,128)(2,1)S(1)}, u32[]{:S(2)}, u32[]{:S(2)}) collective-permute-start(bf16[12,4096]{1,0:T(8,128)(2,1)S(1)} %get-tuple-element.15), channel_id=1, source_target_pairs={{0,96},{8,40},{16,112},{24,56},{32,0},{40,72},{48,16},{56,88},{64,... | collective-permute-start | bytes 294920 | tf_op jit(solution)/shard_map/ppermute | solution.py:42
  136.0 12.8 %collective-permute-start.22 = (bf16[12,4096]{1,0:T(8,128)(2,1)S(1)}, bf16[12,4096]{1,0:T(8,128)(2,1)S(1)}, u32[]{:S(2)}, u32[]{:S(2)}) collective-permute-start(bf16[12,4096]{1,0:T(8,128)(2,1)S(1)} %get-tuple-element.14), channel_id=1, source_target_pairs={{0,80},{8,56},{16,96},{24,72},{32,112},{40,88},{48,0},{56,104},{64... | collective-permute-start | bytes 294920 | tf_op jit(solution)/shard_map/ppermute | solution.py:42
  137.1 12.5 %collective-permute-start.19 = (bf16[6,4096]{1,0:T(8,128)(2,1)S(1)}, bf16[6,4096]{1,0:T(8,128)(2,1)S(1)}, u32[]{:S(2)}, u32[]{:S(2)}) collective-permute-start(bf16[6,4096]{1,0:T(8,128)(2,1)S(1)} %slice.114), channel_id=1, source_target_pairs={{0,64},{8,72},{16,80},{24,88},{32,96},{40,104},{48,112},{56,120},{... | collective-permute-start | bytes 147464 | tf_op jit(solution)/shard_map/ppermute | solution.py:42
  148.9 1.3 collective-permute-start.23
  (14 other events, 28.6 us)

commit v2 on v1

v2 whole, which is shorter than its diff:
```python
import jax
import jax.numpy as jnp
from jax import lax
from jax.experimental import pallas as pl
from jax.experimental.pallas import tpu as pltpu
from jax.sharding import PartitionSpec as P

TILES = 4
ADAPTER_SCALE = 2.0
EPS = 1e-05
PLANE = ("section", "tensor")
NZ = 8


def plane_pairs(route):
    def index(x, z, core):
        return (((x // 2) * NZ + z) * 2 + core) * 2 + x % 2

    return [
        (index(x, z, core), index(*route(x, z, core)))
        for x in range(4)
        for z in range(NZ)
        for core in range(2)
    ]


SIBLING = plane_pairs(lambda x, z, core: (x, z, 1 - core))
RISE = {
    k: plane_pairs(lambda x, z, core, k=k: (x, (z + (k if core == 0 else -k)) % NZ, core))
    for k in (1, 2, 3, 4)
}
FALL = {
    k: plane_pairs(lambda x, z, core, k=k: (x, (z - (k if core == 0 else -k)) % NZ, core))
    for k in (1, 2, 3, 4)
}
NEAR = plane_pairs(lambda x, z, core: (x ^ 1 if core == 0 else 3 - x, z, core))
FAR = plane_pairs(lambda x, z, core: (3 - x if core == 0 else x ^ 1, z, core))
TENSOR_SWAP = [(0, 1), (1, 0)]
DP_NEAR = [(i, i ^ 1) for i in range(4)]
DP_FAR = [(i, 3 - i) for i in range(4)]


def move(block, pairs):
    return lax.ppermute(block, PLANE, pairs)


def after(value, *others):
    return lax.optimization_barrier((value, *others))[0]


NT = (((1,), (1,)), ((), ()))
TN = (((0,), (0,)), ((), ()))
F32, LOW = jnp.float32, jnp.bfloat16
ROOM = pltpu.CompilerParams(vmem_limit_bytes=48 * 1024 * 1024)


def dot(first, second, dims=(((1,), (0,)), ((), ()))):
    return lax.dot_general(first, second, dims, preferred_element_type=F32)


def cost(flops, moved):
    return pl.CostEstimate(flops=int(flops), bytes_accessed=int(moved), transcendentals=0)


def pair_kernel(gain_ref, query_ref, context_ref, pair_ref):
    gain = gain_ref[0:1, :].astype(F32)
    head = gain.shape[1]
    text = query_ref.shape[1]
    kv_heads = pair_ref.shape[0]
    group = query_ref.shape[2] // (head * kv_heads)
    for kv in range(kv_heads):
        for member in range(group):
            columns = slice((kv * group + member) * head, (kv * group + member + 1) * head)
            rows = slice(member * text, (member + 1) * text)
            query = query_ref[0, :, columns].astype(F32)
            scale = lax.rsqrt(jnp.mean(query * query, axis=-1, keepdims=True) + EPS)
            pair_ref[kv, rows, 0:head] = (query * scale * gain).astype(LOW)
            pair_ref[kv, rows, head : 2 * head] = context_ref[0, :, columns]


def pair_queries(queries, context, gains, kv_heads):
    batches, text, wide = queries.shape
    head = gains.shape[1]
    rows = wide // (kv_heads * head) * text
    block = pl.BlockSpec((1, text, wide), lambda b: (b, 0, 0))
    return pl.pallas_call(
        pair_kernel,
        out_shape=jax.ShapeDtypeStruct((batches * kv_heads, rows, 2 * head), LOW),
        grid=(batches,),
        in_specs=[pl.BlockSpec(gains.shape, lambda b: (0, 0)), block, block],
        out_specs=pl.BlockSpec((kv_heads, rows, 2 * head), lambda b: (b, 0, 0)),
        compiler_params=ROOM,
        cost_estimate=cost(2e8, 4 * queries.size * 2),
        name="pair_queries",
    )(gains, queries, context)


def project_kernel(which_ref, *refs):
    *row_refs, w_ref, a_ref, y_ref, r_ref = refs
    rows = jnp.concatenate([ref[...] for ref in row_refs])
    maps = a_ref[...].reshape(-1, a_ref.shape[2])

    @pl.when(pl.program_id(0) == 0)
    def _():
        y_ref[...] = jnp.zeros_like(y_ref)
        r_ref[...] = jnp.zeros_like(r_ref)

    for part in range(2):
        y_ref[part] += dot(rows, w_ref[part])
    r_ref[...] += dot(rows, maps, NT)


def project(blocks, weights, down_maps, which):
    count, half = len(blocks) * blocks[0].shape[0], blocks[0].shape[1]
    chunk = 1024
    steps = half // chunk
    width, ranks = weights.shape[2], 2 * down_maps.shape[1]
    grid_spec = pltpu.PrefetchScalarGridSpec(
        num_scalar_prefetch=1,
        grid=(steps,),
        in_specs=[pl.BlockSpec((block.shape[0], chunk), lambda i, s: (0, i)) for block in blocks]
        + [
            pl.BlockSpec((2, chunk, width), lambda i, s: (0, s[0] * steps + i, 0)),
            pl.BlockSpec((2, ranks // 2, chunk), lambda i, s: (0, 0, s[0] * steps + i)),
        ],
        out_specs=[
            pl.BlockSpec((2, count, width), lambda i, s: (0, 0, 0)),
            pl.BlockSpec((count, ranks), lambda i, s: (0, 0)),
        ],
    )
    return pl.pallas_call(
        project_kernel,
        out_shape=[
            jax.ShapeDtypeStruct((2, count, width), F32),
            jax.ShapeDtypeStruct((count, ranks), F32),
        ],
        grid_spec=grid_spec,
        compiler_params=ROOM,
        cost_estimate=cost(4 * 192 * half * width, 4 * half * width + 2 * count * half),
        name="project",
    )(which, *blocks, weights, down_maps)


def attention_kernel(
    count_ref, start_ref, y0, y1, y2, r0, r1, r2, own_map, other_map, own_back, other_back,
    up_diagonal, gains_ref, pair_ref, g_own, m_own, g_other, m_other, up_ref, grad_ref,
):
    width = y0.shape[2]
    head = gains_ref.shape[1]
    kv_heads = width // head
    batches = pair_ref.shape[0] // kv_heads
    tokens = own_map.shape[0] // batches
    ranks = r0.shape[1]
    text = 128
    scale = head ** (-0.5)

    def ordered(own, other):
        total = None
        for mapping, values in ((own_map, own), (other_map, other)):
            high = values.astype(LOW)
            rest = values - high.astype(F32)
            middle = rest.astype(LOW)
            lowest = (rest - middle.astype(F32)).astype(LOW)
            for term in (lowest, middle, high):
                moved = dot(mapping[...], term)
                total = moved if total is None else total + moved
        return total

    reduced = ordered(jnp.concatenate([r0[...], r1[...]]), r2[...]).astype(LOW)
    adapted = ADAPTER_SCALE * dot(reduced, up_diagonal[...])
    raw = [
        ordered(jnp.concatenate([y0[part], y1[part]]), y2[part])
        + adapted[:, part * width : (part + 1) * width]
        for part in range(2)
    ]
    gain = gains_ref[1:2, :].astype(F32)
    lane = lax.broadcasted_iota(jnp.int32, (1, pair_ref.shape[1]), 1) % text
    token = lax.broadcasted_iota(jnp.int32, (tokens, 1), 0)
    for kv in range(kv_heads):
        columns = slice(kv * head, (kv + 1) * head)
        key_raw = raw[0][:, columns]
        key_scale = lax.rsqrt(jnp.mean(key_raw * key_raw, axis=-1, keepdims=True) + EPS)
        unit = key_raw * key_scale
        keys = (unit * gain).astype(LOW)
        values = raw[1][:, columns].astype(LOW)
        for batch in range(batches):
            rows = slice(batch * tokens, (batch + 1) * tokens)
            none = jnp.zeros((tokens, head), LOW)
            both = jnp.concatenate(
                [
                    jnp.concatenate([keys[rows], none], 1),
                    jnp.concatenate([none, values[rows]], 1),
                ]
            )
            pair = pair_ref[batch * kv_heads + kv]
            scores = dot(both, pair, NT)
            allowed = token < count_ref[batch] * (tokens // TILES)
            live = (lane >= start_ref[batch]).astype(F32)
            weighted = jnp.where(allowed, jnp.exp(scores[:tokens] * scale), 0.0)
            attention = weighted * (live / jnp.sum(weighted, axis=0, keepdims=True))
            probs = scores[tokens:]
            mean = jnp.sum(attention * probs, axis=0, keepdims=True)
            grads = attention * (probs - mean) * scale
            out = dot(jnp.concatenate([grads.astype(LOW), attention.astype(LOW)]), pair)
            gained = out[:tokens, :head] * gain
            inner = jnp.mean(gained * unit[rows], axis=-1, keepdims=True)
            grad_ref[rows, columns] = (key_scale[rows] * (gained - unit[rows] * inner)).astype(LOW)
            grad_ref[rows, width + kv * head : width + (kv + 1) * head] = out[
                tokens:, head:
            ].astype(LOW)
    grad = grad_ref[...]
    middle = dot(grad, up_diagonal[...], NT).astype(LOW)
    up = ADAPTER_SCALE * dot(reduced, grad, TN)
    for part in range(2):
        half = slice(part * ranks // 2, (part + 1) * ranks // 2)
        up_ref[half, :] = up[half, part * width : (part + 1) * width]
    for back, g_ref, m_ref in ((own_back, g_own, m_own), (other_back, g_other, m_other)):
        g_ref[...] = dot(back[...], grad).astype(LOW)
        m_ref[...] = (ADAPTER_SCALE * dot(back[...], middle)).astype(LOW)


def attend(counts, starts, projected, maps, up_diagonal, gains, pair):
    (y0, r0), (y1, r1), (y2, r2) = projected
    rows, ranks, width = y2.shape[1], r0.shape[1], y0.shape[2]
    scalar = pl.BlockSpec(memory_space=pltpu.SMEM)
    vector = pl.BlockSpec(memory_space=pltpu.VMEM)
    return pl.pallas_call(
        attention_kernel,
        out_shape=[
            jax.ShapeDtypeStruct((rows, 2 * width), LOW),
            jax.ShapeDtypeStruct((rows, ranks), LOW),
            jax.ShapeDtypeStruct((rows, 2 * width), LOW),
            jax.ShapeDtypeStruct((rows, ranks), LOW),
            jax.ShapeDtypeStruct((ranks, width), F32),
        ],
        in_specs=[scalar, scalar] + [vector] * 13,
        out_specs=[vector] * 5,
        scratch_shapes=[pltpu.VMEM((rows, 2 * width), LOW)],
        compiler_params=ROOM,
        cost_estimate=cost(1e9, 2 * pair.size),
        name="attend",
    )(counts, starts, y0, y1, y2, r0, r1, r2, *maps, up_diagonal, gains, pair)


def feature_kernel(which_ref, g_ref, m_ref, w_ref, a_ref, *out_refs):
    width = w_ref.shape[2]
    total = dot(m_ref[...], a_ref[...].reshape(-1, a_ref.shape[2]))
    for part in range(2):
        total += dot(g_ref[:, part * width : (part + 1) * width], w_ref[part], NT)
    cut = out_refs[0].shape[0]
    for i, ref in enumerate(out_refs):
        ref[...] = total[i * cut : (i + 1) * cut].astype(LOW)


def feature_grad(grad, middle, weights, down_maps, which):
    rows, wide = grad.shape
    ranks = middle.shape[1]
    half = weights.shape[1] // 2
    chunk = 1024
    steps = half // chunk
    cut = rows // 4
    grid_spec = pltpu.PrefetchScalarGridSpec(
        num_scalar_prefetch=1,
        grid=(steps,),
        in_specs=[
            pl.BlockSpec((rows, wide), lambda i, s: (0, 0)),
            pl.BlockSpec((rows, ranks), lambda i, s: (0, 0)),
            pl.BlockSpec((2, chunk, wide // 2), lambda i, s: (0, s[0] * steps + i, 0)),
            pl.BlockSpec((2, ranks // 2, chunk), lambda i, s: (0, 0, s[0] * steps + i)),
        ],
        out_specs=[pl.BlockSpec((cut, chunk), lambda i, s: (0, i))] * 4,
    )
    return pl.pallas_call(
        feature_kernel,
        out_shape=[jax.ShapeDtypeStruct((cut, half), LOW)] * 4,
        grid_spec=grid_spec,
        compiler_params=ROOM,
        cost_estimate=cost(2 * rows * half * wide, 2 * half * (wide + rows)),
        name="feature_grad",
    )(which, grad, middle, weights, down_maps)


def down_kernel(m_ref, *refs):
    *row_refs, out_ref = refs
    rows = jnp.concatenate([ref[...] for ref in row_refs])
    out_ref[...] = dot(m_ref[...], rows, TN).astype(out_ref.dtype)


def down_grad(middle, blocks, dtype):
    half = blocks[0].shape[1]
    chunk = 1024
    return pl.pallas_call(
        down_kernel,
        out_shape=jax.ShapeDtypeStruct((middle.shape[1], half), dtype),
        grid=(half // chunk,),
        in_specs=[pl.BlockSpec(middle.shape, lambda i: (0, 0))]
        + [pl.BlockSpec((block.shape[0], chunk), lambda i: (0, i)) for block in blocks],
        out_specs=pl.BlockSpec((middle.shape[1], chunk), lambda i: (0, i)),
        compiler_params=ROOM,
        cost_estimate=cost(5e8, 2 * 200 * half),
        name="down_grad",
    )(middle, *blocks)


def row_tokens(x_hi, z, core, x_lo):
    def base_rows(chain, x_high):
        step = jnp.where(chain == 0, 1, -1)
        places = []
        for k in (1, 2, 3):
            for other in (0, 1):
                places.append(((z - step * k) % NZ, jnp.where(other == 0, chain, 1 - chain)))
        places += [((z - step * 4) % NZ, chain), (z, chain)]
        rows = []
        for level, which in places:
            token = ((x_high * NZ + level) * 2 + which) * 2
            for batch in range(3):
                rows += [batch * 64 + token, batch * 64 + token + 1]
        return jnp.stack(rows)

    own_half, other_half = [], []
    for chain in (core, 1 - core):
        own_half += [base_rows(chain, x_hi)]
        near = jnp.where(chain == 0, x_hi, 1 - x_hi)
        other_half += [base_rows(chain, near), base_rows(chain, 1 - near)]
    for chain in (core, 1 - core):
        own_half += [base_rows(chain, 1 - x_hi)]
    return jnp.concatenate(own_half), jnp.concatenate(other_half)


def per_device(
    queries,
    context_gradient,
    vision_feature_states,
    key_value_weight,
    adapter_down_maps,
    adapter_up_maps,
    norm_gain_pair,
    image_tile_count,
    text_start_position,
):
    weights, down_maps, gains = key_value_weight[0], adapter_down_maps[0], norm_gain_pair[0]
    section, side = lax.axis_index("section"), lax.axis_index("tensor")
    width, half = weights.shape[2], vision_feature_states.shape[2]
    ranks = 2 * down_maps.shape[1]
    here = side.reshape(1).astype(jnp.int32)
    opposite = 1 - here
    up_maps = lax.dynamic_slice_in_dim(adapter_up_maps[0], side * width, width, 2)
    up_diagonal = jnp.concatenate(
        [jnp.pad(up_maps[0], ((0, 0), (0, width))), jnp.pad(up_maps[1], ((0, 0), (width, 0)))]
    )

    own = vision_feature_states.reshape(-1, half)
    chip = jnp.concatenate([own, move(own, SIBLING)])
    parts = [move(chip, RISE[k]) for k in (1, 2, 3)] + [move(own, RISE[4]), own]
    pair = pair_queries(
        after(queries[0], chip), context_gradient[0], gains, width // gains.shape[1]
    )
    base = jnp.concatenate(parts)
    first = move(base, NEAR)
    second = move(base, FAR)
    base_there = move(base, SIBLING)
    step_a = project([base, base_there], weights, down_maps, here)
    third = move(first, FAR)
    first_there = move(first, SIBLING)
    second_there = move(second, SIBLING)
    others = [first, second, first_there, second_there]
    step_b = project(others, weights, down_maps, opposite)
    third_there = move(third, SIBLING)
    step_c = project([third, third_there], weights, down_maps, here)
    owns = [base, base_there, third, third_there]

    own_token, other_token = row_tokens(section // 16, (section // 2) % NZ, section % 2, side)
    line = jnp.arange(own_token.shape[0])
    maps = [
        (line[:, None] == own_token[None]).astype(LOW),
        (line[:, None] == other_token[None]).astype(LOW),
        (own_token[:, None] == line[None]).astype(LOW),
        (other_token[:, None] == line[None]).astype(LOW),
    ]
    g_own, m_own, g_other, m_other, up_part = attend(
        image_tile_count,
        text_start_position,
        (step_a, step_c, step_b),
        maps,
        up_diagonal,
        gains,
        pair,
    )

    down_other = down_grad(m_other, others, LOW)
    down_facing = lax.ppermute(down_other, "tensor", TENSOR_SWAP)
    base, base_out, third, third_out = feature_grad(
        after(g_own, down_other), m_own, weights, down_maps, here
    )
    down_own = down_grad(m_own, owns, F32)
    first, second, first_out, second_out = feature_grad(
        after(g_other, base), m_other, weights, down_maps, opposite
    )

    def add(mine, theirs):
        return mine.astype(F32) + theirs.astype(F32)

    third = add(third, move(third_out, SIBLING)).astype(LOW)
    second = add(second, move(second_out, SIBLING)).astype(LOW)
    first = add(first, move(first_out, SIBLING))
    base = add(base, move(base_out, SIBLING))

    sums = jnp.concatenate(
        [down_own + after(down_facing, first_out).astype(F32), up_part], 1
    ).astype(LOW)
    near_sums = lax.ppermute(sums, "dp", DP_NEAR)
    third_in = move(third, FAR)
    second_in = move(second, FAR)
    first = (first + third_in.astype(F32)).astype(LOW)
    first_in = move(first, NEAR)
    sums = add(sums, after(near_sums, first)).astype(LOW)
    far_sums = lax.ppermute(sums, "dp", DP_FAR)
    base = base + second_in.astype(F32) + first_in.astype(F32)
    sent = base[:42].astype(LOW)
    sums = add(sums, after(far_sums, sent)).astype(LOW)
    facing = lax.ppermute(sums, "tensor", TENSOR_SWAP)
    low_rows = [move(sent[12 * i : 12 * i + 12], FALL[k]) for i, k in enumerate((1, 2, 3))]
    own = base[42:] + move(sent[36:42], FALL[4]).astype(F32)
    chip = sum(block.astype(F32) for block in low_rows)
    passed = move(chip[6:].astype(LOW), SIBLING)
    own_grad = own + chip[:6] + passed.astype(F32)

    left = jnp.where(side == 0, sums, facing).astype(F32)
    right = jnp.where(side == 0, facing, sums).astype(F32)
    down_total = jnp.concatenate([left[:, :half], right[:, :half]], 1)
    up_total = jnp.concatenate([left[:, half:], right[:, half:]], 1)
    return (
        own_grad.reshape(vision_feature_states.shape),
        down_total.reshape(1, 2, ranks // 2, 2 * half),
        up_total.reshape(1, 2, ranks // 2, 2 * width),
    )


def solution(mesh):
    in_specs = (
        P("section", "dp", None, "tensor"),
        P("section", "dp", None, "tensor"),
        P("dp", "section", "tensor"),
        P("section", None, None, "tensor"),
        P("section", None, None, None),
        P("section", None, None, None),
        P("section", None, None),
        P("dp"),
        P("dp"),
    )
    out_specs = (
        P("dp", "section", "tensor"),
        P("section", None, None, None),
        P("section", None, None, None),
    )
    return jax.shard_map(
        per_device, mesh=mesh, in_specs=in_specs, out_specs=out_specs, check_vma=False
    )
```

time: 153 us -> 125 us (0.82)
  the two profiles are of different devices: /device:TPU:24 before, /device:TPU:64 now
where the time goes in v2:
time: 125 us; the launch traced here: 124 us
  waiting for transfers between devices  50.6 us (40%)
  starting transfers between devices  32.3 us (26%)
  Pallas kernels  30.1 us (24%)
  local copies, waits for them, and re-layouts  6.24 us (5%)
  other arithmetic  4.22 us (3%)
    ppermute x24, waiting for transfers between devices, move(): return lax.ppermute(block, PLANE, pairs)  43.3 us
    ppermute x24, starting transfers between devices, move(): return lax.ppermute(block, PLANE, pairs)  27.7 us
    pallas_call x3, Pallas kernels, project(): pl.pallas_call(project_kernel, out_shape=[jax.ShapeDtypeStruct((2, count,...  12.1 us
    pallas_call x2, Pallas kernels, feature_grad(): pl.pallas_call(feature_kernel, out_shape=[jax.ShapeDtypeStruct((cut, half...  9.03 us
    ppermute x1, waiting for transfers between devices, per_device(): facing = lax.ppermute(sums, 'tensor', TENSOR_SWAP)  7.23 us
    pallas_call x1, Pallas kernels, attend(): pl.pallas_call(attention_kernel, out_shape=[jax.ShapeDtypeStruct((rows, 2...  4.06 us
    pallas_call x1, Pallas kernels, pair_queries(): pl.pallas_call(pair_kernel, out_shape=jax.ShapeDtypeStruct((batches * kv_...  2.81 us
  transfers between devices with their start and end apart: 28, of which 11 were waited for; matrix products, arithmetic and copies ran while one was open for 5% of the time, Pallas kernels for 17%

profile of v2, /device:TPU:64, one launch (start us, length us, event | category | flops | bytes accessed | tf_op | source)
XLA Modules:
  0.0 124.5 jit_solution(16606556008027698429)
XLA Ops:
  1.7 1.2 collective-permute-done
  3.0 2.0 %collective-permute-start.1 = (bf16[12,4096]{1,0:T(8,128)(2,1)S(1)}, bf16[12,4096]{1,0:T(8,128)(2,1)S(1)}, u32[]{:S(2)}, u32[]{:S(2)}) collective-permute-start(bf16[12,4096]{1,0:T(8,128)(2,1)S(1)} %pad_maximum_fusion.2), channel_id=1, source_target_pairs={{0,16},{8,120},{16,32},{24,8},{32,48},{40,24},{48,64},{56,40},{64,... | collective-permute-start | bytes 294920 | tf_op jit(solution)/shard_map/ppermute | solution.py:44
  5.0 3.6 %collective-permute-start.2 = (bf16[12,4096]{1,0:T(8,128)(2,1)S(1)}, bf16[12,4096]{1,0:T(8,128)(2,1)S(1)}, u32[]{:S(2)}, u32[]{:S(2)}) collective-permute-start(bf16[12,4096]{1,0:T(8,128)(2,1)S(1)} %pad_maximum_fusion.2), channel_id=1, source_target_pairs={{0,32},{8,104},{16,48},{24,120},{32,64},{40,8},{48,80},{56,24},{64... | collective-permute-start | bytes 294920 | tf_op jit(solution)/shard_map/ppermute | solution.py:44
  8.6 1.0 collective-permute-start.3
  9.6 4.5 %collective-permute-start.4 = (bf16[6,4096]{1,0:T(8,128)(2,1)S(1)}, bf16[6,4096]{1,0:T(8,128)(2,1)S(1)}, u32[]{:S(2)}, u32[]{:S(2)}) collective-permute-start(bf16[6,4096]{1,0:T(8,128)(2,1)S(1)} %reshape.31), channel_id=1, source_target_pairs={{0,64},{8,72},{16,80},{24,88},{32,96},{40,104},{48,112},{56,120},{... | collective-permute-start | bytes 147464 | tf_op jit(solution)/shard_map/ppermute | solution.py:44
  14.0 8.6 %collective-permute-done.4 = bf16[6,4096]{1,0:T(8,128)(2,1)S(1)} collective-permute-done((bf16[6,4096]{1,0:T(8,128)(2,1)S(1)}, bf16[6,4096]{1,0:T(8,128)(2,1)S(1)}, u32[]{:S(2)}, u32[]{:S(2)}) %collective-permute-start.4) | collective-permute-done | bytes 49184 | tf_op jit(solution)/shard_map/ppermute | solution.py:44
  23.3 1.6 %collective-permute-start.6 = (bf16[48,4096]{1,0:T(8,128)(2,1)S(1)}, bf16[48,4096]{1,0:T(8,128)(2,1)S(1)}, u32[]{:S(2)}, u32[]{:S(2)}) collective-permute-start(bf16[48,4096]{1,0:T(8,128)(2,1)S(1)} %concatenate.26.refs_0_), channel_id=1, source_target_pairs={{0,4},{8,140},{16,20},{24,156},{32,36},{40,172},{48,52},{56,188},{... | collective-permute-start | bytes 1179656 | tf_op jit(solution)/shard_map/ppermute | solution.py:44
  24.8 2.1 %collective-permute-start.9 = (bf16[48,4096]{1,0:T(8,128)(2,1)S(1)}, bf16[48,4096]{1,0:T(8,128)(2,1)S(1)}, u32[]{:S(2)}, u32[]{:S(2)}) collective-permute-start(bf16[48,4096]{1,0:T(8,128)(2,1)S(1)} %concatenate.26.refs_0_), channel_id=1, source_target_pairs={{0,132},{8,12},{16,148},{24,28},{32,164},{40,44},{48,180},{56,60},... | collective-permute-start | bytes 1179656 | tf_op jit(solution)/shard_map/ppermute | solution.py:44
  26.9 8.5 %collective-permute-done.6.refs_0_ = bf16[48,4096]{1,0:T(8,128)(2,1)S(1)} collective-permute-done((bf16[48,4096]{1,0:T(8,128)(2,1)S(1)}, bf16[48,4096]{1,0:T(8,128)(2,1)S(1)}, u32[]{:S(2)}, u32[]{:S(2)}) %collective-permute-start.6) | collective-permute-done | bytes 393248 | tf_op jit(solution)/shard_map/ppermute | solution.py:44
  35.4 1.3 %dynamic-slice_bitcast_fusion.1 = (bf16[16,256]{1,0:T(8,128)(2,1)S(1)}, bf16[16,256]{1,0:T(8,128)(2,1)}) fusion(bf16[1,2,16,512]{3,2,1,0:T(8,128)(2,1)} %param.14, s32[]{:T(128)S(6)} %select_n.245, s32[]{:T(128)S(6)} %add.2257), kind=kLoop, calls=%fused_computation.32 | loop fusion | bytes 32776 | tf_op jit(solution)/shard_map/squeeze | solution.py:349
  39.1 5.3 %collective-permute-done.7.refs_0_.refs_2_ = bf16[48,4096]{1,0:T(8,128)(2,1)S(1)} collective-permute-done((bf16[48,4096]{1,0:T(8,128)(2,1)S(1)}, bf16[48,4096]{1,0:T(8,128)(2,1)S(1)}, u32[]{:S(2)}, u32[]{:S(2)}) %collective-permute-start.7) | collective-permute-done | bytes 393248 | tf_op jit(solution)/shard_map/ppermute | solution.py:44
  45.3 1.4 %copy-done.3 = bf16[1,3,128,2048]{3,2,1,0:T(8,128)(2,1)S(1)} copy-done((bf16[1,3,128,2048]{3,2,1,0:T(8,128)(2,1)S(1)}, bf16[1,3,128,2048]{3,2,1,0:T(8,128)(2,1)}, u32[]{:S(2)}) %copy-start.3) | copy-done | bytes 1572888
  46.7 2.8 %pair_queries.1.pair_ref = bf16[6,1024,256]{2,1,0:T(8,128)(2,1)} custom-call(bf16[2,128]{1,0:T(2,128)(2,1)S(1)} %bitcast.403, bf16[3,128,2048]{2,1,0:T(8,128)(2,1)S(1)} %bitcast.401, bf16[3,128,2048]{2,1,0:T(8,128)(2,1)S(1)} %bitcast.402), custom_call_target="tpu_custom_call" | custom-call | flops 200000000 | bytes 6291456 | tf_op jit(solution)/shard_map/pair_queries/pallas_call | solution.py:86
  49.5 3.8 %project.3 = (f32[2,96,256]{2,1,0:T(8,128)S(1)}, f32[96,32]{1,0:T(8,128)S(1)}) custom-call(s32[1]{0:T(128)} %bitcast.which_ref, bf16[48,4096]{1,0:T(8,128)(2,1)S(1)} %concatenate.26.refs_0_, bf16[48,4096]{1,0:T(8,128)(2,1)S(1)} %collective-permute-done.5.refs_1_, bf16[2,8192,256]{2,1,0:T(8,128)(2,1)} %bitcast.405, bf16[2,16,8192]{2,1,0:T(8,128)(2,1)S(1)} %bitcast.396), custom_call_target="tpu_custom_call" | custom-call | flops 805306368 | bytes 4980736 | tf_op jit(solution)/shard_map/project/pallas_call | solution.py:131
  53.3 4.3 %project.5 = (f32[2,192,256]{2,1,0:T(8,128)S(1)}, f32[192,32]{1,0:T(8,128)S(1)}) custom-call(s32[1]{0:T(128)S(6)} %sub.33.which_ref, bf16[48,4096]{1,0:T(8,128)(2,1)S(1)} %collective-permute-done.6.refs_0_, bf16[48,4096]{1,0:T(8,128)(2,1)S(1)} %collective-permute-done.9.refs_1_, bf16[48,4096]{1,0:T(8,128)(2,1)S(1)} %collective-permute-done.10.refs_2_, ...), custom_call_target="tpu_custom_call" | custom-call | flops 805306368 | bytes 5767168 | tf_op jit(solution)/shard_map/project/pallas_call | solution.py:131
  57.7 4.0 %project.4 = (f32[2,96,256]{2,1,0:T(8,128)S(1)}, f32[96,32]{1,0:T(8,128)S(1)}) custom-call(s32[1]{0:T(128)} %bitcast.which_ref, bf16[48,4096]{1,0:T(8,128)(2,1)S(1)} %collective-permute-done.7.refs_0_.refs_2_, bf16[48,4096]{1,0:T(8,128)(2,1)S(1)} %collective-permute-done.8.refs_1_.refs_3_, bf16[2,8192,256]{2,1,0:T(8,128)(2,1)} %bitcast.407, ...), custom_call_target="tpu_custom_call" | custom-call | flops 805306368 | bytes 4980736 | tf_op jit(solution)/shard_map/project/pallas_call | solution.py:131
  61.8 4.1 %attend.1 = (bf16[192,512]{1,0:T(8,128)(2,1)S(1)}, bf16[192,32]{1,0:T(8,128)(2,1)S(1)}, bf16[192,512]{1,0:T(8,128)(2,1)S(1)}, bf16[192,32]{1,0:T(8,128)(2,1)S(1)}, f32[32,256]{1,0:T(8,128)S(1)}) custom-call(s32[3]{0:T(128)S(1)} %copy-done.5, s32[3]{0:T(128)S(1)} %copy-done.6, f32[2,96,256]{2,1,0:T(8,128)S(1)} %get-tuple-element.27.y0, ...), custom_call_target="tpu_custom_call" | custom-call | flops 1000000000 | bytes 3145728 | tf_op jit(solution)/shard_map/attend/pallas_call | solution.py:227
  65.8 1.0 down_grad.2
  67.0 4.5 %feature_grad.2 = (bf16[48,4096]{1,0:T(8,128)(2,1)S(1)}, bf16[48,4096]{1,0:T(8,128)(2,1)S(1)}, bf16[48,4096]{1,0:T(8,128)(2,1)S(1)}, bf16[48,4096]{1,0:T(8,128)(2,1)S(1)}) custom-call(s32[1]{0:T(128)} %bitcast.which_ref, bf16[192,512]{1,0:T(8,128)(2,1)S(1)} %get-tuple-element.36.g_ref, bf16[192,32]{1,0:T(8,128)(2,1)S(1)} %get-tuple-element.37.m_ref, ...), custom_call_target="tpu_custom_call" | custom-call | flops 805306368 | bytes 5767168 | tf_op jit(solution)/shard_map/feature_grad/pallas_call | solution.py:273
  71.5 4.5 %feature_grad.3 = (bf16[48,4096]{1,0:T(8,128)(2,1)S(1)}, bf16[48,4096]{1,0:T(8,128)(2,1)S(1)}, bf16[48,4096]{1,0:T(8,128)(2,1)S(1)}, bf16[48,4096]{1,0:T(8,128)(2,1)S(1)}) custom-call(s32[1]{0:T(128)S(6)} %sub.33.which_ref, bf16[192,512]{1,0:T(8,128)(2,1)S(1)} %get-tuple-element.41.g_ref, bf16[192,32]{1,0:T(8,128)(2,1)S(1)} %get-tuple-element.35.m_ref, ...), custom_call_target="tpu_custom_call" | custom-call | flops 805306368 | bytes 5767168 | tf_op jit(solution)/shard_map/feature_grad/pallas_call | solution.py:273
  77.2 1.0 down_grad.3
  78.4 1.7 %collective-permute-start.25 = (bf16[32,4352]{1,0:T(8,128)(2,1)S(1)}, bf16[32,4352]{1,0:T(8,128)(2,1)S(1)}, u32[]{:S(2)}, u32[]{:S(2)}) collective-permute-start(bf16[32,4352]{1,0:T(8,128)(2,1)S(1)} %pad_maximum_fusion.1), channel_id=1, source_target_pairs={{0,1},{1,0},{2,3},{3,2},{4,5},{5,4},{6,7},{7,6},{8,9},{9,8},{10,11... | collective-permute-start | bytes 835592 | tf_op jit(solution)/shard_map/ppermute | solution.py:411
  80.8 2.8 %collective-permute-start.14 = (bf16[48,4096]{1,0:T(8,128)(2,1)S(1)}, bf16[48,4096]{1,0:T(8,128)(2,1)S(1)}, u32[]{:S(2)}, u32[]{:S(2)}) collective-permute-start(bf16[48,4096]{1,0:T(8,128)(2,1)S(1)} %add_convert_fusion.2), channel_id=1, source_target_pairs={{0,132},{8,12},{16,148},{24,28},{32,164},{40,44},{48,180},{56,60},... | collective-permute-start | bytes 1179656 | tf_op jit(solution)/shard_map/ppermute | solution.py:44
  83.6 5.6 %collective-permute-done.17 = bf16[48,4096]{1,0:T(8,128)(2,1)S(1)} collective-permute-done((bf16[48,4096]{1,0:T(8,128)(2,1)S(1)}, bf16[48,4096]{1,0:T(8,128)(2,1)S(1)}, u32[]{:S(2)}, u32[]{:S(2)}) %collective-permute-start.17) | collective-permute-done | bytes 393248 | tf_op jit(solution)/shard_map/ppermute | solution.py:44
  90.2 2.3 %collective-permute-start.26 = (bf16[32,4352]{1,0:T(8,128)(2,1)S(1)}, bf16[32,4352]{1,0:T(8,128)(2,1)S(1)}, u32[]{:S(2)}, u32[]{:S(2)}) collective-permute-start(bf16[32,4352]{1,0:T(8,128)(2,1)S(1)} %add_convert_fusion.4), channel_id=1, source_target_pairs={{0,3},{1,2},{2,1},{3,0},{4,7},{5,6},{6,5},{7,4},{8,11},{9,10},{10,... | collective-permute-start | bytes 835592 | tf_op jit(solution)/shard_map/ppermute | solution.py:417
  92.5 3.0 %collective-permute-done.14 = bf16[48,4096]{1,0:T(8,128)(2,1)S(1)} collective-permute-done((bf16[48,4096]{1,0:T(8,128)(2,1)S(1)}, bf16[48,4096]{1,0:T(8,128)(2,1)S(1)}, u32[]{:S(2)}, u32[]{:S(2)}) %collective-permute-start.14) | collective-permute-done | bytes 393248 | tf_op jit(solution)/shard_map/ppermute | solution.py:44
  95.4 1.8 %collective-permute-done.18 = bf16[48,4096]{1,0:T(8,128)(2,1)S(1)} collective-permute-done((bf16[48,4096]{1,0:T(8,128)(2,1)S(1)}, bf16[48,4096]{1,0:T(8,128)(2,1)S(1)}, u32[]{:S(2)}, u32[]{:S(2)}) %collective-permute-start.18) | collective-permute-done | bytes 393248 | tf_op jit(solution)/shard_map/ppermute | solution.py:44
  98.7 3.0 %collective-permute-start.22 = (bf16[12,4096]{1,0:T(8,128)(2,1)S(1)}, bf16[12,4096]{1,0:T(8,128)(2,1)S(1)}, u32[]{:S(2)}, u32[]{:S(2)}) collective-permute-start(bf16[12,4096]{1,0:T(8,128)(2,1)S(1)} %get-tuple-element.56), channel_id=1, source_target_pairs={{0,80},{8,56},{16,96},{24,72},{32,112},{40,88},{48,0},{56,104},{64... | collective-permute-start | bytes 294920 | tf_op jit(solution)/shard_map/ppermute | solution.py:44
  101.7 2.7 %collective-permute-start.19 = (bf16[6,4096]{1,0:T(8,128)(2,1)S(1)}, bf16[6,4096]{1,0:T(8,128)(2,1)S(1)}, u32[]{:S(2)}, u32[]{:S(2)}) collective-permute-start(bf16[6,4096]{1,0:T(8,128)(2,1)S(1)} %slice.62), channel_id=1, source_target_pairs={{0,64},{8,72},{16,80},{24,88},{32,96},{40,104},{48,112},{56,120},{... | collective-permute-start | bytes 147464 | tf_op jit(solution)/shard_map/ppermute | solution.py:44
  105.0 8.2 %collective-permute-done.22 = bf16[12,4096]{1,0:T(8,128)(2,1)S(1)} collective-permute-done((bf16[12,4096]{1,0:T(8,128)(2,1)S(1)}, bf16[12,4096]{1,0:T(8,128)(2,1)S(1)}, u32[]{:S(2)}, u32[]{:S(2)}) %collective-permute-start.22) | collective-permute-done | bytes 98336 | tf_op jit(solution)/shard_map/ppermute | solution.py:44
  115.3 7.2 %collective-permute-done.27 = bf16[32,4352]{1,0:T(8,128)(2,1)S(1)} collective-permute-done((bf16[32,4352]{1,0:T(8,128)(2,1)S(1)}, bf16[32,4352]{1,0:T(8,128)(2,1)S(1)}, u32[]{:S(2)}, u32[]{:S(2)}) %collective-permute-start.27) | collective-permute-done | bytes 278560 | tf_op jit(solution)/shard_map/ppermute | solution.py:421
  123.4 1.0 pad_maximum_fusion
  (77 shorter events, 13.2 us)
Async XLA Ops:
  0.6 44.6 %copy-start.2 = (bf16[1,3,128,2048]{3,2,1,0:T(8,128)(2,1)S(1)}, bf16[1,3,128,2048]{3,2,1,0:T(8,128)(2,1)}, u32[]{:S(2)}) copy-start(bf16[1,3,128,2048]{3,2,1,0:T(8,128)(2,1)} %param.9) | copy-start | bytes 4718596
  0.6 44.6 %copy-start.4 = (bf16[1,2,128]{2,1,0:T(2,128)(2,1)S(1)}, bf16[1,2,128]{2,1,0:T(2,128)(2,1)}, u32[]{:S(2)}) copy-start(bf16[1,2,128]{2,1,0:T(2,128)(2,1)} %param.15) | copy-start | bytes 1540
  1.6 1.3 %collective-permute-start = (bf16[6,4096]{1,0:T(8,128)(2,1)S(1)}, bf16[6,4096]{1,0:T(8,128)(2,1)S(1)}, u32[]{:S(2)}, u32[]{:S(2)}) collective-permute-start(bf16[6,4096]{1,0:T(8,128)(2,1)S(1)} %reshape.31), channel_id=1, source_target_pairs={{0,8},{8,0},{16,24},{24,16},{32,40},{40,32},{48,56},{56,48},{64,72... | collective-permute-start | bytes 147464 | tf_op jit(solution)/shard_map/ppermute | solution.py:44
  3.0 19.7 %collective-permute-start.1 = (bf16[12,4096]{1,0:T(8,128)(2,1)S(1)}, bf16[12,4096]{1,0:T(8,128)(2,1)S(1)}, u32[]{:S(2)}, u32[]{:S(2)}) collective-permute-start(bf16[12,4096]{1,0:T(8,128)(2,1)S(1)} %pad_maximum_fusion.2), channel_id=1, source_target_pairs={{0,16},{8,120},{16,32},{24,8},{32,48},{40,24},{48,64},{56,40},{64,... | collective-permute-start | bytes 294920 | tf_op jit(solution)/shard_map/ppermute | solution.py:44
  5.0 17.7 %collective-permute-start.2 = (bf16[12,4096]{1,0:T(8,128)(2,1)S(1)}, bf16[12,4096]{1,0:T(8,128)(2,1)S(1)}, u32[]{:S(2)}, u32[]{:S(2)}) collective-permute-start(bf16[12,4096]{1,0:T(8,128)(2,1)S(1)} %pad_maximum_fusion.2), channel_id=1, source_target_pairs={{0,32},{8,104},{16,48},{24,120},{32,64},{40,8},{48,80},{56,24},{64... | collective-permute-start | bytes 294920 | tf_op jit(solution)/shard_map/ppermute | solution.py:44
  8.6 14.1 %collective-permute-start.3 = (bf16[12,4096]{1,0:T(8,128)(2,1)S(1)}, bf16[12,4096]{1,0:T(8,128)(2,1)S(1)}, u32[]{:S(2)}, u32[]{:S(2)}) collective-permute-start(bf16[12,4096]{1,0:T(8,128)(2,1)S(1)} %pad_maximum_fusion.2), channel_id=1, source_target_pairs={{0,48},{8,88},{16,64},{24,104},{32,80},{40,120},{48,96},{56,8},{64... | collective-permute-start | bytes 294920 | tf_op jit(solution)/shard_map/ppermute | solution.py:44
  9.6 13.1 %collective-permute-start.4 = (bf16[6,4096]{1,0:T(8,128)(2,1)S(1)}, bf16[6,4096]{1,0:T(8,128)(2,1)S(1)}, u32[]{:S(2)}, u32[]{:S(2)}) collective-permute-start(bf16[6,4096]{1,0:T(8,128)(2,1)S(1)} %reshape.31), channel_id=1, source_target_pairs={{0,64},{8,72},{16,80},{24,88},{32,96},{40,104},{48,112},{56,120},{... | collective-permute-start | bytes 147464 | tf_op jit(solution)/shard_map/ppermute | solution.py:44
  23.3 12.1 %collective-permute-start.6 = (bf16[48,4096]{1,0:T(8,128)(2,1)S(1)}, bf16[48,4096]{1,0:T(8,128)(2,1)S(1)}, u32[]{:S(2)}, u32[]{:S(2)}) collective-permute-start(bf16[48,4096]{1,0:T(8,128)(2,1)S(1)} %concatenate.26.refs_0_), channel_id=1, source_target_pairs={{0,4},{8,140},{16,20},{24,156},{32,36},{40,172},{48,52},{56,188},{... | collective-permute-start | bytes 1179656 | tf_op jit(solution)/shard_map/ppermute | solution.py:44
  24.8 13.5 %collective-permute-start.9 = (bf16[48,4096]{1,0:T(8,128)(2,1)S(1)}, bf16[48,4096]{1,0:T(8,128)(2,1)S(1)}, u32[]{:S(2)}, u32[]{:S(2)}) collective-permute-start(bf16[48,4096]{1,0:T(8,128)(2,1)S(1)} %concatenate.26.refs_0_), channel_id=1, source_target_pairs={{0,132},{8,12},{16,148},{24,28},{32,164},{40,44},{48,180},{56,60},... | collective-permute-start | bytes 1179656 | tf_op jit(solution)/shard_map/ppermute | solution.py:44
  35.4 9.0 %collective-permute-start.7 = (bf16[48,4096]{1,0:T(8,128)(2,1)S(1)}, bf16[48,4096]{1,0:T(8,128)(2,1)S(1)}, u32[]{:S(2)}, u32[]{:S(2)}) collective-permute-start(bf16[48,4096]{1,0:T(8,128)(2,1)S(1)} %collective-permute-done.6.refs_0_), channel_id=1, source_target_pairs={{0,132},{8,12},{16,148},{24,28},{32,164},{40,44},{48,180},{56,60},... | collective-permute-start | bytes 1179656 | tf_op jit(solution)/shard_map/ppermute | solution.py:44
  36.7 12.8 %collective-permute-start.5 = (bf16[48,4096]{1,0:T(8,128)(2,1)S(1)}, bf16[48,4096]{1,0:T(8,128)(2,1)S(1)}, u32[]{:S(2)}, u32[]{:S(2)}) collective-permute-start(bf16[48,4096]{1,0:T(8,128)(2,1)S(1)} %concatenate.26.refs_0_), channel_id=1, source_target_pairs={{0,8},{8,0},{16,24},{24,16},{32,40},{40,32},{48,56},{56,48},{64,72... | collective-permute-start | bytes 1179656 | tf_op jit(solution)/shard_map/ppermute | solution.py:44
  37.9 15.5 %collective-permute-start.10 = (bf16[48,4096]{1,0:T(8,128)(2,1)S(1)}, bf16[48,4096]{1,0:T(8,128)(2,1)S(1)}, u32[]{:S(2)}, u32[]{:S(2)}) collective-permute-start(bf16[48,4096]{1,0:T(8,128)(2,1)S(1)} %collective-permute-done.6.refs_0_), channel_id=1, source_target_pairs={{0,8},{8,0},{16,24},{24,16},{32,40},{40,32},{48,56},{56,48},{64,72... | collective-permute-start | bytes 1179656 | tf_op jit(solution)/shard_map/ppermute | solution.py:44
  38.4 15.0 %collective-permute-start.11 = (bf16[48,4096]{1,0:T(8,128)(2,1)S(1)}, bf16[48,4096]{1,0:T(8,128)(2,1)S(1)}, u32[]{:S(2)}, u32[]{:S(2)}) collective-permute-start(bf16[48,4096]{1,0:T(8,128)(2,1)S(1)} %collective-permute-done.9.refs_1_), channel_id=1, source_target_pairs={{0,8},{8,0},{16,24},{24,16},{32,40},{40,32},{48,56},{56,48},{64,72... | collective-permute-start | bytes 1179656 | tf_op jit(solution)/shard_map/ppermute | solution.py:44
  44.4 13.3 %collective-permute-start.8 = (bf16[48,4096]{1,0:T(8,128)(2,1)S(1)}, bf16[48,4096]{1,0:T(8,128)(2,1)S(1)}, u32[]{:S(2)}, u32[]{:S(2)}) collective-permute-start(bf16[48,4096]{1,0:T(8,128)(2,1)S(1)} %collective-permute-done.7.refs_0_.refs_2_), channel_id=1, source_target_pairs={{0,8},{8,0},{16,24},{24,16},{32,40},{40,32},{48,56},{56,48},{64,72... | collective-permute-start | bytes 1179656 | tf_op jit(solution)/shard_map/ppermute | solution.py:44
  57.7 4.0 %copy-start.1 = (bf16[6,1024,256]{2,1,0:T(8,128)(2,1)S(1)}, bf16[6,1024,256]{2,1,0:T(8,128)(2,1)}, u32[]{:S(2)}) copy-start(bf16[6,1024,256]{2,1,0:T(8,128)(2,1)} %pair_queries.1.pair_ref) | copy-start | bytes 9437188
  57.7 4.0 %copy-start.5 = (s32[3]{0:T(128)S(1)}, s32[3]{0:T(128)}, u32[]{:S(2)}) copy-start(s32[3]{0:T(128)} %count_ref.1) | copy-start | bytes 40
  66.9 11.4 %collective-permute-start.24 = (bf16[32,4096]{1,0:T(8,128)(2,1)S(1)}, bf16[32,4096]{1,0:T(8,128)(2,1)S(1)}, u32[]{:S(2)}, u32[]{:S(2)}) collective-permute-start(bf16[32,4096]{1,0:T(8,128)(2,1)S(1)} %down_grad.2), channel_id=1, source_target_pairs={{0,4},{4,0},{1,5},{5,1},{2,6},{6,2},{3,7},{7,3},{8,12},{12,8},{9,1... | collective-permute-start | bytes 786440 | tf_op jit(solution)/shard_map/ppermute | solution.py:391
  76.0 7.6 %collective-permute-start.15 = (bf16[48,4096]{1,0:T(8,128)(2,1)S(1)}, bf16[48,4096]{1,0:T(8,128)(2,1)S(1)}, u32[]{:S(2)}, u32[]{:S(2)}) collective-permute-start(bf16[48,4096]{1,0:T(8,128)(2,1)S(1)} %get-tuple-element.45), channel_id=1, source_target_pairs={{0,8},{8,0},{16,24},{24,16},{32,40},{40,32},{48,56},{56,48},{64,72... | collective-permute-start | bytes 1179656 | tf_op jit(solution)/shard_map/ppermute | solution.py:44
  76.6 3.4 %collective-permute-start.16 = (bf16[48,4096]{1,0:T(8,128)(2,1)S(1)}, bf16[48,4096]{1,0:T(8,128)(2,1)S(1)}, u32[]{:S(2)}, u32[]{:S(2)}) collective-permute-start(bf16[48,4096]{1,0:T(8,128)(2,1)S(1)} %get-tuple-element.47), channel_id=1, source_target_pairs={{0,8},{8,0},{16,24},{24,16},{32,40},{40,32},{48,56},{56,48},{64,72... | collective-permute-start | bytes 1179656 | tf_op jit(solution)/shard_map/ppermute | solution.py:44
  76.7 4.0 %collective-permute-start.13 = (bf16[48,4096]{1,0:T(8,128)(2,1)S(1)}, bf16[48,4096]{1,0:T(8,128)(2,1)S(1)}, u32[]{:S(2)}, u32[]{:S(2)}) collective-permute-start(bf16[48,4096]{1,0:T(8,128)(2,1)S(1)} %get-tuple-element.43), channel_id=1, source_target_pairs={{0,8},{8,0},{16,24},{24,16},{32,40},{40,32},{48,56},{56,48},{64,72... | collective-permute-start | bytes 1179656 | tf_op jit(solution)/shard_map/ppermute | solution.py:44
  77.1 15.3 %collective-permute-start.12 = (bf16[48,4096]{1,0:T(8,128)(2,1)S(1)}, bf16[48,4096]{1,0:T(8,128)(2,1)S(1)}, u32[]{:S(2)}, u32[]{:S(2)}) collective-permute-start(bf16[48,4096]{1,0:T(8,128)(2,1)S(1)} %get-tuple-element.39), channel_id=1, source_target_pairs={{0,8},{8,0},{16,24},{24,16},{32,40},{40,32},{48,56},{56,48},{64,72... | collective-permute-start | bytes 1179656 | tf_op jit(solution)/shard_map/ppermute | solution.py:44
  78.4 11.8 %collective-permute-start.25 = (bf16[32,4352]{1,0:T(8,128)(2,1)S(1)}, bf16[32,4352]{1,0:T(8,128)(2,1)S(1)}, u32[]{:S(2)}, u32[]{:S(2)}) collective-permute-start(bf16[32,4352]{1,0:T(8,128)(2,1)S(1)} %pad_maximum_fusion.1), channel_id=1, source_target_pairs={{0,1},{1,0},{2,3},{3,2},{4,5},{5,4},{6,7},{7,6},{8,9},{9,8},{10,11... | collective-permute-start | bytes 835592 | tf_op jit(solution)/shard_map/ppermute | solution.py:411
  80.1 9.1 %collective-permute-start.17 = (bf16[48,4096]{1,0:T(8,128)(2,1)S(1)}, bf16[48,4096]{1,0:T(8,128)(2,1)S(1)}, u32[]{:S(2)}, u32[]{:S(2)}) collective-permute-start(bf16[48,4096]{1,0:T(8,128)(2,1)S(1)} %add_convert_fusion.1), channel_id=1, source_target_pairs={{0,132},{8,12},{16,148},{24,28},{32,164},{40,44},{48,180},{56,60},... | collective-permute-start | bytes 1179656 | tf_op jit(solution)/shard_map/ppermute | solution.py:44
  80.8 14.6 %collective-permute-start.14 = (bf16[48,4096]{1,0:T(8,128)(2,1)S(1)}, bf16[48,4096]{1,0:T(8,128)(2,1)S(1)}, u32[]{:S(2)}, u32[]{:S(2)}) collective-permute-start(bf16[48,4096]{1,0:T(8,128)(2,1)S(1)} %add_convert_fusion.2), channel_id=1, source_target_pairs={{0,132},{8,12},{16,148},{24,28},{32,164},{40,44},{48,180},{56,60},... | collective-permute-start | bytes 1179656 | tf_op jit(solution)/shard_map/ppermute | solution.py:44
  89.3 7.9 %collective-permute-start.18 = (bf16[48,4096]{1,0:T(8,128)(2,1)S(1)}, bf16[48,4096]{1,0:T(8,128)(2,1)S(1)}, u32[]{:S(2)}, u32[]{:S(2)}) collective-permute-start(bf16[48,4096]{1,0:T(8,128)(2,1)S(1)} %add_convert_fusion), channel_id=1, source_target_pairs={{0,4},{8,140},{16,20},{24,156},{32,36},{40,172},{48,52},{56,188},{... | collective-permute-start | bytes 1179656 | tf_op jit(solution)/shard_map/ppermute | solution.py:44
  90.2 11.5 %collective-permute-start.26 = (bf16[32,4352]{1,0:T(8,128)(2,1)S(1)}, bf16[32,4352]{1,0:T(8,128)(2,1)S(1)}, u32[]{:S(2)}, u32[]{:S(2)}) collective-permute-start(bf16[32,4352]{1,0:T(8,128)(2,1)S(1)} %add_convert_fusion.4), channel_id=1, source_target_pairs={{0,3},{1,2},{2,1},{3,0},{4,7},{5,6},{6,5},{7,4},{8,11},{9,10},{10,... | collective-permute-start | bytes 835592 | tf_op jit(solution)/shard_map/ppermute | solution.py:417
  97.5 6.9 %collective-permute-start.20 = (bf16[12,4096]{1,0:T(8,128)(2,1)S(1)}, bf16[12,4096]{1,0:T(8,128)(2,1)S(1)}, u32[]{:S(2)}, u32[]{:S(2)}) collective-permute-start(bf16[12,4096]{1,0:T(8,128)(2,1)S(1)} %get-tuple-element.55), channel_id=1, source_target_pairs={{0,112},{8,24},{16,0},{24,40},{32,16},{40,56},{48,32},{56,72},{64,... | collective-permute-start | bytes 294920 | tf_op jit(solution)/shard_map/ppermute | solution.py:44
  97.8 7.3 %collective-permute-start.21 = (bf16[12,4096]{1,0:T(8,128)(2,1)S(1)}, bf16[12,4096]{1,0:T(8,128)(2,1)S(1)}, u32[]{:S(2)}, u32[]{:S(2)}) collective-permute-start(bf16[12,4096]{1,0:T(8,128)(2,1)S(1)} %get-tuple-element.57), channel_id=1, source_target_pairs={{0,96},{8,40},{16,112},{24,56},{32,0},{40,72},{48,16},{56,88},{64,... | collective-permute-start | bytes 294920 | tf_op jit(solution)/shard_map/ppermute | solution.py:44
  98.7 14.5 %collective-permute-start.22 = (bf16[12,4096]{1,0:T(8,128)(2,1)S(1)}, bf16[12,4096]{1,0:T(8,128)(2,1)S(1)}, u32[]{:S(2)}, u32[]{:S(2)}) collective-permute-start(bf16[12,4096]{1,0:T(8,128)(2,1)S(1)} %get-tuple-element.56), channel_id=1, source_target_pairs={{0,80},{8,56},{16,96},{24,72},{32,112},{40,88},{48,0},{56,104},{64... | collective-permute-start | bytes 294920 | tf_op jit(solution)/shard_map/ppermute | solution.py:44
  101.7 12.4 %collective-permute-start.19 = (bf16[6,4096]{1,0:T(8,128)(2,1)S(1)}, bf16[6,4096]{1,0:T(8,128)(2,1)S(1)}, u32[]{:S(2)}, u32[]{:S(2)}) collective-permute-start(bf16[6,4096]{1,0:T(8,128)(2,1)S(1)} %slice.62), channel_id=1, source_target_pairs={{0,64},{8,72},{16,80},{24,88},{32,96},{40,104},{48,112},{56,120},{... | collective-permute-start | bytes 147464 | tf_op jit(solution)/shard_map/ppermute | solution.py:44
  113.3 1.3 %collective-permute-start.23 = (bf16[6,4096]{1,0:T(8,128)(2,1)S(1)}, bf16[6,4096]{1,0:T(8,128)(2,1)S(1)}, u32[]{:S(2)}, u32[]{:S(2)}) collective-permute-start(bf16[6,4096]{1,0:T(8,128)(2,1)S(1)} %slice.79), channel_id=1, source_target_pairs={{0,8},{8,0},{16,24},{24,16},{32,40},{40,32},{48,56},{56,48},{64,72... | collective-permute-start | bytes 147464 | tf_op jit(solution)/shard_map/ppermute | solution.py:44
  113.4 9.1 %collective-permute-start.27 = (bf16[32,4352]{1,0:T(8,128)(2,1)S(1)}, bf16[32,4352]{1,0:T(8,128)(2,1)S(1)}, u32[]{:S(2)}, u32[]{:S(2)}) collective-permute-start(bf16[32,4352]{1,0:T(8,128)(2,1)S(1)} %add_convert_fusion.3), channel_id=1, source_target_pairs={{0,4},{4,0},{1,5},{5,1},{2,6},{6,2},{3,7},{7,3},{8,12},{12,8},{9,1... | collective-permute-start | bytes 835592 | tf_op jit(solution)/shard_map/ppermute | solution.py:421
  (3 other events, 8.3 us)

commit v3 on v2

--- a/solution.py
+++ b/solution.py
@@ -25,13 +25,9 @@
 
 
 SIBLING = plane_pairs(lambda x, z, core: (x, z, 1 - core))
-RISE = {
-    k: plane_pairs(lambda x, z, core, k=k: (x, (z + (k if core == 0 else -k)) % NZ, core))
-    for k in (1, 2, 3, 4)
-}
-FALL = {
-    k: plane_pairs(lambda x, z, core, k=k: (x, (z - (k if core == 0 else -k)) % NZ, core))
-    for k in (1, 2, 3, 4)
+SHIFTS = (4, 3, 5, 2, 6, 1, 7)
+ALONG = {
+    k: plane_pairs(lambda x, z, core, k=k: (x, (z + k) % NZ, core)) for k in SHIFTS
 }
 NEAR = plane_pairs(lambda x, z, core: (x ^ 1 if core == 0 else 3 - x, z, core))
 FAR = plane_pairs(lambda x, z, core: (3 - x if core == 0 else x ^ 1, z, core))
@@ -304,15 +300,9 @@
 
 def row_tokens(x_hi, z, core, x_lo):
     def base_rows(chain, x_high):
-        step = jnp.where(chain == 0, 1, -1)
-        places = []
-        for k in (1, 2, 3):
-            for other in (0, 1):
-                places.append(((z - step * k) % NZ, jnp.where(other == 0, chain, 1 - chain)))
-        places += [((z - step * 4) % NZ, chain), (z, chain)]
         rows = []
-        for level, which in places:
-            token = ((x_high * NZ + level) * 2 + which) * 2
+        for k in (*SHIFTS, 0):
+            token = ((x_high * NZ + (z - k) % NZ) * 2 + chain) * 2
             for batch in range(3):
                 rows += [batch * 64 + token, batch * 64 + token + 1]
         return jnp.stack(rows)
@@ -344,32 +334,21 @@
     ranks = 2 * down_maps.shape[1]
     here = side.reshape(1).astype(jnp.int32)
     opposite = 1 - here
-    up_maps = lax.dynamic_slice_in_dim(adapter_up_maps[0], side * width, width, 2)
-    up_diagonal = jnp.concatenate(
-        [jnp.pad(up_maps[0], ((0, 0), (0, width))), jnp.pad(up_maps[1], ((0, 0), (width, 0)))]
-    )
 
     own = vision_feature_states.reshape(-1, half)
-    chip = jnp.concatenate([own, move(own, SIBLING)])
-    parts = [move(chip, RISE[k]) for k in (1, 2, 3)] + [move(own, RISE[4]), own]
-    pair = pair_queries(
-        after(queries[0], chip), context_gradient[0], gains, width // gains.shape[1]
-    )
-    base = jnp.concatenate(parts)
+    base = jnp.concatenate([move(own, ALONG[k]) for k in SHIFTS] + [own])
     first = move(base, NEAR)
     second = move(base, FAR)
     base_there = move(base, SIBLING)
-    step_a = project([base, base_there], weights, down_maps, here)
-    third = move(first, FAR)
-    first_there = move(first, SIBLING)
-    second_there = move(second, SIBLING)
-    others = [first, second, first_there, second_there]
-    step_b = project(others, weights, down_maps, opposite)
-    third_there = move(third, SIBLING)
-    step_c = project([third, third_there], weights, down_maps, here)
-    owns = [base, base_there, third, third_there]
-
-    own_token, other_token = row_tokens(section // 16, (section // 2) % NZ, section % 2, side)
+    late_side = after(side, base)
+    late_section = after(section, base)
+    up_maps = lax.dynamic_slice_in_dim(adapter_up_maps[0], late_side * width, width, 2)
+    up_diagonal = jnp.concatenate(
+        [jnp.pad(up_maps[0], ((0, 0), (0, width))), jnp.pad(up_maps[1], ((0, 0), (width, 0)))]
+    )
+    own_token, other_token = row_tokens(
+        late_section // 16, (late_section // 2) % NZ, late_section % 2, late_side
+    )
     line = jnp.arange(own_token.shape[0])
     maps = [
         (line[:, None] == own_token[None]).astype(LOW),
@@ -377,6 +356,21 @@
         (own_token[:, None] == line[None]).astype(LOW),
         (other_token[:, None] == line[None]).astype(LOW),
     ]
+    pair = pair_queries(
+        after(queries[0], base), context_gradient[0], gains, width // gains.shape[1]
+    )
+    step_a = project([base, base_there], weights, down_maps, here)
+    first = after(first, pair, *step_a, up_diagonal, *maps)
+    third = move(first, FAR)
+    first_there = move(first, SIBLING)
+    second_there = move(second, SIBLING)
+    others = [first, second, first_there, second_there]
+    step_b = project(others, weights, down_maps, opposite)
+    third = after(third, *step_b)
+    third_there = move(third, SIBLING)
+    step_c = project([third, third_there], weights, down_maps, here)
+    owns = [base, base_there, third, third_there]
+
     g_own, m_own, g_other, m_other, up_part = attend(
         image_tile_count,
         text_start_position,
@@ -393,37 +387,36 @@
         after(g_own, down_other), m_own, weights, down_maps, here
     )
     down_own = down_grad(m_own, owns, F32)
-    first, second, first_out, second_out = feature_grad(
-        after(g_other, base), m_other, weights, down_maps, opposite
-    )
+    sums = jnp.concatenate(
+        [down_own + after(down_facing, base).astype(F32), up_part], 1
+    ).astype(LOW)
+    near_sums = lax.ppermute(sums, "dp", DP_NEAR)
 
     def add(mine, theirs):
         return mine.astype(F32) + theirs.astype(F32)
 
     third = add(third, move(third_out, SIBLING)).astype(LOW)
+    third_in = move(third, FAR)
+    first, second, first_out, second_out = feature_grad(
+        after(g_other, sums, third), m_other, weights, down_maps, opposite
+    )
     second = add(second, move(second_out, SIBLING)).astype(LOW)
     first = add(first, move(first_out, SIBLING))
     base = add(base, move(base_out, SIBLING))
 
-    sums = jnp.concatenate(
-        [down_own + after(down_facing, first_out).astype(F32), up_part], 1
-    ).astype(LOW)
-    near_sums = lax.ppermute(sums, "dp", DP_NEAR)
-    third_in = move(third, FAR)
     second_in = move(second, FAR)
+    sums = add(sums, after(near_sums, second)).astype(LOW)
+    far_sums = lax.ppermute(sums, "dp", DP_FAR)
     first = (first + third_in.astype(F32)).astype(LOW)
     first_in = move(first, NEAR)
-    sums = add(sums, after(near_sums, first)).astype(LOW)
-    far_sums = lax.ppermute(sums, "dp", DP_FAR)
+    sums = add(sums, after(far_sums, first)).astype(LOW)
+    facing = lax.ppermute(sums, "tensor", TENSOR_SWAP)
     base = base + second_in.astype(F32) + first_in.astype(F32)
-    sent = base[:42].astype(LOW)
-    sums = add(sums, after(far_sums, sent)).astype(LOW)
-    facing = lax.ppermute(sums, "tensor", TENSOR_SWAP)
-    low_rows = [move(sent[12 * i : 12 * i + 12], FALL[k]) for i, k in enumerate((1, 2, 3))]
-    own = base[42:] + move(sent[36:42], FALL[4]).astype(F32)
-    chip = sum(block.astype(F32) for block in low_rows)
-    passed = move(chip[6:].astype(LOW), SIBLING)
-    own_grad = own + chip[:6] + passed.astype(F32)
+    low_base = base.astype(LOW)
+    count = own.shape[0]
+    own_grad = base[len(SHIFTS) * count :]
+    for i, k in enumerate(SHIFTS):
+        own_grad += move(low_base[i * count : (i + 1) * count], ALONG[NZ - k]).astype(F32)
 
     left = jnp.where(side == 0, sums, facing).astype(F32)
     right = jnp.where(side == 0, facing, sums).astype(F32)

time: 125 us -> 117 us (0.936)
  the two profiles are of different devices: /device:TPU:64 before, /device:TPU:24 now
where the time goes in v3:
time: 117 us; the launch traced here: 115 us
  starting transfers between devices  45.8 us (39%)
  waiting for transfers between devices  30.2 us (26%)
  Pallas kernels  29.9 us (26%)
  local copies, waits for them, and re-layouts  5.36 us (5%)
  other arithmetic  2.71 us (2%)
  between operations  1.3 us (1%)
    ppermute x28, starting transfers between devices, move(): return lax.ppermute(block, PLANE, pairs)  43.8 us
    ppermute x28, waiting for transfers between devices, move(): return lax.ppermute(block, PLANE, pairs)  20.8 us
    pallas_call x3, Pallas kernels, project(): pl.pallas_call(project_kernel, out_shape=[jax.ShapeDtypeStruct((2, count,...  12 us
    pallas_call x2, Pallas kernels, feature_grad(): pl.pallas_call(feature_kernel, out_shape=[jax.ShapeDtypeStruct((cut, half...  9.03 us
    ppermute x1, waiting for transfers between devices, per_device(): near_sums = lax.ppermute(sums, 'dp', DP_NEAR)  4.49 us
    pallas_call x1, Pallas kernels, attend(): pl.pallas_call(attention_kernel, out_shape=[jax.ShapeDtypeStruct((rows, 2...  4.05 us
    pallas_call x1, Pallas kernels, pair_queries(): pl.pallas_call(pair_kernel, out_shape=jax.ShapeDtypeStruct((batches * kv_...  2.78 us
    ppermute x1, waiting for transfers between devices, per_device(): down_facing = lax.ppermute(down_other, 'tensor', TENSOR_SWAP)  2.55 us
  transfers between devices with their start and end apart: 32, of which 18 were waited for; matrix products, arithmetic and copies ran while one was open for 3% of the time, Pallas kernels for 14%

profile of v3, /device:TPU:24, one launch (start us, length us, event | category | flops | bytes accessed | tf_op | source)
XLA Modules:
  0.0 115.3 jit_solution(9656071567012449688)
XLA Ops:
  1.6 7.3 %collective-permute-start = (bf16[6,4096]{1,0:T(8,128)(2,1)S(1)}, bf16[6,4096]{1,0:T(8,128)(2,1)S(1)}, u32[]{:S(2)}, u32[]{:S(2)}) collective-permute-start(bf16[6,4096]{1,0:T(8,128)(2,1)S(1)} %reshape.31), channel_id=1, source_target_pairs={{0,64},{8,72},{16,80},{24,88},{32,96},{40,104},{48,112},{56,120},{... | collective-permute-start | bytes 147464 | tf_op jit(solution)/shard_map/ppermute | solution.py:40
  8.9 1.9 %collective-permute-start.1 = (bf16[6,4096]{1,0:T(8,128)(2,1)S(1)}, bf16[6,4096]{1,0:T(8,128)(2,1)S(1)}, u32[]{:S(2)}, u32[]{:S(2)}) collective-permute-start(bf16[6,4096]{1,0:T(8,128)(2,1)S(1)} %reshape.31), channel_id=1, source_target_pairs={{0,48},{8,56},{16,64},{24,72},{32,80},{40,88},{48,96},{56,104},{64... | collective-permute-start | bytes 147464 | tf_op jit(solution)/shard_map/ppermute | solution.py:40
  10.8 3.1 %collective-permute-start.2 = (bf16[6,4096]{1,0:T(8,128)(2,1)S(1)}, bf16[6,4096]{1,0:T(8,128)(2,1)S(1)}, u32[]{:S(2)}, u32[]{:S(2)}) collective-permute-start(bf16[6,4096]{1,0:T(8,128)(2,1)S(1)} %reshape.31), channel_id=1, source_target_pairs={{0,80},{8,88},{16,96},{24,104},{32,112},{40,120},{48,0},{56,8},{64... | collective-permute-start | bytes 147464 | tf_op jit(solution)/shard_map/ppermute | solution.py:40
  13.9 1.5 %collective-permute-start.3 = (bf16[6,4096]{1,0:T(8,128)(2,1)S(1)}, bf16[6,4096]{1,0:T(8,128)(2,1)S(1)}, u32[]{:S(2)}, u32[]{:S(2)}) collective-permute-start(bf16[6,4096]{1,0:T(8,128)(2,1)S(1)} %reshape.31), channel_id=1, source_target_pairs={{0,32},{8,40},{16,48},{24,56},{32,64},{40,72},{48,80},{56,88},{64,... | collective-permute-start | bytes 147464 | tf_op jit(solution)/shard_map/ppermute | solution.py:40
  15.4 2.7 %collective-permute-start.4 = (bf16[6,4096]{1,0:T(8,128)(2,1)S(1)}, bf16[6,4096]{1,0:T(8,128)(2,1)S(1)}, u32[]{:S(2)}, u32[]{:S(2)}) collective-permute-start(bf16[6,4096]{1,0:T(8,128)(2,1)S(1)} %reshape.31), channel_id=1, source_target_pairs={{0,96},{8,104},{16,112},{24,120},{32,0},{40,8},{48,16},{56,24},{64... | collective-permute-start | bytes 147464 | tf_op jit(solution)/shard_map/ppermute | solution.py:40
  19.1 2.2 %collective-permute-start.6 = (bf16[6,4096]{1,0:T(8,128)(2,1)S(1)}, bf16[6,4096]{1,0:T(8,128)(2,1)S(1)}, u32[]{:S(2)}, u32[]{:S(2)}) collective-permute-start(bf16[6,4096]{1,0:T(8,128)(2,1)S(1)} %reshape.31), channel_id=1, source_target_pairs={{0,112},{8,120},{16,0},{24,8},{32,16},{40,24},{48,32},{56,40},{64,... | collective-permute-start | bytes 147464 | tf_op jit(solution)/shard_map/ppermute | solution.py:40
  24.9 1.6 %collective-permute-start.8 = (bf16[48,4096]{1,0:T(8,128)(2,1)S(1)}, bf16[48,4096]{1,0:T(8,128)(2,1)S(1)}, u32[]{:S(2)}, u32[]{:S(2)}) collective-permute-start(bf16[48,4096]{1,0:T(8,128)(2,1)S(1)} %concatenate.22.refs_0_), channel_id=1, source_target_pairs={{0,4},{8,140},{16,20},{24,156},{32,36},{40,172},{48,52},{56,188},{... | collective-permute-start | bytes 1179656 | tf_op jit(solution)/shard_map/ppermute | solution.py:40
  26.4 2.1 %collective-permute-start.10 = (bf16[48,4096]{1,0:T(8,128)(2,1)S(1)}, bf16[48,4096]{1,0:T(8,128)(2,1)S(1)}, u32[]{:S(2)}, u32[]{:S(2)}) collective-permute-start(bf16[48,4096]{1,0:T(8,128)(2,1)S(1)} %concatenate.22.refs_0_), channel_id=1, source_target_pairs={{0,132},{8,12},{16,148},{24,28},{32,164},{40,44},{48,180},{56,60},... | collective-permute-start | bytes 1179656 | tf_op jit(solution)/shard_map/ppermute | solution.py:40
  31.3 2.8 %pair_queries.1.pair_ref = bf16[6,1024,256]{2,1,0:T(8,128)(2,1)} custom-call(bf16[2,128]{1,0:T(2,128)(2,1)S(1)} %bitcast.403, bf16[3,128,2048]{2,1,0:T(8,128)(2,1)S(1)} %bitcast.401, bf16[3,128,2048]{2,1,0:T(8,128)(2,1)S(1)} %bitcast.402), custom_call_target="tpu_custom_call" | custom-call | flops 200000000 | bytes 6291456 | tf_op jit(solution)/shard_map/pair_queries/pallas_call | solution.py:82
  34.2 3.8 %project.3 = (f32[2,96,256]{2,1,0:T(8,128)S(1)}, f32[96,32]{1,0:T(8,128)S(1)}) custom-call(s32[1]{0:T(128)} %bitcast.which_ref, bf16[48,4096]{1,0:T(8,128)(2,1)S(1)} %concatenate.22.refs_0_, bf16[48,4096]{1,0:T(8,128)(2,1)S(1)} %collective-permute-done.7.refs_1_, bf16[2,8192,256]{2,1,0:T(8,128)(2,1)} %bitcast.405, bf16[2,16,8192]{2,1,0:T(8,128)(2,1)S(1)} %bitcast.396), custom_call_target="tpu_custom_call" | custom-call | flops 805306368 | bytes 4980736 | tf_op jit(solution)/shard_map/project/pallas_call | solution.py:127
  38.7 1.7 %collective-permute-start.9 = (bf16[48,4096]{1,0:T(8,128)(2,1)S(1)}, bf16[48,4096]{1,0:T(8,128)(2,1)S(1)}, u32[]{:S(2)}, u32[]{:S(2)}) collective-permute-start(bf16[48,4096]{1,0:T(8,128)(2,1)S(1)} %collective-permute-done.8.refs_0_), channel_id=1, source_target_pairs={{0,132},{8,12},{16,148},{24,28},{32,164},{40,44},{48,180},{56,60},... | collective-permute-start | bytes 1179656 | tf_op jit(solution)/shard_map/ppermute | solution.py:40
  40.4 4.3 %project.4 = (f32[2,192,256]{2,1,0:T(8,128)S(1)}, f32[192,32]{1,0:T(8,128)S(1)}) custom-call(s32[1]{0:T(128)S(6)} %sub.44.which_ref, bf16[48,4096]{1,0:T(8,128)(2,1)S(1)} %collective-permute-done.8.refs_0_, bf16[48,4096]{1,0:T(8,128)(2,1)S(1)} %collective-permute-done.10.refs_1_, bf16[48,4096]{1,0:T(8,128)(2,1)S(1)} %collective-permute-done.11.refs_2_, ...), custom_call_target="tpu_custom_call" | custom-call | flops 805306368 | bytes 5767168 | tf_op jit(solution)/shard_map/project/pallas_call | solution.py:127
  44.7 2.9 %collective-permute-done.9.refs_0_.refs_2_ = bf16[48,4096]{1,0:T(8,128)(2,1)S(1)} collective-permute-done((bf16[48,4096]{1,0:T(8,128)(2,1)S(1)}, bf16[48,4096]{1,0:T(8,128)(2,1)S(1)}, u32[]{:S(2)}, u32[]{:S(2)}) %collective-permute-start.9) | collective-permute-done | bytes 393248 | tf_op jit(solution)/shard_map/ppermute | solution.py:40
  47.7 1.7 %collective-permute-done.13.refs_1_.refs_3_ = bf16[48,4096]{1,0:T(8,128)(2,1)S(1)} collective-permute-done((bf16[48,4096]{1,0:T(8,128)(2,1)S(1)}, bf16[48,4096]{1,0:T(8,128)(2,1)S(1)}, u32[]{:S(2)}, u32[]{:S(2)}) %collective-permute-start.13) | collective-permute-done | bytes 393248 | tf_op jit(solution)/shard_map/ppermute | solution.py:40
  49.4 3.8 %project.5 = (f32[2,96,256]{2,1,0:T(8,128)S(1)}, f32[96,32]{1,0:T(8,128)S(1)}) custom-call(s32[1]{0:T(128)} %bitcast.which_ref, bf16[48,4096]{1,0:T(8,128)(2,1)S(1)} %collective-permute-done.9.refs_0_.refs_2_, bf16[48,4096]{1,0:T(8,128)(2,1)S(1)} %collective-permute-done.13.refs_1_.refs_3_, bf16[2,8192,256]{2,1,0:T(8,128)(2,1)} %bitcast.407, ...), custom_call_target="tpu_custom_call" | custom-call | flops 805306368 | bytes 4980736 | tf_op jit(solution)/shard_map/project/pallas_call | solution.py:127
  53.2 4.1 %attend.1 = (bf16[192,512]{1,0:T(8,128)(2,1)S(1)}, bf16[192,32]{1,0:T(8,128)(2,1)S(1)}, bf16[192,512]{1,0:T(8,128)(2,1)S(1)}, bf16[192,32]{1,0:T(8,128)(2,1)S(1)}, f32[32,256]{1,0:T(8,128)S(1)}) custom-call(s32[3]{0:T(128)S(1)} %copy-done.5, s32[3]{0:T(128)S(1)} %copy-done.6, f32[2,96,256]{2,1,0:T(8,128)S(1)} %get-tuple-element.32.y0, ...), custom_call_target="tpu_custom_call" | custom-call | flops 1000000000 | bytes 3145728 | tf_op jit(solution)/shard_map/attend/pallas_call | solution.py:223
  58.4 4.5 %feature_grad.2 = (bf16[48,4096]{1,0:T(8,128)(2,1)S(1)}, bf16[48,4096]{1,0:T(8,128)(2,1)S(1)}, bf16[48,4096]{1,0:T(8,128)(2,1)S(1)}, bf16[48,4096]{1,0:T(8,128)(2,1)S(1)}) custom-call(s32[1]{0:T(128)} %bitcast.which_ref, bf16[192,512]{1,0:T(8,128)(2,1)S(1)} %get-tuple-element.45.g_ref, bf16[192,32]{1,0:T(8,128)(2,1)S(1)} %get-tuple-element.46.m_ref, ...), custom_call_target="tpu_custom_call" | custom-call | flops 805306368 | bytes 5767168 | tf_op jit(solution)/shard_map/feature_grad/pallas_call | solution.py:269
  64.2 2.5 %collective-permute-done.15 = bf16[32,4096]{1,0:T(8,128)(2,1)S(1)} collective-permute-done((bf16[32,4096]{1,0:T(8,128)(2,1)S(1)}, bf16[32,4096]{1,0:T(8,128)(2,1)S(1)}, u32[]{:S(2)}, u32[]{:S(2)}) %collective-permute-start.15) | collective-permute-done | bytes 262176 | tf_op jit(solution)/shard_map/ppermute | solution.py:385
  67.0 4.5 %feature_grad.3 = (bf16[48,4096]{1,0:T(8,128)(2,1)S(1)}, bf16[48,4096]{1,0:T(8,128)(2,1)S(1)}, bf16[48,4096]{1,0:T(8,128)(2,1)S(1)}, bf16[48,4096]{1,0:T(8,128)(2,1)S(1)}) custom-call(s32[1]{0:T(128)S(6)} %sub.44.which_ref, bf16[192,512]{1,0:T(8,128)(2,1)S(1)} %get-tuple-element.54.g_ref, bf16[192,32]{1,0:T(8,128)(2,1)S(1)} %get-tuple-element.44.m_ref, ...), custom_call_target="tpu_custom_call" | custom-call | flops 805306368 | bytes 5767168 | tf_op jit(solution)/shard_map/feature_grad/pallas_call | solution.py:269
  72.8 1.7 %collective-permute-start.20 = (bf16[48,4096]{1,0:T(8,128)(2,1)S(1)}, bf16[48,4096]{1,0:T(8,128)(2,1)S(1)}, u32[]{:S(2)}, u32[]{:S(2)}) collective-permute-start(bf16[48,4096]{1,0:T(8,128)(2,1)S(1)} %add_convert_fusion.2), channel_id=1, source_target_pairs={{0,132},{8,12},{16,148},{24,28},{32,164},{40,44},{48,180},{56,60},... | collective-permute-start | bytes 1179656 | tf_op jit(solution)/shard_map/ppermute | solution.py:40
  74.6 1.6 %collective-permute-start.18 = (bf16[48,4096]{1,0:T(8,128)(2,1)S(1)}, bf16[48,4096]{1,0:T(8,128)(2,1)S(1)}, u32[]{:S(2)}, u32[]{:S(2)}) collective-permute-start(bf16[48,4096]{1,0:T(8,128)(2,1)S(1)} %add_convert_fusion.1), channel_id=1, source_target_pairs={{0,132},{8,12},{16,148},{24,28},{32,164},{40,44},{48,180},{56,60},... | collective-permute-start | bytes 1179656 | tf_op jit(solution)/shard_map/ppermute | solution.py:40
  76.3 4.5 %collective-permute-done.29 = bf16[32,4352]{1,0:T(8,128)(2,1)S(1)} collective-permute-done((bf16[32,4352]{1,0:T(8,128)(2,1)S(1)}, bf16[32,4352]{1,0:T(8,128)(2,1)S(1)}, u32[]{:S(2)}, u32[]{:S(2)}) %collective-permute-start.29) | collective-permute-done | bytes 278560 | tf_op jit(solution)/shard_map/ppermute | solution.py:393
  83.3 4.6 %collective-permute-done.18 = bf16[48,4096]{1,0:T(8,128)(2,1)S(1)} collective-permute-done((bf16[48,4096]{1,0:T(8,128)(2,1)S(1)}, bf16[48,4096]{1,0:T(8,128)(2,1)S(1)}, u32[]{:S(2)}, u32[]{:S(2)}) %collective-permute-start.18) | collective-permute-done | bytes 393248 | tf_op jit(solution)/shard_map/ppermute | solution.py:40
  87.9 1.9 %collective-permute-done.21 = bf16[48,4096]{1,0:T(8,128)(2,1)S(1)} collective-permute-done((bf16[48,4096]{1,0:T(8,128)(2,1)S(1)}, bf16[48,4096]{1,0:T(8,128)(2,1)S(1)}, u32[]{:S(2)}, u32[]{:S(2)}) %collective-permute-start.21) | collective-permute-done | bytes 393248 | tf_op jit(solution)/shard_map/ppermute | solution.py:40
  90.1 3.2 %collective-permute-start.22 = (bf16[6,4096]{1,0:T(8,128)(2,1)S(1)}, bf16[6,4096]{1,0:T(8,128)(2,1)S(1)}, u32[]{:S(2)}, u32[]{:S(2)}) collective-permute-start(bf16[6,4096]{1,0:T(8,128)(2,1)S(1)} %get-tuple-element.65), channel_id=1, source_target_pairs={{0,64},{8,72},{16,80},{24,88},{32,96},{40,104},{48,112},{56,120},{... | collective-permute-start | bytes 147464 | tf_op jit(solution)/shard_map/ppermute | solution.py:40
  93.4 1.4 %collective-permute-start.23 = (bf16[6,4096]{1,0:T(8,128)(2,1)S(1)}, bf16[6,4096]{1,0:T(8,128)(2,1)S(1)}, u32[]{:S(2)}, u32[]{:S(2)}) collective-permute-start(bf16[6,4096]{1,0:T(8,128)(2,1)S(1)} %get-tuple-element.71), channel_id=1, source_target_pairs={{0,80},{8,88},{16,96},{24,104},{32,112},{40,120},{48,0},{56,8},{64... | collective-permute-start | bytes 147464 | tf_op jit(solution)/shard_map/ppermute | solution.py:40
  94.8 2.4 %collective-permute-start.24 = (bf16[6,4096]{1,0:T(8,128)(2,1)S(1)}, bf16[6,4096]{1,0:T(8,128)(2,1)S(1)}, u32[]{:S(2)}, u32[]{:S(2)}) collective-permute-start(bf16[6,4096]{1,0:T(8,128)(2,1)S(1)} %get-tuple-element.70), channel_id=1, source_target_pairs={{0,48},{8,56},{16,64},{24,72},{32,80},{40,88},{48,96},{56,104},{64... | collective-permute-start | bytes 147464 | tf_op jit(solution)/shard_map/ppermute | solution.py:40
  97.2 2.1 %collective-permute-start.25 = (bf16[6,4096]{1,0:T(8,128)(2,1)S(1)}, bf16[6,4096]{1,0:T(8,128)(2,1)S(1)}, u32[]{:S(2)}, u32[]{:S(2)}) collective-permute-start(bf16[6,4096]{1,0:T(8,128)(2,1)S(1)} %get-tuple-element.69), channel_id=1, source_target_pairs={{0,96},{8,104},{16,112},{24,120},{32,0},{40,8},{48,16},{56,24},{64... | collective-permute-start | bytes 147464 | tf_op jit(solution)/shard_map/ppermute | solution.py:40
  100.1 3.8 %collective-permute-start.27 = (bf16[6,4096]{1,0:T(8,128)(2,1)S(1)}, bf16[6,4096]{1,0:T(8,128)(2,1)S(1)}, u32[]{:S(2)}, u32[]{:S(2)}) collective-permute-start(bf16[6,4096]{1,0:T(8,128)(2,1)S(1)} %get-tuple-element.67), channel_id=1, source_target_pairs={{0,112},{8,120},{16,0},{24,8},{32,16},{40,24},{48,32},{56,40},{64,... | collective-permute-start | bytes 147464 | tf_op jit(solution)/shard_map/ppermute | solution.py:40
  105.0 1.8 %collective-permute-done.25 = bf16[6,4096]{1,0:T(8,128)(2,1)S(1)} collective-permute-done((bf16[6,4096]{1,0:T(8,128)(2,1)S(1)}, bf16[6,4096]{1,0:T(8,128)(2,1)S(1)}, u32[]{:S(2)}, u32[]{:S(2)}) %collective-permute-start.25) | collective-permute-done | bytes 49184 | tf_op jit(solution)/shard_map/ppermute | solution.py:40
  107.8 2.5 %collective-permute-done.28 = bf16[6,4096]{1,0:T(8,128)(2,1)S(1)} collective-permute-done((bf16[6,4096]{1,0:T(8,128)(2,1)S(1)}, bf16[6,4096]{1,0:T(8,128)(2,1)S(1)}, u32[]{:S(2)}, u32[]{:S(2)}) %collective-permute-start.28) | collective-permute-done | bytes 49184 | tf_op jit(solution)/shard_map/ppermute | solution.py:40
  111.1 2.4 %collective-permute-done.31 = bf16[32,4352]{1,0:T(8,128)(2,1)S(1)} collective-permute-done((bf16[32,4352]{1,0:T(8,128)(2,1)S(1)}, bf16[32,4352]{1,0:T(8,128)(2,1)S(1)}, u32[]{:S(2)}, u32[]{:S(2)}) %collective-permute-start.31) | collective-permute-done | bytes 278560 | tf_op jit(solution)/shard_map/ppermute | solution.py:413
  (81 shorter events, 21.0 us)
Async XLA Ops:
  1.6 16.5 %collective-permute-start = (bf16[6,4096]{1,0:T(8,128)(2,1)S(1)}, bf16[6,4096]{1,0:T(8,128)(2,1)S(1)}, u32[]{:S(2)}, u32[]{:S(2)}) collective-permute-start(bf16[6,4096]{1,0:T(8,128)(2,1)S(1)} %reshape.31), channel_id=1, source_target_pairs={{0,64},{8,72},{16,80},{24,88},{32,96},{40,104},{48,112},{56,120},{... | collective-permute-start | bytes 147464 | tf_op jit(solution)/shard_map/ppermute | solution.py:40
  8.9 10.2 %collective-permute-start.1 = (bf16[6,4096]{1,0:T(8,128)(2,1)S(1)}, bf16[6,4096]{1,0:T(8,128)(2,1)S(1)}, u32[]{:S(2)}, u32[]{:S(2)}) collective-permute-start(bf16[6,4096]{1,0:T(8,128)(2,1)S(1)} %reshape.31), channel_id=1, source_target_pairs={{0,48},{8,56},{16,64},{24,72},{32,80},{40,88},{48,96},{56,104},{64... | collective-permute-start | bytes 147464 | tf_op jit(solution)/shard_map/ppermute | solution.py:40
  10.8 10.5 %collective-permute-start.2 = (bf16[6,4096]{1,0:T(8,128)(2,1)S(1)}, bf16[6,4096]{1,0:T(8,128)(2,1)S(1)}, u32[]{:S(2)}, u32[]{:S(2)}) collective-permute-start(bf16[6,4096]{1,0:T(8,128)(2,1)S(1)} %reshape.31), channel_id=1, source_target_pairs={{0,80},{8,88},{16,96},{24,104},{32,112},{40,120},{48,0},{56,8},{64... | collective-permute-start | bytes 147464 | tf_op jit(solution)/shard_map/ppermute | solution.py:40
  13.9 7.7 %collective-permute-start.3 = (bf16[6,4096]{1,0:T(8,128)(2,1)S(1)}, bf16[6,4096]{1,0:T(8,128)(2,1)S(1)}, u32[]{:S(2)}, u32[]{:S(2)}) collective-permute-start(bf16[6,4096]{1,0:T(8,128)(2,1)S(1)} %reshape.31), channel_id=1, source_target_pairs={{0,32},{8,40},{16,48},{24,56},{32,64},{40,72},{48,80},{56,88},{64,... | collective-permute-start | bytes 147464 | tf_op jit(solution)/shard_map/ppermute | solution.py:40
  15.4 7.0 %collective-permute-start.4 = (bf16[6,4096]{1,0:T(8,128)(2,1)S(1)}, bf16[6,4096]{1,0:T(8,128)(2,1)S(1)}, u32[]{:S(2)}, u32[]{:S(2)}) collective-permute-start(bf16[6,4096]{1,0:T(8,128)(2,1)S(1)} %reshape.31), channel_id=1, source_target_pairs={{0,96},{8,104},{16,112},{24,120},{32,0},{40,8},{48,16},{56,24},{64... | collective-permute-start | bytes 147464 | tf_op jit(solution)/shard_map/ppermute | solution.py:40
  18.0 5.5 %collective-permute-start.5 = (bf16[6,4096]{1,0:T(8,128)(2,1)S(1)}, bf16[6,4096]{1,0:T(8,128)(2,1)S(1)}, u32[]{:S(2)}, u32[]{:S(2)}) collective-permute-start(bf16[6,4096]{1,0:T(8,128)(2,1)S(1)} %reshape.31), channel_id=1, source_target_pairs={{0,16},{8,24},{16,32},{24,40},{32,48},{40,56},{48,64},{56,72},{64,... | collective-permute-start | bytes 147464 | tf_op jit(solution)/shard_map/ppermute | solution.py:40
  19.1 4.6 %collective-permute-start.6 = (bf16[6,4096]{1,0:T(8,128)(2,1)S(1)}, bf16[6,4096]{1,0:T(8,128)(2,1)S(1)}, u32[]{:S(2)}, u32[]{:S(2)}) collective-permute-start(bf16[6,4096]{1,0:T(8,128)(2,1)S(1)} %reshape.31), channel_id=1, source_target_pairs={{0,112},{8,120},{16,0},{24,8},{32,16},{40,24},{48,32},{56,40},{64,... | collective-permute-start | bytes 147464 | tf_op jit(solution)/shard_map/ppermute | solution.py:40
  24.8 9.4 %collective-permute-start.7 = (bf16[48,4096]{1,0:T(8,128)(2,1)S(1)}, bf16[48,4096]{1,0:T(8,128)(2,1)S(1)}, u32[]{:S(2)}, u32[]{:S(2)}) collective-permute-start(bf16[48,4096]{1,0:T(8,128)(2,1)S(1)} %concatenate.22.refs_0_), channel_id=1, source_target_pairs={{0,8},{8,0},{16,24},{24,16},{32,40},{40,32},{48,56},{56,48},{64,72... | collective-permute-start | bytes 1179656 | tf_op jit(solution)/shard_map/ppermute | solution.py:40
  24.9 13.2 %collective-permute-start.8 = (bf16[48,4096]{1,0:T(8,128)(2,1)S(1)}, bf16[48,4096]{1,0:T(8,128)(2,1)S(1)}, u32[]{:S(2)}, u32[]{:S(2)}) collective-permute-start(bf16[48,4096]{1,0:T(8,128)(2,1)S(1)} %concatenate.22.refs_0_), channel_id=1, source_target_pairs={{0,4},{8,140},{16,20},{24,156},{32,36},{40,172},{48,52},{56,188},{... | collective-permute-start | bytes 1179656 | tf_op jit(solution)/shard_map/ppermute | solution.py:40
  26.4 11.7 %collective-permute-start.10 = (bf16[48,4096]{1,0:T(8,128)(2,1)S(1)}, bf16[48,4096]{1,0:T(8,128)(2,1)S(1)}, u32[]{:S(2)}, u32[]{:S(2)}) collective-permute-start(bf16[48,4096]{1,0:T(8,128)(2,1)S(1)} %concatenate.22.refs_0_), channel_id=1, source_target_pairs={{0,132},{8,12},{16,148},{24,28},{32,164},{40,44},{48,180},{56,60},... | collective-permute-start | bytes 1179656 | tf_op jit(solution)/shard_map/ppermute | solution.py:40
  38.0 2.3 %collective-permute-start.11 = (bf16[48,4096]{1,0:T(8,128)(2,1)S(1)}, bf16[48,4096]{1,0:T(8,128)(2,1)S(1)}, u32[]{:S(2)}, u32[]{:S(2)}) collective-permute-start(bf16[48,4096]{1,0:T(8,128)(2,1)S(1)} %collective-permute-done.8.refs_0_), channel_id=1, source_target_pairs={{0,8},{8,0},{16,24},{24,16},{32,40},{40,32},{48,56},{56,48},{64,72... | collective-permute-start | bytes 1179656 | tf_op jit(solution)/shard_map/ppermute | solution.py:40
  38.2 2.3 %collective-permute-start.12 = (bf16[48,4096]{1,0:T(8,128)(2,1)S(1)}, bf16[48,4096]{1,0:T(8,128)(2,1)S(1)}, u32[]{:S(2)}, u32[]{:S(2)}) collective-permute-start(bf16[48,4096]{1,0:T(8,128)(2,1)S(1)} %collective-permute-done.10.refs_1_), channel_id=1, source_target_pairs={{0,8},{8,0},{16,24},{24,16},{32,40},{40,32},{48,56},{56,48},{64,72... | collective-permute-start | bytes 1179656 | tf_op jit(solution)/shard_map/ppermute | solution.py:40
  38.7 9.0 %collective-permute-start.9 = (bf16[48,4096]{1,0:T(8,128)(2,1)S(1)}, bf16[48,4096]{1,0:T(8,128)(2,1)S(1)}, u32[]{:S(2)}, u32[]{:S(2)}) collective-permute-start(bf16[48,4096]{1,0:T(8,128)(2,1)S(1)} %collective-permute-done.8.refs_0_), channel_id=1, source_target_pairs={{0,132},{8,12},{16,148},{24,28},{32,164},{40,44},{48,180},{56,60},... | collective-permute-start | bytes 1179656 | tf_op jit(solution)/shard_map/ppermute | solution.py:40
  47.6 1.7 %collective-permute-start.13 = (bf16[48,4096]{1,0:T(8,128)(2,1)S(1)}, bf16[48,4096]{1,0:T(8,128)(2,1)S(1)}, u32[]{:S(2)}, u32[]{:S(2)}) collective-permute-start(bf16[48,4096]{1,0:T(8,128)(2,1)S(1)} %collective-permute-done.9.refs_0_.refs_2_), channel_id=1, source_target_pairs={{0,8},{8,0},{16,24},{24,16},{32,40},{40,32},{48,56},{56,48},{64,72... | collective-permute-start | bytes 1179656 | tf_op jit(solution)/shard_map/ppermute | solution.py:40
  58.3 8.4 %collective-permute-start.15 = (bf16[32,4096]{1,0:T(8,128)(2,1)S(1)}, bf16[32,4096]{1,0:T(8,128)(2,1)S(1)}, u32[]{:S(2)}, u32[]{:S(2)}) collective-permute-start(bf16[32,4096]{1,0:T(8,128)(2,1)S(1)} %down_grad.2), channel_id=1, source_target_pairs={{0,4},{4,0},{1,5},{5,1},{2,6},{6,2},{3,7},{7,3},{8,12},{12,8},{9,1... | collective-permute-start | bytes 786440 | tf_op jit(solution)/shard_map/ppermute | solution.py:385
  63.0 3.9 %collective-permute-start.16 = (bf16[48,4096]{1,0:T(8,128)(2,1)S(1)}, bf16[48,4096]{1,0:T(8,128)(2,1)S(1)}, u32[]{:S(2)}, u32[]{:S(2)}) collective-permute-start(bf16[48,4096]{1,0:T(8,128)(2,1)S(1)} %get-tuple-element.53), channel_id=1, source_target_pairs={{0,8},{8,0},{16,24},{24,16},{32,40},{40,32},{48,56},{56,48},{64,72... | collective-permute-start | bytes 1179656 | tf_op jit(solution)/shard_map/ppermute | solution.py:40
  71.5 3.0 %collective-permute-start.17 = (bf16[48,4096]{1,0:T(8,128)(2,1)S(1)}, bf16[48,4096]{1,0:T(8,128)(2,1)S(1)}, u32[]{:S(2)}, u32[]{:S(2)}) collective-permute-start(bf16[48,4096]{1,0:T(8,128)(2,1)S(1)} %get-tuple-element.56), channel_id=1, source_target_pairs={{0,8},{8,0},{16,24},{24,16},{32,40},{40,32},{48,56},{56,48},{64,72... | collective-permute-start | bytes 1179656 | tf_op jit(solution)/shard_map/ppermute | solution.py:40
  71.6 11.7 %collective-permute-start.14 = (bf16[48,4096]{1,0:T(8,128)(2,1)S(1)}, bf16[48,4096]{1,0:T(8,128)(2,1)S(1)}, u32[]{:S(2)}, u32[]{:S(2)}) collective-permute-start(bf16[48,4096]{1,0:T(8,128)(2,1)S(1)} %get-tuple-element.48), channel_id=1, source_target_pairs={{0,8},{8,0},{16,24},{24,16},{32,40},{40,32},{48,56},{56,48},{64,72... | collective-permute-start | bytes 1179656 | tf_op jit(solution)/shard_map/ppermute | solution.py:40
  72.1 8.7 %collective-permute-start.29 = (bf16[32,4352]{1,0:T(8,128)(2,1)S(1)}, bf16[32,4352]{1,0:T(8,128)(2,1)S(1)}, u32[]{:S(2)}, u32[]{:S(2)}) collective-permute-start(bf16[32,4352]{1,0:T(8,128)(2,1)S(1)} %pad_maximum_fusion.1), channel_id=1, source_target_pairs={{0,1},{1,0},{2,3},{3,2},{4,5},{5,4},{6,7},{7,6},{8,9},{9,8},{10,11... | collective-permute-start | bytes 835592 | tf_op jit(solution)/shard_map/ppermute | solution.py:393
  72.8 9.0 %collective-permute-start.20 = (bf16[48,4096]{1,0:T(8,128)(2,1)S(1)}, bf16[48,4096]{1,0:T(8,128)(2,1)S(1)}, u32[]{:S(2)}, u32[]{:S(2)}) collective-permute-start(bf16[48,4096]{1,0:T(8,128)(2,1)S(1)} %add_convert_fusion.2), channel_id=1, source_target_pairs={{0,132},{8,12},{16,148},{24,28},{32,164},{40,44},{48,180},{56,60},... | collective-permute-start | bytes 1179656 | tf_op jit(solution)/shard_map/ppermute | solution.py:40
  74.5 6.2 %collective-permute-start.19 = (bf16[48,4096]{1,0:T(8,128)(2,1)S(1)}, bf16[48,4096]{1,0:T(8,128)(2,1)S(1)}, u32[]{:S(2)}, u32[]{:S(2)}) collective-permute-start(bf16[48,4096]{1,0:T(8,128)(2,1)S(1)} %get-tuple-element.58), channel_id=1, source_target_pairs={{0,8},{8,0},{16,24},{24,16},{32,40},{40,32},{48,56},{56,48},{64,72... | collective-permute-start | bytes 1179656 | tf_op jit(solution)/shard_map/ppermute | solution.py:40
  74.6 13.3 %collective-permute-start.18 = (bf16[48,4096]{1,0:T(8,128)(2,1)S(1)}, bf16[48,4096]{1,0:T(8,128)(2,1)S(1)}, u32[]{:S(2)}, u32[]{:S(2)}) collective-permute-start(bf16[48,4096]{1,0:T(8,128)(2,1)S(1)} %add_convert_fusion.1), channel_id=1, source_target_pairs={{0,132},{8,12},{16,148},{24,28},{32,164},{40,44},{48,180},{56,60},... | collective-permute-start | bytes 1179656 | tf_op jit(solution)/shard_map/ppermute | solution.py:40
  82.0 7.9 %collective-permute-start.21 = (bf16[48,4096]{1,0:T(8,128)(2,1)S(1)}, bf16[48,4096]{1,0:T(8,128)(2,1)S(1)}, u32[]{:S(2)}, u32[]{:S(2)}) collective-permute-start(bf16[48,4096]{1,0:T(8,128)(2,1)S(1)} %add_convert_fusion), channel_id=1, source_target_pairs={{0,4},{8,140},{16,20},{24,156},{32,36},{40,172},{48,52},{56,188},{... | collective-permute-start | bytes 1179656 | tf_op jit(solution)/shard_map/ppermute | solution.py:40
  82.1 12.6 %collective-permute-start.30 = (bf16[32,4352]{1,0:T(8,128)(2,1)S(1)}, bf16[32,4352]{1,0:T(8,128)(2,1)S(1)}, u32[]{:S(2)}, u32[]{:S(2)}) collective-permute-start(bf16[32,4352]{1,0:T(8,128)(2,1)S(1)} %add_convert_fusion.4), channel_id=1, source_target_pairs={{0,3},{1,2},{2,1},{3,0},{4,7},{5,6},{6,5},{7,4},{8,11},{9,10},{10,... | collective-permute-start | bytes 835592 | tf_op jit(solution)/shard_map/ppermute | solution.py:409
  90.1 10.0 %collective-permute-start.22 = (bf16[6,4096]{1,0:T(8,128)(2,1)S(1)}, bf16[6,4096]{1,0:T(8,128)(2,1)S(1)}, u32[]{:S(2)}, u32[]{:S(2)}) collective-permute-start(bf16[6,4096]{1,0:T(8,128)(2,1)S(1)} %get-tuple-element.65), channel_id=1, source_target_pairs={{0,64},{8,72},{16,80},{24,88},{32,96},{40,104},{48,112},{56,120},{... | collective-permute-start | bytes 147464 | tf_op jit(solution)/shard_map/ppermute | solution.py:40
  93.4 11.4 %collective-permute-start.23 = (bf16[6,4096]{1,0:T(8,128)(2,1)S(1)}, bf16[6,4096]{1,0:T(8,128)(2,1)S(1)}, u32[]{:S(2)}, u32[]{:S(2)}) collective-permute-start(bf16[6,4096]{1,0:T(8,128)(2,1)S(1)} %get-tuple-element.71), channel_id=1, source_target_pairs={{0,80},{8,88},{16,96},{24,104},{32,112},{40,120},{48,0},{56,8},{64... | collective-permute-start | bytes 147464 | tf_op jit(solution)/shard_map/ppermute | solution.py:40
  94.8 10.1 %collective-permute-start.24 = (bf16[6,4096]{1,0:T(8,128)(2,1)S(1)}, bf16[6,4096]{1,0:T(8,128)(2,1)S(1)}, u32[]{:S(2)}, u32[]{:S(2)}) collective-permute-start(bf16[6,4096]{1,0:T(8,128)(2,1)S(1)} %get-tuple-element.70), channel_id=1, source_target_pairs={{0,48},{8,56},{16,64},{24,72},{32,80},{40,88},{48,96},{56,104},{64... | collective-permute-start | bytes 147464 | tf_op jit(solution)/shard_map/ppermute | solution.py:40
  97.2 9.6 %collective-permute-start.25 = (bf16[6,4096]{1,0:T(8,128)(2,1)S(1)}, bf16[6,4096]{1,0:T(8,128)(2,1)S(1)}, u32[]{:S(2)}, u32[]{:S(2)}) collective-permute-start(bf16[6,4096]{1,0:T(8,128)(2,1)S(1)} %get-tuple-element.69), channel_id=1, source_target_pairs={{0,96},{8,104},{16,112},{24,120},{32,0},{40,8},{48,16},{56,24},{64... | collective-permute-start | bytes 147464 | tf_op jit(solution)/shard_map/ppermute | solution.py:40
  99.3 7.5 %collective-permute-start.26 = (bf16[6,4096]{1,0:T(8,128)(2,1)S(1)}, bf16[6,4096]{1,0:T(8,128)(2,1)S(1)}, u32[]{:S(2)}, u32[]{:S(2)}) collective-permute-start(bf16[6,4096]{1,0:T(8,128)(2,1)S(1)} %get-tuple-element.68), channel_id=1, source_target_pairs={{0,32},{8,40},{16,48},{24,56},{32,64},{40,72},{48,80},{56,88},{64,... | collective-permute-start | bytes 147464 | tf_op jit(solution)/shard_map/ppermute | solution.py:40
  100.1 7.6 %collective-permute-start.27 = (bf16[6,4096]{1,0:T(8,128)(2,1)S(1)}, bf16[6,4096]{1,0:T(8,128)(2,1)S(1)}, u32[]{:S(2)}, u32[]{:S(2)}) collective-permute-start(bf16[6,4096]{1,0:T(8,128)(2,1)S(1)} %get-tuple-element.67), channel_id=1, source_target_pairs={{0,112},{8,120},{16,0},{24,8},{32,16},{40,24},{48,32},{56,40},{64,... | collective-permute-start | bytes 147464 | tf_op jit(solution)/shard_map/ppermute | solution.py:40
  104.8 5.5 %collective-permute-start.28 = (bf16[6,4096]{1,0:T(8,128)(2,1)S(1)}, bf16[6,4096]{1,0:T(8,128)(2,1)S(1)}, u32[]{:S(2)}, u32[]{:S(2)}) collective-permute-start(bf16[6,4096]{1,0:T(8,128)(2,1)S(1)} %get-tuple-element.66), channel_id=1, source_target_pairs={{0,16},{8,24},{16,32},{24,40},{32,48},{40,56},{48,64},{56,72},{64,... | collective-permute-start | bytes 147464 | tf_op jit(solution)/shard_map/ppermute | solution.py:40
  104.9 8.5 %collective-permute-start.31 = (bf16[32,4352]{1,0:T(8,128)(2,1)S(1)}, bf16[32,4352]{1,0:T(8,128)(2,1)S(1)}, u32[]{:S(2)}, u32[]{:S(2)}) collective-permute-start(bf16[32,4352]{1,0:T(8,128)(2,1)S(1)} %add_convert_fusion.3), channel_id=1, source_target_pairs={{0,4},{4,0},{1,5},{5,1},{2,6},{6,2},{3,7},{7,3},{8,12},{12,8},{9,1... | collective-permute-start | bytes 835592 | tf_op jit(solution)/shard_map/ppermute | solution.py:413
  (7 other events, 79.4 us)

commit v4 on v3

--- a/solution.py
+++ b/solution.py
@@ -47,7 +47,10 @@
 NT = (((1,), (1,)), ((), ()))
 TN = (((0,), (0,)), ((), ()))
 F32, LOW = jnp.float32, jnp.bfloat16
-ROOM = pltpu.CompilerParams(vmem_limit_bytes=48 * 1024 * 1024)
+ROOM = pltpu.CompilerParams(vmem_limit_bytes=20 * 1024 * 1024)
+SCALAR = pl.BlockSpec(memory_space=pltpu.SMEM)
+VECTOR = pl.BlockSpec(memory_space=pltpu.VMEM)
+CHUNK = 1024
 
 
 def dot(first, second, dims=(((1,), (0,)), ((), ()))):
@@ -91,46 +94,51 @@
     )(gains, queries, context)
 
 
+def hold_kernel(ready_ref, from_ref, to_ref, semaphore):
+    copy = pltpu.make_async_copy(from_ref, to_ref, semaphore)
+    copy.start()
+    copy.wait()
+
+
+def hold(array, ready):
+    return pl.pallas_call(
+        hold_kernel,
+        out_shape=pltpu.VMEM(array.shape, array.dtype),
+        in_specs=[pl.BlockSpec(memory_space=pl.ANY), pl.BlockSpec(memory_space=pltpu.HBM)],
+        scratch_shapes=[pltpu.SemaphoreType.DMA],
+        out_specs=VECTOR,
+        compiler_params=ROOM,
+        cost_estimate=cost(0, 2 * array.size),
+        name="hold",
+    )(ready, array)
+
+
 def project_kernel(which_ref, *refs):
     *row_refs, w_ref, a_ref, y_ref, r_ref = refs
-    rows = jnp.concatenate([ref[...] for ref in row_refs])
-    maps = a_ref[...].reshape(-1, a_ref.shape[2])
-
-    @pl.when(pl.program_id(0) == 0)
-    def _():
-        y_ref[...] = jnp.zeros_like(y_ref)
-        r_ref[...] = jnp.zeros_like(r_ref)
-
-    for part in range(2):
-        y_ref[part] += dot(rows, w_ref[part])
-    r_ref[...] += dot(rows, maps, NT)
+    half = row_refs[0].shape[1]
+    totals = [None, None, None]
+    for i in range(half // CHUNK):
+        rows = jnp.concatenate([ref[:, i * CHUNK : (i + 1) * CHUNK] for ref in row_refs])
+        place = pl.ds(pl.multiple_of(which_ref[0] * half + i * CHUNK, CHUNK), CHUNK)
+        maps = a_ref[:, :, place].reshape(-1, CHUNK)
+        terms = [dot(rows, w_ref[part, place, :]) for part in range(2)] + [dot(rows, maps, NT)]
+        totals = [new if old is None else old + new for old, new in zip(totals, terms)]
+    y_ref[0] = totals[0]
+    y_ref[1] = totals[1]
+    r_ref[...] = totals[2]
 
 
 def project(blocks, weights, down_maps, which):
     count, half = len(blocks) * blocks[0].shape[0], blocks[0].shape[1]
-    chunk = 1024
-    steps = half // chunk
     width, ranks = weights.shape[2], 2 * down_maps.shape[1]
-    grid_spec = pltpu.PrefetchScalarGridSpec(
-        num_scalar_prefetch=1,
-        grid=(steps,),
-        in_specs=[pl.BlockSpec((block.shape[0], chunk), lambda i, s: (0, i)) for block in blocks]
-        + [
-            pl.BlockSpec((2, chunk, width), lambda i, s: (0, s[0] * steps + i, 0)),
-            pl.BlockSpec((2, ranks // 2, chunk), lambda i, s: (0, 0, s[0] * steps + i)),
-        ],
-        out_specs=[
-            pl.BlockSpec((2, count, width), lambda i, s: (0, 0, 0)),
-            pl.BlockSpec((count, ranks), lambda i, s: (0, 0)),
-        ],
-    )
     return pl.pallas_call(
         project_kernel,
         out_shape=[
             jax.ShapeDtypeStruct((2, count, width), F32),
             jax.ShapeDtypeStruct((count, ranks), F32),
         ],
-        grid_spec=grid_spec,
+        in_specs=[SCALAR] + [VECTOR] * (len(blocks) + 2),
+        out_specs=[VECTOR] * 2,
         compiler_params=ROOM,
         cost_estimate=cost(4 * 192 * half * width, 4 * half * width + 2 * count * half),
         name="project",
@@ -240,36 +248,24 @@
 
 def feature_kernel(which_ref, g_ref, m_ref, w_ref, a_ref, *out_refs):
     width = w_ref.shape[2]
-    total = dot(m_ref[...], a_ref[...].reshape(-1, a_ref.shape[2]))
-    for part in range(2):
-        total += dot(g_ref[:, part * width : (part + 1) * width], w_ref[part], NT)
-    cut = out_refs[0].shape[0]
-    for i, ref in enumerate(out_refs):
-        ref[...] = total[i * cut : (i + 1) * cut].astype(LOW)
+    cut, half = out_refs[0].shape
+    for i in range(half // CHUNK):
+        place = pl.ds(pl.multiple_of(which_ref[0] * half + i * CHUNK, CHUNK), CHUNK)
+        total = dot(m_ref[...], a_ref[:, :, place].reshape(-1, CHUNK))
+        for part in range(2):
+            total += dot(g_ref[:, part * width : (part + 1) * width], w_ref[part, place, :], NT)
+        for j, ref in enumerate(out_refs):
+            ref[:, i * CHUNK : (i + 1) * CHUNK] = total[j * cut : (j + 1) * cut].astype(LOW)
 
 
 def feature_grad(grad, middle, weights, down_maps, which):
     rows, wide = grad.shape
-    ranks = middle.shape[1]
     half = weights.shape[1] // 2
-    chunk = 1024
-    steps = half // chunk
-    cut = rows // 4
-    grid_spec = pltpu.PrefetchScalarGridSpec(
-        num_scalar_prefetch=1,
-        grid=(steps,),
-        in_specs=[
-            pl.BlockSpec((rows, wide), lambda i, s: (0, 0)),
-            pl.BlockSpec((rows, ranks), lambda i, s: (0, 0)),
-            pl.BlockSpec((2, chunk, wide // 2), lambda i, s: (0, s[0] * steps + i, 0)),
-            pl.BlockSpec((2, ranks // 2, chunk), lambda i, s: (0, 0, s[0] * steps + i)),
-        ],
-        out_specs=[pl.BlockSpec((cut, chunk), lambda i, s: (0, i))] * 4,
-    )
     return pl.pallas_call(
         feature_kernel,
-        out_shape=[jax.ShapeDtypeStruct((cut, half), LOW)] * 4,
-        grid_spec=grid_spec,
+        out_shape=[jax.ShapeDtypeStruct((rows // 4, half), LOW)] * 4,
+        in_specs=[SCALAR] + [VECTOR] * 4,
+        out_specs=[VECTOR] * 4,
         compiler_params=ROOM,
         cost_estimate=cost(2 * rows * half * wide, 2 * half * (wide + rows)),
         name="feature_grad",
@@ -284,16 +280,13 @@
 
 def down_grad(middle, blocks, dtype):
     half = blocks[0].shape[1]
-    chunk = 1024
     return pl.pallas_call(
         down_kernel,
         out_shape=jax.ShapeDtypeStruct((middle.shape[1], half), dtype),
-        grid=(half // chunk,),
-        in_specs=[pl.BlockSpec(middle.shape, lambda i: (0, 0))]
-        + [pl.BlockSpec((block.shape[0], chunk), lambda i: (0, i)) for block in blocks],
-        out_specs=pl.BlockSpec((middle.shape[1], chunk), lambda i: (0, i)),
-        compiler_params=ROOM,
-        cost_estimate=cost(5e8, 2 * 200 * half),
+        in_specs=[VECTOR] * (1 + len(blocks)),
+        out_specs=VECTOR,
+        compiler_params=ROOM,
+        cost_estimate=cost(5e7, 2 * 200 * half),
         name="down_grad",
     )(middle, *blocks)
 
@@ -361,6 +354,7 @@
     )
     step_a = project([base, base_there], weights, down_maps, here)
     first = after(first, pair, *step_a, up_diagonal, *maps)
+    weights = hold(weights, first)
     third = move(first, FAR)
     first_there = move(first, SIBLING)
     second_there = move(second, SIBLING)
@@ -387,10 +381,6 @@
         after(g_own, down_other), m_own, weights, down_maps, here
     )
     down_own = down_grad(m_own, owns, F32)
-    sums = jnp.concatenate(
-        [down_own + after(down_facing, base).astype(F32), up_part], 1
-    ).astype(LOW)
-    near_sums = lax.ppermute(sums, "dp", DP_NEAR)
 
     def add(mine, theirs):
         return mine.astype(F32) + theirs.astype(F32)
@@ -398,21 +388,25 @@
     third = add(third, move(third_out, SIBLING)).astype(LOW)
     third_in = move(third, FAR)
     first, second, first_out, second_out = feature_grad(
-        after(g_other, sums, third), m_other, weights, down_maps, opposite
+        after(g_other, third, down_own), m_other, weights, down_maps, opposite
     )
     second = add(second, move(second_out, SIBLING)).astype(LOW)
     first = add(first, move(first_out, SIBLING))
     base = add(base, move(base_out, SIBLING))
-
+    sums = jnp.concatenate(
+        [down_own + after(down_facing, first_out).astype(F32), up_part], 1
+    ).astype(LOW)
+    near_sums = lax.ppermute(sums, "dp", DP_NEAR)
     second_in = move(second, FAR)
-    sums = add(sums, after(near_sums, second)).astype(LOW)
-    far_sums = lax.ppermute(sums, "dp", DP_FAR)
     first = (first + third_in.astype(F32)).astype(LOW)
     first_in = move(first, NEAR)
-    sums = add(sums, after(far_sums, first)).astype(LOW)
-    facing = lax.ppermute(sums, "tensor", TENSOR_SWAP)
+    sums = add(sums, after(near_sums, first)).astype(LOW)
+    far_sums = lax.ppermute(sums, "dp", DP_FAR)
     base = base + second_in.astype(F32) + first_in.astype(F32)
     low_base = base.astype(LOW)
+    sums = add(sums, after(far_sums, low_base)).astype(LOW)
+    low_base = after(low_base, sums)
+    facing = lax.ppermute(sums, "tensor", TENSOR_SWAP)
     count = own.shape[0]
     own_grad = base[len(SHIFTS) * count :]
     for i, k in enumerate(SHIFTS):

time: 117 us -> 107 us (0.915)
  Pallas kernels: 29.9 us -> 14 us
  local copies, waits for them, and re-layouts: 5.36 us -> 12.1 us
  starting transfers between devices: 45.8 us -> 47.9 us
  waiting for transfers between devices: 30.2 us -> 28.3 us
    pallas_call x3, Pallas kernels: 12 us -> 3.35 us  [project(): pl.pallas_call(project_kernel, out_shape=[jax.ShapeDtypeStruct((2, count,...]
    unnamed x14 -> x16, local copies, waits for them, and re-layouts: 1.43 us -> 8.18 us
    pallas_call x2 -> x3, Pallas kernels: 9.03 us -> 4.41 us  [the longest x2 3.84 us: feature_grad(): pl.pallas_call(feature_kernel, out_shape=[jax.ShapeDtypeStruct((rows // 4...]
    ppermute x28, waiting for transfers between devices: 20.8 us -> 18.1 us  [move(): return lax.ppermute(block, PLANE, pairs)]
    ppermute x28, starting transfers between devices: 43.8 us -> 46.5 us  [move(): return lax.ppermute(block, PLANE, pairs)]
    ppermute x1, waiting for transfers between devices: 2.35 us -> 0.51 us  [per_device(): facing = lax.ppermute(sums, 'tensor', TENSOR_SWAP)]
    pallas_call x1, Pallas kernels: 2.78 us -> 1.36 us  [pair_queries(): pl.pallas_call(pair_kernel, out_shape=jax.ShapeDtypeStruct((batches * kv_...]
    ppermute x1, waiting for transfers between devices: 0.01 us -> 1.33 us  [per_device(): far_sums = lax.ppermute(sums, 'dp', DP_FAR)]
  transfers between devices with their start and end apart: 32 -> 32, of which waited for: 18 -> 18; matrix products, arithmetic and copies ran while one was open for 3% -> 3% of each run, Pallas kernels for 14% -> 6%
where the time goes in v4:
time: 107 us; the launch traced here: 106 us
  starting transfers between devices  47.9 us (45%)
  waiting for transfers between devices  28.3 us (26%)
  Pallas kernels  14 us (13%)
  local copies, waits for them, and re-layouts  12.1 us (11%)
  other arithmetic  2.73 us (3%)
  between operations  1.26 us (1%)
    ppermute x28, starting transfers between devices, move(): return lax.ppermute(block, PLANE, pairs)  46.5 us
    ppermute x28, waiting for transfers between devices, move(): return lax.ppermute(block, PLANE, pairs)  18.1 us
    unnamed x16, local copies, waits for them, and re-layouts  8.18 us
    ppermute x1, waiting for transfers between devices, per_device(): near_sums = lax.ppermute(sums, 'dp', DP_NEAR)  5.64 us
    pallas_call x1, Pallas kernels, attend(): pl.pallas_call(attention_kernel, out_shape=[jax.ShapeDtypeStruct((rows, 2...  4.05 us
    pallas_call x2, Pallas kernels, feature_grad(): pl.pallas_call(feature_kernel, out_shape=[jax.ShapeDtypeStruct((rows // 4...  3.84 us
    pallas_call x3, Pallas kernels, project(): pl.pallas_call(project_kernel, out_shape=[jax.ShapeDtypeStruct((2, count,...  3.35 us
    ppermute x1, waiting for transfers between devices, per_device(): down_facing = lax.ppermute(down_other, 'tensor', TENSOR_SWAP)  2.77 us
  transfers between devices with their start and end apart: 32, of which 18 were waited for; matrix products, arithmetic and copies ran while one was open for 3% of the time, Pallas kernels for 6%

profile of v4, /device:TPU:24, one launch (start us, length us, event | category | flops | bytes accessed | tf_op | source)
XLA Modules:
  0.0 106.3 jit_solution(4058501540845550016)
XLA Ops:
  1.6 7.3 %collective-permute-start = (bf16[6,4096]{1,0:T(8,128)(2,1)S(1)}, bf16[6,4096]{1,0:T(8,128)(2,1)S(1)}, u32[]{:S(2)}, u32[]{:S(2)}) collective-permute-start(bf16[6,4096]{1,0:T(8,128)(2,1)S(1)} %reshape.31), channel_id=1, source_target_pairs={{0,64},{8,72},{16,80},{24,88},{32,96},{40,104},{48,112},{56,120},{... | collective-permute-start | bytes 147464 | tf_op jit(solution)/shard_map/ppermute | solution.py:40
  8.9 1.9 %collective-permute-start.1 = (bf16[6,4096]{1,0:T(8,128)(2,1)S(1)}, bf16[6,4096]{1,0:T(8,128)(2,1)S(1)}, u32[]{:S(2)}, u32[]{:S(2)}) collective-permute-start(bf16[6,4096]{1,0:T(8,128)(2,1)S(1)} %reshape.31), channel_id=1, source_target_pairs={{0,48},{8,56},{16,64},{24,72},{32,80},{40,88},{48,96},{56,104},{64... | collective-permute-start | bytes 147464 | tf_op jit(solution)/shard_map/ppermute | solution.py:40
  10.8 3.1 %collective-permute-start.2 = (bf16[6,4096]{1,0:T(8,128)(2,1)S(1)}, bf16[6,4096]{1,0:T(8,128)(2,1)S(1)}, u32[]{:S(2)}, u32[]{:S(2)}) collective-permute-start(bf16[6,4096]{1,0:T(8,128)(2,1)S(1)} %reshape.31), channel_id=1, source_target_pairs={{0,80},{8,88},{16,96},{24,104},{32,112},{40,120},{48,0},{56,8},{64... | collective-permute-start | bytes 147464 | tf_op jit(solution)/shard_map/ppermute | solution.py:40
  13.9 1.5 %collective-permute-start.3 = (bf16[6,4096]{1,0:T(8,128)(2,1)S(1)}, bf16[6,4096]{1,0:T(8,128)(2,1)S(1)}, u32[]{:S(2)}, u32[]{:S(2)}) collective-permute-start(bf16[6,4096]{1,0:T(8,128)(2,1)S(1)} %reshape.31), channel_id=1, source_target_pairs={{0,32},{8,40},{16,48},{24,56},{32,64},{40,72},{48,80},{56,88},{64,... | collective-permute-start | bytes 147464 | tf_op jit(solution)/shard_map/ppermute | solution.py:40
  15.4 2.7 %collective-permute-start.4 = (bf16[6,4096]{1,0:T(8,128)(2,1)S(1)}, bf16[6,4096]{1,0:T(8,128)(2,1)S(1)}, u32[]{:S(2)}, u32[]{:S(2)}) collective-permute-start(bf16[6,4096]{1,0:T(8,128)(2,1)S(1)} %reshape.31), channel_id=1, source_target_pairs={{0,96},{8,104},{16,112},{24,120},{32,0},{40,8},{48,16},{56,24},{64... | collective-permute-start | bytes 147464 | tf_op jit(solution)/shard_map/ppermute | solution.py:40
  19.1 2.2 %collective-permute-start.6 = (bf16[6,4096]{1,0:T(8,128)(2,1)S(1)}, bf16[6,4096]{1,0:T(8,128)(2,1)S(1)}, u32[]{:S(2)}, u32[]{:S(2)}) collective-permute-start(bf16[6,4096]{1,0:T(8,128)(2,1)S(1)} %reshape.31), channel_id=1, source_target_pairs={{0,112},{8,120},{16,0},{24,8},{32,16},{40,24},{48,32},{56,40},{64,... | collective-permute-start | bytes 147464 | tf_op jit(solution)/shard_map/ppermute | solution.py:40
  22.4 1.1 %collective-permute-done.5 = bf16[6,4096]{1,0:T(8,128)(2,1)S(1)} collective-permute-done((bf16[6,4096]{1,0:T(8,128)(2,1)S(1)}, bf16[6,4096]{1,0:T(8,128)(2,1)S(1)}, u32[]{:S(2)}, u32[]{:S(2)}) %collective-permute-start.5) | collective-permute-done | bytes 49184 | tf_op jit(solution)/shard_map/ppermute | solution.py:40
  24.9 1.6 %collective-permute-start.8 = (bf16[48,4096]{1,0:T(8,128)(2,1)S(1)}, bf16[48,4096]{1,0:T(8,128)(2,1)S(1)}, u32[]{:S(2)}, u32[]{:S(2)}) collective-permute-start(bf16[48,4096]{1,0:T(8,128)(2,1)S(1)} %concatenate.22.refs_0_), channel_id=1, source_target_pairs={{0,4},{8,140},{16,20},{24,156},{32,36},{40,172},{48,52},{56,188},{... | collective-permute-start | bytes 1179656 | tf_op jit(solution)/shard_map/ppermute | solution.py:40
  26.4 2.1 %collective-permute-start.10 = (bf16[48,4096]{1,0:T(8,128)(2,1)S(1)}, bf16[48,4096]{1,0:T(8,128)(2,1)S(1)}, u32[]{:S(2)}, u32[]{:S(2)}) collective-permute-start(bf16[48,4096]{1,0:T(8,128)(2,1)S(1)} %concatenate.22.refs_0_), channel_id=1, source_target_pairs={{0,132},{8,12},{16,148},{24,28},{32,164},{40,44},{48,180},{56,60},... | collective-permute-start | bytes 1179656 | tf_op jit(solution)/shard_map/ppermute | solution.py:40
  29.9 1.4 %copy-done.4 = bf16[1,3,128,2048]{3,2,1,0:T(8,128)(2,1)S(1)} copy-done((bf16[1,3,128,2048]{3,2,1,0:T(8,128)(2,1)S(1)}, bf16[1,3,128,2048]{3,2,1,0:T(8,128)(2,1)}, u32[]{:S(2)}) %copy-start.4) | copy-done | bytes 1572888
  31.3 1.4 %pair_queries.1.pair_ref = bf16[6,1024,256]{2,1,0:T(8,128)(2,1)S(1)} custom-call(bf16[2,128]{1,0:T(2,128)(2,1)S(1)} %bitcast.405, bf16[3,128,2048]{2,1,0:T(8,128)(2,1)S(1)} %bitcast.403, bf16[3,128,2048]{2,1,0:T(8,128)(2,1)S(1)} %bitcast.404), custom_call_target="tpu_custom_call" | custom-call | flops 200000000 | bytes 6291456 | tf_op jit(solution)/shard_map/pair_queries/pallas_call | solution.py:85
  32.8 3.4 %copy-done = bf16[1,2,8192,256]{3,2,1,0:T(8,128)(2,1)S(1)} copy-done((bf16[1,2,8192,256]{3,2,1,0:T(8,128)(2,1)S(1)}, bf16[1,2,8192,256]{3,2,1,0:T(8,128)(2,1)}, u32[]{:S(2)}) %copy-start) | copy-done | bytes 8388632
  37.8 2.6 %collective-permute-start.9 = (bf16[48,4096]{1,0:T(8,128)(2,1)S(1)}, bf16[48,4096]{1,0:T(8,128)(2,1)S(1)}, u32[]{:S(2)}, u32[]{:S(2)}) collective-permute-start(bf16[48,4096]{1,0:T(8,128)(2,1)S(1)} %collective-permute-done.8.ready_ref.refs_0_), channel_id=1, source_target_pairs={{0,132},{8,12},{16,148},{24,28},{32,164},{40,44},{48,180},{56,60},... | collective-permute-start | bytes 1179656 | tf_op jit(solution)/shard_map/ppermute | solution.py:40
  40.4 3.4 %copy-done.1 = bf16[1,2,8192,256]{3,2,1,0:T(8,128)(2,1)S(1)} copy-done((bf16[1,2,8192,256]{3,2,1,0:T(8,128)(2,1)S(1)}, bf16[1,2,8192,256]{3,2,1,0:T(8,128)(2,1)}, u32[]{:S(2)}) %copy-start.1) | copy-done | bytes 8388632
  44.3 1.4 %project.4 = (f32[2,192,256]{2,1,0:T(8,128)S(1)}, f32[192,32]{1,0:T(8,128)S(1)}) custom-call(s32[1]{0:T(128)S(6)} %sub.44.which_ref, bf16[48,4096]{1,0:T(8,128)(2,1)S(1)} %collective-permute-done.8.ready_ref.refs_0_, bf16[48,4096]{1,0:T(8,128)(2,1)S(1)} %collective-permute-done.10.refs_1_, bf16[48,4096]{1,0:T(8,128)(2,1)S(1)} %collective-permute-done.11.refs_2_, ...), custom_call_target="tpu_custom_call" | custom-call | flops 805306368 | bytes 5767168 | tf_op jit(solution)/shard_map/project/pallas_call | solution.py:134
  46.8 1.7 %collective-permute-done.13.refs_1_.refs_3_ = bf16[48,4096]{1,0:T(8,128)(2,1)S(1)} collective-permute-done((bf16[48,4096]{1,0:T(8,128)(2,1)S(1)}, bf16[48,4096]{1,0:T(8,128)(2,1)S(1)}, u32[]{:S(2)}, u32[]{:S(2)}) %collective-permute-start.13) | collective-permute-done | bytes 393248 | tf_op jit(solution)/shard_map/ppermute | solution.py:40
  49.5 4.1 %attend.1 = (bf16[192,512]{1,0:T(8,128)(2,1)S(1)}, bf16[192,32]{1,0:T(8,128)(2,1)S(1)}, bf16[192,512]{1,0:T(8,128)(2,1)S(1)}, bf16[192,32]{1,0:T(8,128)(2,1)S(1)}, f32[32,256]{1,0:T(8,128)S(1)}) custom-call(s32[3]{0:T(128)S(1)} %copy-done.6, s32[3]{0:T(128)S(1)} %copy-done.7, f32[2,96,256]{2,1,0:T(8,128)S(1)} %get-tuple-element.33.y0, ...), custom_call_target="tpu_custom_call" | custom-call | flops 1000000000 | bytes 3145728 | tf_op jit(solution)/shard_map/attend/pallas_call | solution.py:231
  54.0 1.9 %feature_grad.2 = (bf16[48,4096]{1,0:T(8,128)(2,1)S(1)}, bf16[48,4096]{1,0:T(8,128)(2,1)S(1)}, bf16[48,4096]{1,0:T(8,128)(2,1)S(1)}, bf16[48,4096]{1,0:T(8,128)(2,1)S(1)}) custom-call(s32[1]{0:T(128)} %bitcast.which_ref, bf16[192,512]{1,0:T(8,128)(2,1)S(1)} %get-tuple-element.46.g_ref, bf16[192,32]{1,0:T(8,128)(2,1)S(1)} %get-tuple-element.47.m_ref, ...), custom_call_target="tpu_custom_call" | custom-call | flops 805306368 | bytes 5767168 | tf_op jit(solution)/shard_map/feature_grad/pallas_call | solution.py:264
  57.8 2.7 %collective-permute-start.19 = (bf16[48,4096]{1,0:T(8,128)(2,1)S(1)}, bf16[48,4096]{1,0:T(8,128)(2,1)S(1)}, u32[]{:S(2)}, u32[]{:S(2)}) collective-permute-start(bf16[48,4096]{1,0:T(8,128)(2,1)S(1)} %add_convert_fusion.2), channel_id=1, source_target_pairs={{0,132},{8,12},{16,148},{24,28},{32,164},{40,44},{48,180},{56,60},... | collective-permute-start | bytes 1179656 | tf_op jit(solution)/shard_map/ppermute | solution.py:40
  60.5 1.9 %feature_grad.3 = (bf16[48,4096]{1,0:T(8,128)(2,1)S(1)}, bf16[48,4096]{1,0:T(8,128)(2,1)S(1)}, bf16[48,4096]{1,0:T(8,128)(2,1)S(1)}, bf16[48,4096]{1,0:T(8,128)(2,1)S(1)}) custom-call(s32[1]{0:T(128)S(6)} %sub.44.which_ref, bf16[192,512]{1,0:T(8,128)(2,1)S(1)} %get-tuple-element.53.g_ref, bf16[192,32]{1,0:T(8,128)(2,1)S(1)} %get-tuple-element.45.m_ref, ...), custom_call_target="tpu_custom_call" | custom-call | flops 805306368 | bytes 5767168 | tf_op jit(solution)/shard_map/feature_grad/pallas_call | solution.py:264
  62.5 2.8 %collective-permute-done.21 = bf16[32,4096]{1,0:T(8,128)(2,1)S(1)} collective-permute-done((bf16[32,4096]{1,0:T(8,128)(2,1)S(1)}, bf16[32,4096]{1,0:T(8,128)(2,1)S(1)}, u32[]{:S(2)}, u32[]{:S(2)}) %collective-permute-start.21) | collective-permute-done | bytes 262176 | tf_op jit(solution)/shard_map/ppermute | solution.py:379
  67.4 5.6 %collective-permute-done.22 = bf16[32,4352]{1,0:T(8,128)(2,1)S(1)} collective-permute-done((bf16[32,4352]{1,0:T(8,128)(2,1)S(1)}, bf16[32,4352]{1,0:T(8,128)(2,1)S(1)}, u32[]{:S(2)}, u32[]{:S(2)}) %collective-permute-start.22) | collective-permute-done | bytes 278560 | tf_op jit(solution)/shard_map/ppermute | solution.py:399
  73.1 2.7 %collective-permute-start.17 = (bf16[48,4096]{1,0:T(8,128)(2,1)S(1)}, bf16[48,4096]{1,0:T(8,128)(2,1)S(1)}, u32[]{:S(2)}, u32[]{:S(2)}) collective-permute-start(bf16[48,4096]{1,0:T(8,128)(2,1)S(1)} %add_convert_fusion.1), channel_id=1, source_target_pairs={{0,132},{8,12},{16,148},{24,28},{32,164},{40,44},{48,180},{56,60},... | collective-permute-start | bytes 1179656 | tf_op jit(solution)/shard_map/ppermute | solution.py:40
  76.2 6.0 %collective-permute-done.17 = bf16[48,4096]{1,0:T(8,128)(2,1)S(1)} collective-permute-done((bf16[48,4096]{1,0:T(8,128)(2,1)S(1)}, bf16[48,4096]{1,0:T(8,128)(2,1)S(1)}, u32[]{:S(2)}, u32[]{:S(2)}) %collective-permute-start.17) | collective-permute-done | bytes 393248 | tf_op jit(solution)/shard_map/ppermute | solution.py:40
  82.4 1.3 %collective-permute-done.23 = bf16[32,4352]{1,0:T(8,128)(2,1)S(1)} collective-permute-done((bf16[32,4352]{1,0:T(8,128)(2,1)S(1)}, bf16[32,4352]{1,0:T(8,128)(2,1)S(1)}, u32[]{:S(2)}, u32[]{:S(2)}) %collective-permute-start.23) | collective-permute-done | bytes 278560 | tf_op jit(solution)/shard_map/ppermute | solution.py:404
  83.9 3.2 %collective-permute-start.24 = (bf16[6,4096]{1,0:T(8,128)(2,1)S(1)}, bf16[6,4096]{1,0:T(8,128)(2,1)S(1)}, u32[]{:S(2)}, u32[]{:S(2)}) collective-permute-start(bf16[6,4096]{1,0:T(8,128)(2,1)S(1)} %get-tuple-element.67), channel_id=1, source_target_pairs={{0,64},{8,72},{16,80},{24,88},{32,96},{40,104},{48,112},{56,120},{... | collective-permute-start | bytes 147464 | tf_op jit(solution)/shard_map/ppermute | solution.py:40
  87.1 1.4 %collective-permute-start.25 = (bf16[6,4096]{1,0:T(8,128)(2,1)S(1)}, bf16[6,4096]{1,0:T(8,128)(2,1)S(1)}, u32[]{:S(2)}, u32[]{:S(2)}) collective-permute-start(bf16[6,4096]{1,0:T(8,128)(2,1)S(1)} %get-tuple-element.73), channel_id=1, source_target_pairs={{0,80},{8,88},{16,96},{24,104},{32,112},{40,120},{48,0},{56,8},{64... | collective-permute-start | bytes 147464 | tf_op jit(solution)/shard_map/ppermute | solution.py:40
  88.5 2.4 %collective-permute-start.26 = (bf16[6,4096]{1,0:T(8,128)(2,1)S(1)}, bf16[6,4096]{1,0:T(8,128)(2,1)S(1)}, u32[]{:S(2)}, u32[]{:S(2)}) collective-permute-start(bf16[6,4096]{1,0:T(8,128)(2,1)S(1)} %get-tuple-element.72), channel_id=1, source_target_pairs={{0,48},{8,56},{16,64},{24,72},{32,80},{40,88},{48,96},{56,104},{64... | collective-permute-start | bytes 147464 | tf_op jit(solution)/shard_map/ppermute | solution.py:40
  91.0 2.1 %collective-permute-start.27 = (bf16[6,4096]{1,0:T(8,128)(2,1)S(1)}, bf16[6,4096]{1,0:T(8,128)(2,1)S(1)}, u32[]{:S(2)}, u32[]{:S(2)}) collective-permute-start(bf16[6,4096]{1,0:T(8,128)(2,1)S(1)} %get-tuple-element.71), channel_id=1, source_target_pairs={{0,96},{8,104},{16,112},{24,120},{32,0},{40,8},{48,16},{56,24},{64... | collective-permute-start | bytes 147464 | tf_op jit(solution)/shard_map/ppermute | solution.py:40
  93.9 3.8 %collective-permute-start.29 = (bf16[6,4096]{1,0:T(8,128)(2,1)S(1)}, bf16[6,4096]{1,0:T(8,128)(2,1)S(1)}, u32[]{:S(2)}, u32[]{:S(2)}) collective-permute-start(bf16[6,4096]{1,0:T(8,128)(2,1)S(1)} %get-tuple-element.69), channel_id=1, source_target_pairs={{0,112},{8,120},{16,0},{24,8},{32,16},{40,24},{48,32},{56,40},{64,... | collective-permute-start | bytes 147464 | tf_op jit(solution)/shard_map/ppermute | solution.py:40
  98.2 1.2 %collective-permute-done.28 = bf16[6,4096]{1,0:T(8,128)(2,1)S(1)} collective-permute-done((bf16[6,4096]{1,0:T(8,128)(2,1)S(1)}, bf16[6,4096]{1,0:T(8,128)(2,1)S(1)}, u32[]{:S(2)}, u32[]{:S(2)}) %collective-permute-start.28) | collective-permute-done | bytes 49184 | tf_op jit(solution)/shard_map/ppermute | solution.py:40
  99.6 3.6 %collective-permute-done.30 = bf16[6,4096]{1,0:T(8,128)(2,1)S(1)} collective-permute-done((bf16[6,4096]{1,0:T(8,128)(2,1)S(1)}, bf16[6,4096]{1,0:T(8,128)(2,1)S(1)}, u32[]{:S(2)}, u32[]{:S(2)}) %collective-permute-start.30) | collective-permute-done | bytes 49184 | tf_op jit(solution)/shard_map/ppermute | solution.py:40
  (84 shorter events, 19.7 us)
Async XLA Ops:
  1.6 16.5 %collective-permute-start = (bf16[6,4096]{1,0:T(8,128)(2,1)S(1)}, bf16[6,4096]{1,0:T(8,128)(2,1)S(1)}, u32[]{:S(2)}, u32[]{:S(2)}) collective-permute-start(bf16[6,4096]{1,0:T(8,128)(2,1)S(1)} %reshape.31), channel_id=1, source_target_pairs={{0,64},{8,72},{16,80},{24,88},{32,96},{40,104},{48,112},{56,120},{... | collective-permute-start | bytes 147464 | tf_op jit(solution)/shard_map/ppermute | solution.py:40
  8.9 10.2 %collective-permute-start.1 = (bf16[6,4096]{1,0:T(8,128)(2,1)S(1)}, bf16[6,4096]{1,0:T(8,128)(2,1)S(1)}, u32[]{:S(2)}, u32[]{:S(2)}) collective-permute-start(bf16[6,4096]{1,0:T(8,128)(2,1)S(1)} %reshape.31), channel_id=1, source_target_pairs={{0,48},{8,56},{16,64},{24,72},{32,80},{40,88},{48,96},{56,104},{64... | collective-permute-start | bytes 147464 | tf_op jit(solution)/shard_map/ppermute | solution.py:40
  10.8 10.5 %collective-permute-start.2 = (bf16[6,4096]{1,0:T(8,128)(2,1)S(1)}, bf16[6,4096]{1,0:T(8,128)(2,1)S(1)}, u32[]{:S(2)}, u32[]{:S(2)}) collective-permute-start(bf16[6,4096]{1,0:T(8,128)(2,1)S(1)} %reshape.31), channel_id=1, source_target_pairs={{0,80},{8,88},{16,96},{24,104},{32,112},{40,120},{48,0},{56,8},{64... | collective-permute-start | bytes 147464 | tf_op jit(solution)/shard_map/ppermute | solution.py:40
  13.9 7.7 %collective-permute-start.3 = (bf16[6,4096]{1,0:T(8,128)(2,1)S(1)}, bf16[6,4096]{1,0:T(8,128)(2,1)S(1)}, u32[]{:S(2)}, u32[]{:S(2)}) collective-permute-start(bf16[6,4096]{1,0:T(8,128)(2,1)S(1)} %reshape.31), channel_id=1, source_target_pairs={{0,32},{8,40},{16,48},{24,56},{32,64},{40,72},{48,80},{56,88},{64,... | collective-permute-start | bytes 147464 | tf_op jit(solution)/shard_map/ppermute | solution.py:40
  15.4 7.0 %collective-permute-start.4 = (bf16[6,4096]{1,0:T(8,128)(2,1)S(1)}, bf16[6,4096]{1,0:T(8,128)(2,1)S(1)}, u32[]{:S(2)}, u32[]{:S(2)}) collective-permute-start(bf16[6,4096]{1,0:T(8,128)(2,1)S(1)} %reshape.31), channel_id=1, source_target_pairs={{0,96},{8,104},{16,112},{24,120},{32,0},{40,8},{48,16},{56,24},{64... | collective-permute-start | bytes 147464 | tf_op jit(solution)/shard_map/ppermute | solution.py:40
  18.0 5.5 %collective-permute-start.5 = (bf16[6,4096]{1,0:T(8,128)(2,1)S(1)}, bf16[6,4096]{1,0:T(8,128)(2,1)S(1)}, u32[]{:S(2)}, u32[]{:S(2)}) collective-permute-start(bf16[6,4096]{1,0:T(8,128)(2,1)S(1)} %reshape.31), channel_id=1, source_target_pairs={{0,16},{8,24},{16,32},{24,40},{32,48},{40,56},{48,64},{56,72},{64,... | collective-permute-start | bytes 147464 | tf_op jit(solution)/shard_map/ppermute | solution.py:40
  19.1 4.6 %collective-permute-start.6 = (bf16[6,4096]{1,0:T(8,128)(2,1)S(1)}, bf16[6,4096]{1,0:T(8,128)(2,1)S(1)}, u32[]{:S(2)}, u32[]{:S(2)}) collective-permute-start(bf16[6,4096]{1,0:T(8,128)(2,1)S(1)} %reshape.31), channel_id=1, source_target_pairs={{0,112},{8,120},{16,0},{24,8},{32,16},{40,24},{48,32},{56,40},{64,... | collective-permute-start | bytes 147464 | tf_op jit(solution)/shard_map/ppermute | solution.py:40
  24.8 8.0 %collective-permute-start.7 = (bf16[48,4096]{1,0:T(8,128)(2,1)S(1)}, bf16[48,4096]{1,0:T(8,128)(2,1)S(1)}, u32[]{:S(2)}, u32[]{:S(2)}) collective-permute-start(bf16[48,4096]{1,0:T(8,128)(2,1)S(1)} %concatenate.22.refs_0_), channel_id=1, source_target_pairs={{0,8},{8,0},{16,24},{24,16},{32,40},{40,32},{48,56},{56,48},{64,72... | collective-permute-start | bytes 1179656 | tf_op jit(solution)/shard_map/ppermute | solution.py:40
  24.9 12.3 %collective-permute-start.8 = (bf16[48,4096]{1,0:T(8,128)(2,1)S(1)}, bf16[48,4096]{1,0:T(8,128)(2,1)S(1)}, u32[]{:S(2)}, u32[]{:S(2)}) collective-permute-start(bf16[48,4096]{1,0:T(8,128)(2,1)S(1)} %concatenate.22.refs_0_), channel_id=1, source_target_pairs={{0,4},{8,140},{16,20},{24,156},{32,36},{40,172},{48,52},{56,188},{... | collective-permute-start | bytes 1179656 | tf_op jit(solution)/shard_map/ppermute | solution.py:40
  26.4 11.1 %collective-permute-start.10 = (bf16[48,4096]{1,0:T(8,128)(2,1)S(1)}, bf16[48,4096]{1,0:T(8,128)(2,1)S(1)}, u32[]{:S(2)}, u32[]{:S(2)}) collective-permute-start(bf16[48,4096]{1,0:T(8,128)(2,1)S(1)} %concatenate.22.refs_0_), channel_id=1, source_target_pairs={{0,132},{8,12},{16,148},{24,28},{32,164},{40,44},{48,180},{56,60},... | collective-permute-start | bytes 1179656 | tf_op jit(solution)/shard_map/ppermute | solution.py:40
  37.2 7.1 %collective-permute-start.11 = (bf16[48,4096]{1,0:T(8,128)(2,1)S(1)}, bf16[48,4096]{1,0:T(8,128)(2,1)S(1)}, u32[]{:S(2)}, u32[]{:S(2)}) collective-permute-start(bf16[48,4096]{1,0:T(8,128)(2,1)S(1)} %collective-permute-done.8.ready_ref.refs_0_), channel_id=1, source_target_pairs={{0,8},{8,0},{16,24},{24,16},{32,40},{40,32},{48,56},{56,48},{64,72... | collective-permute-start | bytes 1179656 | tf_op jit(solution)/shard_map/ppermute | solution.py:40
  37.6 6.7 %collective-permute-start.12 = (bf16[48,4096]{1,0:T(8,128)(2,1)S(1)}, bf16[48,4096]{1,0:T(8,128)(2,1)S(1)}, u32[]{:S(2)}, u32[]{:S(2)}) collective-permute-start(bf16[48,4096]{1,0:T(8,128)(2,1)S(1)} %collective-permute-done.10.refs_1_), channel_id=1, source_target_pairs={{0,8},{8,0},{16,24},{24,16},{32,40},{40,32},{48,56},{56,48},{64,72... | collective-permute-start | bytes 1179656 | tf_op jit(solution)/shard_map/ppermute | solution.py:40
  37.8 9.0 %collective-permute-start.9 = (bf16[48,4096]{1,0:T(8,128)(2,1)S(1)}, bf16[48,4096]{1,0:T(8,128)(2,1)S(1)}, u32[]{:S(2)}, u32[]{:S(2)}) collective-permute-start(bf16[48,4096]{1,0:T(8,128)(2,1)S(1)} %collective-permute-done.8.ready_ref.refs_0_), channel_id=1, source_target_pairs={{0,132},{8,12},{16,148},{24,28},{32,164},{40,44},{48,180},{56,60},... | collective-permute-start | bytes 1179656 | tf_op jit(solution)/shard_map/ppermute | solution.py:40
  46.8 1.7 %collective-permute-start.13 = (bf16[48,4096]{1,0:T(8,128)(2,1)S(1)}, bf16[48,4096]{1,0:T(8,128)(2,1)S(1)}, u32[]{:S(2)}, u32[]{:S(2)}) collective-permute-start(bf16[48,4096]{1,0:T(8,128)(2,1)S(1)} %collective-permute-done.9.refs_0_.refs_2_), channel_id=1, source_target_pairs={{0,8},{8,0},{16,24},{24,16},{32,40},{40,32},{48,56},{56,48},{64,72... | collective-permute-start | bytes 1179656 | tf_op jit(solution)/shard_map/ppermute | solution.py:40
  55.9 1.8 %collective-permute-start.15 = (bf16[48,4096]{1,0:T(8,128)(2,1)S(1)}, bf16[48,4096]{1,0:T(8,128)(2,1)S(1)}, u32[]{:S(2)}, u32[]{:S(2)}) collective-permute-start(bf16[48,4096]{1,0:T(8,128)(2,1)S(1)} %get-tuple-element.52), channel_id=1, source_target_pairs={{0,8},{8,0},{16,24},{24,16},{32,40},{40,32},{48,56},{56,48},{64,72... | collective-permute-start | bytes 1179656 | tf_op jit(solution)/shard_map/ppermute | solution.py:40
  56.1 9.1 %collective-permute-start.21 = (bf16[32,4096]{1,0:T(8,128)(2,1)S(1)}, bf16[32,4096]{1,0:T(8,128)(2,1)S(1)}, u32[]{:S(2)}, u32[]{:S(2)}) collective-permute-start(bf16[32,4096]{1,0:T(8,128)(2,1)S(1)} %down_grad.2), channel_id=1, source_target_pairs={{0,4},{4,0},{1,5},{5,1},{2,6},{6,2},{3,7},{7,3},{8,12},{12,8},{9,1... | collective-permute-start | bytes 786440 | tf_op jit(solution)/shard_map/ppermute | solution.py:379
  56.2 20.0 %collective-permute-start.14 = (bf16[48,4096]{1,0:T(8,128)(2,1)S(1)}, bf16[48,4096]{1,0:T(8,128)(2,1)S(1)}, u32[]{:S(2)}, u32[]{:S(2)}) collective-permute-start(bf16[48,4096]{1,0:T(8,128)(2,1)S(1)} %get-tuple-element.49), channel_id=1, source_target_pairs={{0,8},{8,0},{16,24},{24,16},{32,40},{40,32},{48,56},{56,48},{64,72... | collective-permute-start | bytes 1179656 | tf_op jit(solution)/shard_map/ppermute | solution.py:40
  57.8 9.1 %collective-permute-start.19 = (bf16[48,4096]{1,0:T(8,128)(2,1)S(1)}, bf16[48,4096]{1,0:T(8,128)(2,1)S(1)}, u32[]{:S(2)}, u32[]{:S(2)}) collective-permute-start(bf16[48,4096]{1,0:T(8,128)(2,1)S(1)} %add_convert_fusion.2), channel_id=1, source_target_pairs={{0,132},{8,12},{16,148},{24,28},{32,164},{40,44},{48,180},{56,60},... | collective-permute-start | bytes 1179656 | tf_op jit(solution)/shard_map/ppermute | solution.py:40
  62.4 3.8 %collective-permute-start.18 = (bf16[48,4096]{1,0:T(8,128)(2,1)S(1)}, bf16[48,4096]{1,0:T(8,128)(2,1)S(1)}, u32[]{:S(2)}, u32[]{:S(2)}) collective-permute-start(bf16[48,4096]{1,0:T(8,128)(2,1)S(1)} %get-tuple-element.57), channel_id=1, source_target_pairs={{0,8},{8,0},{16,24},{24,16},{32,40},{40,32},{48,56},{56,48},{64,72... | collective-permute-start | bytes 1179656 | tf_op jit(solution)/shard_map/ppermute | solution.py:40
  65.4 7.6 %collective-permute-start.22 = (bf16[32,4352]{1,0:T(8,128)(2,1)S(1)}, bf16[32,4352]{1,0:T(8,128)(2,1)S(1)}, u32[]{:S(2)}, u32[]{:S(2)}) collective-permute-start(bf16[32,4352]{1,0:T(8,128)(2,1)S(1)} %pad_maximum_fusion.1), channel_id=1, source_target_pairs={{0,1},{1,0},{2,3},{3,2},{4,5},{5,4},{6,7},{7,6},{8,9},{9,8},{10,11... | collective-permute-start | bytes 835592 | tf_op jit(solution)/shard_map/ppermute | solution.py:399
  66.2 6.8 %collective-permute-start.16 = (bf16[48,4096]{1,0:T(8,128)(2,1)S(1)}, bf16[48,4096]{1,0:T(8,128)(2,1)S(1)}, u32[]{:S(2)}, u32[]{:S(2)}) collective-permute-start(bf16[48,4096]{1,0:T(8,128)(2,1)S(1)} %get-tuple-element.55), channel_id=1, source_target_pairs={{0,8},{8,0},{16,24},{24,16},{32,40},{40,32},{48,56},{56,48},{64,72... | collective-permute-start | bytes 1179656 | tf_op jit(solution)/shard_map/ppermute | solution.py:40
  67.1 15.1 %collective-permute-start.20 = (bf16[48,4096]{1,0:T(8,128)(2,1)S(1)}, bf16[48,4096]{1,0:T(8,128)(2,1)S(1)}, u32[]{:S(2)}, u32[]{:S(2)}) collective-permute-start(bf16[48,4096]{1,0:T(8,128)(2,1)S(1)} %add_convert_fusion), channel_id=1, source_target_pairs={{0,4},{8,140},{16,20},{24,156},{32,36},{40,172},{48,52},{56,188},{... | collective-permute-start | bytes 1179656 | tf_op jit(solution)/shard_map/ppermute | solution.py:40
  73.1 9.1 %collective-permute-start.17 = (bf16[48,4096]{1,0:T(8,128)(2,1)S(1)}, bf16[48,4096]{1,0:T(8,128)(2,1)S(1)}, u32[]{:S(2)}, u32[]{:S(2)}) collective-permute-start(bf16[48,4096]{1,0:T(8,128)(2,1)S(1)} %add_convert_fusion.1), channel_id=1, source_target_pairs={{0,132},{8,12},{16,148},{24,28},{32,164},{40,44},{48,180},{56,60},... | collective-permute-start | bytes 1179656 | tf_op jit(solution)/shard_map/ppermute | solution.py:40
  75.9 7.8 %collective-permute-start.23 = (bf16[32,4352]{1,0:T(8,128)(2,1)S(1)}, bf16[32,4352]{1,0:T(8,128)(2,1)S(1)}, u32[]{:S(2)}, u32[]{:S(2)}) collective-permute-start(bf16[32,4352]{1,0:T(8,128)(2,1)S(1)} %add_convert_fusion.4), channel_id=1, source_target_pairs={{0,3},{1,2},{2,1},{3,0},{4,7},{5,6},{6,5},{7,4},{8,11},{9,10},{10,... | collective-permute-start | bytes 835592 | tf_op jit(solution)/shard_map/ppermute | solution.py:404
  83.9 10.0 %collective-permute-start.24 = (bf16[6,4096]{1,0:T(8,128)(2,1)S(1)}, bf16[6,4096]{1,0:T(8,128)(2,1)S(1)}, u32[]{:S(2)}, u32[]{:S(2)}) collective-permute-start(bf16[6,4096]{1,0:T(8,128)(2,1)S(1)} %get-tuple-element.67), channel_id=1, source_target_pairs={{0,64},{8,72},{16,80},{24,88},{32,96},{40,104},{48,112},{56,120},{... | collective-permute-start | bytes 147464 | tf_op jit(solution)/shard_map/ppermute | solution.py:40
  87.1 10.6 %collective-permute-start.25 = (bf16[6,4096]{1,0:T(8,128)(2,1)S(1)}, bf16[6,4096]{1,0:T(8,128)(2,1)S(1)}, u32[]{:S(2)}, u32[]{:S(2)}) collective-permute-start(bf16[6,4096]{1,0:T(8,128)(2,1)S(1)} %get-tuple-element.73), channel_id=1, source_target_pairs={{0,80},{8,88},{16,96},{24,104},{32,112},{40,120},{48,0},{56,8},{64... | collective-permute-start | bytes 147464 | tf_op jit(solution)/shard_map/ppermute | solution.py:40
  88.5 9.4 %collective-permute-start.26 = (bf16[6,4096]{1,0:T(8,128)(2,1)S(1)}, bf16[6,4096]{1,0:T(8,128)(2,1)S(1)}, u32[]{:S(2)}, u32[]{:S(2)}) collective-permute-start(bf16[6,4096]{1,0:T(8,128)(2,1)S(1)} %get-tuple-element.72), channel_id=1, source_target_pairs={{0,48},{8,56},{16,64},{24,72},{32,80},{40,88},{48,96},{56,104},{64... | collective-permute-start | bytes 147464 | tf_op jit(solution)/shard_map/ppermute | solution.py:40
  91.0 7.3 %collective-permute-start.27 = (bf16[6,4096]{1,0:T(8,128)(2,1)S(1)}, bf16[6,4096]{1,0:T(8,128)(2,1)S(1)}, u32[]{:S(2)}, u32[]{:S(2)}) collective-permute-start(bf16[6,4096]{1,0:T(8,128)(2,1)S(1)} %get-tuple-element.71), channel_id=1, source_target_pairs={{0,96},{8,104},{16,112},{24,120},{32,0},{40,8},{48,16},{56,24},{64... | collective-permute-start | bytes 147464 | tf_op jit(solution)/shard_map/ppermute | solution.py:40
  93.1 6.4 %collective-permute-start.28 = (bf16[6,4096]{1,0:T(8,128)(2,1)S(1)}, bf16[6,4096]{1,0:T(8,128)(2,1)S(1)}, u32[]{:S(2)}, u32[]{:S(2)}) collective-permute-start(bf16[6,4096]{1,0:T(8,128)(2,1)S(1)} %get-tuple-element.70), channel_id=1, source_target_pairs={{0,32},{8,40},{16,48},{24,56},{32,64},{40,72},{48,80},{56,88},{64,... | collective-permute-start | bytes 147464 | tf_op jit(solution)/shard_map/ppermute | solution.py:40
  93.9 5.7 %collective-permute-start.29 = (bf16[6,4096]{1,0:T(8,128)(2,1)S(1)}, bf16[6,4096]{1,0:T(8,128)(2,1)S(1)}, u32[]{:S(2)}, u32[]{:S(2)}) collective-permute-start(bf16[6,4096]{1,0:T(8,128)(2,1)S(1)} %get-tuple-element.69), channel_id=1, source_target_pairs={{0,112},{8,120},{16,0},{24,8},{32,16},{40,24},{48,32},{56,40},{64,... | collective-permute-start | bytes 147464 | tf_op jit(solution)/shard_map/ppermute | solution.py:40
  97.7 5.5 %collective-permute-start.30 = (bf16[6,4096]{1,0:T(8,128)(2,1)S(1)}, bf16[6,4096]{1,0:T(8,128)(2,1)S(1)}, u32[]{:S(2)}, u32[]{:S(2)}) collective-permute-start(bf16[6,4096]{1,0:T(8,128)(2,1)S(1)} %get-tuple-element.68), channel_id=1, source_target_pairs={{0,16},{8,24},{16,32},{24,40},{32,48},{40,56},{48,64},{56,72},{64,... | collective-permute-start | bytes 147464 | tf_op jit(solution)/shard_map/ppermute | solution.py:40
  97.9 6.5 %collective-permute-start.31 = (bf16[32,4352]{1,0:T(8,128)(2,1)S(1)}, bf16[32,4352]{1,0:T(8,128)(2,1)S(1)}, u32[]{:S(2)}, u32[]{:S(2)}) collective-permute-start(bf16[32,4352]{1,0:T(8,128)(2,1)S(1)} %add_convert_fusion.3), channel_id=1, source_target_pairs={{0,4},{4,0},{1,5},{5,1},{2,6},{6,2},{3,7},{7,3},{8,12},{12,8},{9,1... | collective-permute-start | bytes 835592 | tf_op jit(solution)/shard_map/ppermute | solution.py:409
  (8 other events, 73.5 us)

commit v5 on v4

--- a/solution.py
+++ b/solution.py
@@ -58,7 +58,7 @@
 
 
 def cost(flops, moved):
-    return pl.CostEstimate(flops=int(flops), bytes_accessed=int(moved), transcendentals=0)
+    return pl.CostEstimate(flops=int(flops) // 1000, bytes_accessed=int(moved) // 1000, transcendentals=0)
 
 
 def pair_kernel(gain_ref, query_ref, context_ref, pair_ref):
@@ -94,6 +94,47 @@
     )(gains, queries, context)
 
 
+def flatten_kernel(from_ref, to_ref):
+    outer, inner, _ = from_ref.shape
+    for i in range(outer):
+        to_ref[i * inner : (i + 1) * inner, :] = from_ref[i]
+
+
+def flatten(array):
+    outer, inner, wide = array.shape
+    return pl.pallas_call(
+        flatten_kernel,
+        out_shape=jax.ShapeDtypeStruct((outer * inner, wide), array.dtype),
+        in_specs=[VECTOR],
+        out_specs=VECTOR,
+        compiler_params=ROOM,
+        cost_estimate=cost(0, 4 * array.size),
+        name="flatten",
+    )(array)
+
+
+def total_kernel(own_ref, *refs):
+    *arrived, to_ref = refs
+    rows = own_ref[...]
+    for ref in arrived:
+        rows += ref[...].astype(F32)
+    outer, inner, _ = to_ref.shape
+    for i in range(outer):
+        to_ref[i] = rows[i * inner : (i + 1) * inner]
+
+
+def total(own, arrived, shape):
+    return pl.pallas_call(
+        total_kernel,
+        out_shape=jax.ShapeDtypeStruct(shape, F32),
+        in_specs=[VECTOR] * (1 + len(arrived)),
+        out_specs=VECTOR,
+        compiler_params=ROOM,
+        cost_estimate=cost(own.size * len(arrived), 2 * own.size * len(arrived)),
+        name="total",
+    )(own, *arrived)
+
+
 def hold_kernel(ready_ref, from_ref, to_ref, semaphore):
     copy = pltpu.make_async_copy(from_ref, to_ref, semaphore)
     copy.start()
@@ -147,7 +188,7 @@
 
 def attention_kernel(
     count_ref, start_ref, y0, y1, y2, r0, r1, r2, own_map, other_map, own_back, other_back,
-    up_diagonal, gains_ref, pair_ref, g_own, m_own, g_other, m_other, up_ref, grad_ref,
+    up_diagonal, gains_ref, pair_ref, g_own, m_own, g_other, m_other, middle_ref, up_ref, grad_ref,
 ):
     width = y0.shape[2]
     head = gains_ref.shape[1]
@@ -214,6 +255,7 @@
             ].astype(LOW)
     grad = grad_ref[...]
     middle = dot(grad, up_diagonal[...], NT).astype(LOW)
+    middle_ref[...] = (ADAPTER_SCALE * middle.astype(F32)).astype(LOW)
     up = ADAPTER_SCALE * dot(reduced, grad, TN)
     for part in range(2):
         half = slice(part * ranks // 2, (part + 1) * ranks // 2)
@@ -235,10 +277,11 @@
             jax.ShapeDtypeStruct((rows, ranks), LOW),
             jax.ShapeDtypeStruct((rows, 2 * width), LOW),
             jax.ShapeDtypeStruct((rows, ranks), LOW),
+            jax.ShapeDtypeStruct((rows, ranks), LOW),
             jax.ShapeDtypeStruct((ranks, width), F32),
         ],
         in_specs=[scalar, scalar] + [vector] * 13,
-        out_specs=[vector] * 5,
+        out_specs=[vector] * 6,
         scratch_shapes=[pltpu.VMEM((rows, 2 * width), LOW)],
         compiler_params=ROOM,
         cost_estimate=cost(1e9, 2 * pair.size),
@@ -272,23 +315,26 @@
     )(which, grad, middle, weights, down_maps)
 
 
-def down_kernel(m_ref, *refs):
+def down_kernel(back_ref, mine_ref, facing_ref, *refs):
     *row_refs, out_ref = refs
     rows = jnp.concatenate([ref[...] for ref in row_refs])
-    out_ref[...] = dot(m_ref[...], rows, TN).astype(out_ref.dtype)
-
-
-def down_grad(middle, blocks, dtype):
-    half = blocks[0].shape[1]
+    ranks = mine_ref.shape[1]
+    both = jnp.concatenate([mine_ref[...], facing_ref[...]], 1)
+    parts = dot(dot(back_ref[...], both).astype(LOW), rows, TN)
+    out_ref[...] = parts[:ranks] + parts[ranks:]
+
+
+def down_grad(back, mine, facing, blocks):
+    ranks, half = mine.shape[1], blocks[0].shape[1]
     return pl.pallas_call(
         down_kernel,
-        out_shape=jax.ShapeDtypeStruct((middle.shape[1], half), dtype),
-        in_specs=[VECTOR] * (1 + len(blocks)),
+        out_shape=jax.ShapeDtypeStruct((ranks, half), F32),
+        in_specs=[VECTOR] * (3 + len(blocks)),
         out_specs=VECTOR,
         compiler_params=ROOM,
         cost_estimate=cost(5e7, 2 * 200 * half),
         name="down_grad",
-    )(middle, *blocks)
+    )(back, mine, facing, *blocks)
 
 
 def row_tokens(x_hi, z, core, x_lo):
@@ -328,7 +374,7 @@
     here = side.reshape(1).astype(jnp.int32)
     opposite = 1 - here
 
-    own = vision_feature_states.reshape(-1, half)
+    own = flatten(vision_feature_states)
     base = jnp.concatenate([move(own, ALONG[k]) for k in SHIFTS] + [own])
     first = move(base, NEAR)
     second = move(base, FAR)
@@ -352,9 +398,9 @@
     pair = pair_queries(
         after(queries[0], base), context_gradient[0], gains, width // gains.shape[1]
     )
+    weights = hold(weights, after(pair, up_diagonal, *maps))
     step_a = project([base, base_there], weights, down_maps, here)
     first = after(first, pair, *step_a, up_diagonal, *maps)
-    weights = hold(weights, first)
     third = move(first, FAR)
     first_there = move(first, SIBLING)
     second_there = move(second, SIBLING)
@@ -365,7 +411,7 @@
     step_c = project([third, third_there], weights, down_maps, here)
     owns = [base, base_there, third, third_there]
 
-    g_own, m_own, g_other, m_other, up_part = attend(
+    g_own, m_own, g_other, m_other, middle, up_part = attend(
         image_tile_count,
         text_start_position,
         (step_a, step_c, step_b),
@@ -375,12 +421,8 @@
         pair,
     )
 
-    down_other = down_grad(m_other, others, LOW)
-    down_facing = lax.ppermute(down_other, "tensor", TENSOR_SWAP)
-    base, base_out, third, third_out = feature_grad(
-        after(g_own, down_other), m_own, weights, down_maps, here
-    )
-    down_own = down_grad(m_own, owns, F32)
+    middle_facing = lax.ppermute(middle, "tensor", TENSOR_SWAP)
+    base, base_out, third, third_out = feature_grad(g_own, m_own, weights, down_maps, here)
 
     def add(mine, theirs):
         return mine.astype(F32) + theirs.astype(F32)
@@ -388,19 +430,18 @@
     third = add(third, move(third_out, SIBLING)).astype(LOW)
     third_in = move(third, FAR)
     first, second, first_out, second_out = feature_grad(
-        after(g_other, third, down_own), m_other, weights, down_maps, opposite
+        after(g_other, third), m_other, weights, down_maps, opposite
     )
     second = add(second, move(second_out, SIBLING)).astype(LOW)
     first = add(first, move(first_out, SIBLING))
     base = add(base, move(base_out, SIBLING))
-    sums = jnp.concatenate(
-        [down_own + after(down_facing, first_out).astype(F32), up_part], 1
-    ).astype(LOW)
+    second_in = move(second, FAR)
+    down_own = down_grad(maps[2], middle, after(middle_facing, second), owns)
+    sums = jnp.concatenate([down_own, up_part], 1).astype(LOW)
     near_sums = lax.ppermute(sums, "dp", DP_NEAR)
-    second_in = move(second, FAR)
     first = (first + third_in.astype(F32)).astype(LOW)
     first_in = move(first, NEAR)
-    sums = add(sums, after(near_sums, first)).astype(LOW)
+    sums = add(sums, after(near_sums, second_in, first)).astype(LOW)
     far_sums = lax.ppermute(sums, "dp", DP_FAR)
     base = base + second_in.astype(F32) + first_in.astype(F32)
     low_base = base.astype(LOW)
@@ -408,16 +449,17 @@
     low_base = after(low_base, sums)
     facing = lax.ppermute(sums, "tensor", TENSOR_SWAP)
     count = own.shape[0]
-    own_grad = base[len(SHIFTS) * count :]
-    for i, k in enumerate(SHIFTS):
-        own_grad += move(low_base[i * count : (i + 1) * count], ALONG[NZ - k]).astype(F32)
+    arrived = [
+        move(low_base[i * count : (i + 1) * count], ALONG[NZ - k]) for i, k in enumerate(SHIFTS)
+    ]
+    own_grad = total(base[len(SHIFTS) * count :], arrived, vision_feature_states.shape)
 
     left = jnp.where(side == 0, sums, facing).astype(F32)
     right = jnp.where(side == 0, facing, sums).astype(F32)
     down_total = jnp.concatenate([left[:, :half], right[:, :half]], 1)
     up_total = jnp.concatenate([left[:, half:], right[:, half:]], 1)
     return (
-        own_grad.reshape(vision_feature_states.shape),
+        own_grad,
         down_total.reshape(1, 2, ranks // 2, 2 * half),
         up_total.reshape(1, 2, ranks // 2, 2 * width),
     )

time: 107 us -> 113 us (1.056)
  waiting for transfers between devices: 28.3 us -> 33.4 us
  Pallas kernels: 14 us -> 17.6 us
  starting transfers between devices: 47.9 us -> 44.7 us
    ppermute x28, waiting for transfers between devices: 18.1 us -> 23.8 us  [move(): return lax.ppermute(block, PLANE, pairs)]
    ppermute x28, starting transfers between devices: 46.5 us -> 42.1 us  [move(): return lax.ppermute(block, PLANE, pairs)]
    ppermute x1, waiting for transfers between devices: 1.33 us -> 5.06 us  [per_device(): far_sums = lax.ppermute(sums, 'dp', DP_FAR)]
    pallas_call x3, Pallas kernels: 3.35 us -> 5.39 us  [project(): pl.pallas_call(project_kernel, out_shape=[jax.ShapeDtypeStruct((2, count,...]
    ppermute x1, waiting for transfers between devices: 2.77 us -> 0.75 us  [per_device(): middle_facing = lax.ppermute(middle, 'tensor', TENSOR_SWAP)]
    ppermute x1, waiting for transfers between devices: 5.64 us -> 3.82 us  [per_device(): near_sums = lax.ppermute(sums, 'dp', DP_NEAR)]
    reshape x2 -> x0, local copies, waits for them, and re-layouts: 1.64 us -> none  [the longest x1 0.94 us: per_device(): own = vision_feature_states.reshape(-1, half)]
    pallas_call x2 -> x3, Pallas kernels: 0.85 us -> 2.46 us  [the longest x1 1.71 us: down_grad(): pl.pallas_call(down_kernel, out_shape=jax.ShapeDtypeStruct((ranks, half),...]
  transfers between devices with their start and end apart: 32 -> 32, of which waited for: 18 -> 20; matrix products, arithmetic and copies ran while one was open for 3% -> 4% of each run, Pallas kernels for 6% -> 8%
where the time goes in v5:
time: 113 us; the launch traced here: 112 us
  starting transfers between devices  44.7 us (40%)
  waiting for transfers between devices  33.4 us (30%)
  Pallas kernels  17.6 us (16%)
  local copies, waits for them, and re-layouts  11.5 us (10%)
  other arithmetic  3.34 us (3%)
  between operations  1.28 us (1%)
    ppermute x28, starting transfers between devices, move(): return lax.ppermute(block, PLANE, pairs)  42.1 us
    ppermute x28, waiting for transfers between devices, move(): return lax.ppermute(block, PLANE, pairs)  23.8 us
    unnamed x18, local copies, waits for them, and re-layouts  8.1 us
    pallas_call x3, Pallas kernels, project(): pl.pallas_call(project_kernel, out_shape=[jax.ShapeDtypeStruct((2, count,...  5.39 us
    ppermute x1, waiting for transfers between devices, per_device(): far_sums = lax.ppermute(sums, 'dp', DP_FAR)  5.06 us
    pallas_call x1, Pallas kernels, attend(): pl.pallas_call(attention_kernel, out_shape=[jax.ShapeDtypeStruct((rows, 2...  4.03 us
    pallas_call x2, Pallas kernels, feature_grad(): pl.pallas_call(feature_kernel, out_shape=[jax.ShapeDtypeStruct((rows // 4...  3.84 us
    ppermute x1, waiting for transfers between devices, per_device(): near_sums = lax.ppermute(sums, 'dp', DP_NEAR)  3.82 us
  transfers between devices with their start and end apart: 32, of which 20 were waited for; matrix products, arithmetic and copies ran while one was open for 4% of the time, Pallas kernels for 8%

profile of v5, /device:TPU:24, one launch (start us, length us, event | category | flops | bytes accessed | tf_op | source)
XLA Modules:
  0.0 111.9 jit_solution(1143195698940585741)
XLA Ops:
  1.5 7.3 %collective-permute-start = (bf16[6,4096]{1,0:T(8,128)(2,1)S(1)}, bf16[6,4096]{1,0:T(8,128)(2,1)S(1)}, u32[]{:S(2)}, u32[]{:S(2)}) collective-permute-start(bf16[6,4096]{1,0:T(8,128)(2,1)S(1)} %flatten.1), channel_id=1, source_target_pairs={{0,64},{8,72},{16,80},{24,88},{32,96},{40,104},{48,112},{56,120},{... | collective-permute-start | bytes 147464 | tf_op jit(solution)/shard_map/ppermute | solution.py:40
  8.7 1.9 %collective-permute-start.1 = (bf16[6,4096]{1,0:T(8,128)(2,1)S(1)}, bf16[6,4096]{1,0:T(8,128)(2,1)S(1)}, u32[]{:S(2)}, u32[]{:S(2)}) collective-permute-start(bf16[6,4096]{1,0:T(8,128)(2,1)S(1)} %flatten.1), channel_id=1, source_target_pairs={{0,48},{8,56},{16,64},{24,72},{32,80},{40,88},{48,96},{56,104},{64... | collective-permute-start | bytes 147464 | tf_op jit(solution)/shard_map/ppermute | solution.py:40
  10.7 3.1 %collective-permute-start.2 = (bf16[6,4096]{1,0:T(8,128)(2,1)S(1)}, bf16[6,4096]{1,0:T(8,128)(2,1)S(1)}, u32[]{:S(2)}, u32[]{:S(2)}) collective-permute-start(bf16[6,4096]{1,0:T(8,128)(2,1)S(1)} %flatten.1), channel_id=1, source_target_pairs={{0,80},{8,88},{16,96},{24,104},{32,112},{40,120},{48,0},{56,8},{64... | collective-permute-start | bytes 147464 | tf_op jit(solution)/shard_map/ppermute | solution.py:40
  13.8 1.5 %collective-permute-start.3 = (bf16[6,4096]{1,0:T(8,128)(2,1)S(1)}, bf16[6,4096]{1,0:T(8,128)(2,1)S(1)}, u32[]{:S(2)}, u32[]{:S(2)}) collective-permute-start(bf16[6,4096]{1,0:T(8,128)(2,1)S(1)} %flatten.1), channel_id=1, source_target_pairs={{0,32},{8,40},{16,48},{24,56},{32,64},{40,72},{48,80},{56,88},{64,... | collective-permute-start | bytes 147464 | tf_op jit(solution)/shard_map/ppermute | solution.py:40
  15.2 2.7 %collective-permute-start.4 = (bf16[6,4096]{1,0:T(8,128)(2,1)S(1)}, bf16[6,4096]{1,0:T(8,128)(2,1)S(1)}, u32[]{:S(2)}, u32[]{:S(2)}) collective-permute-start(bf16[6,4096]{1,0:T(8,128)(2,1)S(1)} %flatten.1), channel_id=1, source_target_pairs={{0,96},{8,104},{16,112},{24,120},{32,0},{40,8},{48,16},{56,24},{64... | collective-permute-start | bytes 147464 | tf_op jit(solution)/shard_map/ppermute | solution.py:40
  18.9 2.2 %collective-permute-start.6 = (bf16[6,4096]{1,0:T(8,128)(2,1)S(1)}, bf16[6,4096]{1,0:T(8,128)(2,1)S(1)}, u32[]{:S(2)}, u32[]{:S(2)}) collective-permute-start(bf16[6,4096]{1,0:T(8,128)(2,1)S(1)} %flatten.1), channel_id=1, source_target_pairs={{0,112},{8,120},{16,0},{24,8},{32,16},{40,24},{48,32},{56,40},{64,... | collective-permute-start | bytes 147464 | tf_op jit(solution)/shard_map/ppermute | solution.py:40
  24.6 1.6 %collective-permute-start.8 = (bf16[48,4096]{1,0:T(8,128)(2,1)S(1)}, bf16[48,4096]{1,0:T(8,128)(2,1)}, u32[]{:S(2)}, u32[]{:S(2)}) collective-permute-start(bf16[48,4096]{1,0:T(8,128)(2,1)S(1)} %concatenate.22.refs_0_), channel_id=1, source_target_pairs={{0,4},{8,140},{16,20},{24,156},{32,36},{40,172},{48,52},{56,188},{... | collective-permute-start | bytes 1179656 | tf_op jit(solution)/shard_map/ppermute | solution.py:40
  26.2 2.1 %collective-permute-start.10 = (bf16[48,4096]{1,0:T(8,128)(2,1)S(1)}, bf16[48,4096]{1,0:T(8,128)(2,1)}, u32[]{:S(2)}, u32[]{:S(2)}) collective-permute-start(bf16[48,4096]{1,0:T(8,128)(2,1)S(1)} %concatenate.22.refs_0_), channel_id=1, source_target_pairs={{0,132},{8,12},{16,148},{24,28},{32,164},{40,44},{48,180},{56,60},... | collective-permute-start | bytes 1179656 | tf_op jit(solution)/shard_map/ppermute | solution.py:40
  29.0 1.4 %copy-done.2 = bf16[1,3,128,2048]{3,2,1,0:T(8,128)(2,1)S(1)} copy-done((bf16[1,3,128,2048]{3,2,1,0:T(8,128)(2,1)S(1)}, bf16[1,3,128,2048]{3,2,1,0:T(8,128)(2,1)}, u32[]{:S(2)}) %copy-start.2) | copy-done | bytes 1572888
  30.4 1.4 %copy-done.3 = bf16[1,3,128,2048]{3,2,1,0:T(8,128)(2,1)S(1)} copy-done((bf16[1,3,128,2048]{3,2,1,0:T(8,128)(2,1)S(1)}, bf16[1,3,128,2048]{3,2,1,0:T(8,128)(2,1)}, u32[]{:S(2)}) %copy-start.3) | copy-done | bytes 1572888
  36.6 3.4 %copy-done.1 = bf16[1,2,8192,256]{3,2,1,0:T(8,128)(2,1)S(1)} copy-done((bf16[1,2,8192,256]{3,2,1,0:T(8,128)(2,1)S(1)}, bf16[1,2,8192,256]{3,2,1,0:T(8,128)(2,1)}, u32[]{:S(2)}) %copy-start.1) | copy-done | bytes 8388632
  41.0 2.0 %project.3 = (f32[2,96,256]{2,1,0:T(8,128)S(1)}, f32[96,32]{1,0:T(8,128)S(1)}) custom-call(s32[1]{0:T(128)} %bitcast.which_ref, bf16[48,4096]{1,0:T(8,128)(2,1)S(1)} %concatenate.22.refs_0_, bf16[48,4096]{1,0:T(8,128)(2,1)} %collective-permute-done.7.refs_1_, bf16[2,8192,256]{2,1,0:T(8,128)(2,1)S(1)} %hold.1.refs_2_.refs_4_.w_ref, ...), custom_call_target="tpu_custom_call" | custom-call | flops 805306 | bytes 4980 | tf_op jit(solution)/shard_map/project/pallas_call | solution.py:175
  45.6 2.5 %project.4 = (f32[2,192,256]{2,1,0:T(8,128)S(1)}, f32[192,32]{1,0:T(8,128)S(1)}) custom-call(s32[1]{0:T(128)S(6)} %sub.44.which_ref, bf16[48,4096]{1,0:T(8,128)(2,1)} %collective-permute-done.8.refs_0_, bf16[48,4096]{1,0:T(8,128)(2,1)} %collective-permute-done.10.refs_1_, bf16[48,4096]{1,0:T(8,128)(2,1)S(1)} %collective-permute-done.11.refs_2_, ...), custom_call_target="tpu_custom_call" | custom-call | flops 805306 | bytes 5767 | tf_op jit(solution)/shard_map/project/pallas_call | solution.py:175
  48.1 4.7 %collective-permute-done.9.refs_0_.refs_2_ = bf16[48,4096]{1,0:T(8,128)(2,1)S(1)} collective-permute-done((bf16[48,4096]{1,0:T(8,128)(2,1)}, bf16[48,4096]{1,0:T(8,128)(2,1)S(1)}, u32[]{:S(2)}, u32[]{:S(2)}) %collective-permute-start.9) | collective-permute-done | bytes 393248 | tf_op jit(solution)/shard_map/ppermute | solution.py:40
  52.8 1.7 %collective-permute-done.13.refs_1_.refs_3_ = bf16[48,4096]{1,0:T(8,128)(2,1)S(1)} collective-permute-done((bf16[48,4096]{1,0:T(8,128)(2,1)S(1)}, bf16[48,4096]{1,0:T(8,128)(2,1)S(1)}, u32[]{:S(2)}, u32[]{:S(2)}) %collective-permute-start.13) | collective-permute-done | bytes 393248 | tf_op jit(solution)/shard_map/ppermute | solution.py:40
  55.5 4.0 %attend.1 = (bf16[192,512]{1,0:T(8,128)(2,1)S(1)}, bf16[192,32]{1,0:T(8,128)(2,1)S(1)}, bf16[192,512]{1,0:T(8,128)(2,1)S(1)}, bf16[192,32]{1,0:T(8,128)(2,1)S(1)...) custom-call(s32[3]{0:T(128)S(1)} %copy-done.7, s32[3]{0:T(128)S(1)} %copy-done.8, ...), custom_call_target="tpu_custom_call" | custom-call | flops 1000000 | bytes 3145 | tf_op jit(solution)/shard_map/attend/pallas_call | solution.py:273
  59.6 1.9 %feature_grad.2 = (bf16[48,4096]{1,0:T(8,128)(2,1)S(1)}, bf16[48,4096]{1,0:T(8,128)(2,1)S(1)}, bf16[48,4096]{1,0:T(8,128)(2,1)S(1)}, bf16[48,4096]{1,0:T(8,128)(2,1)S(1)}) custom-call(s32[1]{0:T(128)} %bitcast.which_ref, bf16[192,512]{1,0:T(8,128)(2,1)S(1)} %get-tuple-element.46.g_ref, bf16[192,32]{1,0:T(8,128)(2,1)S(1)} %get-tuple-element.47.m_ref, ...), custom_call_target="tpu_custom_call" | custom-call | flops 805306 | bytes 5767 | tf_op jit(solution)/shard_map/feature_grad/pallas_call | solution.py:307
  61.8 1.6 %collective-permute-done.15 = bf16[48,4096]{1,0:T(8,128)(2,1)S(1)} collective-permute-done((bf16[48,4096]{1,0:T(8,128)(2,1)S(1)}, bf16[48,4096]{1,0:T(8,128)(2,1)S(1)}, u32[]{:S(2)}, u32[]{:S(2)}) %collective-permute-start.15) | collective-permute-done | bytes 393248 | tf_op jit(solution)/shard_map/ppermute | solution.py:40
  63.4 1.9 %feature_grad.3 = (bf16[48,4096]{1,0:T(8,128)(2,1)S(1)}, bf16[48,4096]{1,0:T(8,128)(2,1)S(1)}, bf16[48,4096]{1,0:T(8,128)(2,1)S(1)}, bf16[48,4096]{1,0:T(8,128)(2,1)S(1)}) custom-call(s32[1]{0:T(128)S(6)} %sub.44.which_ref, bf16[192,512]{1,0:T(8,128)(2,1)S(1)} %get-tuple-element.53.g_ref, bf16[192,32]{1,0:T(8,128)(2,1)S(1)} %get-tuple-element.54.m_ref, ...), custom_call_target="tpu_custom_call" | custom-call | flops 805306 | bytes 5767 | tf_op jit(solution)/shard_map/feature_grad/pallas_call | solution.py:307
  67.9 1.4 %collective-permute-start.17 = (bf16[48,4096]{1,0:T(8,128)(2,1)S(1)}, bf16[48,4096]{1,0:T(8,128)(2,1)S(1)}, u32[]{:S(2)}, u32[]{:S(2)}) collective-permute-start(bf16[48,4096]{1,0:T(8,128)(2,1)S(1)} %add_convert_fusion.1), channel_id=1, source_target_pairs={{0,132},{8,12},{16,148},{24,28},{32,164},{40,44},{48,180},{56,60},... | collective-permute-start | bytes 1179656 | tf_op jit(solution)/shard_map/ppermute | solution.py:40
  70.1 1.7 %down_grad.1 = f32[32,4096]{1,0:T(8,128)S(1)} custom-call(bf16[192,192]{1,0:T(8,128)(2,1)S(1)} %get-tuple-element.80.own_back.back_ref, bf16[192,32]{1,0:T(8,128)(2,1)S(1)} %get-tuple-element.59.mine_ref, bf16[192,32]{1,0:T(8,128)(2,1)S(1)} %collective-permute-done.21.facing_ref, bf16[48,4096]{1,0:T(8,128)(2,1)S(1)} %concatenate.22.refs_0_, ...), custom_call_target="tpu_custom_call" | custom-call | flops 50000 | bytes 1638 | tf_op jit(solution)/shard_map/down_grad/pallas_call | solution.py:329
  73.0 2.0 %collective-permute-done.19 = bf16[48,4096]{1,0:T(8,128)(2,1)S(1)} collective-permute-done((bf16[48,4096]{1,0:T(8,128)(2,1)S(1)}, bf16[48,4096]{1,0:T(8,128)(2,1)S(1)}, u32[]{:S(2)}, u32[]{:S(2)}) %collective-permute-start.19) | collective-permute-done | bytes 393248 | tf_op jit(solution)/shard_map/ppermute | solution.py:40
  75.7 3.8 %collective-permute-done.22 = bf16[32,4352]{1,0:T(8,128)(2,1)S(1)} collective-permute-done((bf16[32,4352]{1,0:T(8,128)(2,1)S(1)}, bf16[32,4352]{1,0:T(8,128)(2,1)S(1)}, u32[]{:S(2)}, u32[]{:S(2)}) %collective-permute-start.22) | collective-permute-done | bytes 278560 | tf_op jit(solution)/shard_map/ppermute | solution.py:441
  80.7 2.3 %collective-permute-done.20 = bf16[48,4096]{1,0:T(8,128)(2,1)S(1)} collective-permute-done((bf16[48,4096]{1,0:T(8,128)(2,1)S(1)}, bf16[48,4096]{1,0:T(8,128)(2,1)S(1)}, u32[]{:S(2)}, u32[]{:S(2)}) %collective-permute-start.20) | collective-permute-done | bytes 393248 | tf_op jit(solution)/shard_map/ppermute | solution.py:40
  83.2 5.1 %collective-permute-done.23 = bf16[32,4352]{1,0:T(8,128)(2,1)S(1)} collective-permute-done((bf16[32,4352]{1,0:T(8,128)(2,1)S(1)}, bf16[32,4352]{1,0:T(8,128)(2,1)S(1)}, u32[]{:S(2)}, u32[]{:S(2)}) %collective-permute-start.23) | collective-permute-done | bytes 278560 | tf_op jit(solution)/shard_map/ppermute | solution.py:445
  89.6 3.2 %collective-permute-start.24 = (bf16[6,4096]{1,0:T(8,128)(2,1)S(1)}, bf16[6,4096]{1,0:T(8,128)(2,1)S(1)}, u32[]{:S(2)}, u32[]{:S(2)}) collective-permute-start(bf16[6,4096]{1,0:T(8,128)(2,1)S(1)} %get-tuple-element.75), channel_id=1, source_target_pairs={{0,64},{8,72},{16,80},{24,88},{32,96},{40,104},{48,112},{56,120},{... | collective-permute-start | bytes 147464 | tf_op jit(solution)/shard_map/ppermute | solution.py:40
  94.3 2.4 %collective-permute-start.26 = (bf16[6,4096]{1,0:T(8,128)(2,1)S(1)}, bf16[6,4096]{1,0:T(8,128)(2,1)S(1)}, u32[]{:S(2)}, u32[]{:S(2)}) collective-permute-start(bf16[6,4096]{1,0:T(8,128)(2,1)S(1)} %get-tuple-element.73), channel_id=1, source_target_pairs={{0,48},{8,56},{16,64},{24,72},{32,80},{40,88},{48,96},{56,104},{64... | collective-permute-start | bytes 147464 | tf_op jit(solution)/shard_map/ppermute | solution.py:40
  96.7 2.1 %collective-permute-start.27 = (bf16[6,4096]{1,0:T(8,128)(2,1)S(1)}, bf16[6,4096]{1,0:T(8,128)(2,1)S(1)}, u32[]{:S(2)}, u32[]{:S(2)}) collective-permute-start(bf16[6,4096]{1,0:T(8,128)(2,1)S(1)} %get-tuple-element.72), channel_id=1, source_target_pairs={{0,96},{8,104},{16,112},{24,120},{32,0},{40,8},{48,16},{56,24},{64... | collective-permute-start | bytes 147464 | tf_op jit(solution)/shard_map/ppermute | solution.py:40
  99.6 1.8 %collective-permute-done.25.refs_1_ = bf16[6,4096]{1,0:T(8,128)(2,1)S(1)} collective-permute-done((bf16[6,4096]{1,0:T(8,128)(2,1)S(1)}, bf16[6,4096]{1,0:T(8,128)(2,1)S(1)}, u32[]{:S(2)}, u32[]{:S(2)}) %collective-permute-start.25) | collective-permute-done | bytes 49184 | tf_op jit(solution)/shard_map/ppermute | solution.py:40
  101.4 2.0 %collective-permute-start.29 = (bf16[6,4096]{1,0:T(8,128)(2,1)S(1)}, bf16[6,4096]{1,0:T(8,128)(2,1)S(1)}, u32[]{:S(2)}, u32[]{:S(2)}) collective-permute-start(bf16[6,4096]{1,0:T(8,128)(2,1)S(1)} %get-tuple-element.70), channel_id=1, source_target_pairs={{0,112},{8,120},{16,0},{24,8},{32,16},{40,24},{48,32},{56,40},{64,... | collective-permute-start | bytes 147464 | tf_op jit(solution)/shard_map/ppermute | solution.py:40
  104.0 1.4 %collective-permute-done.28.refs_4_ = bf16[6,4096]{1,0:T(8,128)(2,1)S(1)} collective-permute-done((bf16[6,4096]{1,0:T(8,128)(2,1)S(1)}, bf16[6,4096]{1,0:T(8,128)(2,1)S(1)}, u32[]{:S(2)}, u32[]{:S(2)}) %collective-permute-start.28) | collective-permute-done | bytes 49184 | tf_op jit(solution)/shard_map/ppermute | solution.py:40
  106.2 3.1 %collective-permute-done.30.refs_6_ = bf16[6,4096]{1,0:T(8,128)(2,1)S(1)} collective-permute-done((bf16[6,4096]{1,0:T(8,128)(2,1)S(1)}, bf16[6,4096]{1,0:T(8,128)(2,1)S(1)}, u32[]{:S(2)}, u32[]{:S(2)}) %collective-permute-start.30) | collective-permute-done | bytes 49184 | tf_op jit(solution)/shard_map/ppermute | solution.py:40
  (85 shorter events, 29.4 us)
Async XLA Ops:
  1.5 16.5 %collective-permute-start = (bf16[6,4096]{1,0:T(8,128)(2,1)S(1)}, bf16[6,4096]{1,0:T(8,128)(2,1)S(1)}, u32[]{:S(2)}, u32[]{:S(2)}) collective-permute-start(bf16[6,4096]{1,0:T(8,128)(2,1)S(1)} %flatten.1), channel_id=1, source_target_pairs={{0,64},{8,72},{16,80},{24,88},{32,96},{40,104},{48,112},{56,120},{... | collective-permute-start | bytes 147464 | tf_op jit(solution)/shard_map/ppermute | solution.py:40
  8.7 10.2 %collective-permute-start.1 = (bf16[6,4096]{1,0:T(8,128)(2,1)S(1)}, bf16[6,4096]{1,0:T(8,128)(2,1)S(1)}, u32[]{:S(2)}, u32[]{:S(2)}) collective-permute-start(bf16[6,4096]{1,0:T(8,128)(2,1)S(1)} %flatten.1), channel_id=1, source_target_pairs={{0,48},{8,56},{16,64},{24,72},{32,80},{40,88},{48,96},{56,104},{64... | collective-permute-start | bytes 147464 | tf_op jit(solution)/shard_map/ppermute | solution.py:40
  10.7 10.5 %collective-permute-start.2 = (bf16[6,4096]{1,0:T(8,128)(2,1)S(1)}, bf16[6,4096]{1,0:T(8,128)(2,1)S(1)}, u32[]{:S(2)}, u32[]{:S(2)}) collective-permute-start(bf16[6,4096]{1,0:T(8,128)(2,1)S(1)} %flatten.1), channel_id=1, source_target_pairs={{0,80},{8,88},{16,96},{24,104},{32,112},{40,120},{48,0},{56,8},{64... | collective-permute-start | bytes 147464 | tf_op jit(solution)/shard_map/ppermute | solution.py:40
  13.8 7.7 %collective-permute-start.3 = (bf16[6,4096]{1,0:T(8,128)(2,1)S(1)}, bf16[6,4096]{1,0:T(8,128)(2,1)S(1)}, u32[]{:S(2)}, u32[]{:S(2)}) collective-permute-start(bf16[6,4096]{1,0:T(8,128)(2,1)S(1)} %flatten.1), channel_id=1, source_target_pairs={{0,32},{8,40},{16,48},{24,56},{32,64},{40,72},{48,80},{56,88},{64,... | collective-permute-start | bytes 147464 | tf_op jit(solution)/shard_map/ppermute | solution.py:40
  15.2 7.0 %collective-permute-start.4 = (bf16[6,4096]{1,0:T(8,128)(2,1)S(1)}, bf16[6,4096]{1,0:T(8,128)(2,1)S(1)}, u32[]{:S(2)}, u32[]{:S(2)}) collective-permute-start(bf16[6,4096]{1,0:T(8,128)(2,1)S(1)} %flatten.1), channel_id=1, source_target_pairs={{0,96},{8,104},{16,112},{24,120},{32,0},{40,8},{48,16},{56,24},{64... | collective-permute-start | bytes 147464 | tf_op jit(solution)/shard_map/ppermute | solution.py:40
  17.9 5.5 %collective-permute-start.5 = (bf16[6,4096]{1,0:T(8,128)(2,1)S(1)}, bf16[6,4096]{1,0:T(8,128)(2,1)S(1)}, u32[]{:S(2)}, u32[]{:S(2)}) collective-permute-start(bf16[6,4096]{1,0:T(8,128)(2,1)S(1)} %flatten.1), channel_id=1, source_target_pairs={{0,16},{8,24},{16,32},{24,40},{32,48},{40,56},{48,64},{56,72},{64,... | collective-permute-start | bytes 147464 | tf_op jit(solution)/shard_map/ppermute | solution.py:40
  18.9 4.6 %collective-permute-start.6 = (bf16[6,4096]{1,0:T(8,128)(2,1)S(1)}, bf16[6,4096]{1,0:T(8,128)(2,1)S(1)}, u32[]{:S(2)}, u32[]{:S(2)}) collective-permute-start(bf16[6,4096]{1,0:T(8,128)(2,1)S(1)} %flatten.1), channel_id=1, source_target_pairs={{0,112},{8,120},{16,0},{24,8},{32,16},{40,24},{48,32},{56,40},{64,... | collective-permute-start | bytes 147464 | tf_op jit(solution)/shard_map/ppermute | solution.py:40
  24.5 16.1 %collective-permute-start.7 = (bf16[48,4096]{1,0:T(8,128)(2,1)S(1)}, bf16[48,4096]{1,0:T(8,128)(2,1)}, u32[]{:S(2)}, u32[]{:S(2)}) collective-permute-start(bf16[48,4096]{1,0:T(8,128)(2,1)S(1)} %concatenate.22.refs_0_), channel_id=1, source_target_pairs={{0,8},{8,0},{16,24},{24,16},{32,40},{40,32},{48,56},{56,48},{64,72... | collective-permute-start | bytes 1179656 | tf_op jit(solution)/shard_map/ppermute | solution.py:40
  24.6 18.4 %collective-permute-start.8 = (bf16[48,4096]{1,0:T(8,128)(2,1)S(1)}, bf16[48,4096]{1,0:T(8,128)(2,1)}, u32[]{:S(2)}, u32[]{:S(2)}) collective-permute-start(bf16[48,4096]{1,0:T(8,128)(2,1)S(1)} %concatenate.22.refs_0_), channel_id=1, source_target_pairs={{0,4},{8,140},{16,20},{24,156},{32,36},{40,172},{48,52},{56,188},{... | collective-permute-start | bytes 1179656 | tf_op jit(solution)/shard_map/ppermute | solution.py:40
  26.2 17.0 %collective-permute-start.10 = (bf16[48,4096]{1,0:T(8,128)(2,1)S(1)}, bf16[48,4096]{1,0:T(8,128)(2,1)}, u32[]{:S(2)}, u32[]{:S(2)}) collective-permute-start(bf16[48,4096]{1,0:T(8,128)(2,1)S(1)} %concatenate.22.refs_0_), channel_id=1, source_target_pairs={{0,132},{8,12},{16,148},{24,28},{32,164},{40,44},{48,180},{56,60},... | collective-permute-start | bytes 1179656 | tf_op jit(solution)/shard_map/ppermute | solution.py:40
  43.0 2.0 %collective-permute-start.11 = (bf16[48,4096]{1,0:T(8,128)(2,1)}, bf16[48,4096]{1,0:T(8,128)(2,1)S(1)}, u32[]{:S(2)}, u32[]{:S(2)}) collective-permute-start(bf16[48,4096]{1,0:T(8,128)(2,1)} %collective-permute-done.8.refs_0_), channel_id=1, source_target_pairs={{0,8},{8,0},{16,24},{24,16},{32,40},{40,32},{48,56},{56,48},{64,72... | collective-permute-start | bytes 1179656 | tf_op jit(solution)/shard_map/ppermute | solution.py:40
  43.1 2.5 %collective-permute-start.12 = (bf16[48,4096]{1,0:T(8,128)(2,1)}, bf16[48,4096]{1,0:T(8,128)(2,1)S(1)}, u32[]{:S(2)}, u32[]{:S(2)}) collective-permute-start(bf16[48,4096]{1,0:T(8,128)(2,1)} %collective-permute-done.10.refs_1_), channel_id=1, source_target_pairs={{0,8},{8,0},{16,24},{24,16},{32,40},{40,32},{48,56},{56,48},{64,72... | collective-permute-start | bytes 1179656 | tf_op jit(solution)/shard_map/ppermute | solution.py:40
  43.6 9.2 %collective-permute-start.9 = (bf16[48,4096]{1,0:T(8,128)(2,1)}, bf16[48,4096]{1,0:T(8,128)(2,1)S(1)}, u32[]{:S(2)}, u32[]{:S(2)}) collective-permute-start(bf16[48,4096]{1,0:T(8,128)(2,1)} %collective-permute-done.8.refs_0_), channel_id=1, source_target_pairs={{0,132},{8,12},{16,148},{24,28},{32,164},{40,44},{48,180},{56,60},... | collective-permute-start | bytes 1179656 | tf_op jit(solution)/shard_map/ppermute | solution.py:40
  52.8 1.7 %collective-permute-start.13 = (bf16[48,4096]{1,0:T(8,128)(2,1)S(1)}, bf16[48,4096]{1,0:T(8,128)(2,1)S(1)}, u32[]{:S(2)}, u32[]{:S(2)}) collective-permute-start(bf16[48,4096]{1,0:T(8,128)(2,1)S(1)} %collective-permute-done.9.refs_0_.refs_2_), channel_id=1, source_target_pairs={{0,8},{8,0},{16,24},{24,16},{32,40},{40,32},{48,56},{56,48},{64,72... | collective-permute-start | bytes 1179656 | tf_op jit(solution)/shard_map/ppermute | solution.py:40
  61.5 1.8 %collective-permute-start.15 = (bf16[48,4096]{1,0:T(8,128)(2,1)S(1)}, bf16[48,4096]{1,0:T(8,128)(2,1)S(1)}, u32[]{:S(2)}, u32[]{:S(2)}) collective-permute-start(bf16[48,4096]{1,0:T(8,128)(2,1)S(1)} %get-tuple-element.52), channel_id=1, source_target_pairs={{0,8},{8,0},{16,24},{24,16},{32,40},{40,32},{48,56},{56,48},{64,72... | collective-permute-start | bytes 1179656 | tf_op jit(solution)/shard_map/ppermute | solution.py:40
  65.3 2.5 %collective-permute-start.16 = (bf16[48,4096]{1,0:T(8,128)(2,1)S(1)}, bf16[48,4096]{1,0:T(8,128)(2,1)S(1)}, u32[]{:S(2)}, u32[]{:S(2)}) collective-permute-start(bf16[48,4096]{1,0:T(8,128)(2,1)S(1)} %get-tuple-element.56), channel_id=1, source_target_pairs={{0,8},{8,0},{16,24},{24,16},{32,40},{40,32},{48,56},{56,48},{64,72... | collective-permute-start | bytes 1179656 | tf_op jit(solution)/shard_map/ppermute | solution.py:40
  65.6 4.6 %collective-permute-start.21 = (bf16[192,32]{1,0:T(8,128)(2,1)S(1)}, bf16[192,32]{1,0:T(8,128)(2,1)S(1)}, u32[]{:S(2)}, u32[]{:S(2)}) collective-permute-start(bf16[192,32]{1,0:T(8,128)(2,1)S(1)} %get-tuple-element.59.mine_ref), channel_id=1, source_target_pairs={{0,4},{4,0},{1,5},{5,1},{2,6},{6,2},{3,7},{7,3},{8,12},{12,8},{9,1... | collective-permute-start | bytes 36872 | tf_op jit(solution)/shard_map/ppermute | solution.py:424
  65.6 15.1 %collective-permute-start.14 = (bf16[48,4096]{1,0:T(8,128)(2,1)S(1)}, bf16[48,4096]{1,0:T(8,128)(2,1)S(1)}, u32[]{:S(2)}, u32[]{:S(2)}) collective-permute-start(bf16[48,4096]{1,0:T(8,128)(2,1)S(1)} %get-tuple-element.49), channel_id=1, source_target_pairs={{0,8},{8,0},{16,24},{24,16},{32,40},{40,32},{48,56},{56,48},{64,72... | collective-permute-start | bytes 1179656 | tf_op jit(solution)/shard_map/ppermute | solution.py:40
  66.0 9.0 %collective-permute-start.19 = (bf16[48,4096]{1,0:T(8,128)(2,1)S(1)}, bf16[48,4096]{1,0:T(8,128)(2,1)S(1)}, u32[]{:S(2)}, u32[]{:S(2)}) collective-permute-start(bf16[48,4096]{1,0:T(8,128)(2,1)S(1)} %add_convert_fusion.2), channel_id=1, source_target_pairs={{0,132},{8,12},{16,148},{24,28},{32,164},{40,44},{48,180},{56,60},... | collective-permute-start | bytes 1179656 | tf_op jit(solution)/shard_map/ppermute | solution.py:40
  67.1 5.9 %collective-permute-start.18 = (bf16[48,4096]{1,0:T(8,128)(2,1)S(1)}, bf16[48,4096]{1,0:T(8,128)(2,1)S(1)}, u32[]{:S(2)}, u32[]{:S(2)}) collective-permute-start(bf16[48,4096]{1,0:T(8,128)(2,1)S(1)} %get-tuple-element.58), channel_id=1, source_target_pairs={{0,8},{8,0},{16,24},{24,16},{32,40},{40,32},{48,56},{56,48},{64,72... | collective-permute-start | bytes 1179656 | tf_op jit(solution)/shard_map/ppermute | solution.py:40
  67.9 12.4 %collective-permute-start.17 = (bf16[48,4096]{1,0:T(8,128)(2,1)S(1)}, bf16[48,4096]{1,0:T(8,128)(2,1)S(1)}, u32[]{:S(2)}, u32[]{:S(2)}) collective-permute-start(bf16[48,4096]{1,0:T(8,128)(2,1)S(1)} %add_convert_fusion.1), channel_id=1, source_target_pairs={{0,132},{8,12},{16,148},{24,28},{32,164},{40,44},{48,180},{56,60},... | collective-permute-start | bytes 1179656 | tf_op jit(solution)/shard_map/ppermute | solution.py:40
  71.9 7.6 %collective-permute-start.22 = (bf16[32,4352]{1,0:T(8,128)(2,1)S(1)}, bf16[32,4352]{1,0:T(8,128)(2,1)S(1)}, u32[]{:S(2)}, u32[]{:S(2)}) collective-permute-start(bf16[32,4352]{1,0:T(8,128)(2,1)S(1)} %pad_maximum_fusion.1), channel_id=1, source_target_pairs={{0,1},{1,0},{2,3},{3,2},{4,5},{5,4},{6,7},{7,6},{8,9},{9,8},{10,11... | collective-permute-start | bytes 835592 | tf_op jit(solution)/shard_map/ppermute | solution.py:441
  75.1 7.9 %collective-permute-start.20 = (bf16[48,4096]{1,0:T(8,128)(2,1)S(1)}, bf16[48,4096]{1,0:T(8,128)(2,1)S(1)}, u32[]{:S(2)}, u32[]{:S(2)}) collective-permute-start(bf16[48,4096]{1,0:T(8,128)(2,1)S(1)} %add_convert_fusion), channel_id=1, source_target_pairs={{0,4},{8,140},{16,20},{24,156},{32,36},{40,172},{48,52},{56,188},{... | collective-permute-start | bytes 1179656 | tf_op jit(solution)/shard_map/ppermute | solution.py:40
  80.4 7.8 %collective-permute-start.23 = (bf16[32,4352]{1,0:T(8,128)(2,1)S(1)}, bf16[32,4352]{1,0:T(8,128)(2,1)S(1)}, u32[]{:S(2)}, u32[]{:S(2)}) collective-permute-start(bf16[32,4352]{1,0:T(8,128)(2,1)S(1)} %add_convert_fusion.4), channel_id=1, source_target_pairs={{0,3},{1,2},{2,1},{3,0},{4,7},{5,6},{6,5},{7,4},{8,11},{9,10},{10,... | collective-permute-start | bytes 835592 | tf_op jit(solution)/shard_map/ppermute | solution.py:445
  88.3 21.8 %collective-permute-start.31 = (bf16[32,4352]{1,0:T(8,128)(2,1)S(1)}, bf16[32,4352]{1,0:T(8,128)(2,1)S(1)}, u32[]{:S(2)}, u32[]{:S(2)}) collective-permute-start(bf16[32,4352]{1,0:T(8,128)(2,1)S(1)} %add_convert_fusion.3), channel_id=1, source_target_pairs={{0,4},{4,0},{1,5},{5,1},{2,6},{6,2},{3,7},{7,3},{8,12},{12,8},{9,1... | collective-permute-start | bytes 835592 | tf_op jit(solution)/shard_map/ppermute | solution.py:450
  89.6 9.2 %collective-permute-start.24 = (bf16[6,4096]{1,0:T(8,128)(2,1)S(1)}, bf16[6,4096]{1,0:T(8,128)(2,1)S(1)}, u32[]{:S(2)}, u32[]{:S(2)}) collective-permute-start(bf16[6,4096]{1,0:T(8,128)(2,1)S(1)} %get-tuple-element.75), channel_id=1, source_target_pairs={{0,64},{8,72},{16,80},{24,88},{32,96},{40,104},{48,112},{56,120},{... | collective-permute-start | bytes 147464 | tf_op jit(solution)/shard_map/ppermute | solution.py:40
  92.9 8.5 %collective-permute-start.25 = (bf16[6,4096]{1,0:T(8,128)(2,1)S(1)}, bf16[6,4096]{1,0:T(8,128)(2,1)S(1)}, u32[]{:S(2)}, u32[]{:S(2)}) collective-permute-start(bf16[6,4096]{1,0:T(8,128)(2,1)S(1)} %get-tuple-element.74), channel_id=1, source_target_pairs={{0,80},{8,88},{16,96},{24,104},{32,112},{40,120},{48,0},{56,8},{64... | collective-permute-start | bytes 147464 | tf_op jit(solution)/shard_map/ppermute | solution.py:40
  94.3 9.6 %collective-permute-start.26 = (bf16[6,4096]{1,0:T(8,128)(2,1)S(1)}, bf16[6,4096]{1,0:T(8,128)(2,1)S(1)}, u32[]{:S(2)}, u32[]{:S(2)}) collective-permute-start(bf16[6,4096]{1,0:T(8,128)(2,1)S(1)} %get-tuple-element.73), channel_id=1, source_target_pairs={{0,48},{8,56},{16,64},{24,72},{32,80},{40,88},{48,96},{56,104},{64... | collective-permute-start | bytes 147464 | tf_op jit(solution)/shard_map/ppermute | solution.py:40
  96.7 7.3 %collective-permute-start.27 = (bf16[6,4096]{1,0:T(8,128)(2,1)S(1)}, bf16[6,4096]{1,0:T(8,128)(2,1)S(1)}, u32[]{:S(2)}, u32[]{:S(2)}) collective-permute-start(bf16[6,4096]{1,0:T(8,128)(2,1)S(1)} %get-tuple-element.72), channel_id=1, source_target_pairs={{0,96},{8,104},{16,112},{24,120},{32,0},{40,8},{48,16},{56,24},{64... | collective-permute-start | bytes 147464 | tf_op jit(solution)/shard_map/ppermute | solution.py:40
  98.8 6.7 %collective-permute-start.28 = (bf16[6,4096]{1,0:T(8,128)(2,1)S(1)}, bf16[6,4096]{1,0:T(8,128)(2,1)S(1)}, u32[]{:S(2)}, u32[]{:S(2)}) collective-permute-start(bf16[6,4096]{1,0:T(8,128)(2,1)S(1)} %get-tuple-element.71), channel_id=1, source_target_pairs={{0,32},{8,40},{16,48},{24,56},{32,64},{40,72},{48,80},{56,88},{64,... | collective-permute-start | bytes 147464 | tf_op jit(solution)/shard_map/ppermute | solution.py:40
  101.4 4.8 %collective-permute-start.29 = (bf16[6,4096]{1,0:T(8,128)(2,1)S(1)}, bf16[6,4096]{1,0:T(8,128)(2,1)S(1)}, u32[]{:S(2)}, u32[]{:S(2)}) collective-permute-start(bf16[6,4096]{1,0:T(8,128)(2,1)S(1)} %get-tuple-element.70), channel_id=1, source_target_pairs={{0,112},{8,120},{16,0},{24,8},{32,16},{40,24},{48,32},{56,40},{64,... | collective-permute-start | bytes 147464 | tf_op jit(solution)/shard_map/ppermute | solution.py:40
  103.9 5.5 %collective-permute-start.30 = (bf16[6,4096]{1,0:T(8,128)(2,1)S(1)}, bf16[6,4096]{1,0:T(8,128)(2,1)S(1)}, u32[]{:S(2)}, u32[]{:S(2)}) collective-permute-start(bf16[6,4096]{1,0:T(8,128)(2,1)S(1)} %get-tuple-element.69), channel_id=1, source_target_pairs={{0,16},{8,24},{16,32},{24,40},{32,48},{40,56},{48,64},{56,72},{64,... | collective-permute-start | bytes 147464 | tf_op jit(solution)/shard_map/ppermute | solution.py:40
  (9 other events, 16.8 us)

commit v6 on v5

--- a/solution.py
+++ b/solution.py
@@ -34,6 +34,7 @@
 TENSOR_SWAP = [(0, 1), (1, 0)]
 DP_NEAR = [(i, i ^ 1) for i in range(4)]
 DP_FAR = [(i, 3 - i) for i in range(4)]
+DP_ACROSS = [(i, i ^ 2) for i in range(4)]
 
 
 def move(block, pairs):
@@ -379,7 +380,7 @@
     first = move(base, NEAR)
     second = move(base, FAR)
     base_there = move(base, SIBLING)
-    late_side = after(side, base)
+    late_side = after(side, base_there)
     late_section = after(section, base)
     up_maps = lax.dynamic_slice_in_dim(adapter_up_maps[0], late_side * width, width, 2)
     up_diagonal = jnp.concatenate(
@@ -398,9 +399,9 @@
     pair = pair_queries(
         after(queries[0], base), context_gradient[0], gains, width // gains.shape[1]
     )
-    weights = hold(weights, after(pair, up_diagonal, *maps))
     step_a = project([base, base_there], weights, down_maps, here)
     first = after(first, pair, *step_a, up_diagonal, *maps)
+    weights = hold(weights, first)
     third = move(first, FAR)
     first_there = move(first, SIBLING)
     second_there = move(second, SIBLING)
@@ -438,20 +439,19 @@
     second_in = move(second, FAR)
     down_own = down_grad(maps[2], middle, after(middle_facing, second), owns)
     sums = jnp.concatenate([down_own, up_part], 1).astype(LOW)
-    near_sums = lax.ppermute(sums, "dp", DP_NEAR)
+    near_sums, far_sums, across_sums = (
+        lax.ppermute(sums, "dp", pairs) for pairs in (DP_NEAR, DP_FAR, DP_ACROSS)
+    )
     first = (first + third_in.astype(F32)).astype(LOW)
     first_in = move(first, NEAR)
-    sums = add(sums, after(near_sums, second_in, first)).astype(LOW)
-    far_sums = lax.ppermute(sums, "dp", DP_FAR)
     base = base + second_in.astype(F32) + first_in.astype(F32)
     low_base = base.astype(LOW)
-    sums = add(sums, after(far_sums, low_base)).astype(LOW)
-    low_base = after(low_base, sums)
-    facing = lax.ppermute(sums, "tensor", TENSOR_SWAP)
     count = own.shape[0]
     arrived = [
         move(low_base[i * count : (i + 1) * count], ALONG[NZ - k]) for i, k in enumerate(SHIFTS)
     ]
+    sums = (add(sums, after(near_sums, *arrived[:3])) + add(far_sums, across_sums)).astype(LOW)
+    facing = lax.ppermute(sums, "tensor", TENSOR_SWAP)
     own_grad = total(base[len(SHIFTS) * count :], arrived, vision_feature_states.shape)
 
     left = jnp.where(side == 0, sums, facing).astype(F32)

time: 113 us -> 109 us (0.965)
  waiting for transfers between devices: 33.4 us -> 27 us
  starting transfers between devices: 44.7 us -> 49.3 us
  Pallas kernels: 17.6 us -> 14.7 us
  local copies, waits for them, and re-layouts: 11.5 us -> 14.3 us
    ppermute x2 -> x3, waiting for transfers between devices: 8.89 us -> 0.01 us  [per_device(): lax.ppermute(sums, 'dp', pairs)]
    unnamed x18 -> x26, local copies, waits for them, and re-layouts: 8.1 us -> 12.7 us
    ppermute x2 -> x3, starting transfers between devices: 1.37 us -> 4.18 us  [per_device(): lax.ppermute(sums, 'dp', pairs)]
    ppermute x28, waiting for transfers between devices: 23.8 us -> 26.3 us  [move(): return lax.ppermute(block, PLANE, pairs)]
    ppermute x28, starting transfers between devices: 42.1 us -> 44.5 us  [move(): return lax.ppermute(block, PLANE, pairs)]
    pallas_call x3, Pallas kernels: 5.39 us -> 3.35 us  [project(): pl.pallas_call(project_kernel, out_shape=[jax.ShapeDtypeStruct((2, count,...]
    concatenate x2, local copies, waits for them, and re-layouts: 1.72 us -> 0.58 us  [row_tokens(): return (jnp.concatenate(own_half), jnp.concatenate(other_half))]
  transfers between devices with their start and end apart: 32 -> 33, of which waited for: 20 -> 15; matrix products, arithmetic and copies ran while one was open for 4% -> 1% of each run, Pallas kernels for 8% -> 5%
where the time goes in v6:
time: 109 us
  starting transfers between devices  49.3 us (45%)
  waiting for transfers between devices  27 us (25%)
  Pallas kernels  14.7 us (13%)
  local copies, waits for them, and re-layouts  14.3 us (13%)
  other arithmetic  2.62 us (2%)
    ppermute x28, starting transfers between devices, move(): return lax.ppermute(block, PLANE, pairs)  44.5 us
    ppermute x28, waiting for transfers between devices, move(): return lax.ppermute(block, PLANE, pairs)  26.3 us
    unnamed x26, local copies, waits for them, and re-layouts  12.7 us
    ppermute x3, starting transfers between devices, per_device(): lax.ppermute(sums, 'dp', pairs)  4.18 us
    pallas_call x1, Pallas kernels, attend(): pl.pallas_call(attention_kernel, out_shape=[jax.ShapeDtypeStruct((rows, 2...  4.06 us
    pallas_call x2, Pallas kernels, feature_grad(): pl.pallas_call(feature_kernel, out_shape=[jax.ShapeDtypeStruct((rows // 4...  3.85 us
    pallas_call x3, Pallas kernels, project(): pl.pallas_call(project_kernel, out_shape=[jax.ShapeDtypeStruct((2, count,...  3.35 us
  transfers between devices with their start and end apart: 33, of which 15 were waited for; matrix products, arithmetic and copies ran while one was open for 1% of the time, Pallas kernels for 5%

profile of v6, /device:TPU:24, one launch (start us, length us, event | category | flops | bytes accessed | tf_op | source)
XLA Modules:
  0.0 108.8 jit_solution(15342053896603534260)
XLA Ops:
  1.5 7.3 %collective-permute-start = (bf16[6,4096]{1,0:T(8,128)(2,1)S(1)}, bf16[6,4096]{1,0:T(8,128)(2,1)S(1)}, u32[]{:S(2)}, u32[]{:S(2)}) collective-permute-start(bf16[6,4096]{1,0:T(8,128)(2,1)S(1)} %flatten.1), channel_id=1, source_target_pairs={{0,64},{8,72},{16,80},{24,88},{32,96},{40,104},{48,112},{56,120},{... | collective-permute-start | bytes 147464 | tf_op jit(solution)/shard_map/ppermute | solution.py:41
  8.7 1.9 %collective-permute-start.1 = (bf16[6,4096]{1,0:T(8,128)(2,1)S(1)}, bf16[6,4096]{1,0:T(8,128)(2,1)S(1)}, u32[]{:S(2)}, u32[]{:S(2)}) collective-permute-start(bf16[6,4096]{1,0:T(8,128)(2,1)S(1)} %flatten.1), channel_id=1, source_target_pairs={{0,48},{8,56},{16,64},{24,72},{32,80},{40,88},{48,96},{56,104},{64... | collective-permute-start | bytes 147464 | tf_op jit(solution)/shard_map/ppermute | solution.py:41
  10.7 3.1 %collective-permute-start.2 = (bf16[6,4096]{1,0:T(8,128)(2,1)S(1)}, bf16[6,4096]{1,0:T(8,128)(2,1)S(1)}, u32[]{:S(2)}, u32[]{:S(2)}) collective-permute-start(bf16[6,4096]{1,0:T(8,128)(2,1)S(1)} %flatten.1), channel_id=1, source_target_pairs={{0,80},{8,88},{16,96},{24,104},{32,112},{40,120},{48,0},{56,8},{64... | collective-permute-start | bytes 147464 | tf_op jit(solution)/shard_map/ppermute | solution.py:41
  13.8 1.5 %collective-permute-start.3 = (bf16[6,4096]{1,0:T(8,128)(2,1)S(1)}, bf16[6,4096]{1,0:T(8,128)(2,1)S(1)}, u32[]{:S(2)}, u32[]{:S(2)}) collective-permute-start(bf16[6,4096]{1,0:T(8,128)(2,1)S(1)} %flatten.1), channel_id=1, source_target_pairs={{0,32},{8,40},{16,48},{24,56},{32,64},{40,72},{48,80},{56,88},{64,... | collective-permute-start | bytes 147464 | tf_op jit(solution)/shard_map/ppermute | solution.py:41
  15.2 2.7 %collective-permute-start.4 = (bf16[6,4096]{1,0:T(8,128)(2,1)S(1)}, bf16[6,4096]{1,0:T(8,128)(2,1)S(1)}, u32[]{:S(2)}, u32[]{:S(2)}) collective-permute-start(bf16[6,4096]{1,0:T(8,128)(2,1)S(1)} %flatten.1), channel_id=1, source_target_pairs={{0,96},{8,104},{16,112},{24,120},{32,0},{40,8},{48,16},{56,24},{64... | collective-permute-start | bytes 147464 | tf_op jit(solution)/shard_map/ppermute | solution.py:41
  18.9 2.2 %collective-permute-start.6 = (bf16[6,4096]{1,0:T(8,128)(2,1)S(1)}, bf16[6,4096]{1,0:T(8,128)(2,1)S(1)}, u32[]{:S(2)}, u32[]{:S(2)}) collective-permute-start(bf16[6,4096]{1,0:T(8,128)(2,1)S(1)} %flatten.1), channel_id=1, source_target_pairs={{0,112},{8,120},{16,0},{24,8},{32,16},{40,24},{48,32},{56,40},{64,... | collective-permute-start | bytes 147464 | tf_op jit(solution)/shard_map/ppermute | solution.py:41
  24.4 1.6 %collective-permute-start.8 = (bf16[48,4096]{1,0:T(8,128)(2,1)S(1)}, bf16[48,4096]{1,0:T(8,128)(2,1)S(1)}, u32[]{:S(2)}, u32[]{:S(2)}) collective-permute-start(bf16[48,4096]{1,0:T(8,128)(2,1)S(1)} %concatenate.22.refs_0_), channel_id=1, source_target_pairs={{0,4},{8,140},{16,20},{24,156},{32,36},{40,172},{48,52},{56,188},{... | collective-permute-start | bytes 1179656 | tf_op jit(solution)/shard_map/ppermute | solution.py:41
  26.0 2.1 %collective-permute-start.10 = (bf16[48,4096]{1,0:T(8,128)(2,1)S(1)}, bf16[48,4096]{1,0:T(8,128)(2,1)S(1)}, u32[]{:S(2)}, u32[]{:S(2)}) collective-permute-start(bf16[48,4096]{1,0:T(8,128)(2,1)S(1)} %concatenate.22.refs_0_), channel_id=1, source_target_pairs={{0,132},{8,12},{16,148},{24,28},{32,164},{40,44},{48,180},{56,60},... | collective-permute-start | bytes 1179656 | tf_op jit(solution)/shard_map/ppermute | solution.py:41
  28.1 1.4 %copy-done.5 = bf16[1,3,128,2048]{3,2,1,0:T(8,128)(2,1)S(1)} copy-done((bf16[1,3,128,2048]{3,2,1,0:T(8,128)(2,1)S(1)}, bf16[1,3,128,2048]{3,2,1,0:T(8,128)(2,1)}, u32[]{:S(2)}) %copy-start.5) | copy-done | bytes 1572888
  29.5 1.4 %copy-done.6 = bf16[1,3,128,2048]{3,2,1,0:T(8,128)(2,1)S(1)} copy-done((bf16[1,3,128,2048]{3,2,1,0:T(8,128)(2,1)S(1)}, bf16[1,3,128,2048]{3,2,1,0:T(8,128)(2,1)}, u32[]{:S(2)}) %copy-start.6) | copy-done | bytes 1572888
  31.6 1.4 %pair_queries.1.pair_ref = bf16[6,1024,256]{2,1,0:T(8,128)(2,1)S(1)} custom-call(bf16[2,128]{1,0:T(2,128)(2,1)S(1)} %bitcast.405, bf16[3,128,2048]{2,1,0:T(8,128)(2,1)S(1)} %bitcast.403, bf16[3,128,2048]{2,1,0:T(8,128)(2,1)S(1)} %bitcast.404), custom_call_target="tpu_custom_call" | custom-call | flops 200000 | bytes 6291 | tf_op jit(solution)/shard_map/pair_queries/pallas_call | solution.py:86
  33.0 1.6 %copy-done.3 = bf16[6,1024,256]{2,1,0:T(8,128)(2,1)} copy-done((bf16[6,1024,256]{2,1,0:T(8,128)(2,1)}, bf16[6,1024,256]{2,1,0:T(8,128)(2,1)S(1)}, u32[]{:S(2)}) %copy-start.3) | copy-done | bytes 3145752
  35.3 3.4 %copy-done = bf16[1,2,8192,256]{3,2,1,0:T(8,128)(2,1)S(1)} copy-done((bf16[1,2,8192,256]{3,2,1,0:T(8,128)(2,1)S(1)}, bf16[1,2,8192,256]{3,2,1,0:T(8,128)(2,1)}, u32[]{:S(2)}) %copy-start) | copy-done | bytes 8388632
  41.5 3.4 %copy-done.1 = bf16[1,2,8192,256]{3,2,1,0:T(8,128)(2,1)S(1)} copy-done((bf16[1,2,8192,256]{3,2,1,0:T(8,128)(2,1)S(1)}, bf16[1,2,8192,256]{3,2,1,0:T(8,128)(2,1)}, u32[]{:S(2)}) %copy-start.1) | copy-done | bytes 8388632
  45.5 1.4 %project.4 = (f32[2,192,256]{2,1,0:T(8,128)S(1)}, f32[192,32]{1,0:T(8,128)S(1)}) custom-call(s32[1]{0:T(128)S(6)} %sub.44.which_ref, bf16[48,4096]{1,0:T(8,128)(2,1)S(1)} %collective-permute-done.8.ready_ref.refs_0_, bf16[48,4096]{1,0:T(8,128)(2,1)S(1)} %collective-permute-done.10.refs_1_, bf16[48,4096]{1,0:T(8,128)(2,1)S(1)} %collective-permute-done.11.refs_2_, ...), custom_call_target="tpu_custom_call" | custom-call | flops 805306 | bytes 5767 | tf_op jit(solution)/shard_map/project/pallas_call | solution.py:176
  46.9 2.5 %collective-permute-done.9.refs_0_.refs_2_ = bf16[48,4096]{1,0:T(8,128)(2,1)S(1)} collective-permute-done((bf16[48,4096]{1,0:T(8,128)(2,1)S(1)}, bf16[48,4096]{1,0:T(8,128)(2,1)S(1)}, u32[]{:S(2)}, u32[]{:S(2)}) %collective-permute-start.9) | collective-permute-done | bytes 393248 | tf_op jit(solution)/shard_map/ppermute | solution.py:41
  49.4 1.7 %collective-permute-done.13.refs_1_.refs_3_ = bf16[48,4096]{1,0:T(8,128)(2,1)S(1)} collective-permute-done((bf16[48,4096]{1,0:T(8,128)(2,1)S(1)}, bf16[48,4096]{1,0:T(8,128)(2,1)S(1)}, u32[]{:S(2)}, u32[]{:S(2)}) %collective-permute-start.13) | collective-permute-done | bytes 393248 | tf_op jit(solution)/shard_map/ppermute | solution.py:41
  52.2 4.1 %attend.1 = (bf16[192,512]{1,0:T(8,128)(2,1)S(1)}, bf16[192,32]{1,0:T(8,128)(2,1)S(1)}, bf16[192,512]{1,0:T(8,128)(2,1)S(1)}, bf16[192,32]{1,0:T(8,128)(2,1)S(1)...) custom-call(s32[3]{0:T(128)S(1)} %copy-done.10, s32[3]{0:T(128)S(1)} %copy-done.11, ...), custom_call_target="tpu_custom_call" | custom-call | flops 1000000 | bytes 3145 | tf_op jit(solution)/shard_map/attend/pallas_call | solution.py:274
  56.2 1.9 %feature_grad.2 = (bf16[48,4096]{1,0:T(8,128)(2,1)S(1)}, bf16[48,4096]{1,0:T(8,128)(2,1)S(1)}, bf16[48,4096]{1,0:T(8,128)(2,1)S(1)}, bf16[48,4096]{1,0:T(8,128)(2,1)S(1)}) custom-call(s32[1]{0:T(128)} %bitcast.which_ref, bf16[192,512]{1,0:T(8,128)(2,1)S(1)} %get-tuple-element.42.g_ref, bf16[192,32]{1,0:T(8,128)(2,1)S(1)} %get-tuple-element.43.m_ref, ...), custom_call_target="tpu_custom_call" | custom-call | flops 805306 | bytes 5767 | tf_op jit(solution)/shard_map/feature_grad/pallas_call | solution.py:308
  58.4 1.6 %collective-permute-done.15 = bf16[48,4096]{1,0:T(8,128)(2,1)S(1)} collective-permute-done((bf16[48,4096]{1,0:T(8,128)(2,1)S(1)}, bf16[48,4096]{1,0:T(8,128)(2,1)S(1)}, u32[]{:S(2)}, u32[]{:S(2)}) %collective-permute-start.15) | collective-permute-done | bytes 393248 | tf_op jit(solution)/shard_map/ppermute | solution.py:41
  60.1 1.9 %feature_grad.3 = (bf16[48,4096]{1,0:T(8,128)(2,1)S(1)}, bf16[48,4096]{1,0:T(8,128)(2,1)S(1)}, bf16[48,4096]{1,0:T(8,128)(2,1)S(1)}, bf16[48,4096]{1,0:T(8,128)(2,1)S(1)}) custom-call(s32[1]{0:T(128)S(6)} %sub.44.which_ref, bf16[192,512]{1,0:T(8,128)(2,1)S(1)} %get-tuple-element.49.g_ref, bf16[192,32]{1,0:T(8,128)(2,1)S(1)} %get-tuple-element.50.m_ref, ...), custom_call_target="tpu_custom_call" | custom-call | flops 805306 | bytes 5767 | tf_op jit(solution)/shard_map/feature_grad/pallas_call | solution.py:308
  64.6 1.4 %collective-permute-start.17 = (bf16[48,4096]{1,0:T(8,128)(2,1)S(1)}, bf16[48,4096]{1,0:T(8,128)(2,1)S(1)}, u32[]{:S(2)}, u32[]{:S(2)}) collective-permute-start(bf16[48,4096]{1,0:T(8,128)(2,1)S(1)} %add_convert_fusion.1), channel_id=1, source_target_pairs={{0,132},{8,12},{16,148},{24,28},{32,164},{40,44},{48,180},{56,60},... | collective-permute-start | bytes 1179656 | tf_op jit(solution)/shard_map/ppermute | solution.py:41
  67.6 4.0 %collective-permute-done.19 = bf16[48,4096]{1,0:T(8,128)(2,1)S(1)} collective-permute-done((bf16[48,4096]{1,0:T(8,128)(2,1)S(1)}, bf16[48,4096]{1,0:T(8,128)(2,1)S(1)}, u32[]{:S(2)}, u32[]{:S(2)}) %collective-permute-start.19) | collective-permute-done | bytes 393248 | tf_op jit(solution)/shard_map/ppermute | solution.py:41
  74.5 2.3 %collective-permute-start.31 = (bf16[32,4352]{1,0:T(8,128)(2,1)S(1)}, bf16[32,4352]{1,0:T(8,128)(2,1)S(1)}, u32[]{:S(2)}, u32[]{:S(2)}) collective-permute-start(bf16[32,4352]{1,0:T(8,128)(2,1)S(1)} %pad_maximum_fusion.1), channel_id=1, source_target_pairs={{0,2},{1,3},{2,0},{3,1},{4,6},{5,7},{6,4},{7,5},{8,10},{9,11},{10,... | collective-permute-start | bytes 835592 | tf_op jit(solution)/shard_map/ppermute | solution.py:443
  76.8 3.1 %collective-permute-done.20 = bf16[48,4096]{1,0:T(8,128)(2,1)S(1)} collective-permute-done((bf16[48,4096]{1,0:T(8,128)(2,1)S(1)}, bf16[48,4096]{1,0:T(8,128)(2,1)S(1)}, u32[]{:S(2)}, u32[]{:S(2)}) %collective-permute-start.20) | collective-permute-done | bytes 393248 | tf_op jit(solution)/shard_map/ppermute | solution.py:41
  80.2 3.2 %collective-permute-start.21 = (bf16[6,4096]{1,0:T(8,128)(2,1)S(1)}, bf16[6,4096]{1,0:T(8,128)(2,1)S(1)}, u32[]{:S(2)}, u32[]{:S(2)}) collective-permute-start(bf16[6,4096]{1,0:T(8,128)(2,1)S(1)} %get-tuple-element.69), channel_id=1, source_target_pairs={{0,64},{8,72},{16,80},{24,88},{32,96},{40,104},{48,112},{56,120},{... | collective-permute-start | bytes 147464 | tf_op jit(solution)/shard_map/ppermute | solution.py:41
  83.4 1.4 %collective-permute-start.22 = (bf16[6,4096]{1,0:T(8,128)(2,1)S(1)}, bf16[6,4096]{1,0:T(8,128)(2,1)S(1)}, u32[]{:S(2)}, u32[]{:S(2)}) collective-permute-start(bf16[6,4096]{1,0:T(8,128)(2,1)S(1)} %get-tuple-element.68), channel_id=1, source_target_pairs={{0,80},{8,88},{16,96},{24,104},{32,112},{40,120},{48,0},{56,8},{64... | collective-permute-start | bytes 147464 | tf_op jit(solution)/shard_map/ppermute | solution.py:41
  84.8 2.4 %collective-permute-start.23 = (bf16[6,4096]{1,0:T(8,128)(2,1)S(1)}, bf16[6,4096]{1,0:T(8,128)(2,1)S(1)}, u32[]{:S(2)}, u32[]{:S(2)}) collective-permute-start(bf16[6,4096]{1,0:T(8,128)(2,1)S(1)} %get-tuple-element.67), channel_id=1, source_target_pairs={{0,48},{8,56},{16,64},{24,72},{32,80},{40,88},{48,96},{56,104},{64... | collective-permute-start | bytes 147464 | tf_op jit(solution)/shard_map/ppermute | solution.py:41
  88.5 4.5 %collective-permute-done.22.refs_1_ = bf16[6,4096]{1,0:T(8,128)(2,1)S(1)} collective-permute-done((bf16[6,4096]{1,0:T(8,128)(2,1)S(1)}, bf16[6,4096]{1,0:T(8,128)(2,1)S(1)}, u32[]{:S(2)}, u32[]{:S(2)}) %collective-permute-start.22) | collective-permute-done | bytes 49184 | tf_op jit(solution)/shard_map/ppermute | solution.py:41
  94.0 5.1 %collective-permute-start.24 = (bf16[6,4096]{1,0:T(8,128)(2,1)S(1)}, bf16[6,4096]{1,0:T(8,128)(2,1)S(1)}, u32[]{:S(2)}, u32[]{:S(2)}) collective-permute-start(bf16[6,4096]{1,0:T(8,128)(2,1)S(1)} %get-tuple-element.66), channel_id=1, source_target_pairs={{0,96},{8,104},{16,112},{24,120},{32,0},{40,8},{48,16},{56,24},{64... | collective-permute-start | bytes 147464 | tf_op jit(solution)/shard_map/ppermute | solution.py:41
  99.9 1.3 %collective-permute-start.27 = (bf16[6,4096]{1,0:T(8,128)(2,1)S(1)}, bf16[6,4096]{1,0:T(8,128)(2,1)S(1)}, u32[]{:S(2)}, u32[]{:S(2)}) collective-permute-start(bf16[6,4096]{1,0:T(8,128)(2,1)S(1)} %get-tuple-element.63), channel_id=1, source_target_pairs={{0,16},{8,24},{16,32},{24,40},{32,48},{40,56},{48,64},{56,72},{64,... | collective-permute-start | bytes 147464 | tf_op jit(solution)/shard_map/ppermute | solution.py:41
  101.2 4.3 %collective-permute-done.25.refs_4_ = bf16[6,4096]{1,0:T(8,128)(2,1)S(1)} collective-permute-done((bf16[6,4096]{1,0:T(8,128)(2,1)S(1)}, bf16[6,4096]{1,0:T(8,128)(2,1)S(1)}, u32[]{:S(2)}, u32[]{:S(2)}) %collective-permute-start.25) | collective-permute-done | bytes 49184 | tf_op jit(solution)/shard_map/ppermute | solution.py:41
  (94 shorter events, 24.7 us)
Async XLA Ops:
  1.5 16.5 %collective-permute-start = (bf16[6,4096]{1,0:T(8,128)(2,1)S(1)}, bf16[6,4096]{1,0:T(8,128)(2,1)S(1)}, u32[]{:S(2)}, u32[]{:S(2)}) collective-permute-start(bf16[6,4096]{1,0:T(8,128)(2,1)S(1)} %flatten.1), channel_id=1, source_target_pairs={{0,64},{8,72},{16,80},{24,88},{32,96},{40,104},{48,112},{56,120},{... | collective-permute-start | bytes 147464 | tf_op jit(solution)/shard_map/ppermute | solution.py:41
  8.7 10.2 %collective-permute-start.1 = (bf16[6,4096]{1,0:T(8,128)(2,1)S(1)}, bf16[6,4096]{1,0:T(8,128)(2,1)S(1)}, u32[]{:S(2)}, u32[]{:S(2)}) collective-permute-start(bf16[6,4096]{1,0:T(8,128)(2,1)S(1)} %flatten.1), channel_id=1, source_target_pairs={{0,48},{8,56},{16,64},{24,72},{32,80},{40,88},{48,96},{56,104},{64... | collective-permute-start | bytes 147464 | tf_op jit(solution)/shard_map/ppermute | solution.py:41
  10.7 10.5 %collective-permute-start.2 = (bf16[6,4096]{1,0:T(8,128)(2,1)S(1)}, bf16[6,4096]{1,0:T(8,128)(2,1)S(1)}, u32[]{:S(2)}, u32[]{:S(2)}) collective-permute-start(bf16[6,4096]{1,0:T(8,128)(2,1)S(1)} %flatten.1), channel_id=1, source_target_pairs={{0,80},{8,88},{16,96},{24,104},{32,112},{40,120},{48,0},{56,8},{64... | collective-permute-start | bytes 147464 | tf_op jit(solution)/shard_map/ppermute | solution.py:41
  13.8 7.7 %collective-permute-start.3 = (bf16[6,4096]{1,0:T(8,128)(2,1)S(1)}, bf16[6,4096]{1,0:T(8,128)(2,1)S(1)}, u32[]{:S(2)}, u32[]{:S(2)}) collective-permute-start(bf16[6,4096]{1,0:T(8,128)(2,1)S(1)} %flatten.1), channel_id=1, source_target_pairs={{0,32},{8,40},{16,48},{24,56},{32,64},{40,72},{48,80},{56,88},{64,... | collective-permute-start | bytes 147464 | tf_op jit(solution)/shard_map/ppermute | solution.py:41
  15.2 7.0 %collective-permute-start.4 = (bf16[6,4096]{1,0:T(8,128)(2,1)S(1)}, bf16[6,4096]{1,0:T(8,128)(2,1)S(1)}, u32[]{:S(2)}, u32[]{:S(2)}) collective-permute-start(bf16[6,4096]{1,0:T(8,128)(2,1)S(1)} %flatten.1), channel_id=1, source_target_pairs={{0,96},{8,104},{16,112},{24,120},{32,0},{40,8},{48,16},{56,24},{64... | collective-permute-start | bytes 147464 | tf_op jit(solution)/shard_map/ppermute | solution.py:41
  17.9 5.5 %collective-permute-start.5 = (bf16[6,4096]{1,0:T(8,128)(2,1)S(1)}, bf16[6,4096]{1,0:T(8,128)(2,1)S(1)}, u32[]{:S(2)}, u32[]{:S(2)}) collective-permute-start(bf16[6,4096]{1,0:T(8,128)(2,1)S(1)} %flatten.1), channel_id=1, source_target_pairs={{0,16},{8,24},{16,32},{24,40},{32,48},{40,56},{48,64},{56,72},{64,... | collective-permute-start | bytes 147464 | tf_op jit(solution)/shard_map/ppermute | solution.py:41
  18.9 4.6 %collective-permute-start.6 = (bf16[6,4096]{1,0:T(8,128)(2,1)S(1)}, bf16[6,4096]{1,0:T(8,128)(2,1)S(1)}, u32[]{:S(2)}, u32[]{:S(2)}) collective-permute-start(bf16[6,4096]{1,0:T(8,128)(2,1)S(1)} %flatten.1), channel_id=1, source_target_pairs={{0,112},{8,120},{16,0},{24,8},{32,16},{40,24},{48,32},{56,40},{64,... | collective-permute-start | bytes 147464 | tf_op jit(solution)/shard_map/ppermute | solution.py:41
  24.3 11.0 %collective-permute-start.7 = (bf16[48,4096]{1,0:T(8,128)(2,1)S(1)}, bf16[48,4096]{1,0:T(8,128)(2,1)S(1)}, u32[]{:S(2)}, u32[]{:S(2)}) collective-permute-start(bf16[48,4096]{1,0:T(8,128)(2,1)S(1)} %concatenate.22.refs_0_), channel_id=1, source_target_pairs={{0,8},{8,0},{16,24},{24,16},{32,40},{40,32},{48,56},{56,48},{64,72... | collective-permute-start | bytes 1179656 | tf_op jit(solution)/shard_map/ppermute | solution.py:41
  24.4 15.3 %collective-permute-start.8 = (bf16[48,4096]{1,0:T(8,128)(2,1)S(1)}, bf16[48,4096]{1,0:T(8,128)(2,1)S(1)}, u32[]{:S(2)}, u32[]{:S(2)}) collective-permute-start(bf16[48,4096]{1,0:T(8,128)(2,1)S(1)} %concatenate.22.refs_0_), channel_id=1, source_target_pairs={{0,4},{8,140},{16,20},{24,156},{32,36},{40,172},{48,52},{56,188},{... | collective-permute-start | bytes 1179656 | tf_op jit(solution)/shard_map/ppermute | solution.py:41
  26.0 13.8 %collective-permute-start.10 = (bf16[48,4096]{1,0:T(8,128)(2,1)S(1)}, bf16[48,4096]{1,0:T(8,128)(2,1)S(1)}, u32[]{:S(2)}, u32[]{:S(2)}) collective-permute-start(bf16[48,4096]{1,0:T(8,128)(2,1)S(1)} %concatenate.22.refs_0_), channel_id=1, source_target_pairs={{0,132},{8,12},{16,148},{24,28},{32,164},{40,44},{48,180},{56,60},... | collective-permute-start | bytes 1179656 | tf_op jit(solution)/shard_map/ppermute | solution.py:41
  39.7 5.7 %collective-permute-start.11 = (bf16[48,4096]{1,0:T(8,128)(2,1)S(1)}, bf16[48,4096]{1,0:T(8,128)(2,1)S(1)}, u32[]{:S(2)}, u32[]{:S(2)}) collective-permute-start(bf16[48,4096]{1,0:T(8,128)(2,1)S(1)} %collective-permute-done.8.ready_ref.refs_0_), channel_id=1, source_target_pairs={{0,8},{8,0},{16,24},{24,16},{32,40},{40,32},{48,56},{56,48},{64,72... | collective-permute-start | bytes 1179656 | tf_op jit(solution)/shard_map/ppermute | solution.py:41
  39.9 5.6 %collective-permute-start.12 = (bf16[48,4096]{1,0:T(8,128)(2,1)S(1)}, bf16[48,4096]{1,0:T(8,128)(2,1)S(1)}, u32[]{:S(2)}, u32[]{:S(2)}) collective-permute-start(bf16[48,4096]{1,0:T(8,128)(2,1)S(1)} %collective-permute-done.10.refs_1_), channel_id=1, source_target_pairs={{0,8},{8,0},{16,24},{24,16},{32,40},{40,32},{48,56},{56,48},{64,72... | collective-permute-start | bytes 1179656 | tf_op jit(solution)/shard_map/ppermute | solution.py:41
  40.3 9.0 %collective-permute-start.9 = (bf16[48,4096]{1,0:T(8,128)(2,1)S(1)}, bf16[48,4096]{1,0:T(8,128)(2,1)S(1)}, u32[]{:S(2)}, u32[]{:S(2)}) collective-permute-start(bf16[48,4096]{1,0:T(8,128)(2,1)S(1)} %collective-permute-done.8.ready_ref.refs_0_), channel_id=1, source_target_pairs={{0,132},{8,12},{16,148},{24,28},{32,164},{40,44},{48,180},{56,60},... | collective-permute-start | bytes 1179656 | tf_op jit(solution)/shard_map/ppermute | solution.py:41
  49.3 1.8 %collective-permute-start.13 = (bf16[48,4096]{1,0:T(8,128)(2,1)S(1)}, bf16[48,4096]{1,0:T(8,128)(2,1)S(1)}, u32[]{:S(2)}, u32[]{:S(2)}) collective-permute-start(bf16[48,4096]{1,0:T(8,128)(2,1)S(1)} %collective-permute-done.9.refs_0_.refs_2_), channel_id=1, source_target_pairs={{0,8},{8,0},{16,24},{24,16},{32,40},{40,32},{48,56},{56,48},{64,72... | collective-permute-start | bytes 1179656 | tf_op jit(solution)/shard_map/ppermute | solution.py:41
  62.0 2.5 %collective-permute-start.16 = (bf16[48,4096]{1,0:T(8,128)(2,1)S(1)}, bf16[48,4096]{1,0:T(8,128)(2,1)S(1)}, u32[]{:S(2)}, u32[]{:S(2)}) collective-permute-start(bf16[48,4096]{1,0:T(8,128)(2,1)S(1)} %get-tuple-element.52), channel_id=1, source_target_pairs={{0,8},{8,0},{16,24},{24,16},{32,40},{40,32},{48,56},{56,48},{64,72... | collective-permute-start | bytes 1179656 | tf_op jit(solution)/shard_map/ppermute | solution.py:41
  62.2 4.6 %collective-permute-start.28 = (bf16[192,32]{1,0:T(8,128)(2,1)S(1)}, bf16[192,32]{1,0:T(8,128)(2,1)S(1)}, u32[]{:S(2)}, u32[]{:S(2)}) collective-permute-start(bf16[192,32]{1,0:T(8,128)(2,1)S(1)} %get-tuple-element.55.mine_ref), channel_id=1, source_target_pairs={{0,4},{4,0},{1,5},{5,1},{2,6},{6,2},{3,7},{7,3},{8,12},{12,8},{9,1... | collective-permute-start | bytes 36872 | tf_op jit(solution)/shard_map/ppermute | solution.py:425
  62.2 12.3 %collective-permute-start.14 = (bf16[48,4096]{1,0:T(8,128)(2,1)S(1)}, bf16[48,4096]{1,0:T(8,128)(2,1)S(1)}, u32[]{:S(2)}, u32[]{:S(2)}) collective-permute-start(bf16[48,4096]{1,0:T(8,128)(2,1)S(1)} %get-tuple-element.45), channel_id=1, source_target_pairs={{0,8},{8,0},{16,24},{24,16},{32,40},{40,32},{48,56},{56,48},{64,72... | collective-permute-start | bytes 1179656 | tf_op jit(solution)/shard_map/ppermute | solution.py:41
  62.6 9.0 %collective-permute-start.19 = (bf16[48,4096]{1,0:T(8,128)(2,1)S(1)}, bf16[48,4096]{1,0:T(8,128)(2,1)S(1)}, u32[]{:S(2)}, u32[]{:S(2)}) collective-permute-start(bf16[48,4096]{1,0:T(8,128)(2,1)S(1)} %add_convert_fusion.2), channel_id=1, source_target_pairs={{0,132},{8,12},{16,148},{24,28},{32,164},{40,44},{48,180},{56,60},... | collective-permute-start | bytes 1179656 | tf_op jit(solution)/shard_map/ppermute | solution.py:41
  63.8 3.8 %collective-permute-start.18 = (bf16[48,4096]{1,0:T(8,128)(2,1)S(1)}, bf16[48,4096]{1,0:T(8,128)(2,1)S(1)}, u32[]{:S(2)}, u32[]{:S(2)}) collective-permute-start(bf16[48,4096]{1,0:T(8,128)(2,1)S(1)} %get-tuple-element.54), channel_id=1, source_target_pairs={{0,8},{8,0},{16,24},{24,16},{32,40},{40,32},{48,56},{56,48},{64,72... | collective-permute-start | bytes 1179656 | tf_op jit(solution)/shard_map/ppermute | solution.py:41
  64.6 12.2 %collective-permute-start.17 = (bf16[48,4096]{1,0:T(8,128)(2,1)S(1)}, bf16[48,4096]{1,0:T(8,128)(2,1)S(1)}, u32[]{:S(2)}, u32[]{:S(2)}) collective-permute-start(bf16[48,4096]{1,0:T(8,128)(2,1)S(1)} %add_convert_fusion.1), channel_id=1, source_target_pairs={{0,132},{8,12},{16,148},{24,28},{32,164},{40,44},{48,180},{56,60},... | collective-permute-start | bytes 1179656 | tf_op jit(solution)/shard_map/ppermute | solution.py:41
  71.8 8.1 %collective-permute-start.20 = (bf16[48,4096]{1,0:T(8,128)(2,1)S(1)}, bf16[48,4096]{1,0:T(8,128)(2,1)S(1)}, u32[]{:S(2)}, u32[]{:S(2)}) collective-permute-start(bf16[48,4096]{1,0:T(8,128)(2,1)S(1)} %add_convert_fusion), channel_id=1, source_target_pairs={{0,4},{8,140},{16,20},{24,156},{32,36},{40,172},{48,52},{56,188},{... | collective-permute-start | bytes 1179656 | tf_op jit(solution)/shard_map/ppermute | solution.py:41
  72.6 12.2 %collective-permute-start.29 = (bf16[32,4352]{1,0:T(8,128)(2,1)S(1)}, bf16[32,4352]{1,0:T(8,128)(2,1)S(1)}, u32[]{:S(2)}, u32[]{:S(2)}) collective-permute-start(bf16[32,4352]{1,0:T(8,128)(2,1)S(1)} %pad_maximum_fusion.1), channel_id=1, source_target_pairs={{0,1},{1,0},{2,3},{3,2},{4,5},{5,4},{6,7},{7,6},{8,9},{9,8},{10,11... | collective-permute-start | bytes 835592 | tf_op jit(solution)/shard_map/ppermute | solution.py:443
  73.5 19.8 %collective-permute-start.30 = (bf16[32,4352]{1,0:T(8,128)(2,1)S(1)}, bf16[32,4352]{1,0:T(8,128)(2,1)S(1)}, u32[]{:S(2)}, u32[]{:S(2)}) collective-permute-start(bf16[32,4352]{1,0:T(8,128)(2,1)S(1)} %pad_maximum_fusion.1), channel_id=1, source_target_pairs={{0,3},{1,2},{2,1},{3,0},{4,7},{5,6},{6,5},{7,4},{8,11},{9,10},{10,... | collective-permute-start | bytes 835592 | tf_op jit(solution)/shard_map/ppermute | solution.py:443
  74.5 18.7 %collective-permute-start.31 = (bf16[32,4352]{1,0:T(8,128)(2,1)S(1)}, bf16[32,4352]{1,0:T(8,128)(2,1)S(1)}, u32[]{:S(2)}, u32[]{:S(2)}) collective-permute-start(bf16[32,4352]{1,0:T(8,128)(2,1)S(1)} %pad_maximum_fusion.1), channel_id=1, source_target_pairs={{0,2},{1,3},{2,0},{3,1},{4,6},{5,7},{6,4},{7,5},{8,10},{9,11},{10,... | collective-permute-start | bytes 835592 | tf_op jit(solution)/shard_map/ppermute | solution.py:443
  80.2 8.3 %collective-permute-start.21 = (bf16[6,4096]{1,0:T(8,128)(2,1)S(1)}, bf16[6,4096]{1,0:T(8,128)(2,1)S(1)}, u32[]{:S(2)}, u32[]{:S(2)}) collective-permute-start(bf16[6,4096]{1,0:T(8,128)(2,1)S(1)} %get-tuple-element.69), channel_id=1, source_target_pairs={{0,64},{8,72},{16,80},{24,88},{32,96},{40,104},{48,112},{56,120},{... | collective-permute-start | bytes 147464 | tf_op jit(solution)/shard_map/ppermute | solution.py:41
  83.4 9.6 %collective-permute-start.22 = (bf16[6,4096]{1,0:T(8,128)(2,1)S(1)}, bf16[6,4096]{1,0:T(8,128)(2,1)S(1)}, u32[]{:S(2)}, u32[]{:S(2)}) collective-permute-start(bf16[6,4096]{1,0:T(8,128)(2,1)S(1)} %get-tuple-element.68), channel_id=1, source_target_pairs={{0,80},{8,88},{16,96},{24,104},{32,112},{40,120},{48,0},{56,8},{64... | collective-permute-start | bytes 147464 | tf_op jit(solution)/shard_map/ppermute | solution.py:41
  84.8 8.4 %collective-permute-start.23 = (bf16[6,4096]{1,0:T(8,128)(2,1)S(1)}, bf16[6,4096]{1,0:T(8,128)(2,1)S(1)}, u32[]{:S(2)}, u32[]{:S(2)}) collective-permute-start(bf16[6,4096]{1,0:T(8,128)(2,1)S(1)} %get-tuple-element.67), channel_id=1, source_target_pairs={{0,48},{8,56},{16,64},{24,72},{32,80},{40,88},{48,96},{56,104},{64... | collective-permute-start | bytes 147464 | tf_op jit(solution)/shard_map/ppermute | solution.py:41
  93.4 13.5 %collective-permute-start.32 = (bf16[32,4352]{1,0:T(8,128)(2,1)S(1)}, bf16[32,4352]{1,0:T(8,128)(2,1)S(1)}, u32[]{:S(2)}, u32[]{:S(2)}) collective-permute-start(bf16[32,4352]{1,0:T(8,128)(2,1)S(1)} %add_convert_fusion.3), channel_id=1, source_target_pairs={{0,4},{4,0},{1,5},{5,1},{2,6},{6,2},{3,7},{7,3},{8,12},{12,8},{9,1... | collective-permute-start | bytes 835592 | tf_op jit(solution)/shard_map/ppermute | solution.py:454
  94.0 7.2 %collective-permute-start.24 = (bf16[6,4096]{1,0:T(8,128)(2,1)S(1)}, bf16[6,4096]{1,0:T(8,128)(2,1)S(1)}, u32[]{:S(2)}, u32[]{:S(2)}) collective-permute-start(bf16[6,4096]{1,0:T(8,128)(2,1)S(1)} %get-tuple-element.66), channel_id=1, source_target_pairs={{0,96},{8,104},{16,112},{24,120},{32,0},{40,8},{48,16},{56,24},{64... | collective-permute-start | bytes 147464 | tf_op jit(solution)/shard_map/ppermute | solution.py:41
  99.2 6.4 %collective-permute-start.25 = (bf16[6,4096]{1,0:T(8,128)(2,1)S(1)}, bf16[6,4096]{1,0:T(8,128)(2,1)S(1)}, u32[]{:S(2)}, u32[]{:S(2)}) collective-permute-start(bf16[6,4096]{1,0:T(8,128)(2,1)S(1)} %get-tuple-element.65), channel_id=1, source_target_pairs={{0,32},{8,40},{16,48},{24,56},{32,64},{40,72},{48,80},{56,88},{64,... | collective-permute-start | bytes 147464 | tf_op jit(solution)/shard_map/ppermute | solution.py:41
  99.2 6.4 %collective-permute-start.26 = (bf16[6,4096]{1,0:T(8,128)(2,1)S(1)}, bf16[6,4096]{1,0:T(8,128)(2,1)S(1)}, u32[]{:S(2)}, u32[]{:S(2)}) collective-permute-start(bf16[6,4096]{1,0:T(8,128)(2,1)S(1)} %get-tuple-element.64), channel_id=1, source_target_pairs={{0,112},{8,120},{16,0},{24,8},{32,16},{40,24},{48,32},{56,40},{64,... | collective-permute-start | bytes 147464 | tf_op jit(solution)/shard_map/ppermute | solution.py:41
  99.9 6.3 %collective-permute-start.27 = (bf16[6,4096]{1,0:T(8,128)(2,1)S(1)}, bf16[6,4096]{1,0:T(8,128)(2,1)S(1)}, u32[]{:S(2)}, u32[]{:S(2)}) collective-permute-start(bf16[6,4096]{1,0:T(8,128)(2,1)S(1)} %get-tuple-element.63), channel_id=1, source_target_pairs={{0,16},{8,24},{16,32},{24,40},{32,48},{40,56},{48,64},{56,72},{64,... | collective-permute-start | bytes 147464 | tf_op jit(solution)/shard_map/ppermute | solution.py:41
  (14 other events, 30.5 us)

commit v7 on v5

--- a/solution.py
+++ b/solution.py
@@ -1,5 +1,6 @@
 import jax
 import jax.numpy as jnp
+import numpy as np
 from jax import lax
 from jax.experimental import pallas as pl
 from jax.experimental.pallas import tpu as pltpu
@@ -58,10 +59,10 @@
 
 
 def cost(flops, moved):
-    return pl.CostEstimate(flops=int(flops) // 1000, bytes_accessed=int(moved) // 1000, transcendentals=0)
-
-
-def pair_kernel(gain_ref, query_ref, context_ref, pair_ref):
+    return pl.CostEstimate(flops=int(flops), bytes_accessed=int(moved), transcendentals=0)
+
+
+def pair_kernel(ready_ref, gain_ref, query_ref, context_ref, pair_ref):
     gain = gain_ref[0:1, :].astype(F32)
     head = gain.shape[1]
     text = query_ref.shape[1]
@@ -77,7 +78,7 @@
             pair_ref[kv, rows, head : 2 * head] = context_ref[0, :, columns]
 
 
-def pair_queries(queries, context, gains, kv_heads):
+def pair_queries(ready, queries, context, gains, kv_heads):
     batches, text, wide = queries.shape
     head = gains.shape[1]
     rows = wide // (kv_heads * head) * text
@@ -86,12 +87,17 @@
         pair_kernel,
         out_shape=jax.ShapeDtypeStruct((batches * kv_heads, rows, 2 * head), LOW),
         grid=(batches,),
-        in_specs=[pl.BlockSpec(gains.shape, lambda b: (0, 0)), block, block],
+        in_specs=[
+            pl.BlockSpec(memory_space=pl.ANY),
+            pl.BlockSpec(gains.shape, lambda b: (0, 0)),
+            block,
+            block,
+        ],
         out_specs=pl.BlockSpec((kv_heads, rows, 2 * head), lambda b: (b, 0, 0)),
         compiler_params=ROOM,
         cost_estimate=cost(2e8, 4 * queries.size * 2),
         name="pair_queries",
-    )(gains, queries, context)
+    )(ready, gains, queries, context)
 
 
 def flatten_kernel(from_ref, to_ref):
@@ -188,7 +194,7 @@
 
 def attention_kernel(
     count_ref, start_ref, y0, y1, y2, r0, r1, r2, own_map, other_map, own_back, other_back,
-    up_diagonal, gains_ref, pair_ref, g_own, m_own, g_other, m_other, middle_ref, up_ref, grad_ref,
+    up_diagonal, gains_ref, pair_ref, g_own, m_own, g_other, m_other, up_ref, grad_ref,
 ):
     width = y0.shape[2]
     head = gains_ref.shape[1]
@@ -255,7 +261,6 @@
             ].astype(LOW)
     grad = grad_ref[...]
     middle = dot(grad, up_diagonal[...], NT).astype(LOW)
-    middle_ref[...] = (ADAPTER_SCALE * middle.astype(F32)).astype(LOW)
     up = ADAPTER_SCALE * dot(reduced, grad, TN)
     for part in range(2):
         half = slice(part * ranks // 2, (part + 1) * ranks // 2)
@@ -277,11 +282,10 @@
             jax.ShapeDtypeStruct((rows, ranks), LOW),
             jax.ShapeDtypeStruct((rows, 2 * width), LOW),
             jax.ShapeDtypeStruct((rows, ranks), LOW),
-            jax.ShapeDtypeStruct((rows, ranks), LOW),
             jax.ShapeDtypeStruct((ranks, width), F32),
         ],
         in_specs=[scalar, scalar] + [vector] * 13,
-        out_specs=[vector] * 6,
+        out_specs=[vector] * 5,
         scratch_shapes=[pltpu.VMEM((rows, 2 * width), LOW)],
         compiler_params=ROOM,
         cost_estimate=cost(1e9, 2 * pair.size),
@@ -315,45 +319,38 @@
     )(which, grad, middle, weights, down_maps)
 
 
-def down_kernel(back_ref, mine_ref, facing_ref, *refs):
+def down_kernel(m_ref, *refs):
     *row_refs, out_ref = refs
     rows = jnp.concatenate([ref[...] for ref in row_refs])
-    ranks = mine_ref.shape[1]
-    both = jnp.concatenate([mine_ref[...], facing_ref[...]], 1)
-    parts = dot(dot(back_ref[...], both).astype(LOW), rows, TN)
-    out_ref[...] = parts[:ranks] + parts[ranks:]
-
-
-def down_grad(back, mine, facing, blocks):
-    ranks, half = mine.shape[1], blocks[0].shape[1]
+    out_ref[...] = dot(m_ref[...], rows, TN).astype(out_ref.dtype)
+
+
+def down_grad(middle, blocks, dtype):
+    half = blocks[0].shape[1]
     return pl.pallas_call(
         down_kernel,
-        out_shape=jax.ShapeDtypeStruct((ranks, half), F32),
-        in_specs=[VECTOR] * (3 + len(blocks)),
+        out_shape=jax.ShapeDtypeStruct((middle.shape[1], half), dtype),
+        in_specs=[VECTOR] * (1 + len(blocks)),
         out_specs=VECTOR,
         compiler_params=ROOM,
         cost_estimate=cost(5e7, 2 * 200 * half),
         name="down_grad",
-    )(back, mine, facing, *blocks)
-
-
-def row_tokens(x_hi, z, core, x_lo):
-    def base_rows(chain, x_high):
-        rows = []
-        for k in (*SHIFTS, 0):
-            token = ((x_high * NZ + (z - k) % NZ) * 2 + chain) * 2
-            for batch in range(3):
-                rows += [batch * 64 + token, batch * 64 + token + 1]
-        return jnp.stack(rows)
-
-    own_half, other_half = [], []
-    for chain in (core, 1 - core):
-        own_half += [base_rows(chain, x_hi)]
-        near = jnp.where(chain == 0, x_hi, 1 - x_hi)
-        other_half += [base_rows(chain, near), base_rows(chain, 1 - near)]
-    for chain in (core, 1 - core):
-        own_half += [base_rows(chain, 1 - x_hi)]
-    return jnp.concatenate(own_half), jnp.concatenate(other_half)
+    )(middle, *blocks)
+
+
+def row_tokens(x_hi, z, core):
+    row = np.arange(192)
+    shift = np.array((*SHIFTS, 0))[row % 48 // 6]
+    place = row % 6 // 2 * 64 + row % 2
+
+    def rows(theirs, flip):
+        chain = jnp.where(theirs, 1 - core, core)
+        x_high = jnp.where(flip(chain), 1 - x_hi, x_hi)
+        return place + ((x_high * NZ + (z - shift + NZ) % NZ) * 2 + chain) * 2
+
+    own = rows(row // 48 % 2 == 1, lambda chain: row // 96 == 1)
+    other = rows(row // 96 == 1, lambda chain: (row // 48 % 2) != chain)
+    return own, other
 
 
 def per_device(
@@ -386,7 +383,7 @@
         [jnp.pad(up_maps[0], ((0, 0), (0, width))), jnp.pad(up_maps[1], ((0, 0), (width, 0)))]
     )
     own_token, other_token = row_tokens(
-        late_section // 16, (late_section // 2) % NZ, late_section % 2, late_side
+        late_section // 16, (late_section // 2) % NZ, late_section % 2
     )
     line = jnp.arange(own_token.shape[0])
     maps = [
@@ -396,22 +393,22 @@
         (other_token[:, None] == line[None]).astype(LOW),
     ]
     pair = pair_queries(
-        after(queries[0], base), context_gradient[0], gains, width // gains.shape[1]
+        base, queries[0], context_gradient[0], gains, width // gains.shape[1]
     )
     weights = hold(weights, after(pair, up_diagonal, *maps))
+    first = after(first, weights)
     step_a = project([base, base_there], weights, down_maps, here)
-    first = after(first, pair, *step_a, up_diagonal, *maps)
     third = move(first, FAR)
     first_there = move(first, SIBLING)
     second_there = move(second, SIBLING)
     others = [first, second, first_there, second_there]
     step_b = project(others, weights, down_maps, opposite)
-    third = after(third, *step_b)
+    third = after(third, *step_a, *step_b)
     third_there = move(third, SIBLING)
     step_c = project([third, third_there], weights, down_maps, here)
     owns = [base, base_there, third, third_there]
 
-    g_own, m_own, g_other, m_other, middle, up_part = attend(
+    g_own, m_own, g_other, m_other, up_part = attend(
         image_tile_count,
         text_start_position,
         (step_a, step_c, step_b),
@@ -421,8 +418,12 @@
         pair,
     )
 
-    middle_facing = lax.ppermute(middle, "tensor", TENSOR_SWAP)
-    base, base_out, third, third_out = feature_grad(g_own, m_own, weights, down_maps, here)
+    down_other = down_grad(m_other, others, LOW)
+    down_facing = lax.ppermute(down_other, "tensor", TENSOR_SWAP)
+    base, base_out, third, third_out = feature_grad(
+        after(g_own, down_other), m_own, weights, down_maps, here
+    )
+    down_own = down_grad(m_own, owns, F32)
 
     def add(mine, theirs):
         return mine.astype(F32) + theirs.astype(F32)
@@ -430,15 +431,16 @@
     third = add(third, move(third_out, SIBLING)).astype(LOW)
     third_in = move(third, FAR)
     first, second, first_out, second_out = feature_grad(
-        after(g_other, third), m_other, weights, down_maps, opposite
+        after(g_other, third, down_own), m_other, weights, down_maps, opposite
     )
     second = add(second, move(second_out, SIBLING)).astype(LOW)
     first = add(first, move(first_out, SIBLING))
     base = add(base, move(base_out, SIBLING))
+    sums = jnp.concatenate(
+        [down_own + after(down_facing, first_out).astype(F32), up_part], 1
+    ).astype(LOW)
+    near_sums = lax.ppermute(sums, "dp", DP_NEAR)
     second_in = move(second, FAR)
-    down_own = down_grad(maps[2], middle, after(middle_facing, second), owns)
-    sums = jnp.concatenate([down_own, up_part], 1).astype(LOW)
-    near_sums = lax.ppermute(sums, "dp", DP_NEAR)
     first = (first + third_in.astype(F32)).astype(LOW)
     first_in = move(first, NEAR)
     sums = add(sums, after(near_sums, second_in, first)).astype(LOW)

time: 113 us -> 112 us (level)
  waiting for transfers between devices: 33.4 us -> 41.5 us
  Pallas kernels: 17.6 us -> 14.7 us
  starting transfers between devices: 44.7 us -> 42 us
  local copies, waits for them, and re-layouts: 11.5 us -> 9.38 us
    ppermute x1, waiting for transfers between devices: 0.75 us -> 4.2 us  [per_device(): down_facing = lax.ppermute(down_other, 'tensor', TENSOR_SWAP)]
    ppermute x1, waiting for transfers between devices: 5.06 us -> 7.31 us  [per_device(): far_sums = lax.ppermute(sums, 'dp', DP_FAR)]
    pallas_call x3, Pallas kernels: 5.39 us -> 3.32 us  [project(): pl.pallas_call(project_kernel, out_shape=[jax.ShapeDtypeStruct((2, count,...]
    ppermute x1, waiting for transfers between devices: 3.82 us -> 5.87 us  [per_device(): near_sums = lax.ppermute(sums, 'dp', DP_NEAR)]
    concatenate x2 -> x0, local copies, waits for them, and re-layouts: 1.72 us -> none  [row_tokens(): return (jnp.concatenate(own_half), jnp.concatenate(other_half))]
    ppermute x28, starting transfers between devices: 42.1 us -> 40.5 us  [move(): return lax.ppermute(block, PLANE, pairs)]
    ppermute x1, starting transfers between devices: 1.23 us -> 0.09 us  [per_device(): facing = lax.ppermute(sums, 'tensor', TENSOR_SWAP)]
    unnamed x18 -> x16, local copies, waits for them, and re-layouts: 8.1 us -> 7.65 us
  transfers between devices with their start and end apart: 32 -> 32, of which waited for: 20 -> 17; matrix products, arithmetic and copies ran while one was open for 4% -> 2% of each run, Pallas kernels for 8% -> 7%
where the time goes in v7:
time: 112 us
  starting transfers between devices  42 us (38%)
  waiting for transfers between devices  41.5 us (37%)
  Pallas kernels  14.7 us (13%)
  local copies, waits for them, and re-layouts  9.38 us (8%)
  other arithmetic  3.37 us (3%)
    ppermute x28, starting transfers between devices, move(): return lax.ppermute(block, PLANE, pairs)  40.5 us
    ppermute x28, waiting for transfers between devices, move(): return lax.ppermute(block, PLANE, pairs)  24.1 us
    unnamed x16, local copies, waits for them, and re-layouts  7.65 us
    ppermute x1, waiting for transfers between devices, per_device(): far_sums = lax.ppermute(sums, 'dp', DP_FAR)  7.31 us
    ppermute x1, waiting for transfers between devices, per_device(): near_sums = lax.ppermute(sums, 'dp', DP_NEAR)  5.87 us
    ppermute x1, waiting for transfers between devices, per_device(): down_facing = lax.ppermute(down_other, 'tensor', TENSOR_SWAP)  4.2 us
    pallas_call x1, Pallas kernels, attend(): pl.pallas_call(attention_kernel, out_shape=[jax.ShapeDtypeStruct((rows, 2...  4.03 us
    pallas_call x2, Pallas kernels, feature_grad(): pl.pallas_call(feature_kernel, out_shape=[jax.ShapeDtypeStruct((rows // 4...  3.85 us
  transfers between devices with their start and end apart: 32, of which 17 were waited for; matrix products, arithmetic and copies ran while one was open for 2% of the time, Pallas kernels for 7%

profile of v7, /device:TPU:24, one launch (start us, length us, event | category | flops | bytes accessed | tf_op | source)
XLA Modules:
  0.0 112.0 jit_solution(13886104612541838679)
XLA Ops:
  1.5 7.3 %collective-permute-start = (bf16[6,4096]{1,0:T(8,128)(2,1)S(1)}, bf16[6,4096]{1,0:T(8,128)(2,1)S(1)}, u32[]{:S(2)}, u32[]{:S(2)}) collective-permute-start(bf16[6,4096]{1,0:T(8,128)(2,1)S(1)} %flatten.1), channel_id=1, source_target_pairs={{0,64},{8,72},{16,80},{24,88},{32,96},{40,104},{48,112},{56,120},{... | collective-permute-start | bytes 147464 | tf_op jit(solution)/shard_map/ppermute | solution.py:41
  8.7 1.9 %collective-permute-start.1 = (bf16[6,4096]{1,0:T(8,128)(2,1)S(1)}, bf16[6,4096]{1,0:T(8,128)(2,1)S(1)}, u32[]{:S(2)}, u32[]{:S(2)}) collective-permute-start(bf16[6,4096]{1,0:T(8,128)(2,1)S(1)} %flatten.1), channel_id=1, source_target_pairs={{0,48},{8,56},{16,64},{24,72},{32,80},{40,88},{48,96},{56,104},{64... | collective-permute-start | bytes 147464 | tf_op jit(solution)/shard_map/ppermute | solution.py:41
  10.7 3.1 %collective-permute-start.2 = (bf16[6,4096]{1,0:T(8,128)(2,1)S(1)}, bf16[6,4096]{1,0:T(8,128)(2,1)S(1)}, u32[]{:S(2)}, u32[]{:S(2)}) collective-permute-start(bf16[6,4096]{1,0:T(8,128)(2,1)S(1)} %flatten.1), channel_id=1, source_target_pairs={{0,80},{8,88},{16,96},{24,104},{32,112},{40,120},{48,0},{56,8},{64... | collective-permute-start | bytes 147464 | tf_op jit(solution)/shard_map/ppermute | solution.py:41
  13.8 1.5 %collective-permute-start.3 = (bf16[6,4096]{1,0:T(8,128)(2,1)S(1)}, bf16[6,4096]{1,0:T(8,128)(2,1)S(1)}, u32[]{:S(2)}, u32[]{:S(2)}) collective-permute-start(bf16[6,4096]{1,0:T(8,128)(2,1)S(1)} %flatten.1), channel_id=1, source_target_pairs={{0,32},{8,40},{16,48},{24,56},{32,64},{40,72},{48,80},{56,88},{64,... | collective-permute-start | bytes 147464 | tf_op jit(solution)/shard_map/ppermute | solution.py:41
  15.2 2.7 %collective-permute-start.4 = (bf16[6,4096]{1,0:T(8,128)(2,1)S(1)}, bf16[6,4096]{1,0:T(8,128)(2,1)S(1)}, u32[]{:S(2)}, u32[]{:S(2)}) collective-permute-start(bf16[6,4096]{1,0:T(8,128)(2,1)S(1)} %flatten.1), channel_id=1, source_target_pairs={{0,96},{8,104},{16,112},{24,120},{32,0},{40,8},{48,16},{56,24},{64... | collective-permute-start | bytes 147464 | tf_op jit(solution)/shard_map/ppermute | solution.py:41
  18.9 2.2 %collective-permute-start.6 = (bf16[6,4096]{1,0:T(8,128)(2,1)S(1)}, bf16[6,4096]{1,0:T(8,128)(2,1)S(1)}, u32[]{:S(2)}, u32[]{:S(2)}) collective-permute-start(bf16[6,4096]{1,0:T(8,128)(2,1)S(1)} %flatten.1), channel_id=1, source_target_pairs={{0,112},{8,120},{16,0},{24,8},{32,16},{40,24},{48,32},{56,40},{64,... | collective-permute-start | bytes 147464 | tf_op jit(solution)/shard_map/ppermute | solution.py:41
  24.4 1.6 %collective-permute-start.8 = (bf16[48,4096]{1,0:T(8,128)(2,1)S(1)}, bf16[48,4096]{1,0:T(8,128)(2,1)S(1)}, u32[]{:S(2)}, u32[]{:S(2)}) collective-permute-start(bf16[48,4096]{1,0:T(8,128)(2,1)S(1)} %concatenate.16.ready_ref.refs_0_), channel_id=1, source_target_pairs={{0,4},{8,140},{16,20},{24,156},{32,36},{40,172},{48,52},{56,188},{... | collective-permute-start | bytes 1179656 | tf_op jit(solution)/shard_map/ppermute | solution.py:41
  25.9 2.1 %collective-permute-start.10 = (bf16[48,4096]{1,0:T(8,128)(2,1)S(1)}, bf16[48,4096]{1,0:T(8,128)(2,1)S(1)}, u32[]{:S(2)}, u32[]{:S(2)}) collective-permute-start(bf16[48,4096]{1,0:T(8,128)(2,1)S(1)} %concatenate.16.ready_ref.refs_0_), channel_id=1, source_target_pairs={{0,132},{8,12},{16,148},{24,28},{32,164},{40,44},{48,180},{56,60},... | collective-permute-start | bytes 1179656 | tf_op jit(solution)/shard_map/ppermute | solution.py:41
  29.5 1.4 %copy-done.2 = bf16[1,3,128,2048]{3,2,1,0:T(8,128)(2,1)S(1)} copy-done((bf16[1,3,128,2048]{3,2,1,0:T(8,128)(2,1)S(1)}, bf16[1,3,128,2048]{3,2,1,0:T(8,128)(2,1)}, u32[]{:S(2)}) %copy-start.2) | copy-done | bytes 1572888
  30.9 1.4 %copy-done.3 = bf16[1,3,128,2048]{3,2,1,0:T(8,128)(2,1)S(1)} copy-done((bf16[1,3,128,2048]{3,2,1,0:T(8,128)(2,1)S(1)}, bf16[1,3,128,2048]{3,2,1,0:T(8,128)(2,1)}, u32[]{:S(2)}) %copy-start.3) | copy-done | bytes 1572888
  33.0 1.4 %pair_queries.1.ready_ref.pair_ref = bf16[6,1024,256]{2,1,0:T(8,128)(2,1)S(1)} custom-call(bf16[48,4096]{1,0:T(8,128)(2,1)S(1)} %concatenate.16.ready_ref.refs_0_, bf16[2,128]{1,0:T(2,128)(2,1)S(1)} %bitcast.20, bf16[3,128,2048]{2,1,0:T(8,128)(2,1)S(1)} %bitcast.18, bf16[3,128,2048]{2,1,0:T(8,128)(2,1)S(1)} %bitcast.19), custom_call_target="tpu_custom_call" | custom-call | flops 200000000 | bytes 6291456 | tf_op jit(solution)/shard_map/pair_queries/pallas_call | solution.py:86
  34.5 3.4 %copy-done.1 = bf16[1,2,8192,256]{3,2,1,0:T(8,128)(2,1)S(1)} copy-done((bf16[1,2,8192,256]{3,2,1,0:T(8,128)(2,1)S(1)}, bf16[1,2,8192,256]{3,2,1,0:T(8,128)(2,1)}, u32[]{:S(2)}) %copy-start.1) | copy-done | bytes 8388632
  41.3 1.4 %project.4 = (f32[2,192,256]{2,1,0:T(8,128)S(1)}, f32[192,32]{1,0:T(8,128)S(1)}) custom-call(s32[1]{0:T(128)S(6)} %sub.32.which_ref, bf16[48,4096]{1,0:T(8,128)(2,1)S(1)} %collective-permute-done.8.refs_0_, bf16[48,4096]{1,0:T(8,128)(2,1)S(1)} %collective-permute-done.10.refs_1_, bf16[48,4096]{1,0:T(8,128)(2,1)S(1)} %collective-permute-done.11.refs_2_, ...), custom_call_target="tpu_custom_call" | custom-call | flops 805306368 | bytes 5767168 | tf_op jit(solution)/shard_map/project/pallas_call | solution.py:181
  42.7 5.5 %collective-permute-done.9.refs_0_.refs_2_ = bf16[48,4096]{1,0:T(8,128)(2,1)S(1)} collective-permute-done((bf16[48,4096]{1,0:T(8,128)(2,1)S(1)}, bf16[48,4096]{1,0:T(8,128)(2,1)S(1)}, u32[]{:S(2)}, u32[]{:S(2)}) %collective-permute-start.9) | collective-permute-done | bytes 393248 | tf_op jit(solution)/shard_map/ppermute | solution.py:41
  48.1 1.7 %collective-permute-done.13.refs_1_.refs_3_ = bf16[48,4096]{1,0:T(8,128)(2,1)S(1)} collective-permute-done((bf16[48,4096]{1,0:T(8,128)(2,1)S(1)}, bf16[48,4096]{1,0:T(8,128)(2,1)S(1)}, u32[]{:S(2)}, u32[]{:S(2)}) %collective-permute-start.13) | collective-permute-done | bytes 393248 | tf_op jit(solution)/shard_map/ppermute | solution.py:41
  50.9 4.0 %attend.1 = (bf16[192,512]{1,0:T(8,128)(2,1)S(1)}, bf16[192,32]{1,0:T(8,128)(2,1)S(1)}, bf16[192,512]{1,0:T(8,128)(2,1)S(1)}, bf16[192,32]{1,0:T(8,128)(2,1)S(1)}, f32[32,256]{1,0:T(8,128)S(1)}) custom-call(s32[3]{0:T(128)S(1)} %copy-done.6, s32[3]{0:T(128)S(1)} %copy-done.7, f32[2,96,256]{2,1,0:T(8,128)S(1)} %get-tuple-element.36.y0, ...), custom_call_target="tpu_custom_call" | custom-call | flops 1000000000 | bytes 3145728 | tf_op jit(solution)/shard_map/attend/pallas_call | solution.py:278
  55.3 1.9 %feature_grad.2 = (bf16[48,4096]{1,0:T(8,128)(2,1)S(1)}, bf16[48,4096]{1,0:T(8,128)(2,1)S(1)}, bf16[48,4096]{1,0:T(8,128)(2,1)S(1)}, bf16[48,4096]{1,0:T(8,128)(2,1)S(1)}) custom-call(s32[1]{0:T(128)} %bitcast.which_ref, bf16[192,512]{1,0:T(8,128)(2,1)S(1)} %get-tuple-element.46.g_ref, bf16[192,32]{1,0:T(8,128)(2,1)S(1)} %get-tuple-element.47.m_ref, ...), custom_call_target="tpu_custom_call" | custom-call | flops 805306368 | bytes 5767168 | tf_op jit(solution)/shard_map/feature_grad/pallas_call | solution.py:311
  59.2 1.2 %collective-permute-start.19 = (bf16[48,4096]{1,0:T(8,128)(2,1)S(1)}, bf16[48,4096]{1,0:T(8,128)(2,1)S(1)}, u32[]{:S(2)}, u32[]{:S(2)}) collective-permute-start(bf16[48,4096]{1,0:T(8,128)(2,1)S(1)} %add_convert_fusion.2), channel_id=1, source_target_pairs={{0,132},{8,12},{16,148},{24,28},{32,164},{40,44},{48,180},{56,60},... | collective-permute-start | bytes 1179656 | tf_op jit(solution)/shard_map/ppermute | solution.py:41
  60.4 1.9 %feature_grad.3 = (bf16[48,4096]{1,0:T(8,128)(2,1)S(1)}, bf16[48,4096]{1,0:T(8,128)(2,1)S(1)}, bf16[48,4096]{1,0:T(8,128)(2,1)S(1)}, bf16[48,4096]{1,0:T(8,128)(2,1)S(1)}) custom-call(s32[1]{0:T(128)S(6)} %sub.32.which_ref, bf16[192,512]{1,0:T(8,128)(2,1)S(1)} %get-tuple-element.53.g_ref, bf16[192,32]{1,0:T(8,128)(2,1)S(1)} %get-tuple-element.45.m_ref, ...), custom_call_target="tpu_custom_call" | custom-call | flops 805306368 | bytes 5767168 | tf_op jit(solution)/shard_map/feature_grad/pallas_call | solution.py:311
  62.4 4.2 %collective-permute-done.21 = bf16[32,4096]{1,0:T(8,128)(2,1)S(1)} collective-permute-done((bf16[32,4096]{1,0:T(8,128)(2,1)S(1)}, bf16[32,4096]{1,0:T(8,128)(2,1)S(1)}, u32[]{:S(2)}, u32[]{:S(2)}) %collective-permute-start.21) | collective-permute-done | bytes 262176 | tf_op jit(solution)/shard_map/ppermute | solution.py:422
  68.6 1.2 %collective-permute-start.17 = (bf16[48,4096]{1,0:T(8,128)(2,1)S(1)}, bf16[48,4096]{1,0:T(8,128)(2,1)S(1)}, u32[]{:S(2)}, u32[]{:S(2)}) collective-permute-start(bf16[48,4096]{1,0:T(8,128)(2,1)S(1)} %add_convert_fusion.1), channel_id=1, source_target_pairs={{0,132},{8,12},{16,148},{24,28},{32,164},{40,44},{48,180},{56,60},... | collective-permute-start | bytes 1179656 | tf_op jit(solution)/shard_map/ppermute | solution.py:41
  70.1 5.9 %collective-permute-done.22 = bf16[32,4352]{1,0:T(8,128)(2,1)S(1)} collective-permute-done((bf16[32,4352]{1,0:T(8,128)(2,1)S(1)}, bf16[32,4352]{1,0:T(8,128)(2,1)S(1)}, u32[]{:S(2)}, u32[]{:S(2)}) %collective-permute-start.22) | collective-permute-done | bytes 278560 | tf_op jit(solution)/shard_map/ppermute | solution.py:442
  75.9 5.3 %collective-permute-done.17 = bf16[48,4096]{1,0:T(8,128)(2,1)S(1)} collective-permute-done((bf16[48,4096]{1,0:T(8,128)(2,1)S(1)}, bf16[48,4096]{1,0:T(8,128)(2,1)S(1)}, u32[]{:S(2)}, u32[]{:S(2)}) %collective-permute-start.17) | collective-permute-done | bytes 393248 | tf_op jit(solution)/shard_map/ppermute | solution.py:41
  82.0 7.3 %collective-permute-done.23 = bf16[32,4352]{1,0:T(8,128)(2,1)S(1)} collective-permute-done((bf16[32,4352]{1,0:T(8,128)(2,1)S(1)}, bf16[32,4352]{1,0:T(8,128)(2,1)S(1)}, u32[]{:S(2)}, u32[]{:S(2)}) %collective-permute-start.23) | collective-permute-done | bytes 278560 | tf_op jit(solution)/shard_map/ppermute | solution.py:447
  89.6 3.2 %collective-permute-start.24 = (bf16[6,4096]{1,0:T(8,128)(2,1)S(1)}, bf16[6,4096]{1,0:T(8,128)(2,1)S(1)}, u32[]{:S(2)}, u32[]{:S(2)}) collective-permute-start(bf16[6,4096]{1,0:T(8,128)(2,1)S(1)} %get-tuple-element.73), channel_id=1, source_target_pairs={{0,64},{8,72},{16,80},{24,88},{32,96},{40,104},{48,112},{56,120},{... | collective-permute-start | bytes 147464 | tf_op jit(solution)/shard_map/ppermute | solution.py:41
  92.9 1.4 %collective-permute-start.25 = (bf16[6,4096]{1,0:T(8,128)(2,1)S(1)}, bf16[6,4096]{1,0:T(8,128)(2,1)S(1)}, u32[]{:S(2)}, u32[]{:S(2)}) collective-permute-start(bf16[6,4096]{1,0:T(8,128)(2,1)S(1)} %get-tuple-element.72), channel_id=1, source_target_pairs={{0,80},{8,88},{16,96},{24,104},{32,112},{40,120},{48,0},{56,8},{64... | collective-permute-start | bytes 147464 | tf_op jit(solution)/shard_map/ppermute | solution.py:41
  94.3 2.4 %collective-permute-start.26 = (bf16[6,4096]{1,0:T(8,128)(2,1)S(1)}, bf16[6,4096]{1,0:T(8,128)(2,1)S(1)}, u32[]{:S(2)}, u32[]{:S(2)}) collective-permute-start(bf16[6,4096]{1,0:T(8,128)(2,1)S(1)} %get-tuple-element.71), channel_id=1, source_target_pairs={{0,48},{8,56},{16,64},{24,72},{32,80},{40,88},{48,96},{56,104},{64... | collective-permute-start | bytes 147464 | tf_op jit(solution)/shard_map/ppermute | solution.py:41
  96.7 2.1 %collective-permute-start.27 = (bf16[6,4096]{1,0:T(8,128)(2,1)S(1)}, bf16[6,4096]{1,0:T(8,128)(2,1)S(1)}, u32[]{:S(2)}, u32[]{:S(2)}) collective-permute-start(bf16[6,4096]{1,0:T(8,128)(2,1)S(1)} %get-tuple-element.70), channel_id=1, source_target_pairs={{0,96},{8,104},{16,112},{24,120},{32,0},{40,8},{48,16},{56,24},{64... | collective-permute-start | bytes 147464 | tf_op jit(solution)/shard_map/ppermute | solution.py:41
  99.6 1.9 %collective-permute-done.25.refs_1_ = bf16[6,4096]{1,0:T(8,128)(2,1)S(1)} collective-permute-done((bf16[6,4096]{1,0:T(8,128)(2,1)S(1)}, bf16[6,4096]{1,0:T(8,128)(2,1)S(1)}, u32[]{:S(2)}, u32[]{:S(2)}) %collective-permute-start.25) | collective-permute-done | bytes 49184 | tf_op jit(solution)/shard_map/ppermute | solution.py:41
  101.5 1.9 %collective-permute-start.29 = (bf16[6,4096]{1,0:T(8,128)(2,1)S(1)}, bf16[6,4096]{1,0:T(8,128)(2,1)S(1)}, u32[]{:S(2)}, u32[]{:S(2)}) collective-permute-start(bf16[6,4096]{1,0:T(8,128)(2,1)S(1)} %get-tuple-element.68), channel_id=1, source_target_pairs={{0,112},{8,120},{16,0},{24,8},{32,16},{40,24},{48,32},{56,40},{64,... | collective-permute-start | bytes 147464 | tf_op jit(solution)/shard_map/ppermute | solution.py:41
  104.0 1.5 %collective-permute-done.28.refs_4_ = bf16[6,4096]{1,0:T(8,128)(2,1)S(1)} collective-permute-done((bf16[6,4096]{1,0:T(8,128)(2,1)S(1)}, bf16[6,4096]{1,0:T(8,128)(2,1)S(1)}, u32[]{:S(2)}, u32[]{:S(2)}) %collective-permute-start.28) | collective-permute-done | bytes 49184 | tf_op jit(solution)/shard_map/ppermute | solution.py:41
  106.2 3.2 %collective-permute-done.30.refs_6_ = bf16[6,4096]{1,0:T(8,128)(2,1)S(1)} collective-permute-done((bf16[6,4096]{1,0:T(8,128)(2,1)S(1)}, bf16[6,4096]{1,0:T(8,128)(2,1)S(1)}, u32[]{:S(2)}, u32[]{:S(2)}) %collective-permute-start.30) | collective-permute-done | bytes 49184 | tf_op jit(solution)/shard_map/ppermute | solution.py:41
  (83 shorter events, 22.0 us)
Async XLA Ops:
  1.5 16.5 %collective-permute-start = (bf16[6,4096]{1,0:T(8,128)(2,1)S(1)}, bf16[6,4096]{1,0:T(8,128)(2,1)S(1)}, u32[]{:S(2)}, u32[]{:S(2)}) collective-permute-start(bf16[6,4096]{1,0:T(8,128)(2,1)S(1)} %flatten.1), channel_id=1, source_target_pairs={{0,64},{8,72},{16,80},{24,88},{32,96},{40,104},{48,112},{56,120},{... | collective-permute-start | bytes 147464 | tf_op jit(solution)/shard_map/ppermute | solution.py:41
  8.7 10.2 %collective-permute-start.1 = (bf16[6,4096]{1,0:T(8,128)(2,1)S(1)}, bf16[6,4096]{1,0:T(8,128)(2,1)S(1)}, u32[]{:S(2)}, u32[]{:S(2)}) collective-permute-start(bf16[6,4096]{1,0:T(8,128)(2,1)S(1)} %flatten.1), channel_id=1, source_target_pairs={{0,48},{8,56},{16,64},{24,72},{32,80},{40,88},{48,96},{56,104},{64... | collective-permute-start | bytes 147464 | tf_op jit(solution)/shard_map/ppermute | solution.py:41
  10.7 10.5 %collective-permute-start.2 = (bf16[6,4096]{1,0:T(8,128)(2,1)S(1)}, bf16[6,4096]{1,0:T(8,128)(2,1)S(1)}, u32[]{:S(2)}, u32[]{:S(2)}) collective-permute-start(bf16[6,4096]{1,0:T(8,128)(2,1)S(1)} %flatten.1), channel_id=1, source_target_pairs={{0,80},{8,88},{16,96},{24,104},{32,112},{40,120},{48,0},{56,8},{64... | collective-permute-start | bytes 147464 | tf_op jit(solution)/shard_map/ppermute | solution.py:41
  13.8 7.7 %collective-permute-start.3 = (bf16[6,4096]{1,0:T(8,128)(2,1)S(1)}, bf16[6,4096]{1,0:T(8,128)(2,1)S(1)}, u32[]{:S(2)}, u32[]{:S(2)}) collective-permute-start(bf16[6,4096]{1,0:T(8,128)(2,1)S(1)} %flatten.1), channel_id=1, source_target_pairs={{0,32},{8,40},{16,48},{24,56},{32,64},{40,72},{48,80},{56,88},{64,... | collective-permute-start | bytes 147464 | tf_op jit(solution)/shard_map/ppermute | solution.py:41
  15.2 7.0 %collective-permute-start.4 = (bf16[6,4096]{1,0:T(8,128)(2,1)S(1)}, bf16[6,4096]{1,0:T(8,128)(2,1)S(1)}, u32[]{:S(2)}, u32[]{:S(2)}) collective-permute-start(bf16[6,4096]{1,0:T(8,128)(2,1)S(1)} %flatten.1), channel_id=1, source_target_pairs={{0,96},{8,104},{16,112},{24,120},{32,0},{40,8},{48,16},{56,24},{64... | collective-permute-start | bytes 147464 | tf_op jit(solution)/shard_map/ppermute | solution.py:41
  17.9 5.5 %collective-permute-start.5 = (bf16[6,4096]{1,0:T(8,128)(2,1)S(1)}, bf16[6,4096]{1,0:T(8,128)(2,1)S(1)}, u32[]{:S(2)}, u32[]{:S(2)}) collective-permute-start(bf16[6,4096]{1,0:T(8,128)(2,1)S(1)} %flatten.1), channel_id=1, source_target_pairs={{0,16},{8,24},{16,32},{24,40},{32,48},{40,56},{48,64},{56,72},{64,... | collective-permute-start | bytes 147464 | tf_op jit(solution)/shard_map/ppermute | solution.py:41
  18.9 4.6 %collective-permute-start.6 = (bf16[6,4096]{1,0:T(8,128)(2,1)S(1)}, bf16[6,4096]{1,0:T(8,128)(2,1)S(1)}, u32[]{:S(2)}, u32[]{:S(2)}) collective-permute-start(bf16[6,4096]{1,0:T(8,128)(2,1)S(1)} %flatten.1), channel_id=1, source_target_pairs={{0,112},{8,120},{16,0},{24,8},{32,16},{40,24},{48,32},{56,40},{64,... | collective-permute-start | bytes 147464 | tf_op jit(solution)/shard_map/ppermute | solution.py:41
  24.4 14.1 %collective-permute-start.8 = (bf16[48,4096]{1,0:T(8,128)(2,1)S(1)}, bf16[48,4096]{1,0:T(8,128)(2,1)S(1)}, u32[]{:S(2)}, u32[]{:S(2)}) collective-permute-start(bf16[48,4096]{1,0:T(8,128)(2,1)S(1)} %concatenate.16.ready_ref.refs_0_), channel_id=1, source_target_pairs={{0,4},{8,140},{16,20},{24,156},{32,36},{40,172},{48,52},{56,188},{... | collective-permute-start | bytes 1179656 | tf_op jit(solution)/shard_map/ppermute | solution.py:41
  25.9 13.1 %collective-permute-start.10 = (bf16[48,4096]{1,0:T(8,128)(2,1)S(1)}, bf16[48,4096]{1,0:T(8,128)(2,1)S(1)}, u32[]{:S(2)}, u32[]{:S(2)}) collective-permute-start(bf16[48,4096]{1,0:T(8,128)(2,1)S(1)} %concatenate.16.ready_ref.refs_0_), channel_id=1, source_target_pairs={{0,132},{8,12},{16,148},{24,28},{32,164},{40,44},{48,180},{56,60},... | collective-permute-start | bytes 1179656 | tf_op jit(solution)/shard_map/ppermute | solution.py:41
  28.0 12.3 %collective-permute-start.7 = (bf16[48,4096]{1,0:T(8,128)(2,1)S(1)}, bf16[48,4096]{1,0:T(8,128)(2,1)S(1)}, u32[]{:S(2)}, u32[]{:S(2)}) collective-permute-start(bf16[48,4096]{1,0:T(8,128)(2,1)S(1)} %concatenate.16.ready_ref.refs_0_), channel_id=1, source_target_pairs={{0,8},{8,0},{16,24},{24,16},{32,40},{40,32},{48,56},{56,48},{64,72... | collective-permute-start | bytes 1179656 | tf_op jit(solution)/shard_map/ppermute | solution.py:41
  38.4 2.8 %collective-permute-start.11 = (bf16[48,4096]{1,0:T(8,128)(2,1)S(1)}, bf16[48,4096]{1,0:T(8,128)(2,1)S(1)}, u32[]{:S(2)}, u32[]{:S(2)}) collective-permute-start(bf16[48,4096]{1,0:T(8,128)(2,1)S(1)} %collective-permute-done.8.refs_0_), channel_id=1, source_target_pairs={{0,8},{8,0},{16,24},{24,16},{32,40},{40,32},{48,56},{56,48},{64,72... | collective-permute-start | bytes 1179656 | tf_op jit(solution)/shard_map/ppermute | solution.py:41
  39.0 2.2 %collective-permute-start.12 = (bf16[48,4096]{1,0:T(8,128)(2,1)S(1)}, bf16[48,4096]{1,0:T(8,128)(2,1)S(1)}, u32[]{:S(2)}, u32[]{:S(2)}) collective-permute-start(bf16[48,4096]{1,0:T(8,128)(2,1)S(1)} %collective-permute-done.10.refs_1_), channel_id=1, source_target_pairs={{0,8},{8,0},{16,24},{24,16},{32,40},{40,32},{48,56},{56,48},{64,72... | collective-permute-start | bytes 1179656 | tf_op jit(solution)/shard_map/ppermute | solution.py:41
  39.1 9.0 %collective-permute-start.9 = (bf16[48,4096]{1,0:T(8,128)(2,1)S(1)}, bf16[48,4096]{1,0:T(8,128)(2,1)S(1)}, u32[]{:S(2)}, u32[]{:S(2)}) collective-permute-start(bf16[48,4096]{1,0:T(8,128)(2,1)S(1)} %collective-permute-done.8.refs_0_), channel_id=1, source_target_pairs={{0,132},{8,12},{16,148},{24,28},{32,164},{40,44},{48,180},{56,60},... | collective-permute-start | bytes 1179656 | tf_op jit(solution)/shard_map/ppermute | solution.py:41
  48.1 1.7 %collective-permute-start.13 = (bf16[48,4096]{1,0:T(8,128)(2,1)S(1)}, bf16[48,4096]{1,0:T(8,128)(2,1)S(1)}, u32[]{:S(2)}, u32[]{:S(2)}) collective-permute-start(bf16[48,4096]{1,0:T(8,128)(2,1)S(1)} %collective-permute-done.9.refs_0_.refs_2_), channel_id=1, source_target_pairs={{0,8},{8,0},{16,24},{24,16},{32,40},{40,32},{48,56},{56,48},{64,72... | collective-permute-start | bytes 1179656 | tf_op jit(solution)/shard_map/ppermute | solution.py:41
  57.3 1.8 %collective-permute-start.15 = (bf16[48,4096]{1,0:T(8,128)(2,1)S(1)}, bf16[48,4096]{1,0:T(8,128)(2,1)S(1)}, u32[]{:S(2)}, u32[]{:S(2)}) collective-permute-start(bf16[48,4096]{1,0:T(8,128)(2,1)S(1)} %get-tuple-element.52), channel_id=1, source_target_pairs={{0,8},{8,0},{16,24},{24,16},{32,40},{40,32},{48,56},{56,48},{64,72... | collective-permute-start | bytes 1179656 | tf_op jit(solution)/shard_map/ppermute | solution.py:41
  57.5 9.1 %collective-permute-start.21 = (bf16[32,4096]{1,0:T(8,128)(2,1)S(1)}, bf16[32,4096]{1,0:T(8,128)(2,1)S(1)}, u32[]{:S(2)}, u32[]{:S(2)}) collective-permute-start(bf16[32,4096]{1,0:T(8,128)(2,1)S(1)} %down_grad.2), channel_id=1, source_target_pairs={{0,4},{4,0},{1,5},{5,1},{2,6},{6,2},{3,7},{7,3},{8,12},{12,8},{9,1... | collective-permute-start | bytes 786440 | tf_op jit(solution)/shard_map/ppermute | solution.py:422
  57.5 24.3 %collective-permute-start.14 = (bf16[48,4096]{1,0:T(8,128)(2,1)S(1)}, bf16[48,4096]{1,0:T(8,128)(2,1)S(1)}, u32[]{:S(2)}, u32[]{:S(2)}) collective-permute-start(bf16[48,4096]{1,0:T(8,128)(2,1)S(1)} %get-tuple-element.49), channel_id=1, source_target_pairs={{0,8},{8,0},{16,24},{24,16},{32,40},{40,32},{48,56},{56,48},{64,72... | collective-permute-start | bytes 1179656 | tf_op jit(solution)/shard_map/ppermute | solution.py:41
  59.2 10.6 %collective-permute-start.19 = (bf16[48,4096]{1,0:T(8,128)(2,1)S(1)}, bf16[48,4096]{1,0:T(8,128)(2,1)S(1)}, u32[]{:S(2)}, u32[]{:S(2)}) collective-permute-start(bf16[48,4096]{1,0:T(8,128)(2,1)S(1)} %add_convert_fusion.2), channel_id=1, source_target_pairs={{0,132},{8,12},{16,148},{24,28},{32,164},{40,44},{48,180},{56,60},... | collective-permute-start | bytes 1179656 | tf_op jit(solution)/shard_map/ppermute | solution.py:41
  62.3 7.5 %collective-permute-start.18 = (bf16[48,4096]{1,0:T(8,128)(2,1)S(1)}, bf16[48,4096]{1,0:T(8,128)(2,1)S(1)}, u32[]{:S(2)}, u32[]{:S(2)}) collective-permute-start(bf16[48,4096]{1,0:T(8,128)(2,1)S(1)} %get-tuple-element.57), channel_id=1, source_target_pairs={{0,8},{8,0},{16,24},{24,16},{32,40},{40,32},{48,56},{56,48},{64,72... | collective-permute-start | bytes 1179656 | tf_op jit(solution)/shard_map/ppermute | solution.py:41
  66.7 1.8 %collective-permute-start.16 = (bf16[48,4096]{1,0:T(8,128)(2,1)S(1)}, bf16[48,4096]{1,0:T(8,128)(2,1)S(1)}, u32[]{:S(2)}, u32[]{:S(2)}) collective-permute-start(bf16[48,4096]{1,0:T(8,128)(2,1)S(1)} %get-tuple-element.55), channel_id=1, source_target_pairs={{0,8},{8,0},{16,24},{24,16},{32,40},{40,32},{48,56},{56,48},{64,72... | collective-permute-start | bytes 1179656 | tf_op jit(solution)/shard_map/ppermute | solution.py:41
  66.8 9.1 %collective-permute-start.22 = (bf16[32,4352]{1,0:T(8,128)(2,1)S(1)}, bf16[32,4352]{1,0:T(8,128)(2,1)S(1)}, u32[]{:S(2)}, u32[]{:S(2)}) collective-permute-start(bf16[32,4352]{1,0:T(8,128)(2,1)S(1)} %pad_maximum_fusion.1), channel_id=1, source_target_pairs={{0,1},{1,0},{2,3},{3,2},{4,5},{5,4},{6,7},{7,6},{8,9},{9,8},{10,11... | collective-permute-start | bytes 835592 | tf_op jit(solution)/shard_map/ppermute | solution.py:442
  68.6 12.6 %collective-permute-start.17 = (bf16[48,4096]{1,0:T(8,128)(2,1)S(1)}, bf16[48,4096]{1,0:T(8,128)(2,1)S(1)}, u32[]{:S(2)}, u32[]{:S(2)}) collective-permute-start(bf16[48,4096]{1,0:T(8,128)(2,1)S(1)} %add_convert_fusion.1), channel_id=1, source_target_pairs={{0,132},{8,12},{16,148},{24,28},{32,164},{40,44},{48,180},{56,60},... | collective-permute-start | bytes 1179656 | tf_op jit(solution)/shard_map/ppermute | solution.py:41
  70.0 11.9 %collective-permute-start.20 = (bf16[48,4096]{1,0:T(8,128)(2,1)S(1)}, bf16[48,4096]{1,0:T(8,128)(2,1)S(1)}, u32[]{:S(2)}, u32[]{:S(2)}) collective-permute-start(bf16[48,4096]{1,0:T(8,128)(2,1)S(1)} %add_convert_fusion), channel_id=1, source_target_pairs={{0,4},{8,140},{16,20},{24,156},{32,36},{40,172},{48,52},{56,188},{... | collective-permute-start | bytes 1179656 | tf_op jit(solution)/shard_map/ppermute | solution.py:41
  81.3 8.1 %collective-permute-start.23 = (bf16[32,4352]{1,0:T(8,128)(2,1)S(1)}, bf16[32,4352]{1,0:T(8,128)(2,1)S(1)}, u32[]{:S(2)}, u32[]{:S(2)}) collective-permute-start(bf16[32,4352]{1,0:T(8,128)(2,1)S(1)} %add_convert_fusion.4), channel_id=1, source_target_pairs={{0,3},{1,2},{2,1},{3,0},{4,7},{5,6},{6,5},{7,4},{8,11},{9,10},{10,... | collective-permute-start | bytes 835592 | tf_op jit(solution)/shard_map/ppermute | solution.py:447
  89.4 20.7 %collective-permute-start.31 = (bf16[32,4352]{1,0:T(8,128)(2,1)S(1)}, bf16[32,4352]{1,0:T(8,128)(2,1)S(1)}, u32[]{:S(2)}, u32[]{:S(2)}) collective-permute-start(bf16[32,4352]{1,0:T(8,128)(2,1)S(1)} %add_convert_fusion.3), channel_id=1, source_target_pairs={{0,4},{4,0},{1,5},{5,1},{2,6},{6,2},{3,7},{7,3},{8,12},{12,8},{9,1... | collective-permute-start | bytes 835592 | tf_op jit(solution)/shard_map/ppermute | solution.py:452
  89.6 9.2 %collective-permute-start.24 = (bf16[6,4096]{1,0:T(8,128)(2,1)S(1)}, bf16[6,4096]{1,0:T(8,128)(2,1)S(1)}, u32[]{:S(2)}, u32[]{:S(2)}) collective-permute-start(bf16[6,4096]{1,0:T(8,128)(2,1)S(1)} %get-tuple-element.73), channel_id=1, source_target_pairs={{0,64},{8,72},{16,80},{24,88},{32,96},{40,104},{48,112},{56,120},{... | collective-permute-start | bytes 147464 | tf_op jit(solution)/shard_map/ppermute | solution.py:41
  92.9 8.6 %collective-permute-start.25 = (bf16[6,4096]{1,0:T(8,128)(2,1)S(1)}, bf16[6,4096]{1,0:T(8,128)(2,1)S(1)}, u32[]{:S(2)}, u32[]{:S(2)}) collective-permute-start(bf16[6,4096]{1,0:T(8,128)(2,1)S(1)} %get-tuple-element.72), channel_id=1, source_target_pairs={{0,80},{8,88},{16,96},{24,104},{32,112},{40,120},{48,0},{56,8},{64... | collective-permute-start | bytes 147464 | tf_op jit(solution)/shard_map/ppermute | solution.py:41
  94.3 9.6 %collective-permute-start.26 = (bf16[6,4096]{1,0:T(8,128)(2,1)S(1)}, bf16[6,4096]{1,0:T(8,128)(2,1)S(1)}, u32[]{:S(2)}, u32[]{:S(2)}) collective-permute-start(bf16[6,4096]{1,0:T(8,128)(2,1)S(1)} %get-tuple-element.71), channel_id=1, source_target_pairs={{0,48},{8,56},{16,64},{24,72},{32,80},{40,88},{48,96},{56,104},{64... | collective-permute-start | bytes 147464 | tf_op jit(solution)/shard_map/ppermute | solution.py:41
  96.7 7.3 %collective-permute-start.27 = (bf16[6,4096]{1,0:T(8,128)(2,1)S(1)}, bf16[6,4096]{1,0:T(8,128)(2,1)S(1)}, u32[]{:S(2)}, u32[]{:S(2)}) collective-permute-start(bf16[6,4096]{1,0:T(8,128)(2,1)S(1)} %get-tuple-element.70), channel_id=1, source_target_pairs={{0,96},{8,104},{16,112},{24,120},{32,0},{40,8},{48,16},{56,24},{64... | collective-permute-start | bytes 147464 | tf_op jit(solution)/shard_map/ppermute | solution.py:41
  98.8 6.7 %collective-permute-start.28 = (bf16[6,4096]{1,0:T(8,128)(2,1)S(1)}, bf16[6,4096]{1,0:T(8,128)(2,1)S(1)}, u32[]{:S(2)}, u32[]{:S(2)}) collective-permute-start(bf16[6,4096]{1,0:T(8,128)(2,1)S(1)} %get-tuple-element.69), channel_id=1, source_target_pairs={{0,32},{8,40},{16,48},{24,56},{32,64},{40,72},{48,80},{56,88},{64,... | collective-permute-start | bytes 147464 | tf_op jit(solution)/shard_map/ppermute | solution.py:41
  101.5 4.7 %collective-permute-start.29 = (bf16[6,4096]{1,0:T(8,128)(2,1)S(1)}, bf16[6,4096]{1,0:T(8,128)(2,1)S(1)}, u32[]{:S(2)}, u32[]{:S(2)}) collective-permute-start(bf16[6,4096]{1,0:T(8,128)(2,1)S(1)} %get-tuple-element.68), channel_id=1, source_target_pairs={{0,112},{8,120},{16,0},{24,8},{32,16},{40,24},{48,32},{56,40},{64,... | collective-permute-start | bytes 147464 | tf_op jit(solution)/shard_map/ppermute | solution.py:41
  103.9 5.5 %collective-permute-start.30 = (bf16[6,4096]{1,0:T(8,128)(2,1)S(1)}, bf16[6,4096]{1,0:T(8,128)(2,1)S(1)}, u32[]{:S(2)}, u32[]{:S(2)}) collective-permute-start(bf16[6,4096]{1,0:T(8,128)(2,1)S(1)} %get-tuple-element.67), channel_id=1, source_target_pairs={{0,16},{8,24},{16,32},{24,40},{32,48},{40,56},{48,64},{56,72},{64,... | collective-permute-start | bytes 147464 | tf_op jit(solution)/shard_map/ppermute | solution.py:41
  (8 other events, 15.5 us)

commit v8 on v4

--- a/solution.py
+++ b/solution.py
@@ -111,6 +111,31 @@
         cost_estimate=cost(0, 2 * array.size),
         name="hold",
     )(ready, array)
+
+
+def finish_kernel(side_ref, mine_ref, facing_ref, down_ref, up_ref):
+    half, width = down_ref.shape[1] // 2, up_ref.shape[1] // 2
+    for ref, place in ((mine_ref, side_ref[0]), (facing_ref, 1 - side_ref[0])):
+        columns = pl.ds(pl.multiple_of(place * half, half), half)
+        down_ref[:, columns] = ref[:, :half].astype(F32)
+        columns = pl.ds(pl.multiple_of(place * width, width), width)
+        up_ref[:, columns] = ref[:, half:].astype(F32)
+
+
+def finish(side, mine, facing, half):
+    ranks, wide = mine.shape
+    return pl.pallas_call(
+        finish_kernel,
+        out_shape=[
+            jax.ShapeDtypeStruct((ranks, 2 * half), F32),
+            jax.ShapeDtypeStruct((ranks, 2 * (wide - half)), F32),
+        ],
+        in_specs=[SCALAR, VECTOR, VECTOR],
+        out_specs=[VECTOR] * 2,
+        compiler_params=ROOM,
+        cost_estimate=cost(0, 8 * mine.size),
+        name="finish",
+    )(side, mine, facing)
 
 
 def project_kernel(which_ref, *refs):
@@ -412,10 +437,7 @@
     for i, k in enumerate(SHIFTS):
         own_grad += move(low_base[i * count : (i + 1) * count], ALONG[NZ - k]).astype(F32)
 
-    left = jnp.where(side == 0, sums, facing).astype(F32)
-    right = jnp.where(side == 0, facing, sums).astype(F32)
-    down_total = jnp.concatenate([left[:, :half], right[:, :half]], 1)
-    up_total = jnp.concatenate([left[:, half:], right[:, half:]], 1)
+    down_total, up_total = finish(here, sums, facing, half)
     return (
         own_grad.reshape(vision_feature_states.shape),
         down_total.reshape(1, 2, ranks // 2, 2 * half),

time: 107 us -> 109 us (1.019)
  waiting for transfers between devices: 28.3 us -> 34.7 us
  starting transfers between devices: 47.9 us -> 44.5 us
  other arithmetic: 2.73 us -> 0.98 us
  Pallas kernels: 14 us -> 15.1 us
    ppermute x28, starting transfers between devices: 46.5 us -> 42.2 us  [move(): return lax.ppermute(block, PLANE, pairs)]
    ppermute x1, waiting for transfers between devices: 0.51 us -> 3.22 us  [per_device(): facing = lax.ppermute(sums, 'tensor', TENSOR_SWAP)]
    ppermute x1, waiting for transfers between devices: 1.33 us -> 3.69 us  [per_device(): far_sums = lax.ppermute(sums, 'dp', DP_FAR)]
    concatenate x2 -> x0, other arithmetic: 1.67 us -> none  [the longest x1 1.04 us: per_device(): down_total = jnp.concatenate([left[:, :half], right[:, :half]], 1)]
    ppermute x1, waiting for transfers between devices: 2.77 us -> 4.13 us  [per_device(): down_facing = lax.ppermute(down_other, 'tensor', TENSOR_SWAP)]
  transfers between devices with their start and end apart: 32 -> 32, of which waited for: 18 -> 12; matrix products, arithmetic and copies ran while one was open for 3% -> 3% of each run, Pallas kernels for 6% -> 6%
where the time goes in v8:
time: 109 us
  starting transfers between devices  44.5 us (41%)
  waiting for transfers between devices  34.7 us (32%)
  Pallas kernels  15.1 us (14%)
  local copies, waits for them, and re-layouts  12 us (11%)
  between operations  1.24 us (1%)
    ppermute x28, starting transfers between devices, move(): return lax.ppermute(block, PLANE, pairs)  42.2 us
    ppermute x28, waiting for transfers between devices, move(): return lax.ppermute(block, PLANE, pairs)  18.1 us
    unnamed x16, local copies, waits for them, and re-layouts  8.18 us
    ppermute x1, waiting for transfers between devices, per_device(): near_sums = lax.ppermute(sums, 'dp', DP_NEAR)  5.58 us
    ppermute x1, waiting for transfers between devices, per_device(): down_facing = lax.ppermute(down_other, 'tensor', TENSOR_SWAP)  4.13 us
    pallas_call x1, Pallas kernels, attend(): pl.pallas_call(attention_kernel, out_shape=[jax.ShapeDtypeStruct((rows, 2...  4.05 us
    pallas_call x2, Pallas kernels, feature_grad(): pl.pallas_call(feature_kernel, out_shape=[jax.ShapeDtypeStruct((rows // 4...  3.86 us
    ppermute x1, waiting for transfers between devices, per_device(): far_sums = lax.ppermute(sums, 'dp', DP_FAR)  3.69 us
  transfers between devices with their start and end apart: 32, of which 12 were waited for; matrix products, arithmetic and copies ran while one was open for 3% of the time, Pallas kernels for 6%

profile of v8, /device:TPU:24, one launch (start us, length us, event | category | flops | bytes accessed | tf_op | source)
XLA Modules:
  0.0 108.6 jit_solution(8383790550801406318)
XLA Ops:
  1.6 5.9 %collective-permute-start.6 = (bf16[6,4096]{1,0:T(8,128)(2,1)S(1)}, bf16[6,4096]{1,0:T(8,128)(2,1)S(1)}, u32[]{:S(2)}, u32[]{:S(2)}) collective-permute-start(bf16[6,4096]{1,0:T(8,128)(2,1)S(1)} %reshape.31), channel_id=1, source_target_pairs={{0,112},{8,120},{16,0},{24,8},{32,16},{40,24},{48,32},{56,40},{64,... | collective-permute-start | bytes 147464 | tf_op jit(solution)/shard_map/ppermute | solution.py:40
  7.5 2.5 %collective-permute-start.4 = (bf16[6,4096]{1,0:T(8,128)(2,1)S(1)}, bf16[6,4096]{1,0:T(8,128)(2,1)S(1)}, u32[]{:S(2)}, u32[]{:S(2)}) collective-permute-start(bf16[6,4096]{1,0:T(8,128)(2,1)S(1)} %reshape.31), channel_id=1, source_target_pairs={{0,96},{8,104},{16,112},{24,120},{32,0},{40,8},{48,16},{56,24},{64... | collective-permute-start | bytes 147464 | tf_op jit(solution)/shard_map/ppermute | solution.py:40
  10.5 2.9 %collective-permute-start.2 = (bf16[6,4096]{1,0:T(8,128)(2,1)S(1)}, bf16[6,4096]{1,0:T(8,128)(2,1)S(1)}, u32[]{:S(2)}, u32[]{:S(2)}) collective-permute-start(bf16[6,4096]{1,0:T(8,128)(2,1)S(1)} %reshape.31), channel_id=1, source_target_pairs={{0,80},{8,88},{16,96},{24,104},{32,112},{40,120},{48,0},{56,8},{64... | collective-permute-start | bytes 147464 | tf_op jit(solution)/shard_map/ppermute | solution.py:40
  14.3 3.9 %collective-permute-start = (bf16[6,4096]{1,0:T(8,128)(2,1)S(1)}, bf16[6,4096]{1,0:T(8,128)(2,1)S(1)}, u32[]{:S(2)}, u32[]{:S(2)}) collective-permute-start(bf16[6,4096]{1,0:T(8,128)(2,1)S(1)} %reshape.31), channel_id=1, source_target_pairs={{0,64},{8,72},{16,80},{24,88},{32,96},{40,104},{48,112},{56,120},{... | collective-permute-start | bytes 147464 | tf_op jit(solution)/shard_map/ppermute | solution.py:40
  18.2 3.9 %collective-permute-done.1 = bf16[6,4096]{1,0:T(8,128)(2,1)S(1)} collective-permute-done((bf16[6,4096]{1,0:T(8,128)(2,1)S(1)}, bf16[6,4096]{1,0:T(8,128)(2,1)S(1)}, u32[]{:S(2)}, u32[]{:S(2)}) %collective-permute-start.1) | collective-permute-done | bytes 49184 | tf_op jit(solution)/shard_map/ppermute | solution.py:40
  22.1 1.4 %collective-permute-done = bf16[6,4096]{1,0:T(8,128)(2,1)S(1)} collective-permute-done((bf16[6,4096]{1,0:T(8,128)(2,1)S(1)}, bf16[6,4096]{1,0:T(8,128)(2,1)S(1)}, u32[]{:S(2)}, u32[]{:S(2)}) %collective-permute-start) | collective-permute-done | bytes 49184 | tf_op jit(solution)/shard_map/ppermute | solution.py:40
  24.7 2.8 %collective-permute-start.10 = (bf16[48,4096]{1,0:T(8,128)(2,1)S(1)}, bf16[48,4096]{1,0:T(8,128)(2,1)S(1)}, u32[]{:S(2)}, u32[]{:S(2)}) collective-permute-start(bf16[48,4096]{1,0:T(8,128)(2,1)S(1)} %concatenate.16.refs_0_), channel_id=1, source_target_pairs={{0,132},{8,12},{16,148},{24,28},{32,164},{40,44},{48,180},{56,60},... | collective-permute-start | bytes 1179656 | tf_op jit(solution)/shard_map/ppermute | solution.py:40
  29.1 1.4 %copy-done.4 = bf16[1,3,128,2048]{3,2,1,0:T(8,128)(2,1)S(1)} copy-done((bf16[1,3,128,2048]{3,2,1,0:T(8,128)(2,1)S(1)}, bf16[1,3,128,2048]{3,2,1,0:T(8,128)(2,1)}, u32[]{:S(2)}) %copy-start.4) | copy-done | bytes 1572888
  30.5 1.4 %pair_queries.1.pair_ref = bf16[6,1024,256]{2,1,0:T(8,128)(2,1)S(1)} custom-call(bf16[2,128]{1,0:T(2,128)(2,1)S(1)} %bitcast.405, bf16[3,128,2048]{2,1,0:T(8,128)(2,1)S(1)} %bitcast.403, bf16[3,128,2048]{2,1,0:T(8,128)(2,1)S(1)} %bitcast.404), custom_call_target="tpu_custom_call" | custom-call | flops 200000000 | bytes 6291456 | tf_op jit(solution)/shard_map/pair_queries/pallas_call | solution.py:85
  32.0 3.4 %copy-done = bf16[1,2,8192,256]{3,2,1,0:T(8,128)(2,1)S(1)} copy-done((bf16[1,2,8192,256]{3,2,1,0:T(8,128)(2,1)S(1)}, bf16[1,2,8192,256]{3,2,1,0:T(8,128)(2,1)}, u32[]{:S(2)}) %copy-start) | copy-done | bytes 8388632
  37.1 1.2 %collective-permute-start.9 = (bf16[48,4096]{1,0:T(8,128)(2,1)S(1)}, bf16[48,4096]{1,0:T(8,128)(2,1)S(1)}, u32[]{:S(2)}, u32[]{:S(2)}) collective-permute-start(bf16[48,4096]{1,0:T(8,128)(2,1)S(1)} %collective-permute-done.8.ready_ref.refs_0_), channel_id=1, source_target_pairs={{0,132},{8,12},{16,148},{24,28},{32,164},{40,44},{48,180},{56,60},... | collective-permute-start | bytes 1179656 | tf_op jit(solution)/shard_map/ppermute | solution.py:40
  38.3 3.4 %copy-done.1 = bf16[1,2,8192,256]{3,2,1,0:T(8,128)(2,1)S(1)} copy-done((bf16[1,2,8192,256]{3,2,1,0:T(8,128)(2,1)S(1)}, bf16[1,2,8192,256]{3,2,1,0:T(8,128)(2,1)}, u32[]{:S(2)}) %copy-start.1) | copy-done | bytes 8388632
  42.3 1.4 %project.4 = (f32[2,192,256]{2,1,0:T(8,128)S(1)}, f32[192,32]{1,0:T(8,128)S(1)}) custom-call(s32[1]{0:T(128)S(6)} %sub.44.which_ref, bf16[48,4096]{1,0:T(8,128)(2,1)S(1)} %collective-permute-done.8.ready_ref.refs_0_, bf16[48,4096]{1,0:T(8,128)(2,1)S(1)} %collective-permute-done.10.refs_1_, bf16[48,4096]{1,0:T(8,128)(2,1)S(1)} %collective-permute-done.11.refs_2_, ...), custom_call_target="tpu_custom_call" | custom-call | flops 805306368 | bytes 5767168 | tf_op jit(solution)/shard_map/project/pallas_call | solution.py:159
  43.7 2.4 %collective-permute-done.9.refs_0_.refs_2_ = bf16[48,4096]{1,0:T(8,128)(2,1)S(1)} collective-permute-done((bf16[48,4096]{1,0:T(8,128)(2,1)S(1)}, bf16[48,4096]{1,0:T(8,128)(2,1)S(1)}, u32[]{:S(2)}, u32[]{:S(2)}) %collective-permute-start.9) | collective-permute-done | bytes 393248 | tf_op jit(solution)/shard_map/ppermute | solution.py:40
  46.1 1.7 %collective-permute-done.13.refs_1_.refs_3_ = bf16[48,4096]{1,0:T(8,128)(2,1)S(1)} collective-permute-done((bf16[48,4096]{1,0:T(8,128)(2,1)S(1)}, bf16[48,4096]{1,0:T(8,128)(2,1)S(1)}, u32[]{:S(2)}, u32[]{:S(2)}) %collective-permute-start.13) | collective-permute-done | bytes 393248 | tf_op jit(solution)/shard_map/ppermute | solution.py:40
  48.8 4.1 %attend.1 = (bf16[192,512]{1,0:T(8,128)(2,1)S(1)}, bf16[192,32]{1,0:T(8,128)(2,1)S(1)}, bf16[192,512]{1,0:T(8,128)(2,1)S(1)}, bf16[192,32]{1,0:T(8,128)(2,1)S(1)}, f32[32,256]{1,0:T(8,128)S(1)}) custom-call(s32[3]{0:T(128)S(1)} %copy-done.6, s32[3]{0:T(128)S(1)} %copy-done.7, f32[2,96,256]{2,1,0:T(8,128)S(1)} %get-tuple-element.35.y0, ...), custom_call_target="tpu_custom_call" | custom-call | flops 1000000000 | bytes 3145728 | tf_op jit(solution)/shard_map/attend/pallas_call | solution.py:256
  53.3 1.9 %feature_grad.2 = (bf16[48,4096]{1,0:T(8,128)(2,1)S(1)}, bf16[48,4096]{1,0:T(8,128)(2,1)S(1)}, bf16[48,4096]{1,0:T(8,128)(2,1)S(1)}, bf16[48,4096]{1,0:T(8,128)(2,1)S(1)}) custom-call(s32[1]{0:T(128)} %bitcast.which_ref.side_ref, bf16[192,512]{1,0:T(8,128)(2,1)S(1)} %get-tuple-element.48.g_ref, bf16[192,32]{1,0:T(8,128)(2,1)S(1)} %get-tuple-element.49.m_ref, ...), custom_call_target="tpu_custom_call" | custom-call | flops 805306368 | bytes 5767168 | tf_op jit(solution)/shard_map/feature_grad/pallas_call | solution.py:289
  57.1 1.3 %collective-permute-start.19 = (bf16[48,4096]{1,0:T(8,128)(2,1)S(1)}, bf16[48,4096]{1,0:T(8,128)(2,1)S(1)}, u32[]{:S(2)}, u32[]{:S(2)}) collective-permute-start(bf16[48,4096]{1,0:T(8,128)(2,1)S(1)} %add_convert_fusion.2), channel_id=1, source_target_pairs={{0,132},{8,12},{16,148},{24,28},{32,164},{40,44},{48,180},{56,60},... | collective-permute-start | bytes 1179656 | tf_op jit(solution)/shard_map/ppermute | solution.py:40
  58.4 1.9 %feature_grad.3 = (bf16[48,4096]{1,0:T(8,128)(2,1)S(1)}, bf16[48,4096]{1,0:T(8,128)(2,1)S(1)}, bf16[48,4096]{1,0:T(8,128)(2,1)S(1)}, bf16[48,4096]{1,0:T(8,128)(2,1)S(1)}) custom-call(s32[1]{0:T(128)S(6)} %sub.44.which_ref, bf16[192,512]{1,0:T(8,128)(2,1)S(1)} %get-tuple-element.55.g_ref, bf16[192,32]{1,0:T(8,128)(2,1)S(1)} %get-tuple-element.47.m_ref, ...), custom_call_target="tpu_custom_call" | custom-call | flops 805306368 | bytes 5767168 | tf_op jit(solution)/shard_map/feature_grad/pallas_call | solution.py:289
  60.5 4.1 %collective-permute-done.21 = bf16[32,4096]{1,0:T(8,128)(2,1)S(1)} collective-permute-done((bf16[32,4096]{1,0:T(8,128)(2,1)S(1)}, bf16[32,4096]{1,0:T(8,128)(2,1)S(1)}, u32[]{:S(2)}, u32[]{:S(2)}) %collective-permute-start.21) | collective-permute-done | bytes 262176 | tf_op jit(solution)/shard_map/ppermute | solution.py:404
  66.5 1.5 %collective-permute-start.17 = (bf16[48,4096]{1,0:T(8,128)(2,1)S(1)}, bf16[48,4096]{1,0:T(8,128)(2,1)S(1)}, u32[]{:S(2)}, u32[]{:S(2)}) collective-permute-start(bf16[48,4096]{1,0:T(8,128)(2,1)S(1)} %add_convert_fusion.1), channel_id=1, source_target_pairs={{0,132},{8,12},{16,148},{24,28},{32,164},{40,44},{48,180},{56,60},... | collective-permute-start | bytes 1179656 | tf_op jit(solution)/shard_map/ppermute | solution.py:40
  68.3 5.6 %collective-permute-done.22 = bf16[32,4352]{1,0:T(8,128)(2,1)S(1)} collective-permute-done((bf16[32,4352]{1,0:T(8,128)(2,1)S(1)}, bf16[32,4352]{1,0:T(8,128)(2,1)S(1)}, u32[]{:S(2)}, u32[]{:S(2)}) %collective-permute-start.22) | collective-permute-done | bytes 278560 | tf_op jit(solution)/shard_map/ppermute | solution.py:424
  74.3 5.3 %collective-permute-done.17 = bf16[48,4096]{1,0:T(8,128)(2,1)S(1)} collective-permute-done((bf16[48,4096]{1,0:T(8,128)(2,1)S(1)}, bf16[48,4096]{1,0:T(8,128)(2,1)S(1)}, u32[]{:S(2)}, u32[]{:S(2)}) %collective-permute-start.17) | collective-permute-done | bytes 393248 | tf_op jit(solution)/shard_map/ppermute | solution.py:40
  79.9 3.7 %collective-permute-done.23 = bf16[32,4352]{1,0:T(8,128)(2,1)S(1)} collective-permute-done((bf16[32,4352]{1,0:T(8,128)(2,1)S(1)}, bf16[32,4352]{1,0:T(8,128)(2,1)S(1)}, u32[]{:S(2)}, u32[]{:S(2)}) %collective-permute-start.23) | collective-permute-done | bytes 278560 | tf_op jit(solution)/shard_map/ppermute | solution.py:429
  83.7 4.8 %collective-permute-start.24 = (bf16[6,4096]{1,0:T(8,128)(2,1)S(1)}, bf16[6,4096]{1,0:T(8,128)(2,1)S(1)}, u32[]{:S(2)}, u32[]{:S(2)}) collective-permute-start(bf16[6,4096]{1,0:T(8,128)(2,1)S(1)} %get-tuple-element.69), channel_id=1, source_target_pairs={{0,64},{8,72},{16,80},{24,88},{32,96},{40,104},{48,112},{56,120},{... | collective-permute-start | bytes 147464 | tf_op jit(solution)/shard_map/ppermute | solution.py:40
  88.6 3.2 %collective-permute-start.29 = (bf16[6,4096]{1,0:T(8,128)(2,1)S(1)}, bf16[6,4096]{1,0:T(8,128)(2,1)S(1)}, u32[]{:S(2)}, u32[]{:S(2)}) collective-permute-start(bf16[6,4096]{1,0:T(8,128)(2,1)S(1)} %get-tuple-element.71), channel_id=1, source_target_pairs={{0,112},{8,120},{16,0},{24,8},{32,16},{40,24},{48,32},{56,40},{64,... | collective-permute-start | bytes 147464 | tf_op jit(solution)/shard_map/ppermute | solution.py:40
  92.6 3.3 %collective-permute-start.27 = (bf16[6,4096]{1,0:T(8,128)(2,1)S(1)}, bf16[6,4096]{1,0:T(8,128)(2,1)S(1)}, u32[]{:S(2)}, u32[]{:S(2)}) collective-permute-start(bf16[6,4096]{1,0:T(8,128)(2,1)S(1)} %get-tuple-element.73), channel_id=1, source_target_pairs={{0,96},{8,104},{16,112},{24,120},{32,0},{40,8},{48,16},{56,24},{64... | collective-permute-start | bytes 147464 | tf_op jit(solution)/shard_map/ppermute | solution.py:40
  95.9 1.1 %collective-permute-start.26 = (bf16[6,4096]{1,0:T(8,128)(2,1)S(1)}, bf16[6,4096]{1,0:T(8,128)(2,1)S(1)}, u32[]{:S(2)}, u32[]{:S(2)}) collective-permute-start(bf16[6,4096]{1,0:T(8,128)(2,1)S(1)} %get-tuple-element.74), channel_id=1, source_target_pairs={{0,48},{8,56},{16,64},{24,72},{32,80},{40,88},{48,96},{56,104},{64... | collective-permute-start | bytes 147464 | tf_op jit(solution)/shard_map/ppermute | solution.py:40
  97.0 3.9 %collective-permute-start.25 = (bf16[6,4096]{1,0:T(8,128)(2,1)S(1)}, bf16[6,4096]{1,0:T(8,128)(2,1)S(1)}, u32[]{:S(2)}, u32[]{:S(2)}) collective-permute-start(bf16[6,4096]{1,0:T(8,128)(2,1)S(1)} %get-tuple-element.75), channel_id=1, source_target_pairs={{0,80},{8,88},{16,96},{24,104},{32,112},{40,120},{48,0},{56,8},{64... | collective-permute-start | bytes 147464 | tf_op jit(solution)/shard_map/ppermute | solution.py:40
  101.6 2.0 %collective-permute-done.26 = bf16[6,4096]{1,0:T(8,128)(2,1)S(1)} collective-permute-done((bf16[6,4096]{1,0:T(8,128)(2,1)S(1)}, bf16[6,4096]{1,0:T(8,128)(2,1)S(1)}, u32[]{:S(2)}, u32[]{:S(2)}) %collective-permute-start.26) | collective-permute-done | bytes 49184 | tf_op jit(solution)/shard_map/ppermute | solution.py:40
  104.3 3.2 %collective-permute-done.31.facing_ref = bf16[32,4352]{1,0:T(8,128)(2,1)S(1)} collective-permute-done((bf16[32,4352]{1,0:T(8,128)(2,1)S(1)}, bf16[32,4352]{1,0:T(8,128)(2,1)S(1)}, u32[]{:S(2)}, u32[]{:S(2)}) %collective-permute-start.31) | collective-permute-done | bytes 278560 | tf_op jit(solution)/shard_map/ppermute | solution.py:434
  107.5 1.0 finish.1
  (78 shorter events, 15.7 us)
Async XLA Ops:
  1.6 11.8 %collective-permute-start.6 = (bf16[6,4096]{1,0:T(8,128)(2,1)S(1)}, bf16[6,4096]{1,0:T(8,128)(2,1)S(1)}, u32[]{:S(2)}, u32[]{:S(2)}) collective-permute-start(bf16[6,4096]{1,0:T(8,128)(2,1)S(1)} %reshape.31), channel_id=1, source_target_pairs={{0,112},{8,120},{16,0},{24,8},{32,16},{40,24},{48,32},{56,40},{64,... | collective-permute-start | bytes 147464 | tf_op jit(solution)/shard_map/ppermute | solution.py:40
  7.5 6.8 %collective-permute-start.5 = (bf16[6,4096]{1,0:T(8,128)(2,1)S(1)}, bf16[6,4096]{1,0:T(8,128)(2,1)S(1)}, u32[]{:S(2)}, u32[]{:S(2)}) collective-permute-start(bf16[6,4096]{1,0:T(8,128)(2,1)S(1)} %reshape.31), channel_id=1, source_target_pairs={{0,16},{8,24},{16,32},{24,40},{32,48},{40,56},{48,64},{56,72},{64,... | collective-permute-start | bytes 147464 | tf_op jit(solution)/shard_map/ppermute | solution.py:40
  7.5 10.6 %collective-permute-start.4 = (bf16[6,4096]{1,0:T(8,128)(2,1)S(1)}, bf16[6,4096]{1,0:T(8,128)(2,1)S(1)}, u32[]{:S(2)}, u32[]{:S(2)}) collective-permute-start(bf16[6,4096]{1,0:T(8,128)(2,1)S(1)} %reshape.31), channel_id=1, source_target_pairs={{0,96},{8,104},{16,112},{24,120},{32,0},{40,8},{48,16},{56,24},{64... | collective-permute-start | bytes 147464 | tf_op jit(solution)/shard_map/ppermute | solution.py:40
  10.0 8.2 %collective-permute-start.3 = (bf16[6,4096]{1,0:T(8,128)(2,1)S(1)}, bf16[6,4096]{1,0:T(8,128)(2,1)S(1)}, u32[]{:S(2)}, u32[]{:S(2)}) collective-permute-start(bf16[6,4096]{1,0:T(8,128)(2,1)S(1)} %reshape.31), channel_id=1, source_target_pairs={{0,32},{8,40},{16,48},{24,56},{32,64},{40,72},{48,80},{56,88},{64,... | collective-permute-start | bytes 147464 | tf_op jit(solution)/shard_map/ppermute | solution.py:40
  10.5 7.7 %collective-permute-start.2 = (bf16[6,4096]{1,0:T(8,128)(2,1)S(1)}, bf16[6,4096]{1,0:T(8,128)(2,1)S(1)}, u32[]{:S(2)}, u32[]{:S(2)}) collective-permute-start(bf16[6,4096]{1,0:T(8,128)(2,1)S(1)} %reshape.31), channel_id=1, source_target_pairs={{0,80},{8,88},{16,96},{24,104},{32,112},{40,120},{48,0},{56,8},{64... | collective-permute-start | bytes 147464 | tf_op jit(solution)/shard_map/ppermute | solution.py:40
  13.4 8.7 %collective-permute-start.1 = (bf16[6,4096]{1,0:T(8,128)(2,1)S(1)}, bf16[6,4096]{1,0:T(8,128)(2,1)S(1)}, u32[]{:S(2)}, u32[]{:S(2)}) collective-permute-start(bf16[6,4096]{1,0:T(8,128)(2,1)S(1)} %reshape.31), channel_id=1, source_target_pairs={{0,48},{8,56},{16,64},{24,72},{32,80},{40,88},{48,96},{56,104},{64... | collective-permute-start | bytes 147464 | tf_op jit(solution)/shard_map/ppermute | solution.py:40
  14.3 9.2 %collective-permute-start = (bf16[6,4096]{1,0:T(8,128)(2,1)S(1)}, bf16[6,4096]{1,0:T(8,128)(2,1)S(1)}, u32[]{:S(2)}, u32[]{:S(2)}) collective-permute-start(bf16[6,4096]{1,0:T(8,128)(2,1)S(1)} %reshape.31), channel_id=1, source_target_pairs={{0,64},{8,72},{16,80},{24,88},{32,96},{40,104},{48,112},{56,120},{... | collective-permute-start | bytes 147464 | tf_op jit(solution)/shard_map/ppermute | solution.py:40
  24.7 11.7 %collective-permute-start.10 = (bf16[48,4096]{1,0:T(8,128)(2,1)S(1)}, bf16[48,4096]{1,0:T(8,128)(2,1)S(1)}, u32[]{:S(2)}, u32[]{:S(2)}) collective-permute-start(bf16[48,4096]{1,0:T(8,128)(2,1)S(1)} %concatenate.16.refs_0_), channel_id=1, source_target_pairs={{0,132},{8,12},{16,148},{24,28},{32,164},{40,44},{48,180},{56,60},... | collective-permute-start | bytes 1179656 | tf_op jit(solution)/shard_map/ppermute | solution.py:40
  27.5 8.9 %collective-permute-start.8 = (bf16[48,4096]{1,0:T(8,128)(2,1)S(1)}, bf16[48,4096]{1,0:T(8,128)(2,1)S(1)}, u32[]{:S(2)}, u32[]{:S(2)}) collective-permute-start(bf16[48,4096]{1,0:T(8,128)(2,1)S(1)} %concatenate.16.refs_0_), channel_id=1, source_target_pairs={{0,4},{8,140},{16,20},{24,156},{32,36},{40,172},{48,52},{56,188},{... | collective-permute-start | bytes 1179656 | tf_op jit(solution)/shard_map/ppermute | solution.py:40
  27.7 4.2 %collective-permute-start.7 = (bf16[48,4096]{1,0:T(8,128)(2,1)S(1)}, bf16[48,4096]{1,0:T(8,128)(2,1)S(1)}, u32[]{:S(2)}, u32[]{:S(2)}) collective-permute-start(bf16[48,4096]{1,0:T(8,128)(2,1)S(1)} %concatenate.16.refs_0_), channel_id=1, source_target_pairs={{0,8},{8,0},{16,24},{24,16},{32,40},{40,32},{48,56},{56,48},{64,72... | collective-permute-start | bytes 1179656 | tf_op jit(solution)/shard_map/ppermute | solution.py:40
  36.4 5.9 %collective-permute-start.12 = (bf16[48,4096]{1,0:T(8,128)(2,1)S(1)}, bf16[48,4096]{1,0:T(8,128)(2,1)S(1)}, u32[]{:S(2)}, u32[]{:S(2)}) collective-permute-start(bf16[48,4096]{1,0:T(8,128)(2,1)S(1)} %collective-permute-done.10.refs_1_), channel_id=1, source_target_pairs={{0,8},{8,0},{16,24},{24,16},{32,40},{40,32},{48,56},{56,48},{64,72... | collective-permute-start | bytes 1179656 | tf_op jit(solution)/shard_map/ppermute | solution.py:40
  37.0 5.3 %collective-permute-start.11 = (bf16[48,4096]{1,0:T(8,128)(2,1)S(1)}, bf16[48,4096]{1,0:T(8,128)(2,1)S(1)}, u32[]{:S(2)}, u32[]{:S(2)}) collective-permute-start(bf16[48,4096]{1,0:T(8,128)(2,1)S(1)} %collective-permute-done.8.ready_ref.refs_0_), channel_id=1, source_target_pairs={{0,8},{8,0},{16,24},{24,16},{32,40},{40,32},{48,56},{56,48},{64,72... | collective-permute-start | bytes 1179656 | tf_op jit(solution)/shard_map/ppermute | solution.py:40
  37.1 9.0 %collective-permute-start.9 = (bf16[48,4096]{1,0:T(8,128)(2,1)S(1)}, bf16[48,4096]{1,0:T(8,128)(2,1)S(1)}, u32[]{:S(2)}, u32[]{:S(2)}) collective-permute-start(bf16[48,4096]{1,0:T(8,128)(2,1)S(1)} %collective-permute-done.8.ready_ref.refs_0_), channel_id=1, source_target_pairs={{0,132},{8,12},{16,148},{24,28},{32,164},{40,44},{48,180},{56,60},... | collective-permute-start | bytes 1179656 | tf_op jit(solution)/shard_map/ppermute | solution.py:40
  46.1 1.7 %collective-permute-start.13 = (bf16[48,4096]{1,0:T(8,128)(2,1)S(1)}, bf16[48,4096]{1,0:T(8,128)(2,1)S(1)}, u32[]{:S(2)}, u32[]{:S(2)}) collective-permute-start(bf16[48,4096]{1,0:T(8,128)(2,1)S(1)} %collective-permute-done.9.refs_0_.refs_2_), channel_id=1, source_target_pairs={{0,8},{8,0},{16,24},{24,16},{32,40},{40,32},{48,56},{56,48},{64,72... | collective-permute-start | bytes 1179656 | tf_op jit(solution)/shard_map/ppermute | solution.py:40
  55.2 1.8 %collective-permute-start.15 = (bf16[48,4096]{1,0:T(8,128)(2,1)S(1)}, bf16[48,4096]{1,0:T(8,128)(2,1)S(1)}, u32[]{:S(2)}, u32[]{:S(2)}) collective-permute-start(bf16[48,4096]{1,0:T(8,128)(2,1)S(1)} %get-tuple-element.54), channel_id=1, source_target_pairs={{0,8},{8,0},{16,24},{24,16},{32,40},{40,32},{48,56},{56,48},{64,72... | collective-permute-start | bytes 1179656 | tf_op jit(solution)/shard_map/ppermute | solution.py:40
  55.4 9.1 %collective-permute-start.21 = (bf16[32,4096]{1,0:T(8,128)(2,1)S(1)}, bf16[32,4096]{1,0:T(8,128)(2,1)S(1)}, u32[]{:S(2)}, u32[]{:S(2)}) collective-permute-start(bf16[32,4096]{1,0:T(8,128)(2,1)S(1)} %down_grad.2), channel_id=1, source_target_pairs={{0,4},{4,0},{1,5},{5,1},{2,6},{6,2},{3,7},{7,3},{8,12},{12,8},{9,1... | collective-permute-start | bytes 786440 | tf_op jit(solution)/shard_map/ppermute | solution.py:404
  56.1 18.3 %collective-permute-start.14 = (bf16[48,4096]{1,0:T(8,128)(2,1)S(1)}, bf16[48,4096]{1,0:T(8,128)(2,1)S(1)}, u32[]{:S(2)}, u32[]{:S(2)}) collective-permute-start(bf16[48,4096]{1,0:T(8,128)(2,1)S(1)} %get-tuple-element.51), channel_id=1, source_target_pairs={{0,8},{8,0},{16,24},{24,16},{32,40},{40,32},{48,56},{56,48},{64,72... | collective-permute-start | bytes 1179656 | tf_op jit(solution)/shard_map/ppermute | solution.py:40
  57.1 11.0 %collective-permute-start.19 = (bf16[48,4096]{1,0:T(8,128)(2,1)S(1)}, bf16[48,4096]{1,0:T(8,128)(2,1)S(1)}, u32[]{:S(2)}, u32[]{:S(2)}) collective-permute-start(bf16[48,4096]{1,0:T(8,128)(2,1)S(1)} %add_convert_fusion.2), channel_id=1, source_target_pairs={{0,132},{8,12},{16,148},{24,28},{32,164},{40,44},{48,180},{56,60},... | collective-permute-start | bytes 1179656 | tf_op jit(solution)/shard_map/ppermute | solution.py:40
  60.4 7.7 %collective-permute-start.18 = (bf16[48,4096]{1,0:T(8,128)(2,1)S(1)}, bf16[48,4096]{1,0:T(8,128)(2,1)S(1)}, u32[]{:S(2)}, u32[]{:S(2)}) collective-permute-start(bf16[48,4096]{1,0:T(8,128)(2,1)S(1)} %get-tuple-element.59), channel_id=1, source_target_pairs={{0,8},{8,0},{16,24},{24,16},{32,40},{40,32},{48,56},{56,48},{64,72... | collective-permute-start | bytes 1179656 | tf_op jit(solution)/shard_map/ppermute | solution.py:40
  64.6 1.8 %collective-permute-start.16 = (bf16[48,4096]{1,0:T(8,128)(2,1)S(1)}, bf16[48,4096]{1,0:T(8,128)(2,1)S(1)}, u32[]{:S(2)}, u32[]{:S(2)}) collective-permute-start(bf16[48,4096]{1,0:T(8,128)(2,1)S(1)} %get-tuple-element.57), channel_id=1, source_target_pairs={{0,8},{8,0},{16,24},{24,16},{32,40},{40,32},{48,56},{56,48},{64,72... | collective-permute-start | bytes 1179656 | tf_op jit(solution)/shard_map/ppermute | solution.py:40
  64.8 9.1 %collective-permute-start.22 = (bf16[32,4352]{1,0:T(8,128)(2,1)S(1)}, bf16[32,4352]{1,0:T(8,128)(2,1)S(1)}, u32[]{:S(2)}, u32[]{:S(2)}) collective-permute-start(bf16[32,4352]{1,0:T(8,128)(2,1)S(1)} %pad_maximum_fusion), channel_id=1, source_target_pairs={{0,1},{1,0},{2,3},{3,2},{4,5},{5,4},{6,7},{7,6},{8,9},{9,8},{10,11... | collective-permute-start | bytes 835592 | tf_op jit(solution)/shard_map/ppermute | solution.py:424
  66.5 13.1 %collective-permute-start.17 = (bf16[48,4096]{1,0:T(8,128)(2,1)S(1)}, bf16[48,4096]{1,0:T(8,128)(2,1)S(1)}, u32[]{:S(2)}, u32[]{:S(2)}) collective-permute-start(bf16[48,4096]{1,0:T(8,128)(2,1)S(1)} %add_convert_fusion.1), channel_id=1, source_target_pairs={{0,132},{8,12},{16,148},{24,28},{32,164},{40,44},{48,180},{56,60},... | collective-permute-start | bytes 1179656 | tf_op jit(solution)/shard_map/ppermute | solution.py:40
  68.2 11.4 %collective-permute-start.20 = (bf16[48,4096]{1,0:T(8,128)(2,1)S(1)}, bf16[48,4096]{1,0:T(8,128)(2,1)S(1)}, u32[]{:S(2)}, u32[]{:S(2)}) collective-permute-start(bf16[48,4096]{1,0:T(8,128)(2,1)S(1)} %add_convert_fusion), channel_id=1, source_target_pairs={{0,4},{8,140},{16,20},{24,156},{32,36},{40,172},{48,52},{56,188},{... | collective-permute-start | bytes 1179656 | tf_op jit(solution)/shard_map/ppermute | solution.py:40
  74.0 9.6 %collective-permute-start.23 = (bf16[32,4352]{1,0:T(8,128)(2,1)S(1)}, bf16[32,4352]{1,0:T(8,128)(2,1)S(1)}, u32[]{:S(2)}, u32[]{:S(2)}) collective-permute-start(bf16[32,4352]{1,0:T(8,128)(2,1)S(1)} %add_convert_fusion.4), channel_id=1, source_target_pairs={{0,3},{1,2},{2,1},{3,0},{4,7},{5,6},{6,5},{7,4},{8,11},{9,10},{10,... | collective-permute-start | bytes 835592 | tf_op jit(solution)/shard_map/ppermute | solution.py:429
  83.7 12.2 %collective-permute-start.24 = (bf16[6,4096]{1,0:T(8,128)(2,1)S(1)}, bf16[6,4096]{1,0:T(8,128)(2,1)S(1)}, u32[]{:S(2)}, u32[]{:S(2)}) collective-permute-start(bf16[6,4096]{1,0:T(8,128)(2,1)S(1)} %get-tuple-element.69), channel_id=1, source_target_pairs={{0,64},{8,72},{16,80},{24,88},{32,96},{40,104},{48,112},{56,120},{... | collective-permute-start | bytes 147464 | tf_op jit(solution)/shard_map/ppermute | solution.py:40
  88.6 8.5 %collective-permute-start.30 = (bf16[6,4096]{1,0:T(8,128)(2,1)S(1)}, bf16[6,4096]{1,0:T(8,128)(2,1)S(1)}, u32[]{:S(2)}, u32[]{:S(2)}) collective-permute-start(bf16[6,4096]{1,0:T(8,128)(2,1)S(1)} %get-tuple-element.70), channel_id=1, source_target_pairs={{0,16},{8,24},{16,32},{24,40},{32,48},{40,56},{48,64},{56,72},{64,... | collective-permute-start | bytes 147464 | tf_op jit(solution)/shard_map/ppermute | solution.py:40
  88.6 12.4 %collective-permute-start.29 = (bf16[6,4096]{1,0:T(8,128)(2,1)S(1)}, bf16[6,4096]{1,0:T(8,128)(2,1)S(1)}, u32[]{:S(2)}, u32[]{:S(2)}) collective-permute-start(bf16[6,4096]{1,0:T(8,128)(2,1)S(1)} %get-tuple-element.71), channel_id=1, source_target_pairs={{0,112},{8,120},{16,0},{24,8},{32,16},{40,24},{48,32},{56,40},{64,... | collective-permute-start | bytes 147464 | tf_op jit(solution)/shard_map/ppermute | solution.py:40
  91.8 9.8 %collective-permute-start.28 = (bf16[6,4096]{1,0:T(8,128)(2,1)S(1)}, bf16[6,4096]{1,0:T(8,128)(2,1)S(1)}, u32[]{:S(2)}, u32[]{:S(2)}) collective-permute-start(bf16[6,4096]{1,0:T(8,128)(2,1)S(1)} %get-tuple-element.72), channel_id=1, source_target_pairs={{0,32},{8,40},{16,48},{24,56},{32,64},{40,72},{48,80},{56,88},{64,... | collective-permute-start | bytes 147464 | tf_op jit(solution)/shard_map/ppermute | solution.py:40
  92.6 8.9 %collective-permute-start.27 = (bf16[6,4096]{1,0:T(8,128)(2,1)S(1)}, bf16[6,4096]{1,0:T(8,128)(2,1)S(1)}, u32[]{:S(2)}, u32[]{:S(2)}) collective-permute-start(bf16[6,4096]{1,0:T(8,128)(2,1)S(1)} %get-tuple-element.73), channel_id=1, source_target_pairs={{0,96},{8,104},{16,112},{24,120},{32,0},{40,8},{48,16},{56,24},{64... | collective-permute-start | bytes 147464 | tf_op jit(solution)/shard_map/ppermute | solution.py:40
  95.9 7.6 %collective-permute-start.26 = (bf16[6,4096]{1,0:T(8,128)(2,1)S(1)}, bf16[6,4096]{1,0:T(8,128)(2,1)S(1)}, u32[]{:S(2)}, u32[]{:S(2)}) collective-permute-start(bf16[6,4096]{1,0:T(8,128)(2,1)S(1)} %get-tuple-element.74), channel_id=1, source_target_pairs={{0,48},{8,56},{16,64},{24,72},{32,80},{40,88},{48,96},{56,104},{64... | collective-permute-start | bytes 147464 | tf_op jit(solution)/shard_map/ppermute | solution.py:40
  97.0 6.5 %collective-permute-start.25 = (bf16[6,4096]{1,0:T(8,128)(2,1)S(1)}, bf16[6,4096]{1,0:T(8,128)(2,1)S(1)}, u32[]{:S(2)}, u32[]{:S(2)}) collective-permute-start(bf16[6,4096]{1,0:T(8,128)(2,1)S(1)} %get-tuple-element.75), channel_id=1, source_target_pairs={{0,80},{8,88},{16,96},{24,104},{32,112},{40,120},{48,0},{56,8},{64... | collective-permute-start | bytes 147464 | tf_op jit(solution)/shard_map/ppermute | solution.py:40
  101.0 6.5 %collective-permute-start.31 = (bf16[32,4352]{1,0:T(8,128)(2,1)S(1)}, bf16[32,4352]{1,0:T(8,128)(2,1)S(1)}, u32[]{:S(2)}, u32[]{:S(2)}) collective-permute-start(bf16[32,4352]{1,0:T(8,128)(2,1)S(1)} %add_convert_fusion.3.mine_ref), channel_id=1, source_target_pairs={{0,4},{4,0},{1,5},{5,1},{2,6},{6,2},{3,7},{7,3},{8,12},{12,8},{9,1... | collective-permute-start | bytes 835592 | tf_op jit(solution)/shard_map/ppermute | solution.py:434
  (8 other events, 71.9 us)

commit v9 on v8

--- a/solution.py
+++ b/solution.py
@@ -172,7 +172,7 @@
 
 def attention_kernel(
     count_ref, start_ref, y0, y1, y2, r0, r1, r2, own_map, other_map, own_back, other_back,
-    up_diagonal, gains_ref, pair_ref, g_own, m_own, g_other, m_other, up_ref, grad_ref,
+    up_diagonal, gains_ref, pair_ref, g_own, m_own, g_other, m_other, middle_ref, up_ref, grad_ref,
 ):
     width = y0.shape[2]
     head = gains_ref.shape[1]
@@ -239,6 +239,7 @@
             ].astype(LOW)
     grad = grad_ref[...]
     middle = dot(grad, up_diagonal[...], NT).astype(LOW)
+    middle_ref[...] = (ADAPTER_SCALE * middle.astype(F32)).astype(LOW)
     up = ADAPTER_SCALE * dot(reduced, grad, TN)
     for part in range(2):
         half = slice(part * ranks // 2, (part + 1) * ranks // 2)
@@ -260,10 +261,11 @@
             jax.ShapeDtypeStruct((rows, ranks), LOW),
             jax.ShapeDtypeStruct((rows, 2 * width), LOW),
             jax.ShapeDtypeStruct((rows, ranks), LOW),
+            jax.ShapeDtypeStruct((rows, ranks), LOW),
             jax.ShapeDtypeStruct((ranks, width), F32),
         ],
         in_specs=[scalar, scalar] + [vector] * 13,
-        out_specs=[vector] * 5,
+        out_specs=[vector] * 6,
         scratch_shapes=[pltpu.VMEM((rows, 2 * width), LOW)],
         compiler_params=ROOM,
         cost_estimate=cost(1e9, 2 * pair.size),
@@ -297,23 +299,26 @@
     )(which, grad, middle, weights, down_maps)
 
 
-def down_kernel(m_ref, *refs):
+def down_kernel(back_ref, mine_ref, facing_ref, *refs):
     *row_refs, out_ref = refs
     rows = jnp.concatenate([ref[...] for ref in row_refs])
-    out_ref[...] = dot(m_ref[...], rows, TN).astype(out_ref.dtype)
-
-
-def down_grad(middle, blocks, dtype):
-    half = blocks[0].shape[1]
+    ranks = mine_ref.shape[1]
+    both = jnp.concatenate([mine_ref[...], facing_ref[...]], 1)
+    parts = dot(dot(back_ref[...], both).astype(LOW), rows, TN)
+    out_ref[...] = parts[:ranks] + parts[ranks:]
+
+
+def down_grad(back, mine, facing, blocks):
+    ranks, half = mine.shape[1], blocks[0].shape[1]
     return pl.pallas_call(
         down_kernel,
-        out_shape=jax.ShapeDtypeStruct((middle.shape[1], half), dtype),
-        in_specs=[VECTOR] * (1 + len(blocks)),
+        out_shape=jax.ShapeDtypeStruct((ranks, half), F32),
+        in_specs=[VECTOR] * (3 + len(blocks)),
         out_specs=VECTOR,
         compiler_params=ROOM,
         cost_estimate=cost(5e7, 2 * 200 * half),
         name="down_grad",
-    )(middle, *blocks)
+    )(back, mine, facing, *blocks)
 
 
 def row_tokens(x_hi, z, core, x_lo):
@@ -390,7 +395,7 @@
     step_c = project([third, third_there], weights, down_maps, here)
     owns = [base, base_there, third, third_there]
 
-    g_own, m_own, g_other, m_other, up_part = attend(
+    g_own, m_own, g_other, m_other, middle, up_part = attend(
         image_tile_count,
         text_start_position,
         (step_a, step_c, step_b),
@@ -400,12 +405,8 @@
         pair,
     )
 
-    down_other = down_grad(m_other, others, LOW)
-    down_facing = lax.ppermute(down_other, "tensor", TENSOR_SWAP)
-    base, base_out, third, third_out = feature_grad(
-        after(g_own, down_other), m_own, weights, down_maps, here
-    )
-    down_own = down_grad(m_own, owns, F32)
+    middle_facing = lax.ppermute(middle, "tensor", TENSOR_SWAP)
+    base, base_out, third, third_out = feature_grad(g_own, m_own, weights, down_maps, here)
 
     def add(mine, theirs):
         return mine.astype(F32) + theirs.astype(F32)
@@ -413,14 +414,13 @@
     third = add(third, move(third_out, SIBLING)).astype(LOW)
     third_in = move(third, FAR)
     first, second, first_out, second_out = feature_grad(
-        after(g_other, third, down_own), m_other, weights, down_maps, opposite
+        after(g_other, third), m_other, weights, down_maps, opposite
     )
     second = add(second, move(second_out, SIBLING)).astype(LOW)
     first = add(first, move(first_out, SIBLING))
     base = add(base, move(base_out, SIBLING))
-    sums = jnp.concatenate(
-        [down_own + after(down_facing, first_out).astype(F32), up_part], 1
-    ).astype(LOW)
+    down_own = down_grad(maps[2], middle, after(middle_facing, first_out), owns)
+    sums = jnp.concatenate([down_own, up_part], 1).astype(LOW)
     near_sums = lax.ppermute(sums, "dp", DP_NEAR)
     second_in = move(second, FAR)
     first = (first + third_in.astype(F32)).astype(LOW)

time: 109 us -> 105 us (0.963)
  waiting for transfers between devices: 34.7 us -> 28.1 us
  starting transfers between devices: 44.5 us -> 47.6 us
    ppermute x1, waiting for transfers between devices: 4.13 us -> 0.01 us  [per_device(): middle_facing = lax.ppermute(middle, 'tensor', TENSOR_SWAP)]
    ppermute x1, waiting for transfers between devices: 3.69 us -> 0.46 us  [per_device(): far_sums = lax.ppermute(sums, 'dp', DP_FAR)]
    ppermute x28, starting transfers between devices: 42.2 us -> 45 us  [move(): return lax.ppermute(block, PLANE, pairs)]
    ppermute x28, waiting for transfers between devices: 18.1 us -> 20.8 us  [move(): return lax.ppermute(block, PLANE, pairs)]
    ppermute x1, waiting for transfers between devices: 3.22 us -> 1.67 us  [per_device(): facing = lax.ppermute(sums, 'tensor', TENSOR_SWAP)]
  transfers between devices with their start and end apart: 32 -> 32, of which waited for: 12 -> 15; matrix products, arithmetic and copies ran while one was open for 3% -> 3% of each run, Pallas kernels for 6% -> 7%
where the time goes in v9:
time: 105 us
  starting transfers between devices  47.6 us (45%)
  waiting for transfers between devices  28.1 us (27%)
  Pallas kernels  15 us (14%)
  local copies, waits for them, and re-layouts  12 us (11%)
  between operations  1.23 us (1%)
    ppermute x28, starting transfers between devices, move(): return lax.ppermute(block, PLANE, pairs)  45 us
    ppermute x28, waiting for transfers between devices, move(): return lax.ppermute(block, PLANE, pairs)  20.8 us
    unnamed x16, local copies, waits for them, and re-layouts  8.18 us
    ppermute x1, waiting for transfers between devices, per_device(): near_sums = lax.ppermute(sums, 'dp', DP_NEAR)  5.08 us
    pallas_call x1, Pallas kernels, attend(): pl.pallas_call(attention_kernel, out_shape=[jax.ShapeDtypeStruct((rows, 2...  4.06 us
    pallas_call x2, Pallas kernels, feature_grad(): pl.pallas_call(feature_kernel, out_shape=[jax.ShapeDtypeStruct((rows // 4...  3.84 us
    pallas_call x3, Pallas kernels, project(): pl.pallas_call(project_kernel, out_shape=[jax.ShapeDtypeStruct((2, count,...  3.35 us
  transfers between devices with their start and end apart: 32, of which 15 were waited for; matrix products, arithmetic and copies ran while one was open for 3% of the time, Pallas kernels for 7%

profile of v9, /device:TPU:24, one launch (start us, length us, event | category | flops | bytes accessed | tf_op | source)
XLA Modules:
  0.0 104.8 jit_solution(9817212541193625455)
XLA Ops:
  1.6 7.3 %collective-permute-start = (bf16[6,4096]{1,0:T(8,128)(2,1)S(1)}, bf16[6,4096]{1,0:T(8,128)(2,1)S(1)}, u32[]{:S(2)}, u32[]{:S(2)}) collective-permute-start(bf16[6,4096]{1,0:T(8,128)(2,1)S(1)} %reshape.31), channel_id=1, source_target_pairs={{0,64},{8,72},{16,80},{24,88},{32,96},{40,104},{48,112},{56,120},{... | collective-permute-start | bytes 147464 | tf_op jit(solution)/shard_map/ppermute | solution.py:40
  8.9 1.9 %collective-permute-start.1 = (bf16[6,4096]{1,0:T(8,128)(2,1)S(1)}, bf16[6,4096]{1,0:T(8,128)(2,1)S(1)}, u32[]{:S(2)}, u32[]{:S(2)}) collective-permute-start(bf16[6,4096]{1,0:T(8,128)(2,1)S(1)} %reshape.31), channel_id=1, source_target_pairs={{0,48},{8,56},{16,64},{24,72},{32,80},{40,88},{48,96},{56,104},{64... | collective-permute-start | bytes 147464 | tf_op jit(solution)/shard_map/ppermute | solution.py:40
  10.8 3.1 %collective-permute-start.2 = (bf16[6,4096]{1,0:T(8,128)(2,1)S(1)}, bf16[6,4096]{1,0:T(8,128)(2,1)S(1)}, u32[]{:S(2)}, u32[]{:S(2)}) collective-permute-start(bf16[6,4096]{1,0:T(8,128)(2,1)S(1)} %reshape.31), channel_id=1, source_target_pairs={{0,80},{8,88},{16,96},{24,104},{32,112},{40,120},{48,0},{56,8},{64... | collective-permute-start | bytes 147464 | tf_op jit(solution)/shard_map/ppermute | solution.py:40
  13.9 1.5 %collective-permute-start.3 = (bf16[6,4096]{1,0:T(8,128)(2,1)S(1)}, bf16[6,4096]{1,0:T(8,128)(2,1)S(1)}, u32[]{:S(2)}, u32[]{:S(2)}) collective-permute-start(bf16[6,4096]{1,0:T(8,128)(2,1)S(1)} %reshape.31), channel_id=1, source_target_pairs={{0,32},{8,40},{16,48},{24,56},{32,64},{40,72},{48,80},{56,88},{64,... | collective-permute-start | bytes 147464 | tf_op jit(solution)/shard_map/ppermute | solution.py:40
  15.4 2.7 %collective-permute-start.4 = (bf16[6,4096]{1,0:T(8,128)(2,1)S(1)}, bf16[6,4096]{1,0:T(8,128)(2,1)S(1)}, u32[]{:S(2)}, u32[]{:S(2)}) collective-permute-start(bf16[6,4096]{1,0:T(8,128)(2,1)S(1)} %reshape.31), channel_id=1, source_target_pairs={{0,96},{8,104},{16,112},{24,120},{32,0},{40,8},{48,16},{56,24},{64... | collective-permute-start | bytes 147464 | tf_op jit(solution)/shard_map/ppermute | solution.py:40
  19.1 2.2 %collective-permute-start.6 = (bf16[6,4096]{1,0:T(8,128)(2,1)S(1)}, bf16[6,4096]{1,0:T(8,128)(2,1)S(1)}, u32[]{:S(2)}, u32[]{:S(2)}) collective-permute-start(bf16[6,4096]{1,0:T(8,128)(2,1)S(1)} %reshape.31), channel_id=1, source_target_pairs={{0,112},{8,120},{16,0},{24,8},{32,16},{40,24},{48,32},{56,40},{64,... | collective-permute-start | bytes 147464 | tf_op jit(solution)/shard_map/ppermute | solution.py:40
  22.4 1.1 %collective-permute-done.5 = bf16[6,4096]{1,0:T(8,128)(2,1)S(1)} collective-permute-done((bf16[6,4096]{1,0:T(8,128)(2,1)S(1)}, bf16[6,4096]{1,0:T(8,128)(2,1)S(1)}, u32[]{:S(2)}, u32[]{:S(2)}) %collective-permute-start.5) | collective-permute-done | bytes 49184 | tf_op jit(solution)/shard_map/ppermute | solution.py:40
  24.9 1.6 %collective-permute-start.8 = (bf16[48,4096]{1,0:T(8,128)(2,1)S(1)}, bf16[48,4096]{1,0:T(8,128)(2,1)S(1)}, u32[]{:S(2)}, u32[]{:S(2)}) collective-permute-start(bf16[48,4096]{1,0:T(8,128)(2,1)S(1)} %concatenate.16.refs_0_), channel_id=1, source_target_pairs={{0,4},{8,140},{16,20},{24,156},{32,36},{40,172},{48,52},{56,188},{... | collective-permute-start | bytes 1179656 | tf_op jit(solution)/shard_map/ppermute | solution.py:40
  26.4 2.1 %collective-permute-start.10 = (bf16[48,4096]{1,0:T(8,128)(2,1)S(1)}, bf16[48,4096]{1,0:T(8,128)(2,1)S(1)}, u32[]{:S(2)}, u32[]{:S(2)}) collective-permute-start(bf16[48,4096]{1,0:T(8,128)(2,1)S(1)} %concatenate.16.refs_0_), channel_id=1, source_target_pairs={{0,132},{8,12},{16,148},{24,28},{32,164},{40,44},{48,180},{56,60},... | collective-permute-start | bytes 1179656 | tf_op jit(solution)/shard_map/ppermute | solution.py:40
  29.9 1.4 %copy-done.4 = bf16[1,3,128,2048]{3,2,1,0:T(8,128)(2,1)S(1)} copy-done((bf16[1,3,128,2048]{3,2,1,0:T(8,128)(2,1)S(1)}, bf16[1,3,128,2048]{3,2,1,0:T(8,128)(2,1)}, u32[]{:S(2)}) %copy-start.4) | copy-done | bytes 1572888
  31.3 1.4 %pair_queries.1.pair_ref = bf16[6,1024,256]{2,1,0:T(8,128)(2,1)S(1)} custom-call(bf16[2,128]{1,0:T(2,128)(2,1)S(1)} %bitcast.405, bf16[3,128,2048]{2,1,0:T(8,128)(2,1)S(1)} %bitcast.403, bf16[3,128,2048]{2,1,0:T(8,128)(2,1)S(1)} %bitcast.404), custom_call_target="tpu_custom_call" | custom-call | flops 200000000 | bytes 6291456 | tf_op jit(solution)/shard_map/pair_queries/pallas_call | solution.py:85
  32.8 3.4 %copy-done = bf16[1,2,8192,256]{3,2,1,0:T(8,128)(2,1)S(1)} copy-done((bf16[1,2,8192,256]{3,2,1,0:T(8,128)(2,1)S(1)}, bf16[1,2,8192,256]{3,2,1,0:T(8,128)(2,1)}, u32[]{:S(2)}) %copy-start) | copy-done | bytes 8388632
  37.8 2.6 %collective-permute-start.9 = (bf16[48,4096]{1,0:T(8,128)(2,1)S(1)}, bf16[48,4096]{1,0:T(8,128)(2,1)S(1)}, u32[]{:S(2)}, u32[]{:S(2)}) collective-permute-start(bf16[48,4096]{1,0:T(8,128)(2,1)S(1)} %collective-permute-done.8.ready_ref.refs_0_), channel_id=1, source_target_pairs={{0,132},{8,12},{16,148},{24,28},{32,164},{40,44},{48,180},{56,60},... | collective-permute-start | bytes 1179656 | tf_op jit(solution)/shard_map/ppermute | solution.py:40
  40.4 3.4 %copy-done.1 = bf16[1,2,8192,256]{3,2,1,0:T(8,128)(2,1)S(1)} copy-done((bf16[1,2,8192,256]{3,2,1,0:T(8,128)(2,1)S(1)}, bf16[1,2,8192,256]{3,2,1,0:T(8,128)(2,1)}, u32[]{:S(2)}) %copy-start.1) | copy-done | bytes 8388632
  44.3 1.4 %project.4 = (f32[2,192,256]{2,1,0:T(8,128)S(1)}, f32[192,32]{1,0:T(8,128)S(1)}) custom-call(s32[1]{0:T(128)S(6)} %sub.44.which_ref, bf16[48,4096]{1,0:T(8,128)(2,1)S(1)} %collective-permute-done.8.ready_ref.refs_0_, bf16[48,4096]{1,0:T(8,128)(2,1)S(1)} %collective-permute-done.10.refs_1_, bf16[48,4096]{1,0:T(8,128)(2,1)S(1)} %collective-permute-done.11.refs_2_, ...), custom_call_target="tpu_custom_call" | custom-call | flops 805306368 | bytes 5767168 | tf_op jit(solution)/shard_map/project/pallas_call | solution.py:159
  46.8 1.7 %collective-permute-done.13.refs_1_.refs_3_ = bf16[48,4096]{1,0:T(8,128)(2,1)S(1)} collective-permute-done((bf16[48,4096]{1,0:T(8,128)(2,1)S(1)}, bf16[48,4096]{1,0:T(8,128)(2,1)S(1)}, u32[]{:S(2)}, u32[]{:S(2)}) %collective-permute-start.13) | collective-permute-done | bytes 393248 | tf_op jit(solution)/shard_map/ppermute | solution.py:40
  49.5 4.1 %attend.1 = (bf16[192,512]{1,0:T(8,128)(2,1)S(1)}, bf16[192,32]{1,0:T(8,128)(2,1)S(1)}, bf16[192,512]{1,0:T(8,128)(2,1)S(1)}, bf16[192,32]{1,0:T(8,128)(2,1)S(1)...) custom-call(s32[3]{0:T(128)S(1)} %copy-done.6, s32[3]{0:T(128)S(1)} %copy-done.7, ...), custom_call_target="tpu_custom_call" | custom-call | flops 1000000000 | bytes 3145728 | tf_op jit(solution)/shard_map/attend/pallas_call | solution.py:257
  53.6 1.9 %feature_grad.2 = (bf16[48,4096]{1,0:T(8,128)(2,1)S(1)}, bf16[48,4096]{1,0:T(8,128)(2,1)S(1)}, bf16[48,4096]{1,0:T(8,128)(2,1)S(1)}, bf16[48,4096]{1,0:T(8,128)(2,1)S(1)}) custom-call(s32[1]{0:T(128)} %bitcast.which_ref.side_ref, bf16[192,512]{1,0:T(8,128)(2,1)S(1)} %get-tuple-element.46.g_ref, bf16[192,32]{1,0:T(8,128)(2,1)S(1)} %get-tuple-element.47.m_ref, ...), custom_call_target="tpu_custom_call" | custom-call | flops 805306368 | bytes 5767168 | tf_op jit(solution)/shard_map/feature_grad/pallas_call | solution.py:291
  56.1 1.2 %collective-permute-done.15 = bf16[48,4096]{1,0:T(8,128)(2,1)S(1)} collective-permute-done((bf16[48,4096]{1,0:T(8,128)(2,1)S(1)}, bf16[48,4096]{1,0:T(8,128)(2,1)S(1)}, u32[]{:S(2)}, u32[]{:S(2)}) %collective-permute-start.15) | collective-permute-done | bytes 393248 | tf_op jit(solution)/shard_map/ppermute | solution.py:40
  57.4 2.7 %collective-permute-start.19 = (bf16[48,4096]{1,0:T(8,128)(2,1)S(1)}, bf16[48,4096]{1,0:T(8,128)(2,1)S(1)}, u32[]{:S(2)}, u32[]{:S(2)}) collective-permute-start(bf16[48,4096]{1,0:T(8,128)(2,1)S(1)} %add_convert_fusion.2), channel_id=1, source_target_pairs={{0,132},{8,12},{16,148},{24,28},{32,164},{40,44},{48,180},{56,60},... | collective-permute-start | bytes 1179656 | tf_op jit(solution)/shard_map/ppermute | solution.py:40
  60.1 1.9 %feature_grad.3 = (bf16[48,4096]{1,0:T(8,128)(2,1)S(1)}, bf16[48,4096]{1,0:T(8,128)(2,1)S(1)}, bf16[48,4096]{1,0:T(8,128)(2,1)S(1)}, bf16[48,4096]{1,0:T(8,128)(2,1)S(1)}) custom-call(s32[1]{0:T(128)S(6)} %sub.44.which_ref, bf16[192,512]{1,0:T(8,128)(2,1)S(1)} %get-tuple-element.53.g_ref, bf16[192,32]{1,0:T(8,128)(2,1)S(1)} %get-tuple-element.54.m_ref, ...), custom_call_target="tpu_custom_call" | custom-call | flops 805306368 | bytes 5767168 | tf_op jit(solution)/shard_map/feature_grad/pallas_call | solution.py:291
  63.9 2.5 %collective-permute-done.19 = bf16[48,4096]{1,0:T(8,128)(2,1)S(1)} collective-permute-done((bf16[48,4096]{1,0:T(8,128)(2,1)S(1)}, bf16[48,4096]{1,0:T(8,128)(2,1)S(1)}, u32[]{:S(2)}, u32[]{:S(2)}) %collective-permute-start.19) | collective-permute-done | bytes 393248 | tf_op jit(solution)/shard_map/ppermute | solution.py:40
  66.9 5.1 %collective-permute-done.22 = bf16[32,4352]{1,0:T(8,128)(2,1)S(1)} collective-permute-done((bf16[32,4352]{1,0:T(8,128)(2,1)S(1)}, bf16[32,4352]{1,0:T(8,128)(2,1)S(1)}, u32[]{:S(2)}, u32[]{:S(2)}) %collective-permute-start.22) | collective-permute-done | bytes 278560 | tf_op jit(solution)/shard_map/ppermute | solution.py:424
  73.4 7.8 %collective-permute-done.17 = bf16[48,4096]{1,0:T(8,128)(2,1)S(1)} collective-permute-done((bf16[48,4096]{1,0:T(8,128)(2,1)S(1)}, bf16[48,4096]{1,0:T(8,128)(2,1)S(1)}, u32[]{:S(2)}, u32[]{:S(2)}) %collective-permute-start.17) | collective-permute-done | bytes 393248 | tf_op jit(solution)/shard_map/ppermute | solution.py:40
  82.0 3.2 %collective-permute-start.24 = (bf16[6,4096]{1,0:T(8,128)(2,1)S(1)}, bf16[6,4096]{1,0:T(8,128)(2,1)S(1)}, u32[]{:S(2)}, u32[]{:S(2)}) collective-permute-start(bf16[6,4096]{1,0:T(8,128)(2,1)S(1)} %get-tuple-element.69), channel_id=1, source_target_pairs={{0,64},{8,72},{16,80},{24,88},{32,96},{40,104},{48,112},{56,120},{... | collective-permute-start | bytes 147464 | tf_op jit(solution)/shard_map/ppermute | solution.py:40
  85.3 1.4 %collective-permute-start.25 = (bf16[6,4096]{1,0:T(8,128)(2,1)S(1)}, bf16[6,4096]{1,0:T(8,128)(2,1)S(1)}, u32[]{:S(2)}, u32[]{:S(2)}) collective-permute-start(bf16[6,4096]{1,0:T(8,128)(2,1)S(1)} %get-tuple-element.75), channel_id=1, source_target_pairs={{0,80},{8,88},{16,96},{24,104},{32,112},{40,120},{48,0},{56,8},{64... | collective-permute-start | bytes 147464 | tf_op jit(solution)/shard_map/ppermute | solution.py:40
  86.7 2.4 %collective-permute-start.26 = (bf16[6,4096]{1,0:T(8,128)(2,1)S(1)}, bf16[6,4096]{1,0:T(8,128)(2,1)S(1)}, u32[]{:S(2)}, u32[]{:S(2)}) collective-permute-start(bf16[6,4096]{1,0:T(8,128)(2,1)S(1)} %get-tuple-element.74), channel_id=1, source_target_pairs={{0,48},{8,56},{16,64},{24,72},{32,80},{40,88},{48,96},{56,104},{64... | collective-permute-start | bytes 147464 | tf_op jit(solution)/shard_map/ppermute | solution.py:40
  89.1 2.1 %collective-permute-start.27 = (bf16[6,4096]{1,0:T(8,128)(2,1)S(1)}, bf16[6,4096]{1,0:T(8,128)(2,1)S(1)}, u32[]{:S(2)}, u32[]{:S(2)}) collective-permute-start(bf16[6,4096]{1,0:T(8,128)(2,1)S(1)} %get-tuple-element.73), channel_id=1, source_target_pairs={{0,96},{8,104},{16,112},{24,120},{32,0},{40,8},{48,16},{56,24},{64... | collective-permute-start | bytes 147464 | tf_op jit(solution)/shard_map/ppermute | solution.py:40
  92.0 3.8 %collective-permute-start.29 = (bf16[6,4096]{1,0:T(8,128)(2,1)S(1)}, bf16[6,4096]{1,0:T(8,128)(2,1)S(1)}, u32[]{:S(2)}, u32[]{:S(2)}) collective-permute-start(bf16[6,4096]{1,0:T(8,128)(2,1)S(1)} %get-tuple-element.71), channel_id=1, source_target_pairs={{0,112},{8,120},{16,0},{24,8},{32,16},{40,24},{48,32},{56,40},{64,... | collective-permute-start | bytes 147464 | tf_op jit(solution)/shard_map/ppermute | solution.py:40
  96.6 1.3 %collective-permute-start.31 = (bf16[32,4352]{1,0:T(8,128)(2,1)S(1)}, bf16[32,4352]{1,0:T(8,128)(2,1)S(1)}, u32[]{:S(2)}, u32[]{:S(2)}) collective-permute-start(bf16[32,4352]{1,0:T(8,128)(2,1)S(1)} %add_convert_fusion.3.mine_ref), channel_id=1, source_target_pairs={{0,4},{4,0},{1,5},{5,1},{2,6},{6,2},{3,7},{7,3},{8,12},{12,8},{9,1... | collective-permute-start | bytes 835592 | tf_op jit(solution)/shard_map/ppermute | solution.py:434
  98.0 3.4 %collective-permute-done.30 = bf16[6,4096]{1,0:T(8,128)(2,1)S(1)} collective-permute-done((bf16[6,4096]{1,0:T(8,128)(2,1)S(1)}, bf16[6,4096]{1,0:T(8,128)(2,1)S(1)}, u32[]{:S(2)}, u32[]{:S(2)}) %collective-permute-start.30) | collective-permute-done | bytes 49184 | tf_op jit(solution)/shard_map/ppermute | solution.py:40
  102.1 1.7 %collective-permute-done.31.facing_ref = bf16[32,4352]{1,0:T(8,128)(2,1)S(1)} collective-permute-done((bf16[32,4352]{1,0:T(8,128)(2,1)S(1)}, bf16[32,4352]{1,0:T(8,128)(2,1)S(1)}, u32[]{:S(2)}, u32[]{:S(2)}) %collective-permute-start.31) | collective-permute-done | bytes 278560 | tf_op jit(solution)/shard_map/ppermute | solution.py:434
  (77 shorter events, 18.4 us)
Async XLA Ops:
  1.6 16.5 %collective-permute-start = (bf16[6,4096]{1,0:T(8,128)(2,1)S(1)}, bf16[6,4096]{1,0:T(8,128)(2,1)S(1)}, u32[]{:S(2)}, u32[]{:S(2)}) collective-permute-start(bf16[6,4096]{1,0:T(8,128)(2,1)S(1)} %reshape.31), channel_id=1, source_target_pairs={{0,64},{8,72},{16,80},{24,88},{32,96},{40,104},{48,112},{56,120},{... | collective-permute-start | bytes 147464 | tf_op jit(solution)/shard_map/ppermute | solution.py:40
  8.9 10.2 %collective-permute-start.1 = (bf16[6,4096]{1,0:T(8,128)(2,1)S(1)}, bf16[6,4096]{1,0:T(8,128)(2,1)S(1)}, u32[]{:S(2)}, u32[]{:S(2)}) collective-permute-start(bf16[6,4096]{1,0:T(8,128)(2,1)S(1)} %reshape.31), channel_id=1, source_target_pairs={{0,48},{8,56},{16,64},{24,72},{32,80},{40,88},{48,96},{56,104},{64... | collective-permute-start | bytes 147464 | tf_op jit(solution)/shard_map/ppermute | solution.py:40
  10.8 10.5 %collective-permute-start.2 = (bf16[6,4096]{1,0:T(8,128)(2,1)S(1)}, bf16[6,4096]{1,0:T(8,128)(2,1)S(1)}, u32[]{:S(2)}, u32[]{:S(2)}) collective-permute-start(bf16[6,4096]{1,0:T(8,128)(2,1)S(1)} %reshape.31), channel_id=1, source_target_pairs={{0,80},{8,88},{16,96},{24,104},{32,112},{40,120},{48,0},{56,8},{64... | collective-permute-start | bytes 147464 | tf_op jit(solution)/shard_map/ppermute | solution.py:40
  13.9 7.7 %collective-permute-start.3 = (bf16[6,4096]{1,0:T(8,128)(2,1)S(1)}, bf16[6,4096]{1,0:T(8,128)(2,1)S(1)}, u32[]{:S(2)}, u32[]{:S(2)}) collective-permute-start(bf16[6,4096]{1,0:T(8,128)(2,1)S(1)} %reshape.31), channel_id=1, source_target_pairs={{0,32},{8,40},{16,48},{24,56},{32,64},{40,72},{48,80},{56,88},{64,... | collective-permute-start | bytes 147464 | tf_op jit(solution)/shard_map/ppermute | solution.py:40
  15.4 7.0 %collective-permute-start.4 = (bf16[6,4096]{1,0:T(8,128)(2,1)S(1)}, bf16[6,4096]{1,0:T(8,128)(2,1)S(1)}, u32[]{:S(2)}, u32[]{:S(2)}) collective-permute-start(bf16[6,4096]{1,0:T(8,128)(2,1)S(1)} %reshape.31), channel_id=1, source_target_pairs={{0,96},{8,104},{16,112},{24,120},{32,0},{40,8},{48,16},{56,24},{64... | collective-permute-start | bytes 147464 | tf_op jit(solution)/shard_map/ppermute | solution.py:40
  18.0 5.5 %collective-permute-start.5 = (bf16[6,4096]{1,0:T(8,128)(2,1)S(1)}, bf16[6,4096]{1,0:T(8,128)(2,1)S(1)}, u32[]{:S(2)}, u32[]{:S(2)}) collective-permute-start(bf16[6,4096]{1,0:T(8,128)(2,1)S(1)} %reshape.31), channel_id=1, source_target_pairs={{0,16},{8,24},{16,32},{24,40},{32,48},{40,56},{48,64},{56,72},{64,... | collective-permute-start | bytes 147464 | tf_op jit(solution)/shard_map/ppermute | solution.py:40
  19.1 4.6 %collective-permute-start.6 = (bf16[6,4096]{1,0:T(8,128)(2,1)S(1)}, bf16[6,4096]{1,0:T(8,128)(2,1)S(1)}, u32[]{:S(2)}, u32[]{:S(2)}) collective-permute-start(bf16[6,4096]{1,0:T(8,128)(2,1)S(1)} %reshape.31), channel_id=1, source_target_pairs={{0,112},{8,120},{16,0},{24,8},{32,16},{40,24},{48,32},{56,40},{64,... | collective-permute-start | bytes 147464 | tf_op jit(solution)/shard_map/ppermute | solution.py:40
  24.8 8.0 %collective-permute-start.7 = (bf16[48,4096]{1,0:T(8,128)(2,1)S(1)}, bf16[48,4096]{1,0:T(8,128)(2,1)S(1)}, u32[]{:S(2)}, u32[]{:S(2)}) collective-permute-start(bf16[48,4096]{1,0:T(8,128)(2,1)S(1)} %concatenate.16.refs_0_), channel_id=1, source_target_pairs={{0,8},{8,0},{16,24},{24,16},{32,40},{40,32},{48,56},{56,48},{64,72... | collective-permute-start | bytes 1179656 | tf_op jit(solution)/shard_map/ppermute | solution.py:40
  24.9 12.3 %collective-permute-start.8 = (bf16[48,4096]{1,0:T(8,128)(2,1)S(1)}, bf16[48,4096]{1,0:T(8,128)(2,1)S(1)}, u32[]{:S(2)}, u32[]{:S(2)}) collective-permute-start(bf16[48,4096]{1,0:T(8,128)(2,1)S(1)} %concatenate.16.refs_0_), channel_id=1, source_target_pairs={{0,4},{8,140},{16,20},{24,156},{32,36},{40,172},{48,52},{56,188},{... | collective-permute-start | bytes 1179656 | tf_op jit(solution)/shard_map/ppermute | solution.py:40
  26.4 11.1 %collective-permute-start.10 = (bf16[48,4096]{1,0:T(8,128)(2,1)S(1)}, bf16[48,4096]{1,0:T(8,128)(2,1)S(1)}, u32[]{:S(2)}, u32[]{:S(2)}) collective-permute-start(bf16[48,4096]{1,0:T(8,128)(2,1)S(1)} %concatenate.16.refs_0_), channel_id=1, source_target_pairs={{0,132},{8,12},{16,148},{24,28},{32,164},{40,44},{48,180},{56,60},... | collective-permute-start | bytes 1179656 | tf_op jit(solution)/shard_map/ppermute | solution.py:40
  37.2 7.1 %collective-permute-start.11 = (bf16[48,4096]{1,0:T(8,128)(2,1)S(1)}, bf16[48,4096]{1,0:T(8,128)(2,1)S(1)}, u32[]{:S(2)}, u32[]{:S(2)}) collective-permute-start(bf16[48,4096]{1,0:T(8,128)(2,1)S(1)} %collective-permute-done.8.ready_ref.refs_0_), channel_id=1, source_target_pairs={{0,8},{8,0},{16,24},{24,16},{32,40},{40,32},{48,56},{56,48},{64,72... | collective-permute-start | bytes 1179656 | tf_op jit(solution)/shard_map/ppermute | solution.py:40
  37.6 6.7 %collective-permute-start.12 = (bf16[48,4096]{1,0:T(8,128)(2,1)S(1)}, bf16[48,4096]{1,0:T(8,128)(2,1)S(1)}, u32[]{:S(2)}, u32[]{:S(2)}) collective-permute-start(bf16[48,4096]{1,0:T(8,128)(2,1)S(1)} %collective-permute-done.10.refs_1_), channel_id=1, source_target_pairs={{0,8},{8,0},{16,24},{24,16},{32,40},{40,32},{48,56},{56,48},{64,72... | collective-permute-start | bytes 1179656 | tf_op jit(solution)/shard_map/ppermute | solution.py:40
  37.8 9.0 %collective-permute-start.9 = (bf16[48,4096]{1,0:T(8,128)(2,1)S(1)}, bf16[48,4096]{1,0:T(8,128)(2,1)S(1)}, u32[]{:S(2)}, u32[]{:S(2)}) collective-permute-start(bf16[48,4096]{1,0:T(8,128)(2,1)S(1)} %collective-permute-done.8.ready_ref.refs_0_), channel_id=1, source_target_pairs={{0,132},{8,12},{16,148},{24,28},{32,164},{40,44},{48,180},{56,60},... | collective-permute-start | bytes 1179656 | tf_op jit(solution)/shard_map/ppermute | solution.py:40
  46.8 1.7 %collective-permute-start.13 = (bf16[48,4096]{1,0:T(8,128)(2,1)S(1)}, bf16[48,4096]{1,0:T(8,128)(2,1)S(1)}, u32[]{:S(2)}, u32[]{:S(2)}) collective-permute-start(bf16[48,4096]{1,0:T(8,128)(2,1)S(1)} %collective-permute-done.9.refs_0_.refs_2_), channel_id=1, source_target_pairs={{0,8},{8,0},{16,24},{24,16},{32,40},{40,32},{48,56},{56,48},{64,72... | collective-permute-start | bytes 1179656 | tf_op jit(solution)/shard_map/ppermute | solution.py:40
  55.5 1.8 %collective-permute-start.15 = (bf16[48,4096]{1,0:T(8,128)(2,1)S(1)}, bf16[48,4096]{1,0:T(8,128)(2,1)S(1)}, u32[]{:S(2)}, u32[]{:S(2)}) collective-permute-start(bf16[48,4096]{1,0:T(8,128)(2,1)S(1)} %get-tuple-element.52), channel_id=1, source_target_pairs={{0,8},{8,0},{16,24},{24,16},{32,40},{40,32},{48,56},{56,48},{64,72... | collective-permute-start | bytes 1179656 | tf_op jit(solution)/shard_map/ppermute | solution.py:40
  55.7 6.4 %collective-permute-start.21 = (bf16[192,32]{1,0:T(8,128)(2,1)S(1)}, bf16[192,32]{1,0:T(8,128)(2,1)S(1)}, u32[]{:S(2)}, u32[]{:S(2)}) collective-permute-start(bf16[192,32]{1,0:T(8,128)(2,1)S(1)} %get-tuple-element.59.mine_ref), channel_id=1, source_target_pairs={{0,4},{4,0},{1,5},{5,1},{2,6},{6,2},{3,7},{7,3},{8,12},{12,8},{9,1... | collective-permute-start | bytes 36872 | tf_op jit(solution)/shard_map/ppermute | solution.py:408
  55.7 17.7 %collective-permute-start.14 = (bf16[48,4096]{1,0:T(8,128)(2,1)S(1)}, bf16[48,4096]{1,0:T(8,128)(2,1)S(1)}, u32[]{:S(2)}, u32[]{:S(2)}) collective-permute-start(bf16[48,4096]{1,0:T(8,128)(2,1)S(1)} %get-tuple-element.49), channel_id=1, source_target_pairs={{0,8},{8,0},{16,24},{24,16},{32,40},{40,32},{48,56},{56,48},{64,72... | collective-permute-start | bytes 1179656 | tf_op jit(solution)/shard_map/ppermute | solution.py:40
  57.4 9.1 %collective-permute-start.19 = (bf16[48,4096]{1,0:T(8,128)(2,1)S(1)}, bf16[48,4096]{1,0:T(8,128)(2,1)S(1)}, u32[]{:S(2)}, u32[]{:S(2)}) collective-permute-start(bf16[48,4096]{1,0:T(8,128)(2,1)S(1)} %add_convert_fusion.2), channel_id=1, source_target_pairs={{0,132},{8,12},{16,148},{24,28},{32,164},{40,44},{48,180},{56,60},... | collective-permute-start | bytes 1179656 | tf_op jit(solution)/shard_map/ppermute | solution.py:40
  62.0 1.9 %collective-permute-start.18 = (bf16[48,4096]{1,0:T(8,128)(2,1)S(1)}, bf16[48,4096]{1,0:T(8,128)(2,1)S(1)}, u32[]{:S(2)}, u32[]{:S(2)}) collective-permute-start(bf16[48,4096]{1,0:T(8,128)(2,1)S(1)} %get-tuple-element.58), channel_id=1, source_target_pairs={{0,8},{8,0},{16,24},{24,16},{32,40},{40,32},{48,56},{56,48},{64,72... | collective-permute-start | bytes 1179656 | tf_op jit(solution)/shard_map/ppermute | solution.py:40
  62.9 9.1 %collective-permute-start.22 = (bf16[32,4352]{1,0:T(8,128)(2,1)S(1)}, bf16[32,4352]{1,0:T(8,128)(2,1)S(1)}, u32[]{:S(2)}, u32[]{:S(2)}) collective-permute-start(bf16[32,4352]{1,0:T(8,128)(2,1)S(1)} %pad_maximum_fusion), channel_id=1, source_target_pairs={{0,1},{1,0},{2,3},{3,2},{4,5},{5,4},{6,7},{7,6},{8,9},{9,8},{10,11... | collective-permute-start | bytes 835592 | tf_op jit(solution)/shard_map/ppermute | solution.py:424
  63.7 8.3 %collective-permute-start.16 = (bf16[48,4096]{1,0:T(8,128)(2,1)S(1)}, bf16[48,4096]{1,0:T(8,128)(2,1)S(1)}, u32[]{:S(2)}, u32[]{:S(2)}) collective-permute-start(bf16[48,4096]{1,0:T(8,128)(2,1)S(1)} %get-tuple-element.56), channel_id=1, source_target_pairs={{0,8},{8,0},{16,24},{24,16},{32,40},{40,32},{48,56},{56,48},{64,72... | collective-permute-start | bytes 1179656 | tf_op jit(solution)/shard_map/ppermute | solution.py:40
  66.6 14.6 %collective-permute-start.20 = (bf16[48,4096]{1,0:T(8,128)(2,1)S(1)}, bf16[48,4096]{1,0:T(8,128)(2,1)S(1)}, u32[]{:S(2)}, u32[]{:S(2)}) collective-permute-start(bf16[48,4096]{1,0:T(8,128)(2,1)S(1)} %add_convert_fusion), channel_id=1, source_target_pairs={{0,4},{8,140},{16,20},{24,156},{32,36},{40,172},{48,52},{56,188},{... | collective-permute-start | bytes 1179656 | tf_op jit(solution)/shard_map/ppermute | solution.py:40
  72.1 9.1 %collective-permute-start.17 = (bf16[48,4096]{1,0:T(8,128)(2,1)S(1)}, bf16[48,4096]{1,0:T(8,128)(2,1)S(1)}, u32[]{:S(2)}, u32[]{:S(2)}) collective-permute-start(bf16[48,4096]{1,0:T(8,128)(2,1)S(1)} %add_convert_fusion.1), channel_id=1, source_target_pairs={{0,132},{8,12},{16,148},{24,28},{32,164},{40,44},{48,180},{56,60},... | collective-permute-start | bytes 1179656 | tf_op jit(solution)/shard_map/ppermute | solution.py:40
  72.9 8.9 %collective-permute-start.23 = (bf16[32,4352]{1,0:T(8,128)(2,1)S(1)}, bf16[32,4352]{1,0:T(8,128)(2,1)S(1)}, u32[]{:S(2)}, u32[]{:S(2)}) collective-permute-start(bf16[32,4352]{1,0:T(8,128)(2,1)S(1)} %add_convert_fusion.4), channel_id=1, source_target_pairs={{0,3},{1,2},{2,1},{3,0},{4,7},{5,6},{6,5},{7,4},{8,11},{9,10},{10,... | collective-permute-start | bytes 835592 | tf_op jit(solution)/shard_map/ppermute | solution.py:429
  82.0 10.0 %collective-permute-start.24 = (bf16[6,4096]{1,0:T(8,128)(2,1)S(1)}, bf16[6,4096]{1,0:T(8,128)(2,1)S(1)}, u32[]{:S(2)}, u32[]{:S(2)}) collective-permute-start(bf16[6,4096]{1,0:T(8,128)(2,1)S(1)} %get-tuple-element.69), channel_id=1, source_target_pairs={{0,64},{8,72},{16,80},{24,88},{32,96},{40,104},{48,112},{56,120},{... | collective-permute-start | bytes 147464 | tf_op jit(solution)/shard_map/ppermute | solution.py:40
  85.3 10.6 %collective-permute-start.25 = (bf16[6,4096]{1,0:T(8,128)(2,1)S(1)}, bf16[6,4096]{1,0:T(8,128)(2,1)S(1)}, u32[]{:S(2)}, u32[]{:S(2)}) collective-permute-start(bf16[6,4096]{1,0:T(8,128)(2,1)S(1)} %get-tuple-element.75), channel_id=1, source_target_pairs={{0,80},{8,88},{16,96},{24,104},{32,112},{40,120},{48,0},{56,8},{64... | collective-permute-start | bytes 147464 | tf_op jit(solution)/shard_map/ppermute | solution.py:40
  86.7 9.9 %collective-permute-start.26 = (bf16[6,4096]{1,0:T(8,128)(2,1)S(1)}, bf16[6,4096]{1,0:T(8,128)(2,1)S(1)}, u32[]{:S(2)}, u32[]{:S(2)}) collective-permute-start(bf16[6,4096]{1,0:T(8,128)(2,1)S(1)} %get-tuple-element.74), channel_id=1, source_target_pairs={{0,48},{8,56},{16,64},{24,72},{32,80},{40,88},{48,96},{56,104},{64... | collective-permute-start | bytes 147464 | tf_op jit(solution)/shard_map/ppermute | solution.py:40
  89.1 8.8 %collective-permute-start.27 = (bf16[6,4096]{1,0:T(8,128)(2,1)S(1)}, bf16[6,4096]{1,0:T(8,128)(2,1)S(1)}, u32[]{:S(2)}, u32[]{:S(2)}) collective-permute-start(bf16[6,4096]{1,0:T(8,128)(2,1)S(1)} %get-tuple-element.73), channel_id=1, source_target_pairs={{0,96},{8,104},{16,112},{24,120},{32,0},{40,8},{48,16},{56,24},{64... | collective-permute-start | bytes 147464 | tf_op jit(solution)/shard_map/ppermute | solution.py:40
  91.2 6.8 %collective-permute-start.28 = (bf16[6,4096]{1,0:T(8,128)(2,1)S(1)}, bf16[6,4096]{1,0:T(8,128)(2,1)S(1)}, u32[]{:S(2)}, u32[]{:S(2)}) collective-permute-start(bf16[6,4096]{1,0:T(8,128)(2,1)S(1)} %get-tuple-element.72), channel_id=1, source_target_pairs={{0,32},{8,40},{16,48},{24,56},{32,64},{40,72},{48,80},{56,88},{64,... | collective-permute-start | bytes 147464 | tf_op jit(solution)/shard_map/ppermute | solution.py:40
  92.0 5.9 %collective-permute-start.29 = (bf16[6,4096]{1,0:T(8,128)(2,1)S(1)}, bf16[6,4096]{1,0:T(8,128)(2,1)S(1)}, u32[]{:S(2)}, u32[]{:S(2)}) collective-permute-start(bf16[6,4096]{1,0:T(8,128)(2,1)S(1)} %get-tuple-element.71), channel_id=1, source_target_pairs={{0,112},{8,120},{16,0},{24,8},{32,16},{40,24},{48,32},{56,40},{64,... | collective-permute-start | bytes 147464 | tf_op jit(solution)/shard_map/ppermute | solution.py:40
  95.9 5.5 %collective-permute-start.30 = (bf16[6,4096]{1,0:T(8,128)(2,1)S(1)}, bf16[6,4096]{1,0:T(8,128)(2,1)S(1)}, u32[]{:S(2)}, u32[]{:S(2)}) collective-permute-start(bf16[6,4096]{1,0:T(8,128)(2,1)S(1)} %get-tuple-element.70), channel_id=1, source_target_pairs={{0,16},{8,24},{16,32},{24,40},{32,48},{40,56},{48,64},{56,72},{64,... | collective-permute-start | bytes 147464 | tf_op jit(solution)/shard_map/ppermute | solution.py:40
  96.6 7.2 %collective-permute-start.31 = (bf16[32,4352]{1,0:T(8,128)(2,1)S(1)}, bf16[32,4352]{1,0:T(8,128)(2,1)S(1)}, u32[]{:S(2)}, u32[]{:S(2)}) collective-permute-start(bf16[32,4352]{1,0:T(8,128)(2,1)S(1)} %add_convert_fusion.3.mine_ref), channel_id=1, source_target_pairs={{0,4},{4,0},{1,5},{5,1},{2,6},{6,2},{3,7},{7,3},{8,12},{12,8},{9,1... | collective-permute-start | bytes 835592 | tf_op jit(solution)/shard_map/ppermute | solution.py:434
  (8 other events, 73.5 us)

commit v10 on v9

--- a/solution.py
+++ b/solution.py
@@ -421,15 +421,25 @@
     base = add(base, move(base_out, SIBLING))
     down_own = down_grad(maps[2], middle, after(middle_facing, first_out), owns)
     sums = jnp.concatenate([down_own, up_part], 1).astype(LOW)
-    near_sums = lax.ppermute(sums, "dp", DP_NEAR)
+    cut = ranks // 2
+    ways = ((sums[:cut], DP_NEAR, DP_FAR), (sums[cut:], DP_FAR, DP_NEAR))
+    early_sums = [lax.ppermute(part, "dp", pairs) for part, pairs, _ in ways]
     second_in = move(second, FAR)
     first = (first + third_in.astype(F32)).astype(LOW)
     first_in = move(first, NEAR)
-    sums = add(sums, after(near_sums, first)).astype(LOW)
-    far_sums = lax.ppermute(sums, "dp", DP_FAR)
+    halves = [
+        add(part, after(arriving, first)).astype(LOW)
+        for (part, _, _), arriving in zip(ways, early_sums)
+    ]
+    late_sums = [lax.ppermute(part, "dp", pairs) for part, (_, _, pairs) in zip(halves, ways)]
     base = base + second_in.astype(F32) + first_in.astype(F32)
     low_base = base.astype(LOW)
-    sums = add(sums, after(far_sums, low_base)).astype(LOW)
+    sums = jnp.concatenate(
+        [
+            add(part, after(arriving, low_base)).astype(LOW)
+            for part, arriving in zip(halves, late_sums)
+        ]
+    )
     low_base = after(low_base, sums)
     facing = lax.ppermute(sums, "tensor", TENSOR_SWAP)
     count = own.shape[0]

time: 105 us -> 104 us (level); the launches traced: 105 us -> 102 us
  waiting for transfers between devices: 28.1 us -> 25.3 us
    ppermute x2 -> x4, waiting for transfers between devices: 5.54 us -> 2.97 us  [the longest x2 2.97 us: per_device(): early_sums = [lax.ppermute(part, 'dp', pairs) for part, pairs, _ in ways]]
    ppermute x1, starting transfers between devices: 1.34 us -> 0.01 us  [per_device(): facing = lax.ppermute(sums, 'tensor', TENSOR_SWAP)]
    ppermute x2 -> x4, starting transfers between devices: 1.28 us -> 2.47 us  [the longest x2 1.89 us: per_device(): early_sums = [lax.ppermute(part, 'dp', pairs) for part, pairs, _ in ways]]
  transfers between devices with their start and end apart: 32 -> 34, of which waited for: 15 -> 16; matrix products, arithmetic and copies ran while one was open for 3% -> 3% of each run, Pallas kernels for 7% -> 7%
where the time goes in v10:
time: 104 us; the launch traced here: 102 us
  starting transfers between devices  47.7 us (46%)
  waiting for transfers between devices  25.3 us (24%)
  Pallas kernels  15 us (14%)
  local copies, waits for them, and re-layouts  12 us (12%)
  between operations  1.27 us (1%)
    ppermute x28, starting transfers between devices, move(): return lax.ppermute(block, PLANE, pairs)  45.2 us
    ppermute x28, waiting for transfers between devices, move(): return lax.ppermute(block, PLANE, pairs)  20.3 us
    unnamed x16, local copies, waits for them, and re-layouts  8.18 us
    pallas_call x1, Pallas kernels, attend(): pl.pallas_call(attention_kernel, out_shape=[jax.ShapeDtypeStruct((rows, 2...  4.06 us
    pallas_call x2, Pallas kernels, feature_grad(): pl.pallas_call(feature_kernel, out_shape=[jax.ShapeDtypeStruct((rows // 4...  3.84 us
    pallas_call x3, Pallas kernels, project(): pl.pallas_call(project_kernel, out_shape=[jax.ShapeDtypeStruct((2, count,...  3.35 us
    ppermute x2, waiting for transfers between devices, per_device(): early_sums = [lax.ppermute(part, 'dp', pairs) for part, pairs, _ in ways]  2.97 us
  transfers between devices with their start and end apart: 34, of which 16 were waited for; matrix products, arithmetic and copies ran while one was open for 3% of the time, Pallas kernels for 7%

profile of v10, /device:TPU:24, one launch (start us, length us, event | category | flops | bytes accessed | tf_op | source)
XLA Modules:
  0.0 102.2 jit_solution(6850909653407836439)
XLA Ops:
  1.6 7.3 %collective-permute-start = (bf16[6,4096]{1,0:T(8,128)(2,1)S(1)}, bf16[6,4096]{1,0:T(8,128)(2,1)S(1)}, u32[]{:S(2)}, u32[]{:S(2)}) collective-permute-start(bf16[6,4096]{1,0:T(8,128)(2,1)S(1)} %reshape.31), channel_id=1, source_target_pairs={{0,64},{8,72},{16,80},{24,88},{32,96},{40,104},{48,112},{56,120},{... | collective-permute-start | bytes 147464 | tf_op jit(solution)/shard_map/ppermute | solution.py:40
  8.9 1.9 %collective-permute-start.1 = (bf16[6,4096]{1,0:T(8,128)(2,1)S(1)}, bf16[6,4096]{1,0:T(8,128)(2,1)S(1)}, u32[]{:S(2)}, u32[]{:S(2)}) collective-permute-start(bf16[6,4096]{1,0:T(8,128)(2,1)S(1)} %reshape.31), channel_id=1, source_target_pairs={{0,48},{8,56},{16,64},{24,72},{32,80},{40,88},{48,96},{56,104},{64... | collective-permute-start | bytes 147464 | tf_op jit(solution)/shard_map/ppermute | solution.py:40
  10.8 3.1 %collective-permute-start.2 = (bf16[6,4096]{1,0:T(8,128)(2,1)S(1)}, bf16[6,4096]{1,0:T(8,128)(2,1)S(1)}, u32[]{:S(2)}, u32[]{:S(2)}) collective-permute-start(bf16[6,4096]{1,0:T(8,128)(2,1)S(1)} %reshape.31), channel_id=1, source_target_pairs={{0,80},{8,88},{16,96},{24,104},{32,112},{40,120},{48,0},{56,8},{64... | collective-permute-start | bytes 147464 | tf_op jit(solution)/shard_map/ppermute | solution.py:40
  13.9 1.5 %collective-permute-start.3 = (bf16[6,4096]{1,0:T(8,128)(2,1)S(1)}, bf16[6,4096]{1,0:T(8,128)(2,1)S(1)}, u32[]{:S(2)}, u32[]{:S(2)}) collective-permute-start(bf16[6,4096]{1,0:T(8,128)(2,1)S(1)} %reshape.31), channel_id=1, source_target_pairs={{0,32},{8,40},{16,48},{24,56},{32,64},{40,72},{48,80},{56,88},{64,... | collective-permute-start | bytes 147464 | tf_op jit(solution)/shard_map/ppermute | solution.py:40
  15.4 2.7 %collective-permute-start.4 = (bf16[6,4096]{1,0:T(8,128)(2,1)S(1)}, bf16[6,4096]{1,0:T(8,128)(2,1)S(1)}, u32[]{:S(2)}, u32[]{:S(2)}) collective-permute-start(bf16[6,4096]{1,0:T(8,128)(2,1)S(1)} %reshape.31), channel_id=1, source_target_pairs={{0,96},{8,104},{16,112},{24,120},{32,0},{40,8},{48,16},{56,24},{64... | collective-permute-start | bytes 147464 | tf_op jit(solution)/shard_map/ppermute | solution.py:40
  19.1 2.2 %collective-permute-start.6 = (bf16[6,4096]{1,0:T(8,128)(2,1)S(1)}, bf16[6,4096]{1,0:T(8,128)(2,1)S(1)}, u32[]{:S(2)}, u32[]{:S(2)}) collective-permute-start(bf16[6,4096]{1,0:T(8,128)(2,1)S(1)} %reshape.31), channel_id=1, source_target_pairs={{0,112},{8,120},{16,0},{24,8},{32,16},{40,24},{48,32},{56,40},{64,... | collective-permute-start | bytes 147464 | tf_op jit(solution)/shard_map/ppermute | solution.py:40
  22.4 1.1 %collective-permute-done.5 = bf16[6,4096]{1,0:T(8,128)(2,1)S(1)} collective-permute-done((bf16[6,4096]{1,0:T(8,128)(2,1)S(1)}, bf16[6,4096]{1,0:T(8,128)(2,1)S(1)}, u32[]{:S(2)}, u32[]{:S(2)}) %collective-permute-start.5) | collective-permute-done | bytes 49184 | tf_op jit(solution)/shard_map/ppermute | solution.py:40
  24.9 1.6 %collective-permute-start.8 = (bf16[48,4096]{1,0:T(8,128)(2,1)S(1)}, bf16[48,4096]{1,0:T(8,128)(2,1)S(1)}, u32[]{:S(2)}, u32[]{:S(2)}) collective-permute-start(bf16[48,4096]{1,0:T(8,128)(2,1)S(1)} %concatenate.19.refs_0_), channel_id=1, source_target_pairs={{0,4},{8,140},{16,20},{24,156},{32,36},{40,172},{48,52},{56,188},{... | collective-permute-start | bytes 1179656 | tf_op jit(solution)/shard_map/ppermute | solution.py:40
  26.4 2.1 %collective-permute-start.10 = (bf16[48,4096]{1,0:T(8,128)(2,1)S(1)}, bf16[48,4096]{1,0:T(8,128)(2,1)S(1)}, u32[]{:S(2)}, u32[]{:S(2)}) collective-permute-start(bf16[48,4096]{1,0:T(8,128)(2,1)S(1)} %concatenate.19.refs_0_), channel_id=1, source_target_pairs={{0,132},{8,12},{16,148},{24,28},{32,164},{40,44},{48,180},{56,60},... | collective-permute-start | bytes 1179656 | tf_op jit(solution)/shard_map/ppermute | solution.py:40
  29.9 1.4 %copy-done.4 = bf16[1,3,128,2048]{3,2,1,0:T(8,128)(2,1)S(1)} copy-done((bf16[1,3,128,2048]{3,2,1,0:T(8,128)(2,1)S(1)}, bf16[1,3,128,2048]{3,2,1,0:T(8,128)(2,1)}, u32[]{:S(2)}) %copy-start.4) | copy-done | bytes 1572888
  31.3 1.4 %pair_queries.1.pair_ref = bf16[6,1024,256]{2,1,0:T(8,128)(2,1)S(1)} custom-call(bf16[2,128]{1,0:T(2,128)(2,1)S(1)} %bitcast.405, bf16[3,128,2048]{2,1,0:T(8,128)(2,1)S(1)} %bitcast.403, bf16[3,128,2048]{2,1,0:T(8,128)(2,1)S(1)} %bitcast.404), custom_call_target="tpu_custom_call" | custom-call | flops 200000000 | bytes 6291456 | tf_op jit(solution)/shard_map/pair_queries/pallas_call | solution.py:85
  32.8 3.4 %copy-done = bf16[1,2,8192,256]{3,2,1,0:T(8,128)(2,1)S(1)} copy-done((bf16[1,2,8192,256]{3,2,1,0:T(8,128)(2,1)S(1)}, bf16[1,2,8192,256]{3,2,1,0:T(8,128)(2,1)}, u32[]{:S(2)}) %copy-start) | copy-done | bytes 8388632
  37.8 2.6 %collective-permute-start.9 = (bf16[48,4096]{1,0:T(8,128)(2,1)S(1)}, bf16[48,4096]{1,0:T(8,128)(2,1)S(1)}, u32[]{:S(2)}, u32[]{:S(2)}) collective-permute-start(bf16[48,4096]{1,0:T(8,128)(2,1)S(1)} %collective-permute-done.8.ready_ref.refs_0_), channel_id=1, source_target_pairs={{0,132},{8,12},{16,148},{24,28},{32,164},{40,44},{48,180},{56,60},... | collective-permute-start | bytes 1179656 | tf_op jit(solution)/shard_map/ppermute | solution.py:40
  40.4 3.4 %copy-done.1 = bf16[1,2,8192,256]{3,2,1,0:T(8,128)(2,1)S(1)} copy-done((bf16[1,2,8192,256]{3,2,1,0:T(8,128)(2,1)S(1)}, bf16[1,2,8192,256]{3,2,1,0:T(8,128)(2,1)}, u32[]{:S(2)}) %copy-start.1) | copy-done | bytes 8388632
  44.3 1.4 %project.4 = (f32[2,192,256]{2,1,0:T(8,128)S(1)}, f32[192,32]{1,0:T(8,128)S(1)}) custom-call(s32[1]{0:T(128)S(6)} %sub.44.which_ref, bf16[48,4096]{1,0:T(8,128)(2,1)S(1)} %collective-permute-done.8.ready_ref.refs_0_, bf16[48,4096]{1,0:T(8,128)(2,1)S(1)} %collective-permute-done.10.refs_1_, bf16[48,4096]{1,0:T(8,128)(2,1)S(1)} %collective-permute-done.11.refs_2_, ...), custom_call_target="tpu_custom_call" | custom-call | flops 805306368 | bytes 5767168 | tf_op jit(solution)/shard_map/project/pallas_call | solution.py:159
  46.8 1.7 %collective-permute-done.13.refs_1_.refs_3_ = bf16[48,4096]{1,0:T(8,128)(2,1)S(1)} collective-permute-done((bf16[48,4096]{1,0:T(8,128)(2,1)S(1)}, bf16[48,4096]{1,0:T(8,128)(2,1)S(1)}, u32[]{:S(2)}, u32[]{:S(2)}) %collective-permute-start.13) | collective-permute-done | bytes 393248 | tf_op jit(solution)/shard_map/ppermute | solution.py:40
  49.5 4.1 %attend.1 = (bf16[192,512]{1,0:T(8,128)(2,1)S(1)}, bf16[192,32]{1,0:T(8,128)(2,1)S(1)}, bf16[192,512]{1,0:T(8,128)(2,1)S(1)}, bf16[192,32]{1,0:T(8,128)(2,1)S(1)...) custom-call(s32[3]{0:T(128)S(1)} %copy-done.6, s32[3]{0:T(128)S(1)} %copy-done.7, ...), custom_call_target="tpu_custom_call" | custom-call | flops 1000000000 | bytes 3145728 | tf_op jit(solution)/shard_map/attend/pallas_call | solution.py:257
  53.6 1.9 %feature_grad.2 = (bf16[48,4096]{1,0:T(8,128)(2,1)S(1)}, bf16[48,4096]{1,0:T(8,128)(2,1)S(1)}, bf16[48,4096]{1,0:T(8,128)(2,1)S(1)}, bf16[48,4096]{1,0:T(8,128)(2,1)S(1)}) custom-call(s32[1]{0:T(128)} %bitcast.which_ref.side_ref, bf16[192,512]{1,0:T(8,128)(2,1)S(1)} %get-tuple-element.48.g_ref, bf16[192,32]{1,0:T(8,128)(2,1)S(1)} %get-tuple-element.49.m_ref, ...), custom_call_target="tpu_custom_call" | custom-call | flops 805306368 | bytes 5767168 | tf_op jit(solution)/shard_map/feature_grad/pallas_call | solution.py:291
  56.1 1.2 %collective-permute-done.15 = bf16[48,4096]{1,0:T(8,128)(2,1)S(1)} collective-permute-done((bf16[48,4096]{1,0:T(8,128)(2,1)S(1)}, bf16[48,4096]{1,0:T(8,128)(2,1)S(1)}, u32[]{:S(2)}, u32[]{:S(2)}) %collective-permute-start.15) | collective-permute-done | bytes 393248 | tf_op jit(solution)/shard_map/ppermute | solution.py:40
  57.4 2.7 %collective-permute-start.19 = (bf16[48,4096]{1,0:T(8,128)(2,1)S(1)}, bf16[48,4096]{1,0:T(8,128)(2,1)S(1)}, u32[]{:S(2)}, u32[]{:S(2)}) collective-permute-start(bf16[48,4096]{1,0:T(8,128)(2,1)S(1)} %add_convert_fusion.2), channel_id=1, source_target_pairs={{0,132},{8,12},{16,148},{24,28},{32,164},{40,44},{48,180},{56,60},... | collective-permute-start | bytes 1179656 | tf_op jit(solution)/shard_map/ppermute | solution.py:40
  60.1 1.9 %feature_grad.3 = (bf16[48,4096]{1,0:T(8,128)(2,1)S(1)}, bf16[48,4096]{1,0:T(8,128)(2,1)S(1)}, bf16[48,4096]{1,0:T(8,128)(2,1)S(1)}, bf16[48,4096]{1,0:T(8,128)(2,1)S(1)}) custom-call(s32[1]{0:T(128)S(6)} %sub.44.which_ref, bf16[192,512]{1,0:T(8,128)(2,1)S(1)} %get-tuple-element.55.g_ref, bf16[192,32]{1,0:T(8,128)(2,1)S(1)} %get-tuple-element.56.m_ref, ...), custom_call_target="tpu_custom_call" | custom-call | flops 805306368 | bytes 5767168 | tf_op jit(solution)/shard_map/feature_grad/pallas_call | solution.py:291
  65.0 1.5 %collective-permute-done.19 = bf16[48,4096]{1,0:T(8,128)(2,1)S(1)} collective-permute-done((bf16[48,4096]{1,0:T(8,128)(2,1)S(1)}, bf16[48,4096]{1,0:T(8,128)(2,1)S(1)}, u32[]{:S(2)}, u32[]{:S(2)}) %collective-permute-start.19) | collective-permute-done | bytes 393248 | tf_op jit(solution)/shard_map/ppermute | solution.py:40
  66.7 2.3 %collective-permute-done.22 = bf16[16,4352]{1,0:T(8,128)(2,1)S(1)} collective-permute-done((bf16[16,4352]{1,0:T(8,128)(2,1)S(1)}, bf16[16,4352]{1,0:T(8,128)(2,1)S(1)}, u32[]{:S(2)}, u32[]{:S(2)}) %collective-permute-start.22) | collective-permute-done | bytes 139296 | tf_op jit(solution)/shard_map/ppermute | solution.py:426
  71.3 7.2 %collective-permute-done.17 = bf16[48,4096]{1,0:T(8,128)(2,1)S(1)} collective-permute-done((bf16[48,4096]{1,0:T(8,128)(2,1)S(1)}, bf16[48,4096]{1,0:T(8,128)(2,1)S(1)}, u32[]{:S(2)}, u32[]{:S(2)}) %collective-permute-start.17) | collective-permute-done | bytes 393248 | tf_op jit(solution)/shard_map/ppermute | solution.py:40
  79.0 3.2 %collective-permute-start.26 = (bf16[6,4096]{1,0:T(8,128)(2,1)S(1)}, bf16[6,4096]{1,0:T(8,128)(2,1)S(1)}, u32[]{:S(2)}, u32[]{:S(2)}) collective-permute-start(bf16[6,4096]{1,0:T(8,128)(2,1)S(1)} %get-tuple-element.73), channel_id=1, source_target_pairs={{0,64},{8,72},{16,80},{24,88},{32,96},{40,104},{48,112},{56,120},{... | collective-permute-start | bytes 147464 | tf_op jit(solution)/shard_map/ppermute | solution.py:40
  82.2 1.4 %collective-permute-start.27 = (bf16[6,4096]{1,0:T(8,128)(2,1)S(1)}, bf16[6,4096]{1,0:T(8,128)(2,1)S(1)}, u32[]{:S(2)}, u32[]{:S(2)}) collective-permute-start(bf16[6,4096]{1,0:T(8,128)(2,1)S(1)} %get-tuple-element.79), channel_id=1, source_target_pairs={{0,80},{8,88},{16,96},{24,104},{32,112},{40,120},{48,0},{56,8},{64... | collective-permute-start | bytes 147464 | tf_op jit(solution)/shard_map/ppermute | solution.py:40
  83.6 2.4 %collective-permute-start.28 = (bf16[6,4096]{1,0:T(8,128)(2,1)S(1)}, bf16[6,4096]{1,0:T(8,128)(2,1)S(1)}, u32[]{:S(2)}, u32[]{:S(2)}) collective-permute-start(bf16[6,4096]{1,0:T(8,128)(2,1)S(1)} %get-tuple-element.78), channel_id=1, source_target_pairs={{0,48},{8,56},{16,64},{24,72},{32,80},{40,88},{48,96},{56,104},{64... | collective-permute-start | bytes 147464 | tf_op jit(solution)/shard_map/ppermute | solution.py:40
  86.1 2.1 %collective-permute-start.29 = (bf16[6,4096]{1,0:T(8,128)(2,1)S(1)}, bf16[6,4096]{1,0:T(8,128)(2,1)S(1)}, u32[]{:S(2)}, u32[]{:S(2)}) collective-permute-start(bf16[6,4096]{1,0:T(8,128)(2,1)S(1)} %get-tuple-element.77), channel_id=1, source_target_pairs={{0,96},{8,104},{16,112},{24,120},{32,0},{40,8},{48,16},{56,24},{64... | collective-permute-start | bytes 147464 | tf_op jit(solution)/shard_map/ppermute | solution.py:40
  89.0 3.8 %collective-permute-start.31 = (bf16[6,4096]{1,0:T(8,128)(2,1)S(1)}, bf16[6,4096]{1,0:T(8,128)(2,1)S(1)}, u32[]{:S(2)}, u32[]{:S(2)}) collective-permute-start(bf16[6,4096]{1,0:T(8,128)(2,1)S(1)} %get-tuple-element.75), channel_id=1, source_target_pairs={{0,112},{8,120},{16,0},{24,8},{32,16},{40,24},{48,32},{56,40},{64,... | collective-permute-start | bytes 147464 | tf_op jit(solution)/shard_map/ppermute | solution.py:40
  93.3 2.0 %collective-permute-done.29 = bf16[6,4096]{1,0:T(8,128)(2,1)S(1)} collective-permute-done((bf16[6,4096]{1,0:T(8,128)(2,1)S(1)}, bf16[6,4096]{1,0:T(8,128)(2,1)S(1)}, u32[]{:S(2)}, u32[]{:S(2)}) %collective-permute-start.29) | collective-permute-done | bytes 49184 | tf_op jit(solution)/shard_map/ppermute | solution.py:40
  96.2 2.1 %collective-permute-done.32 = bf16[6,4096]{1,0:T(8,128)(2,1)S(1)} collective-permute-done((bf16[6,4096]{1,0:T(8,128)(2,1)S(1)}, bf16[6,4096]{1,0:T(8,128)(2,1)S(1)}, u32[]{:S(2)}, u32[]{:S(2)}) %collective-permute-start.32) | collective-permute-done | bytes 49184 | tf_op jit(solution)/shard_map/ppermute | solution.py:40
  99.1 2.0 %collective-permute-done.33.facing_ref = bf16[32,4352]{1,0:T(8,128)(2,1)S(1)} collective-permute-done((bf16[32,4352]{1,0:T(8,128)(2,1)S(1)}, bf16[32,4352]{1,0:T(8,128)(2,1)S(1)}, u32[]{:S(2)}, u32[]{:S(2)}) %collective-permute-start.33) | collective-permute-done | bytes 278560 | tf_op jit(solution)/shard_map/ppermute | solution.py:444
  (84 shorter events, 20.4 us)
Async XLA Ops:
  1.6 16.5 %collective-permute-start = (bf16[6,4096]{1,0:T(8,128)(2,1)S(1)}, bf16[6,4096]{1,0:T(8,128)(2,1)S(1)}, u32[]{:S(2)}, u32[]{:S(2)}) collective-permute-start(bf16[6,4096]{1,0:T(8,128)(2,1)S(1)} %reshape.31), channel_id=1, source_target_pairs={{0,64},{8,72},{16,80},{24,88},{32,96},{40,104},{48,112},{56,120},{... | collective-permute-start | bytes 147464 | tf_op jit(solution)/shard_map/ppermute | solution.py:40
  8.9 10.2 %collective-permute-start.1 = (bf16[6,4096]{1,0:T(8,128)(2,1)S(1)}, bf16[6,4096]{1,0:T(8,128)(2,1)S(1)}, u32[]{:S(2)}, u32[]{:S(2)}) collective-permute-start(bf16[6,4096]{1,0:T(8,128)(2,1)S(1)} %reshape.31), channel_id=1, source_target_pairs={{0,48},{8,56},{16,64},{24,72},{32,80},{40,88},{48,96},{56,104},{64... | collective-permute-start | bytes 147464 | tf_op jit(solution)/shard_map/ppermute | solution.py:40
  10.8 10.5 %collective-permute-start.2 = (bf16[6,4096]{1,0:T(8,128)(2,1)S(1)}, bf16[6,4096]{1,0:T(8,128)(2,1)S(1)}, u32[]{:S(2)}, u32[]{:S(2)}) collective-permute-start(bf16[6,4096]{1,0:T(8,128)(2,1)S(1)} %reshape.31), channel_id=1, source_target_pairs={{0,80},{8,88},{16,96},{24,104},{32,112},{40,120},{48,0},{56,8},{64... | collective-permute-start | bytes 147464 | tf_op jit(solution)/shard_map/ppermute | solution.py:40
  13.9 7.7 %collective-permute-start.3 = (bf16[6,4096]{1,0:T(8,128)(2,1)S(1)}, bf16[6,4096]{1,0:T(8,128)(2,1)S(1)}, u32[]{:S(2)}, u32[]{:S(2)}) collective-permute-start(bf16[6,4096]{1,0:T(8,128)(2,1)S(1)} %reshape.31), channel_id=1, source_target_pairs={{0,32},{8,40},{16,48},{24,56},{32,64},{40,72},{48,80},{56,88},{64,... | collective-permute-start | bytes 147464 | tf_op jit(solution)/shard_map/ppermute | solution.py:40
  15.4 7.0 %collective-permute-start.4 = (bf16[6,4096]{1,0:T(8,128)(2,1)S(1)}, bf16[6,4096]{1,0:T(8,128)(2,1)S(1)}, u32[]{:S(2)}, u32[]{:S(2)}) collective-permute-start(bf16[6,4096]{1,0:T(8,128)(2,1)S(1)} %reshape.31), channel_id=1, source_target_pairs={{0,96},{8,104},{16,112},{24,120},{32,0},{40,8},{48,16},{56,24},{64... | collective-permute-start | bytes 147464 | tf_op jit(solution)/shard_map/ppermute | solution.py:40
  18.0 5.5 %collective-permute-start.5 = (bf16[6,4096]{1,0:T(8,128)(2,1)S(1)}, bf16[6,4096]{1,0:T(8,128)(2,1)S(1)}, u32[]{:S(2)}, u32[]{:S(2)}) collective-permute-start(bf16[6,4096]{1,0:T(8,128)(2,1)S(1)} %reshape.31), channel_id=1, source_target_pairs={{0,16},{8,24},{16,32},{24,40},{32,48},{40,56},{48,64},{56,72},{64,... | collective-permute-start | bytes 147464 | tf_op jit(solution)/shard_map/ppermute | solution.py:40
  19.1 4.6 %collective-permute-start.6 = (bf16[6,4096]{1,0:T(8,128)(2,1)S(1)}, bf16[6,4096]{1,0:T(8,128)(2,1)S(1)}, u32[]{:S(2)}, u32[]{:S(2)}) collective-permute-start(bf16[6,4096]{1,0:T(8,128)(2,1)S(1)} %reshape.31), channel_id=1, source_target_pairs={{0,112},{8,120},{16,0},{24,8},{32,16},{40,24},{48,32},{56,40},{64,... | collective-permute-start | bytes 147464 | tf_op jit(solution)/shard_map/ppermute | solution.py:40
  24.8 8.0 %collective-permute-start.7 = (bf16[48,4096]{1,0:T(8,128)(2,1)S(1)}, bf16[48,4096]{1,0:T(8,128)(2,1)S(1)}, u32[]{:S(2)}, u32[]{:S(2)}) collective-permute-start(bf16[48,4096]{1,0:T(8,128)(2,1)S(1)} %concatenate.19.refs_0_), channel_id=1, source_target_pairs={{0,8},{8,0},{16,24},{24,16},{32,40},{40,32},{48,56},{56,48},{64,72... | collective-permute-start | bytes 1179656 | tf_op jit(solution)/shard_map/ppermute | solution.py:40
  24.9 12.3 %collective-permute-start.8 = (bf16[48,4096]{1,0:T(8,128)(2,1)S(1)}, bf16[48,4096]{1,0:T(8,128)(2,1)S(1)}, u32[]{:S(2)}, u32[]{:S(2)}) collective-permute-start(bf16[48,4096]{1,0:T(8,128)(2,1)S(1)} %concatenate.19.refs_0_), channel_id=1, source_target_pairs={{0,4},{8,140},{16,20},{24,156},{32,36},{40,172},{48,52},{56,188},{... | collective-permute-start | bytes 1179656 | tf_op jit(solution)/shard_map/ppermute | solution.py:40
  26.4 11.1 %collective-permute-start.10 = (bf16[48,4096]{1,0:T(8,128)(2,1)S(1)}, bf16[48,4096]{1,0:T(8,128)(2,1)S(1)}, u32[]{:S(2)}, u32[]{:S(2)}) collective-permute-start(bf16[48,4096]{1,0:T(8,128)(2,1)S(1)} %concatenate.19.refs_0_), channel_id=1, source_target_pairs={{0,132},{8,12},{16,148},{24,28},{32,164},{40,44},{48,180},{56,60},... | collective-permute-start | bytes 1179656 | tf_op jit(solution)/shard_map/ppermute | solution.py:40
  37.2 7.1 %collective-permute-start.11 = (bf16[48,4096]{1,0:T(8,128)(2,1)S(1)}, bf16[48,4096]{1,0:T(8,128)(2,1)S(1)}, u32[]{:S(2)}, u32[]{:S(2)}) collective-permute-start(bf16[48,4096]{1,0:T(8,128)(2,1)S(1)} %collective-permute-done.8.ready_ref.refs_0_), channel_id=1, source_target_pairs={{0,8},{8,0},{16,24},{24,16},{32,40},{40,32},{48,56},{56,48},{64,72... | collective-permute-start | bytes 1179656 | tf_op jit(solution)/shard_map/ppermute | solution.py:40
  37.6 6.7 %collective-permute-start.12 = (bf16[48,4096]{1,0:T(8,128)(2,1)S(1)}, bf16[48,4096]{1,0:T(8,128)(2,1)S(1)}, u32[]{:S(2)}, u32[]{:S(2)}) collective-permute-start(bf16[48,4096]{1,0:T(8,128)(2,1)S(1)} %collective-permute-done.10.refs_1_), channel_id=1, source_target_pairs={{0,8},{8,0},{16,24},{24,16},{32,40},{40,32},{48,56},{56,48},{64,72... | collective-permute-start | bytes 1179656 | tf_op jit(solution)/shard_map/ppermute | solution.py:40
  37.8 9.0 %collective-permute-start.9 = (bf16[48,4096]{1,0:T(8,128)(2,1)S(1)}, bf16[48,4096]{1,0:T(8,128)(2,1)S(1)}, u32[]{:S(2)}, u32[]{:S(2)}) collective-permute-start(bf16[48,4096]{1,0:T(8,128)(2,1)S(1)} %collective-permute-done.8.ready_ref.refs_0_), channel_id=1, source_target_pairs={{0,132},{8,12},{16,148},{24,28},{32,164},{40,44},{48,180},{56,60},... | collective-permute-start | bytes 1179656 | tf_op jit(solution)/shard_map/ppermute | solution.py:40
  55.7 6.4 %collective-permute-start.21 = (bf16[192,32]{1,0:T(8,128)(2,1)S(1)}, bf16[192,32]{1,0:T(8,128)(2,1)S(1)}, u32[]{:S(2)}, u32[]{:S(2)}) collective-permute-start(bf16[192,32]{1,0:T(8,128)(2,1)S(1)} %get-tuple-element.61.mine_ref), channel_id=1, source_target_pairs={{0,4},{4,0},{1,5},{5,1},{2,6},{6,2},{3,7},{7,3},{8,12},{12,8},{9,1... | collective-permute-start | bytes 36872 | tf_op jit(solution)/shard_map/ppermute | solution.py:408
  55.7 15.6 %collective-permute-start.14 = (bf16[48,4096]{1,0:T(8,128)(2,1)S(1)}, bf16[48,4096]{1,0:T(8,128)(2,1)S(1)}, u32[]{:S(2)}, u32[]{:S(2)}) collective-permute-start(bf16[48,4096]{1,0:T(8,128)(2,1)S(1)} %get-tuple-element.51), channel_id=1, source_target_pairs={{0,8},{8,0},{16,24},{24,16},{32,40},{40,32},{48,56},{56,48},{64,72... | collective-permute-start | bytes 1179656 | tf_op jit(solution)/shard_map/ppermute | solution.py:40
  57.4 9.1 %collective-permute-start.19 = (bf16[48,4096]{1,0:T(8,128)(2,1)S(1)}, bf16[48,4096]{1,0:T(8,128)(2,1)S(1)}, u32[]{:S(2)}, u32[]{:S(2)}) collective-permute-start(bf16[48,4096]{1,0:T(8,128)(2,1)S(1)} %add_convert_fusion.2), channel_id=1, source_target_pairs={{0,132},{8,12},{16,148},{24,28},{32,164},{40,44},{48,180},{56,60},... | collective-permute-start | bytes 1179656 | tf_op jit(solution)/shard_map/ppermute | solution.py:40
  62.0 1.9 %collective-permute-start.18 = (bf16[48,4096]{1,0:T(8,128)(2,1)S(1)}, bf16[48,4096]{1,0:T(8,128)(2,1)S(1)}, u32[]{:S(2)}, u32[]{:S(2)}) collective-permute-start(bf16[48,4096]{1,0:T(8,128)(2,1)S(1)} %get-tuple-element.60), channel_id=1, source_target_pairs={{0,8},{8,0},{16,24},{24,16},{32,40},{40,32},{48,56},{56,48},{64,72... | collective-permute-start | bytes 1179656 | tf_op jit(solution)/shard_map/ppermute | solution.py:40
  62.9 6.2 %collective-permute-start.22 = (bf16[16,4352]{1,0:T(8,128)(2,1)S(1)}, bf16[16,4352]{1,0:T(8,128)(2,1)S(1)}, u32[]{:S(2)}, u32[]{:S(2)}) collective-permute-start(bf16[16,4352]{1,0:T(8,128)(2,1)S(1)} %get-tuple-element.80), channel_id=1, source_target_pairs={{0,1},{1,0},{2,3},{3,2},{4,5},{5,4},{6,7},{7,6},{8,9},{9,8},{10,11... | collective-permute-start | bytes 417800 | tf_op jit(solution)/shard_map/ppermute | solution.py:426
  63.7 5.7 %collective-permute-start.16 = (bf16[48,4096]{1,0:T(8,128)(2,1)S(1)}, bf16[48,4096]{1,0:T(8,128)(2,1)S(1)}, u32[]{:S(2)}, u32[]{:S(2)}) collective-permute-start(bf16[48,4096]{1,0:T(8,128)(2,1)S(1)} %get-tuple-element.58), channel_id=1, source_target_pairs={{0,8},{8,0},{16,24},{24,16},{32,40},{40,32},{48,56},{56,48},{64,72... | collective-permute-start | bytes 1179656 | tf_op jit(solution)/shard_map/ppermute | solution.py:40
  63.9 7.1 %collective-permute-start.24 = (bf16[16,4352]{1,0:T(8,128)(2,1)S(1)}, bf16[16,4352]{1,0:T(8,128)(2,1)S(1)}, u32[]{:S(2)}, u32[]{:S(2)}) collective-permute-start(bf16[16,4352]{1,0:T(8,128)(2,1)S(1)} %get-tuple-element.81), channel_id=1, source_target_pairs={{0,3},{1,2},{2,1},{3,0},{4,7},{5,6},{6,5},{7,4},{8,11},{9,10},{10,... | collective-permute-start | bytes 417800 | tf_op jit(solution)/shard_map/ppermute | solution.py:426
  66.6 11.9 %collective-permute-start.20 = (bf16[48,4096]{1,0:T(8,128)(2,1)S(1)}, bf16[48,4096]{1,0:T(8,128)(2,1)S(1)}, u32[]{:S(2)}, u32[]{:S(2)}) collective-permute-start(bf16[48,4096]{1,0:T(8,128)(2,1)S(1)} %add_convert_fusion), channel_id=1, source_target_pairs={{0,4},{8,140},{16,20},{24,156},{32,36},{40,172},{48,52},{56,188},{... | collective-permute-start | bytes 1179656 | tf_op jit(solution)/shard_map/ppermute | solution.py:40
  69.1 9.7 %collective-permute-start.23 = (bf16[16,4352]{1,0:T(8,128)(2,1)S(1)}, bf16[16,4352]{1,0:T(8,128)(2,1)S(1)}, u32[]{:S(2)}, u32[]{:S(2)}) collective-permute-start(bf16[16,4352]{1,0:T(8,128)(2,1)S(1)} %add_convert_fusion.6), channel_id=1, source_target_pairs={{0,3},{1,2},{2,1},{3,0},{4,7},{5,6},{6,5},{7,4},{8,11},{9,10},{10,... | collective-permute-start | bytes 417800 | tf_op jit(solution)/shard_map/ppermute | solution.py:434
  69.5 9.1 %collective-permute-start.17 = (bf16[48,4096]{1,0:T(8,128)(2,1)S(1)}, bf16[48,4096]{1,0:T(8,128)(2,1)S(1)}, u32[]{:S(2)}, u32[]{:S(2)}) collective-permute-start(bf16[48,4096]{1,0:T(8,128)(2,1)S(1)} %add_convert_fusion.1), channel_id=1, source_target_pairs={{0,132},{8,12},{16,148},{24,28},{32,164},{40,44},{48,180},{56,60},... | collective-permute-start | bytes 1179656 | tf_op jit(solution)/shard_map/ppermute | solution.py:40
  71.1 7.8 %collective-permute-start.25 = (bf16[16,4352]{1,0:T(8,128)(2,1)S(1)}, bf16[16,4352]{1,0:T(8,128)(2,1)S(1)}, u32[]{:S(2)}, u32[]{:S(2)}) collective-permute-start(bf16[16,4352]{1,0:T(8,128)(2,1)S(1)} %add_convert_fusion.4), channel_id=1, source_target_pairs={{0,1},{1,0},{2,3},{3,2},{4,5},{5,4},{6,7},{7,6},{8,9},{9,8},{10,11... | collective-permute-start | bytes 417800 | tf_op jit(solution)/shard_map/ppermute | solution.py:434
  79.0 10.0 %collective-permute-start.26 = (bf16[6,4096]{1,0:T(8,128)(2,1)S(1)}, bf16[6,4096]{1,0:T(8,128)(2,1)S(1)}, u32[]{:S(2)}, u32[]{:S(2)}) collective-permute-start(bf16[6,4096]{1,0:T(8,128)(2,1)S(1)} %get-tuple-element.73), channel_id=1, source_target_pairs={{0,64},{8,72},{16,80},{24,88},{32,96},{40,104},{48,112},{56,120},{... | collective-permute-start | bytes 147464 | tf_op jit(solution)/shard_map/ppermute | solution.py:40
  82.2 10.6 %collective-permute-start.27 = (bf16[6,4096]{1,0:T(8,128)(2,1)S(1)}, bf16[6,4096]{1,0:T(8,128)(2,1)S(1)}, u32[]{:S(2)}, u32[]{:S(2)}) collective-permute-start(bf16[6,4096]{1,0:T(8,128)(2,1)S(1)} %get-tuple-element.79), channel_id=1, source_target_pairs={{0,80},{8,88},{16,96},{24,104},{32,112},{40,120},{48,0},{56,8},{64... | collective-permute-start | bytes 147464 | tf_op jit(solution)/shard_map/ppermute | solution.py:40
  83.6 9.7 %collective-permute-start.28 = (bf16[6,4096]{1,0:T(8,128)(2,1)S(1)}, bf16[6,4096]{1,0:T(8,128)(2,1)S(1)}, u32[]{:S(2)}, u32[]{:S(2)}) collective-permute-start(bf16[6,4096]{1,0:T(8,128)(2,1)S(1)} %get-tuple-element.78), channel_id=1, source_target_pairs={{0,48},{8,56},{16,64},{24,72},{32,80},{40,88},{48,96},{56,104},{64... | collective-permute-start | bytes 147464 | tf_op jit(solution)/shard_map/ppermute | solution.py:40
  86.1 9.3 %collective-permute-start.29 = (bf16[6,4096]{1,0:T(8,128)(2,1)S(1)}, bf16[6,4096]{1,0:T(8,128)(2,1)S(1)}, u32[]{:S(2)}, u32[]{:S(2)}) collective-permute-start(bf16[6,4096]{1,0:T(8,128)(2,1)S(1)} %get-tuple-element.77), channel_id=1, source_target_pairs={{0,96},{8,104},{16,112},{24,120},{32,0},{40,8},{48,16},{56,24},{64... | collective-permute-start | bytes 147464 | tf_op jit(solution)/shard_map/ppermute | solution.py:40
  88.2 7.2 %collective-permute-start.30 = (bf16[6,4096]{1,0:T(8,128)(2,1)S(1)}, bf16[6,4096]{1,0:T(8,128)(2,1)S(1)}, u32[]{:S(2)}, u32[]{:S(2)}) collective-permute-start(bf16[6,4096]{1,0:T(8,128)(2,1)S(1)} %get-tuple-element.76), channel_id=1, source_target_pairs={{0,32},{8,40},{16,48},{24,56},{32,64},{40,72},{48,80},{56,88},{64,... | collective-permute-start | bytes 147464 | tf_op jit(solution)/shard_map/ppermute | solution.py:40
  89.0 7.2 %collective-permute-start.31 = (bf16[6,4096]{1,0:T(8,128)(2,1)S(1)}, bf16[6,4096]{1,0:T(8,128)(2,1)S(1)}, u32[]{:S(2)}, u32[]{:S(2)}) collective-permute-start(bf16[6,4096]{1,0:T(8,128)(2,1)S(1)} %get-tuple-element.75), channel_id=1, source_target_pairs={{0,112},{8,120},{16,0},{24,8},{32,16},{40,24},{48,32},{56,40},{64,... | collective-permute-start | bytes 147464 | tf_op jit(solution)/shard_map/ppermute | solution.py:40
  92.8 5.5 %collective-permute-start.32 = (bf16[6,4096]{1,0:T(8,128)(2,1)S(1)}, bf16[6,4096]{1,0:T(8,128)(2,1)S(1)}, u32[]{:S(2)}, u32[]{:S(2)}) collective-permute-start(bf16[6,4096]{1,0:T(8,128)(2,1)S(1)} %get-tuple-element.74), channel_id=1, source_target_pairs={{0,16},{8,24},{16,32},{24,40},{32,48},{40,56},{48,64},{56,72},{64,... | collective-permute-start | bytes 147464 | tf_op jit(solution)/shard_map/ppermute | solution.py:40
  93.3 7.8 %collective-permute-start.33 = (bf16[32,4352]{1,0:T(8,128)(2,1)S(1)}, bf16[32,4352]{1,0:T(8,128)(2,1)S(1)}, u32[]{:S(2)}, u32[]{:S(2)}) collective-permute-start(bf16[32,4352]{1,0:T(8,128)(2,1)S(1)} %pad_maximum_fusion.mine_ref), channel_id=1, source_target_pairs={{0,4},{4,0},{1,5},{5,1},{2,6},{6,2},{3,7},{7,3},{8,12},{12,8},{9,1... | collective-permute-start | bytes 835592 | tf_op jit(solution)/shard_map/ppermute | solution.py:444
  (10 other events, 77.1 us)

commit v11 on v10

--- a/solution.py
+++ b/solution.py
@@ -1,5 +1,6 @@
 import jax
 import jax.numpy as jnp
+import numpy as np
 from jax import lax
 from jax.experimental import pallas as pl
 from jax.experimental.pallas import tpu as pltpu
@@ -321,23 +322,19 @@
     )(back, mine, facing, *blocks)
 
 
-def row_tokens(x_hi, z, core, x_lo):
-    def base_rows(chain, x_high):
-        rows = []
-        for k in (*SHIFTS, 0):
-            token = ((x_high * NZ + (z - k) % NZ) * 2 + chain) * 2
-            for batch in range(3):
-                rows += [batch * 64 + token, batch * 64 + token + 1]
-        return jnp.stack(rows)
-
-    own_half, other_half = [], []
-    for chain in (core, 1 - core):
-        own_half += [base_rows(chain, x_hi)]
-        near = jnp.where(chain == 0, x_hi, 1 - x_hi)
-        other_half += [base_rows(chain, near), base_rows(chain, 1 - near)]
-    for chain in (core, 1 - core):
-        own_half += [base_rows(chain, 1 - x_hi)]
-    return jnp.concatenate(own_half), jnp.concatenate(other_half)
+def row_tokens(x_hi, z, core):
+    row = np.arange(192)
+    shift = np.array((*SHIFTS, 0))[row % 48 // 6]
+    place = row % 6 // 2 * 64 + row % 2
+
+    def rows(theirs, flip):
+        chain = jnp.where(theirs, 1 - core, core)
+        x_high = jnp.where(flip(chain), 1 - x_hi, x_hi)
+        return place + ((x_high * NZ + (z - shift + NZ) % NZ) * 2 + chain) * 2
+
+    own = rows(row // 48 % 2 == 1, lambda chain: row // 96 == 1)
+    other = rows(row // 96 == 1, lambda chain: (row // 48 % 2) != chain)
+    return own, other
 
 
 def per_device(
@@ -370,7 +367,7 @@
         [jnp.pad(up_maps[0], ((0, 0), (0, width))), jnp.pad(up_maps[1], ((0, 0), (width, 0)))]
     )
     own_token, other_token = row_tokens(
-        late_section // 16, (late_section // 2) % NZ, late_section % 2, late_side
+        late_section // 16, (late_section // 2) % NZ, late_section % 2
     )
     line = jnp.arange(own_token.shape[0])
     maps = [

time: 104 us -> 105 us (level)
  waiting for transfers between devices: 25.3 us -> 28.2 us
  local copies, waits for them, and re-layouts: 12 us -> 10.7 us
    ppermute x28, waiting for transfers between devices: 20.3 us -> 25.2 us  [move(): return lax.ppermute(block, PLANE, pairs)]
    ppermute x2, waiting for transfers between devices: 2.97 us -> 0.9 us  [per_device(): early_sums = [lax.ppermute(part, 'dp', pairs) for part, pairs, _ in ways]]
    unnamed x16 -> x18, local copies, waits for them, and re-layouts: 8.18 us -> 7.5 us
  transfers between devices with their start and end apart: 34 -> 34, of which waited for: 16 -> 15; matrix products, arithmetic and copies ran while one was open for 3% -> 3% of each run, Pallas kernels for 7% -> 7%
where the time goes in v11:
time: 105 us; the launch traced here: 104 us
  starting transfers between devices  47.4 us (45%)
  waiting for transfers between devices  28.2 us (27%)
  Pallas kernels  14.9 us (14%)
  local copies, waits for them, and re-layouts  10.7 us (10%)
  other arithmetic  1.69 us (2%)
    ppermute x28, starting transfers between devices, move(): return lax.ppermute(block, PLANE, pairs)  44.2 us
    ppermute x28, waiting for transfers between devices, move(): return lax.ppermute(block, PLANE, pairs)  25.2 us
    unnamed x18, local copies, waits for them, and re-layouts  7.5 us
    pallas_call x1, Pallas kernels, attend(): pl.pallas_call(attention_kernel, out_shape=[jax.ShapeDtypeStruct((rows, 2...  4.06 us
    pallas_call x2, Pallas kernels, feature_grad(): pl.pallas_call(feature_kernel, out_shape=[jax.ShapeDtypeStruct((rows // 4...  3.84 us
    pallas_call x3, Pallas kernels, project(): pl.pallas_call(project_kernel, out_shape=[jax.ShapeDtypeStruct((2, count,...  3.34 us
  transfers between devices with their start and end apart: 34, of which 15 were waited for; matrix products, arithmetic and copies ran while one was open for 3% of the time, Pallas kernels for 7%

profile of v11, /device:TPU:24, one launch (start us, length us, event | category | flops | bytes accessed | tf_op | source)
XLA Modules:
  0.0 103.8 jit_solution(4061344292372931125)
XLA Ops:
  1.5 7.3 %collective-permute-start = (bf16[6,4096]{1,0:T(8,128)(2,1)S(1)}, bf16[6,4096]{1,0:T(8,128)(2,1)S(1)}, u32[]{:S(2)}, u32[]{:S(2)}) collective-permute-start(bf16[6,4096]{1,0:T(8,128)(2,1)S(1)} %reshape.31), channel_id=1, source_target_pairs={{0,64},{8,72},{16,80},{24,88},{32,96},{40,104},{48,112},{56,120},{... | collective-permute-start | bytes 147464 | tf_op jit(solution)/shard_map/ppermute | solution.py:41
  8.7 1.9 %collective-permute-start.1 = (bf16[6,4096]{1,0:T(8,128)(2,1)S(1)}, bf16[6,4096]{1,0:T(8,128)(2,1)S(1)}, u32[]{:S(2)}, u32[]{:S(2)}) collective-permute-start(bf16[6,4096]{1,0:T(8,128)(2,1)S(1)} %reshape.31), channel_id=1, source_target_pairs={{0,48},{8,56},{16,64},{24,72},{32,80},{40,88},{48,96},{56,104},{64... | collective-permute-start | bytes 147464 | tf_op jit(solution)/shard_map/ppermute | solution.py:41
  10.7 3.1 %collective-permute-start.2 = (bf16[6,4096]{1,0:T(8,128)(2,1)S(1)}, bf16[6,4096]{1,0:T(8,128)(2,1)S(1)}, u32[]{:S(2)}, u32[]{:S(2)}) collective-permute-start(bf16[6,4096]{1,0:T(8,128)(2,1)S(1)} %reshape.31), channel_id=1, source_target_pairs={{0,80},{8,88},{16,96},{24,104},{32,112},{40,120},{48,0},{56,8},{64... | collective-permute-start | bytes 147464 | tf_op jit(solution)/shard_map/ppermute | solution.py:41
  13.8 1.5 %collective-permute-start.3 = (bf16[6,4096]{1,0:T(8,128)(2,1)S(1)}, bf16[6,4096]{1,0:T(8,128)(2,1)S(1)}, u32[]{:S(2)}, u32[]{:S(2)}) collective-permute-start(bf16[6,4096]{1,0:T(8,128)(2,1)S(1)} %reshape.31), channel_id=1, source_target_pairs={{0,32},{8,40},{16,48},{24,56},{32,64},{40,72},{48,80},{56,88},{64,... | collective-permute-start | bytes 147464 | tf_op jit(solution)/shard_map/ppermute | solution.py:41
  15.2 2.7 %collective-permute-start.4 = (bf16[6,4096]{1,0:T(8,128)(2,1)S(1)}, bf16[6,4096]{1,0:T(8,128)(2,1)S(1)}, u32[]{:S(2)}, u32[]{:S(2)}) collective-permute-start(bf16[6,4096]{1,0:T(8,128)(2,1)S(1)} %reshape.31), channel_id=1, source_target_pairs={{0,96},{8,104},{16,112},{24,120},{32,0},{40,8},{48,16},{56,24},{64... | collective-permute-start | bytes 147464 | tf_op jit(solution)/shard_map/ppermute | solution.py:41
  18.9 2.2 %collective-permute-start.6 = (bf16[6,4096]{1,0:T(8,128)(2,1)S(1)}, bf16[6,4096]{1,0:T(8,128)(2,1)S(1)}, u32[]{:S(2)}, u32[]{:S(2)}) collective-permute-start(bf16[6,4096]{1,0:T(8,128)(2,1)S(1)} %reshape.31), channel_id=1, source_target_pairs={{0,112},{8,120},{16,0},{24,8},{32,16},{40,24},{48,32},{56,40},{64,... | collective-permute-start | bytes 147464 | tf_op jit(solution)/shard_map/ppermute | solution.py:41
  24.4 1.6 %collective-permute-start.8 = (bf16[48,4096]{1,0:T(8,128)(2,1)S(1)}, bf16[48,4096]{1,0:T(8,128)(2,1)S(1)}, u32[]{:S(2)}, u32[]{:S(2)}) collective-permute-start(bf16[48,4096]{1,0:T(8,128)(2,1)S(1)} %concatenate.13.refs_0_), channel_id=1, source_target_pairs={{0,4},{8,140},{16,20},{24,156},{32,36},{40,172},{48,52},{56,188},{... | collective-permute-start | bytes 1179656 | tf_op jit(solution)/shard_map/ppermute | solution.py:41
  26.0 2.1 %collective-permute-start.10 = (bf16[48,4096]{1,0:T(8,128)(2,1)S(1)}, bf16[48,4096]{1,0:T(8,128)(2,1)S(1)}, u32[]{:S(2)}, u32[]{:S(2)}) collective-permute-start(bf16[48,4096]{1,0:T(8,128)(2,1)S(1)} %concatenate.13.refs_0_), channel_id=1, source_target_pairs={{0,132},{8,12},{16,148},{24,28},{32,164},{40,44},{48,180},{56,60},... | collective-permute-start | bytes 1179656 | tf_op jit(solution)/shard_map/ppermute | solution.py:41
  29.6 1.4 %copy-done.3 = bf16[1,3,128,2048]{3,2,1,0:T(8,128)(2,1)S(1)} copy-done((bf16[1,3,128,2048]{3,2,1,0:T(8,128)(2,1)S(1)}, bf16[1,3,128,2048]{3,2,1,0:T(8,128)(2,1)}, u32[]{:S(2)}) %copy-start.3) | copy-done | bytes 1572888
  31.0 1.4 %copy-done.4 = bf16[1,3,128,2048]{3,2,1,0:T(8,128)(2,1)S(1)} copy-done((bf16[1,3,128,2048]{3,2,1,0:T(8,128)(2,1)S(1)}, bf16[1,3,128,2048]{3,2,1,0:T(8,128)(2,1)}, u32[]{:S(2)}) %copy-start.4) | copy-done | bytes 1572888
  33.1 1.4 %pair_queries.1.pair_ref = bf16[6,1024,256]{2,1,0:T(8,128)(2,1)S(1)} custom-call(bf16[2,128]{1,0:T(2,128)(2,1)S(1)} %bitcast.21, bf16[3,128,2048]{2,1,0:T(8,128)(2,1)S(1)} %bitcast.19, bf16[3,128,2048]{2,1,0:T(8,128)(2,1)S(1)} %bitcast.20), custom_call_target="tpu_custom_call" | custom-call | flops 200000000 | bytes 6291456 | tf_op jit(solution)/shard_map/pair_queries/pallas_call | solution.py:86
  34.6 3.4 %copy-done = bf16[1,2,8192,256]{3,2,1,0:T(8,128)(2,1)S(1)} copy-done((bf16[1,2,8192,256]{3,2,1,0:T(8,128)(2,1)S(1)}, bf16[1,2,8192,256]{3,2,1,0:T(8,128)(2,1)}, u32[]{:S(2)}) %copy-start) | copy-done | bytes 8388632
  39.6 1.2 %collective-permute-start.9 = (bf16[48,4096]{1,0:T(8,128)(2,1)S(1)}, bf16[48,4096]{1,0:T(8,128)(2,1)S(1)}, u32[]{:S(2)}, u32[]{:S(2)}) collective-permute-start(bf16[48,4096]{1,0:T(8,128)(2,1)S(1)} %collective-permute-done.8.ready_ref.refs_0_), channel_id=1, source_target_pairs={{0,132},{8,12},{16,148},{24,28},{32,164},{40,44},{48,180},{56,60},... | collective-permute-start | bytes 1179656 | tf_op jit(solution)/shard_map/ppermute | solution.py:41
  41.9 1.4 %project.4 = (f32[2,192,256]{2,1,0:T(8,128)S(1)}, f32[192,32]{1,0:T(8,128)S(1)}) custom-call(s32[1]{0:T(128)S(6)} %sub.32.which_ref, bf16[48,4096]{1,0:T(8,128)(2,1)S(1)} %collective-permute-done.8.ready_ref.refs_0_, bf16[48,4096]{1,0:T(8,128)(2,1)S(1)} %collective-permute-done.10.refs_1_, bf16[48,4096]{1,0:T(8,128)(2,1)S(1)} %collective-permute-done.11.refs_2_, ...), custom_call_target="tpu_custom_call" | custom-call | flops 805306368 | bytes 5767168 | tf_op jit(solution)/shard_map/project/pallas_call | solution.py:160
  43.4 5.2 %collective-permute-done.9.refs_0_.refs_2_ = bf16[48,4096]{1,0:T(8,128)(2,1)S(1)} collective-permute-done((bf16[48,4096]{1,0:T(8,128)(2,1)S(1)}, bf16[48,4096]{1,0:T(8,128)(2,1)S(1)}, u32[]{:S(2)}, u32[]{:S(2)}) %collective-permute-start.9) | collective-permute-done | bytes 393248 | tf_op jit(solution)/shard_map/ppermute | solution.py:41
  48.6 1.7 %collective-permute-done.13.refs_1_.refs_3_ = bf16[48,4096]{1,0:T(8,128)(2,1)S(1)} collective-permute-done((bf16[48,4096]{1,0:T(8,128)(2,1)S(1)}, bf16[48,4096]{1,0:T(8,128)(2,1)S(1)}, u32[]{:S(2)}, u32[]{:S(2)}) %collective-permute-start.13) | collective-permute-done | bytes 393248 | tf_op jit(solution)/shard_map/ppermute | solution.py:41
  51.3 4.1 %attend.1 = (bf16[192,512]{1,0:T(8,128)(2,1)S(1)}, bf16[192,32]{1,0:T(8,128)(2,1)S(1)}, bf16[192,512]{1,0:T(8,128)(2,1)S(1)}, bf16[192,32]{1,0:T(8,128)(2,1)S(1)...) custom-call(s32[3]{0:T(128)S(1)} %copy-done.7, s32[3]{0:T(128)S(1)} %copy-done.8, ...), custom_call_target="tpu_custom_call" | custom-call | flops 1000000000 | bytes 3145728 | tf_op jit(solution)/shard_map/attend/pallas_call | solution.py:258
  55.4 1.9 %feature_grad.2 = (bf16[48,4096]{1,0:T(8,128)(2,1)S(1)}, bf16[48,4096]{1,0:T(8,128)(2,1)S(1)}, bf16[48,4096]{1,0:T(8,128)(2,1)S(1)}, bf16[48,4096]{1,0:T(8,128)(2,1)S(1)}) custom-call(s32[1]{0:T(128)} %bitcast.which_ref.side_ref, bf16[192,512]{1,0:T(8,128)(2,1)S(1)} %get-tuple-element.48.g_ref, bf16[192,32]{1,0:T(8,128)(2,1)S(1)} %get-tuple-element.49.m_ref, ...), custom_call_target="tpu_custom_call" | custom-call | flops 805306368 | bytes 5767168 | tf_op jit(solution)/shard_map/feature_grad/pallas_call | solution.py:292
  57.9 1.2 %collective-permute-done.15 = bf16[48,4096]{1,0:T(8,128)(2,1)S(1)} collective-permute-done((bf16[48,4096]{1,0:T(8,128)(2,1)S(1)}, bf16[48,4096]{1,0:T(8,128)(2,1)S(1)}, u32[]{:S(2)}, u32[]{:S(2)}) %collective-permute-start.15) | collective-permute-done | bytes 393248 | tf_op jit(solution)/shard_map/ppermute | solution.py:41
  59.2 1.3 %collective-permute-start.19 = (bf16[48,4096]{1,0:T(8,128)(2,1)S(1)}, bf16[48,4096]{1,0:T(8,128)(2,1)S(1)}, u32[]{:S(2)}, u32[]{:S(2)}) collective-permute-start(bf16[48,4096]{1,0:T(8,128)(2,1)S(1)} %add_convert_fusion.2), channel_id=1, source_target_pairs={{0,132},{8,12},{16,148},{24,28},{32,164},{40,44},{48,180},{56,60},... | collective-permute-start | bytes 1179656 | tf_op jit(solution)/shard_map/ppermute | solution.py:41
  60.4 1.9 %feature_grad.3 = (bf16[48,4096]{1,0:T(8,128)(2,1)S(1)}, bf16[48,4096]{1,0:T(8,128)(2,1)S(1)}, bf16[48,4096]{1,0:T(8,128)(2,1)S(1)}, bf16[48,4096]{1,0:T(8,128)(2,1)S(1)}) custom-call(s32[1]{0:T(128)S(6)} %sub.32.which_ref, bf16[192,512]{1,0:T(8,128)(2,1)S(1)} %get-tuple-element.55.g_ref, bf16[192,32]{1,0:T(8,128)(2,1)S(1)} %get-tuple-element.56.m_ref, ...), custom_call_target="tpu_custom_call" | custom-call | flops 805306368 | bytes 5767168 | tf_op jit(solution)/shard_map/feature_grad/pallas_call | solution.py:292
  65.3 2.9 %collective-permute-done.19 = bf16[48,4096]{1,0:T(8,128)(2,1)S(1)} collective-permute-done((bf16[48,4096]{1,0:T(8,128)(2,1)S(1)}, bf16[48,4096]{1,0:T(8,128)(2,1)S(1)}, u32[]{:S(2)}, u32[]{:S(2)}) %collective-permute-start.19) | collective-permute-done | bytes 393248 | tf_op jit(solution)/shard_map/ppermute | solution.py:41
  69.8 2.4 %collective-permute-start.17 = (bf16[48,4096]{1,0:T(8,128)(2,1)S(1)}, bf16[48,4096]{1,0:T(8,128)(2,1)S(1)}, u32[]{:S(2)}, u32[]{:S(2)}) collective-permute-start(bf16[48,4096]{1,0:T(8,128)(2,1)S(1)} %add_convert_fusion.1), channel_id=1, source_target_pairs={{0,132},{8,12},{16,148},{24,28},{32,164},{40,44},{48,180},{56,60},... | collective-permute-start | bytes 1179656 | tf_op jit(solution)/shard_map/ppermute | solution.py:41
  73.3 5.8 %collective-permute-done.17 = bf16[48,4096]{1,0:T(8,128)(2,1)S(1)} collective-permute-done((bf16[48,4096]{1,0:T(8,128)(2,1)S(1)}, bf16[48,4096]{1,0:T(8,128)(2,1)S(1)}, u32[]{:S(2)}, u32[]{:S(2)}) %collective-permute-start.17) | collective-permute-done | bytes 393248 | tf_op jit(solution)/shard_map/ppermute | solution.py:41
  80.6 3.2 %collective-permute-start.26 = (bf16[6,4096]{1,0:T(8,128)(2,1)S(1)}, bf16[6,4096]{1,0:T(8,128)(2,1)S(1)}, u32[]{:S(2)}, u32[]{:S(2)}) collective-permute-start(bf16[6,4096]{1,0:T(8,128)(2,1)S(1)} %get-tuple-element.73), channel_id=1, source_target_pairs={{0,64},{8,72},{16,80},{24,88},{32,96},{40,104},{48,112},{56,120},{... | collective-permute-start | bytes 147464 | tf_op jit(solution)/shard_map/ppermute | solution.py:41
  83.9 1.4 %collective-permute-start.27 = (bf16[6,4096]{1,0:T(8,128)(2,1)S(1)}, bf16[6,4096]{1,0:T(8,128)(2,1)S(1)}, u32[]{:S(2)}, u32[]{:S(2)}) collective-permute-start(bf16[6,4096]{1,0:T(8,128)(2,1)S(1)} %get-tuple-element.79), channel_id=1, source_target_pairs={{0,80},{8,88},{16,96},{24,104},{32,112},{40,120},{48,0},{56,8},{64... | collective-permute-start | bytes 147464 | tf_op jit(solution)/shard_map/ppermute | solution.py:41
  85.3 2.4 %collective-permute-start.28 = (bf16[6,4096]{1,0:T(8,128)(2,1)S(1)}, bf16[6,4096]{1,0:T(8,128)(2,1)S(1)}, u32[]{:S(2)}, u32[]{:S(2)}) collective-permute-start(bf16[6,4096]{1,0:T(8,128)(2,1)S(1)} %get-tuple-element.78), channel_id=1, source_target_pairs={{0,48},{8,56},{16,64},{24,72},{32,80},{40,88},{48,96},{56,104},{64... | collective-permute-start | bytes 147464 | tf_op jit(solution)/shard_map/ppermute | solution.py:41
  87.7 2.1 %collective-permute-start.29 = (bf16[6,4096]{1,0:T(8,128)(2,1)S(1)}, bf16[6,4096]{1,0:T(8,128)(2,1)S(1)}, u32[]{:S(2)}, u32[]{:S(2)}) collective-permute-start(bf16[6,4096]{1,0:T(8,128)(2,1)S(1)} %get-tuple-element.77), channel_id=1, source_target_pairs={{0,96},{8,104},{16,112},{24,120},{32,0},{40,8},{48,16},{56,24},{64... | collective-permute-start | bytes 147464 | tf_op jit(solution)/shard_map/ppermute | solution.py:41
  90.6 3.8 %collective-permute-start.31 = (bf16[6,4096]{1,0:T(8,128)(2,1)S(1)}, bf16[6,4096]{1,0:T(8,128)(2,1)S(1)}, u32[]{:S(2)}, u32[]{:S(2)}) collective-permute-start(bf16[6,4096]{1,0:T(8,128)(2,1)S(1)} %get-tuple-element.75), channel_id=1, source_target_pairs={{0,112},{8,120},{16,0},{24,8},{32,16},{40,24},{48,32},{56,40},{64,... | collective-permute-start | bytes 147464 | tf_op jit(solution)/shard_map/ppermute | solution.py:41
  95.0 2.0 %collective-permute-done.29 = bf16[6,4096]{1,0:T(8,128)(2,1)S(1)} collective-permute-done((bf16[6,4096]{1,0:T(8,128)(2,1)S(1)}, bf16[6,4096]{1,0:T(8,128)(2,1)S(1)}, u32[]{:S(2)}, u32[]{:S(2)}) %collective-permute-start.29) | collective-permute-done | bytes 49184 | tf_op jit(solution)/shard_map/ppermute | solution.py:41
  97.9 2.1 %collective-permute-done.32 = bf16[6,4096]{1,0:T(8,128)(2,1)S(1)} collective-permute-done((bf16[6,4096]{1,0:T(8,128)(2,1)S(1)}, bf16[6,4096]{1,0:T(8,128)(2,1)S(1)}, u32[]{:S(2)}, u32[]{:S(2)}) %collective-permute-start.32) | collective-permute-done | bytes 49184 | tf_op jit(solution)/shard_map/ppermute | solution.py:41
  100.7 2.0 %collective-permute-done.33.facing_ref = bf16[32,4352]{1,0:T(8,128)(2,1)S(1)} collective-permute-done((bf16[32,4352]{1,0:T(8,128)(2,1)S(1)}, bf16[32,4352]{1,0:T(8,128)(2,1)S(1)}, u32[]{:S(2)}, u32[]{:S(2)}) %collective-permute-start.33) | collective-permute-done | bytes 278560 | tf_op jit(solution)/shard_map/ppermute | solution.py:441
  (85 shorter events, 22.9 us)
Async XLA Ops:
  1.5 16.5 %collective-permute-start = (bf16[6,4096]{1,0:T(8,128)(2,1)S(1)}, bf16[6,4096]{1,0:T(8,128)(2,1)S(1)}, u32[]{:S(2)}, u32[]{:S(2)}) collective-permute-start(bf16[6,4096]{1,0:T(8,128)(2,1)S(1)} %reshape.31), channel_id=1, source_target_pairs={{0,64},{8,72},{16,80},{24,88},{32,96},{40,104},{48,112},{56,120},{... | collective-permute-start | bytes 147464 | tf_op jit(solution)/shard_map/ppermute | solution.py:41
  8.7 10.2 %collective-permute-start.1 = (bf16[6,4096]{1,0:T(8,128)(2,1)S(1)}, bf16[6,4096]{1,0:T(8,128)(2,1)S(1)}, u32[]{:S(2)}, u32[]{:S(2)}) collective-permute-start(bf16[6,4096]{1,0:T(8,128)(2,1)S(1)} %reshape.31), channel_id=1, source_target_pairs={{0,48},{8,56},{16,64},{24,72},{32,80},{40,88},{48,96},{56,104},{64... | collective-permute-start | bytes 147464 | tf_op jit(solution)/shard_map/ppermute | solution.py:41
  10.7 10.5 %collective-permute-start.2 = (bf16[6,4096]{1,0:T(8,128)(2,1)S(1)}, bf16[6,4096]{1,0:T(8,128)(2,1)S(1)}, u32[]{:S(2)}, u32[]{:S(2)}) collective-permute-start(bf16[6,4096]{1,0:T(8,128)(2,1)S(1)} %reshape.31), channel_id=1, source_target_pairs={{0,80},{8,88},{16,96},{24,104},{32,112},{40,120},{48,0},{56,8},{64... | collective-permute-start | bytes 147464 | tf_op jit(solution)/shard_map/ppermute | solution.py:41
  13.8 7.7 %collective-permute-start.3 = (bf16[6,4096]{1,0:T(8,128)(2,1)S(1)}, bf16[6,4096]{1,0:T(8,128)(2,1)S(1)}, u32[]{:S(2)}, u32[]{:S(2)}) collective-permute-start(bf16[6,4096]{1,0:T(8,128)(2,1)S(1)} %reshape.31), channel_id=1, source_target_pairs={{0,32},{8,40},{16,48},{24,56},{32,64},{40,72},{48,80},{56,88},{64,... | collective-permute-start | bytes 147464 | tf_op jit(solution)/shard_map/ppermute | solution.py:41
  15.2 7.0 %collective-permute-start.4 = (bf16[6,4096]{1,0:T(8,128)(2,1)S(1)}, bf16[6,4096]{1,0:T(8,128)(2,1)S(1)}, u32[]{:S(2)}, u32[]{:S(2)}) collective-permute-start(bf16[6,4096]{1,0:T(8,128)(2,1)S(1)} %reshape.31), channel_id=1, source_target_pairs={{0,96},{8,104},{16,112},{24,120},{32,0},{40,8},{48,16},{56,24},{64... | collective-permute-start | bytes 147464 | tf_op jit(solution)/shard_map/ppermute | solution.py:41
  17.9 5.5 %collective-permute-start.5 = (bf16[6,4096]{1,0:T(8,128)(2,1)S(1)}, bf16[6,4096]{1,0:T(8,128)(2,1)S(1)}, u32[]{:S(2)}, u32[]{:S(2)}) collective-permute-start(bf16[6,4096]{1,0:T(8,128)(2,1)S(1)} %reshape.31), channel_id=1, source_target_pairs={{0,16},{8,24},{16,32},{24,40},{32,48},{40,56},{48,64},{56,72},{64,... | collective-permute-start | bytes 147464 | tf_op jit(solution)/shard_map/ppermute | solution.py:41
  18.9 4.6 %collective-permute-start.6 = (bf16[6,4096]{1,0:T(8,128)(2,1)S(1)}, bf16[6,4096]{1,0:T(8,128)(2,1)S(1)}, u32[]{:S(2)}, u32[]{:S(2)}) collective-permute-start(bf16[6,4096]{1,0:T(8,128)(2,1)S(1)} %reshape.31), channel_id=1, source_target_pairs={{0,112},{8,120},{16,0},{24,8},{32,16},{40,24},{48,32},{56,40},{64,... | collective-permute-start | bytes 147464 | tf_op jit(solution)/shard_map/ppermute | solution.py:41
  24.3 10.2 %collective-permute-start.7 = (bf16[48,4096]{1,0:T(8,128)(2,1)S(1)}, bf16[48,4096]{1,0:T(8,128)(2,1)S(1)}, u32[]{:S(2)}, u32[]{:S(2)}) collective-permute-start(bf16[48,4096]{1,0:T(8,128)(2,1)S(1)} %concatenate.13.refs_0_), channel_id=1, source_target_pairs={{0,8},{8,0},{16,24},{24,16},{32,40},{40,32},{48,56},{56,48},{64,72... | collective-permute-start | bytes 1179656 | tf_op jit(solution)/shard_map/ppermute | solution.py:41
  24.4 14.5 %collective-permute-start.8 = (bf16[48,4096]{1,0:T(8,128)(2,1)S(1)}, bf16[48,4096]{1,0:T(8,128)(2,1)S(1)}, u32[]{:S(2)}, u32[]{:S(2)}) collective-permute-start(bf16[48,4096]{1,0:T(8,128)(2,1)S(1)} %concatenate.13.refs_0_), channel_id=1, source_target_pairs={{0,4},{8,140},{16,20},{24,156},{32,36},{40,172},{48,52},{56,188},{... | collective-permute-start | bytes 1179656 | tf_op jit(solution)/shard_map/ppermute | solution.py:41
  26.0 13.0 %collective-permute-start.10 = (bf16[48,4096]{1,0:T(8,128)(2,1)S(1)}, bf16[48,4096]{1,0:T(8,128)(2,1)S(1)}, u32[]{:S(2)}, u32[]{:S(2)}) collective-permute-start(bf16[48,4096]{1,0:T(8,128)(2,1)S(1)} %concatenate.13.refs_0_), channel_id=1, source_target_pairs={{0,132},{8,12},{16,148},{24,28},{32,164},{40,44},{48,180},{56,60},... | collective-permute-start | bytes 1179656 | tf_op jit(solution)/shard_map/ppermute | solution.py:41
  39.0 3.0 %collective-permute-start.11 = (bf16[48,4096]{1,0:T(8,128)(2,1)S(1)}, bf16[48,4096]{1,0:T(8,128)(2,1)S(1)}, u32[]{:S(2)}, u32[]{:S(2)}) collective-permute-start(bf16[48,4096]{1,0:T(8,128)(2,1)S(1)} %collective-permute-done.8.ready_ref.refs_0_), channel_id=1, source_target_pairs={{0,8},{8,0},{16,24},{24,16},{32,40},{40,32},{48,56},{56,48},{64,72... | collective-permute-start | bytes 1179656 | tf_op jit(solution)/shard_map/ppermute | solution.py:41
  39.1 2.9 %collective-permute-start.12 = (bf16[48,4096]{1,0:T(8,128)(2,1)S(1)}, bf16[48,4096]{1,0:T(8,128)(2,1)S(1)}, u32[]{:S(2)}, u32[]{:S(2)}) collective-permute-start(bf16[48,4096]{1,0:T(8,128)(2,1)S(1)} %collective-permute-done.10.refs_1_), channel_id=1, source_target_pairs={{0,8},{8,0},{16,24},{24,16},{32,40},{40,32},{48,56},{56,48},{64,72... | collective-permute-start | bytes 1179656 | tf_op jit(solution)/shard_map/ppermute | solution.py:41
  39.6 9.0 %collective-permute-start.9 = (bf16[48,4096]{1,0:T(8,128)(2,1)S(1)}, bf16[48,4096]{1,0:T(8,128)(2,1)S(1)}, u32[]{:S(2)}, u32[]{:S(2)}) collective-permute-start(bf16[48,4096]{1,0:T(8,128)(2,1)S(1)} %collective-permute-done.8.ready_ref.refs_0_), channel_id=1, source_target_pairs={{0,132},{8,12},{16,148},{24,28},{32,164},{40,44},{48,180},{56,60},... | collective-permute-start | bytes 1179656 | tf_op jit(solution)/shard_map/ppermute | solution.py:41
  57.5 5.0 %collective-permute-start.21 = (bf16[192,32]{1,0:T(8,128)(2,1)S(1)}, bf16[192,32]{1,0:T(8,128)(2,1)S(1)}, u32[]{:S(2)}, u32[]{:S(2)}) collective-permute-start(bf16[192,32]{1,0:T(8,128)(2,1)S(1)} %get-tuple-element.61.mine_ref), channel_id=1, source_target_pairs={{0,4},{4,0},{1,5},{5,1},{2,6},{6,2},{3,7},{7,3},{8,12},{12,8},{9,1... | collective-permute-start | bytes 36872 | tf_op jit(solution)/shard_map/ppermute | solution.py:405
  57.5 15.8 %collective-permute-start.14 = (bf16[48,4096]{1,0:T(8,128)(2,1)S(1)}, bf16[48,4096]{1,0:T(8,128)(2,1)S(1)}, u32[]{:S(2)}, u32[]{:S(2)}) collective-permute-start(bf16[48,4096]{1,0:T(8,128)(2,1)S(1)} %get-tuple-element.51), channel_id=1, source_target_pairs={{0,8},{8,0},{16,24},{24,16},{32,40},{40,32},{48,56},{56,48},{64,72... | collective-permute-start | bytes 1179656 | tf_op jit(solution)/shard_map/ppermute | solution.py:41
  59.2 9.1 %collective-permute-start.19 = (bf16[48,4096]{1,0:T(8,128)(2,1)S(1)}, bf16[48,4096]{1,0:T(8,128)(2,1)S(1)}, u32[]{:S(2)}, u32[]{:S(2)}) collective-permute-start(bf16[48,4096]{1,0:T(8,128)(2,1)S(1)} %add_convert_fusion.2), channel_id=1, source_target_pairs={{0,132},{8,12},{16,148},{24,28},{32,164},{40,44},{48,180},{56,60},... | collective-permute-start | bytes 1179656 | tf_op jit(solution)/shard_map/ppermute | solution.py:41
  62.4 1.9 %collective-permute-start.18 = (bf16[48,4096]{1,0:T(8,128)(2,1)S(1)}, bf16[48,4096]{1,0:T(8,128)(2,1)S(1)}, u32[]{:S(2)}, u32[]{:S(2)}) collective-permute-start(bf16[48,4096]{1,0:T(8,128)(2,1)S(1)} %get-tuple-element.60), channel_id=1, source_target_pairs={{0,8},{8,0},{16,24},{24,16},{32,40},{40,32},{48,56},{56,48},{64,72... | collective-permute-start | bytes 1179656 | tf_op jit(solution)/shard_map/ppermute | solution.py:41
  63.3 6.2 %collective-permute-start.22 = (bf16[16,4352]{1,0:T(8,128)(2,1)S(1)}, bf16[16,4352]{1,0:T(8,128)(2,1)S(1)}, u32[]{:S(2)}, u32[]{:S(2)}) collective-permute-start(bf16[16,4352]{1,0:T(8,128)(2,1)S(1)} %get-tuple-element.80), channel_id=1, source_target_pairs={{0,1},{1,0},{2,3},{3,2},{4,5},{5,4},{6,7},{7,6},{8,9},{9,8},{10,11... | collective-permute-start | bytes 417800 | tf_op jit(solution)/shard_map/ppermute | solution.py:423
  64.1 5.6 %collective-permute-start.16 = (bf16[48,4096]{1,0:T(8,128)(2,1)S(1)}, bf16[48,4096]{1,0:T(8,128)(2,1)S(1)}, u32[]{:S(2)}, u32[]{:S(2)}) collective-permute-start(bf16[48,4096]{1,0:T(8,128)(2,1)S(1)} %get-tuple-element.58), channel_id=1, source_target_pairs={{0,8},{8,0},{16,24},{24,16},{32,40},{40,32},{48,56},{56,48},{64,72... | collective-permute-start | bytes 1179656 | tf_op jit(solution)/shard_map/ppermute | solution.py:41
  64.3 7.9 %collective-permute-start.24 = (bf16[16,4352]{1,0:T(8,128)(2,1)S(1)}, bf16[16,4352]{1,0:T(8,128)(2,1)S(1)}, u32[]{:S(2)}, u32[]{:S(2)}) collective-permute-start(bf16[16,4352]{1,0:T(8,128)(2,1)S(1)} %get-tuple-element.81), channel_id=1, source_target_pairs={{0,3},{1,2},{2,1},{3,0},{4,7},{5,6},{6,5},{7,4},{8,11},{9,10},{10,... | collective-permute-start | bytes 417800 | tf_op jit(solution)/shard_map/ppermute | solution.py:423
  68.4 11.8 %collective-permute-start.20 = (bf16[48,4096]{1,0:T(8,128)(2,1)S(1)}, bf16[48,4096]{1,0:T(8,128)(2,1)S(1)}, u32[]{:S(2)}, u32[]{:S(2)}) collective-permute-start(bf16[48,4096]{1,0:T(8,128)(2,1)S(1)} %add_convert_fusion), channel_id=1, source_target_pairs={{0,4},{8,140},{16,20},{24,156},{32,36},{40,172},{48,52},{56,188},{... | collective-permute-start | bytes 1179656 | tf_op jit(solution)/shard_map/ppermute | solution.py:41
  69.5 11.0 %collective-permute-start.23 = (bf16[16,4352]{1,0:T(8,128)(2,1)S(1)}, bf16[16,4352]{1,0:T(8,128)(2,1)S(1)}, u32[]{:S(2)}, u32[]{:S(2)}) collective-permute-start(bf16[16,4352]{1,0:T(8,128)(2,1)S(1)} %add_convert_fusion.6), channel_id=1, source_target_pairs={{0,3},{1,2},{2,1},{3,0},{4,7},{5,6},{6,5},{7,4},{8,11},{9,10},{10,... | collective-permute-start | bytes 417800 | tf_op jit(solution)/shard_map/ppermute | solution.py:431
  69.8 9.3 %collective-permute-start.17 = (bf16[48,4096]{1,0:T(8,128)(2,1)S(1)}, bf16[48,4096]{1,0:T(8,128)(2,1)S(1)}, u32[]{:S(2)}, u32[]{:S(2)}) collective-permute-start(bf16[48,4096]{1,0:T(8,128)(2,1)S(1)} %add_convert_fusion.1), channel_id=1, source_target_pairs={{0,132},{8,12},{16,148},{24,28},{32,164},{40,44},{48,180},{56,60},... | collective-permute-start | bytes 1179656 | tf_op jit(solution)/shard_map/ppermute | solution.py:41
  72.3 8.2 %collective-permute-start.25 = (bf16[16,4352]{1,0:T(8,128)(2,1)S(1)}, bf16[16,4352]{1,0:T(8,128)(2,1)S(1)}, u32[]{:S(2)}, u32[]{:S(2)}) collective-permute-start(bf16[16,4352]{1,0:T(8,128)(2,1)S(1)} %add_convert_fusion.4), channel_id=1, source_target_pairs={{0,1},{1,0},{2,3},{3,2},{4,5},{5,4},{6,7},{7,6},{8,9},{9,8},{10,11... | collective-permute-start | bytes 417800 | tf_op jit(solution)/shard_map/ppermute | solution.py:431
  80.6 10.0 %collective-permute-start.26 = (bf16[6,4096]{1,0:T(8,128)(2,1)S(1)}, bf16[6,4096]{1,0:T(8,128)(2,1)S(1)}, u32[]{:S(2)}, u32[]{:S(2)}) collective-permute-start(bf16[6,4096]{1,0:T(8,128)(2,1)S(1)} %get-tuple-element.73), channel_id=1, source_target_pairs={{0,64},{8,72},{16,80},{24,88},{32,96},{40,104},{48,112},{56,120},{... | collective-permute-start | bytes 147464 | tf_op jit(solution)/shard_map/ppermute | solution.py:41
  83.9 10.6 %collective-permute-start.27 = (bf16[6,4096]{1,0:T(8,128)(2,1)S(1)}, bf16[6,4096]{1,0:T(8,128)(2,1)S(1)}, u32[]{:S(2)}, u32[]{:S(2)}) collective-permute-start(bf16[6,4096]{1,0:T(8,128)(2,1)S(1)} %get-tuple-element.79), channel_id=1, source_target_pairs={{0,80},{8,88},{16,96},{24,104},{32,112},{40,120},{48,0},{56,8},{64... | collective-permute-start | bytes 147464 | tf_op jit(solution)/shard_map/ppermute | solution.py:41
  85.3 9.7 %collective-permute-start.28 = (bf16[6,4096]{1,0:T(8,128)(2,1)S(1)}, bf16[6,4096]{1,0:T(8,128)(2,1)S(1)}, u32[]{:S(2)}, u32[]{:S(2)}) collective-permute-start(bf16[6,4096]{1,0:T(8,128)(2,1)S(1)} %get-tuple-element.78), channel_id=1, source_target_pairs={{0,48},{8,56},{16,64},{24,72},{32,80},{40,88},{48,96},{56,104},{64... | collective-permute-start | bytes 147464 | tf_op jit(solution)/shard_map/ppermute | solution.py:41
  87.7 9.3 %collective-permute-start.29 = (bf16[6,4096]{1,0:T(8,128)(2,1)S(1)}, bf16[6,4096]{1,0:T(8,128)(2,1)S(1)}, u32[]{:S(2)}, u32[]{:S(2)}) collective-permute-start(bf16[6,4096]{1,0:T(8,128)(2,1)S(1)} %get-tuple-element.77), channel_id=1, source_target_pairs={{0,96},{8,104},{16,112},{24,120},{32,0},{40,8},{48,16},{56,24},{64... | collective-permute-start | bytes 147464 | tf_op jit(solution)/shard_map/ppermute | solution.py:41
  89.8 7.2 %collective-permute-start.30 = (bf16[6,4096]{1,0:T(8,128)(2,1)S(1)}, bf16[6,4096]{1,0:T(8,128)(2,1)S(1)}, u32[]{:S(2)}, u32[]{:S(2)}) collective-permute-start(bf16[6,4096]{1,0:T(8,128)(2,1)S(1)} %get-tuple-element.76), channel_id=1, source_target_pairs={{0,32},{8,40},{16,48},{24,56},{32,64},{40,72},{48,80},{56,88},{64,... | collective-permute-start | bytes 147464 | tf_op jit(solution)/shard_map/ppermute | solution.py:41
  90.6 7.2 %collective-permute-start.31 = (bf16[6,4096]{1,0:T(8,128)(2,1)S(1)}, bf16[6,4096]{1,0:T(8,128)(2,1)S(1)}, u32[]{:S(2)}, u32[]{:S(2)}) collective-permute-start(bf16[6,4096]{1,0:T(8,128)(2,1)S(1)} %get-tuple-element.75), channel_id=1, source_target_pairs={{0,112},{8,120},{16,0},{24,8},{32,16},{40,24},{48,32},{56,40},{64,... | collective-permute-start | bytes 147464 | tf_op jit(solution)/shard_map/ppermute | solution.py:41
  94.5 5.5 %collective-permute-start.32 = (bf16[6,4096]{1,0:T(8,128)(2,1)S(1)}, bf16[6,4096]{1,0:T(8,128)(2,1)S(1)}, u32[]{:S(2)}, u32[]{:S(2)}) collective-permute-start(bf16[6,4096]{1,0:T(8,128)(2,1)S(1)} %get-tuple-element.74), channel_id=1, source_target_pairs={{0,16},{8,24},{16,32},{24,40},{32,48},{40,56},{48,64},{56,72},{64,... | collective-permute-start | bytes 147464 | tf_op jit(solution)/shard_map/ppermute | solution.py:41
  95.0 7.8 %collective-permute-start.33 = (bf16[32,4352]{1,0:T(8,128)(2,1)S(1)}, bf16[32,4352]{1,0:T(8,128)(2,1)S(1)}, u32[]{:S(2)}, u32[]{:S(2)}) collective-permute-start(bf16[32,4352]{1,0:T(8,128)(2,1)S(1)} %pad_maximum_fusion.mine_ref), channel_id=1, source_target_pairs={{0,4},{4,0},{1,5},{5,1},{2,6},{6,2},{3,7},{7,3},{8,12},{12,8},{9,1... | collective-permute-start | bytes 835592 | tf_op jit(solution)/shard_map/ppermute | solution.py:441
  (11 other events, 23.4 us)
